TPU v7x, 32 devices: a whole 2x2x4 slice. The times are simulated.
32 devices in a mesh: ctx: 8 (over z, core), fsdp: 4 (over y, x).
Axes of the slice: x: 2, y: 2, z: 4, core: 2. Of those that a mesh axis runs over, the one named last changes fastest.
Arguments:
- layer_input: bfloat16 [4, 8192, 1024], P('fsdp', 'ctx'), may hold values from -6 to 6
- teacher_states: bfloat16 [4, 8192, 1024], P('fsdp', 'ctx'), may hold values from -6 to 6
- out_cotangent: bfloat16 [4, 8192, 1024], P('fsdp', 'ctx'), may hold values from -6 to 6
- doc_start: int32 [4, 8192], P('fsdp'), may hold values from 0 to 8191, as said below
- valid_flag: int32 [4, 8192], P('fsdp', 'ctx'), may hold values from 0 to 1
- query_weight: bfloat16 [1024, 1024], P('fsdp'), may hold values from -0.1875 to 0.1875
- query_bias: bfloat16 [1024], P('fsdp'), may hold values from -3 to 3
- key_weight: bfloat16 [1024, 1024], P('fsdp'), may hold values from -0.1875 to 0.1875
- value_weight: bfloat16 [1024, 1024], P('fsdp'), may hold values from -0.1875 to 0.1875
- value_bias: bfloat16 [1024], P('fsdp'), may hold values from -3 to 3
- proj_weight: bfloat16 [1024, 1024], P('fsdp'), may hold values from -1 to 1
- proj_bias: bfloat16 [1024], P('fsdp'), may hold values from -3 to 3
- attn_gain: bfloat16 [1024], P('fsdp'), may hold values from 0.5 to 1.5
- attn_shift: bfloat16 [1024], P('fsdp'), may hold values from -3 to 3
- inner_weight: bfloat16 [1024, 4096], P('fsdp'), may hold values from -0.1875 to 0.1875
- inner_bias: bfloat16 [4096], P('fsdp'), may hold values from -3 to 3
- outer_weight: bfloat16 [4096, 1024], P('fsdp'), may hold values from -0.09375 to 0.09375
- outer_bias: bfloat16 [1024], P('fsdp'), may hold values from -3 to 3
- final_gain: bfloat16 [1024], P('fsdp'), may hold values from 0.5 to 1.5
- final_shift: bfloat16 [1024], P('fsdp'), may hold values from -3 to 3
Outputs:
- layer_output: bfloat16 [4, 8192, 1024], P('fsdp', 'ctx')
- input_grad: float32 [4, 8192, 1024], P('fsdp', 'ctx')
- mse: float32 [], replicated
- query_weight_grad: float32 [1024, 1024], P('fsdp')
- query_bias_grad: float32 [1024], P('fsdp')
- key_weight_grad: float32 [1024, 1024], P('fsdp')
- value_weight_grad: float32 [1024, 1024], P('fsdp')
- value_bias_grad: float32 [1024], P('fsdp')
- proj_weight_grad: float32 [1024, 1024], P('fsdp')
- proj_bias_grad: float32 [1024], P('fsdp')
- attn_gain_grad: float32 [1024], P('fsdp')
- attn_shift_grad: float32 [1024], P('fsdp')
- inner_weight_grad: float32 [1024, 4096], P('fsdp')
- inner_bias_grad: float32 [4096], P('fsdp')
- outer_weight_grad: float32 [4096, 1024], P('fsdp')
- outer_bias_grad: float32 [1024], P('fsdp')
- final_gain_grad: float32 [1024], P('fsdp')
- final_shift_grad: float32 [1024], P('fsdp')
Inputs may be any that keep to these rules, and one draw needn't show every extreme that they name: doc_start[p, t] is the position in pack p of the first token of the document holding token t: it never falls along t, equals t where a document begins, and t - 512 < doc_start[p, t] <= t; every pack holds a document of exactly 512 tokens.
All inputs are finite; a program needn't handle non-finite values.
Results may differ from a plain program's by a relative error of at most 0.02.
Values may be sent and summed in bfloat16 or wider, within the bound.
No kernel may reach another device: no remote copies, remote signals or barrier semaphores. Data moves between devices by JAX's collectives and lax.ppermute only.
A program may use at most 448 MiB of HBM per device.

v0:
```python
import jax
import jax.numpy as jnp
from jax import lax
from jax.sharding import PartitionSpec as P

D = 1024
HEADS = 16
HEAD = 64
DOC_MAX = 512
QB = 512


norm_eps = 1e-05
masked_score = -1e30


def padded(block, sides, width):
    for axis, dim in sides:
        count = lax.axis_size(axis)
        forward = [(i, i + 1) for i in range(count - 1)]
        backward = [(target, source) for source, target in forward]
        low = lax.ppermute(
            lax.slice_in_dim(block, block.shape[dim] - width, None, axis=dim), axis, forward
        )
        high = lax.ppermute(lax.slice_in_dim(block, 0, width, axis=dim), axis, backward)
        block = jnp.concatenate([low, block, high], axis=dim)
    return block


def from_behind(value, axis, by):
    count = lax.axis_size(axis)
    pairs = [(i, i + by) for i in range(count) if 0 <= i + by < count]
    return lax.ppermute(value, axis, pairs)


def norm_rows(hidden, gain, shift):
    center = hidden - jnp.mean(hidden, axis=-1, keepdims=True)
    spread = jnp.mean(center * center, axis=-1, keepdims=True)
    return center * lax.rsqrt(spread + norm_eps) * gain + shift


def exact_gelu(value):
    return jax.nn.gelu(value, approximate=False)


def product(left, right):
    return jnp.dot(left, right, preferred_element_type=jnp.float32)


def gram_rows(left, right):
    return lax.dot_general(
        left, right, (((0,), (0,)), ((), ())), preferred_element_type=jnp.float32
    )


def back_product(left, right):
    return lax.dot_general(
        left, right, (((1,), (1,)), ((), ())), preferred_element_type=jnp.float32
    )


def column_sum(values):
    return jnp.sum(values.astype(jnp.float32), axis=0)


def split_rows(grad, first, second):
    return grad.reshape((first, second, grad.shape[0] // (first * second)) + grad.shape[1:])


def join_rows(grad):
    return grad.reshape((grad.shape[0] * grad.shape[1] * grad.shape[2],) + grad.shape[3:])


def body(
    layer_input,
    teacher_states,
    out_cotangent,
    doc_start,
    valid_flag,
    query_weight,
    query_bias,
    key_weight,
    value_weight,
    value_bias,
    proj_weight,
    proj_bias,
    attn_gain,
    attn_shift,
    inner_weight,
    inner_bias,
    outer_weight,
    outer_bias,
    final_gain,
    final_shift,
):
    (
        w_query,
        b_query,
        w_key,
        w_value,
        b_value,
        w_proj,
        b_proj,
        g_attn,
        s_attn,
        w_inner,
        b_inner,
        w_outer,
        b_outer,
        g_final,
        s_final,
    ) = (
        lax.all_gather(query_weight, "fsdp", axis=0, tiled=True),
        lax.all_gather(query_bias, "fsdp", axis=0, tiled=True),
        lax.all_gather(key_weight, "fsdp", axis=0, tiled=True),
        lax.all_gather(value_weight, "fsdp", axis=0, tiled=True),
        lax.all_gather(value_bias, "fsdp", axis=0, tiled=True),
        lax.all_gather(proj_weight, "fsdp", axis=0, tiled=True),
        lax.all_gather(proj_bias, "fsdp", axis=0, tiled=True),
        lax.all_gather(attn_gain, "fsdp", axis=0, tiled=True),
        lax.all_gather(attn_shift, "fsdp", axis=0, tiled=True),
        lax.all_gather(inner_weight, "fsdp", axis=0, tiled=True),
        lax.all_gather(inner_bias, "fsdp", axis=0, tiled=True),
        lax.all_gather(outer_weight, "fsdp", axis=0, tiled=True),
        lax.all_gather(outer_bias, "fsdp", axis=0, tiled=True),
        lax.all_gather(final_gain, "fsdp", axis=0, tiled=True),
        lax.all_gather(final_shift, "fsdp", axis=0, tiled=True),
    )
    tokens = layer_input[0]
    rows = tokens.shape[0]
    width = D
    rim = DOC_MAX
    block = QB
    span = block + 2 * rim
    count_blocks = rows // block
    scale = HEAD ** (-0.5)
    n_ctx = lax.axis_size("ctx")
    n_fsdp = lax.axis_size("fsdp")
    position = lax.axis_index("ctx") * rows
    starts = doc_start[0] + 1
    pad_ids = jnp.zeros((rim,), jnp.int32)
    padded_ids = jnp.concatenate([pad_ids, starts, pad_ids], axis=0)
    own_ids = lax.dynamic_slice_in_dim(starts, position, rows)
    near_ids = lax.dynamic_slice_in_dim(padded_ids, position, rows + 2 * rim)
    w_joined = jnp.concatenate([w_query, w_key, w_value], axis=1)
    bias_joined = jnp.concatenate([b_query, jnp.zeros_like(b_value), b_value]).astype(jnp.float32)
    joined = (product(tokens, w_joined) + bias_joined).astype(jnp.bfloat16)
    query = joined[:, :width]
    keys_values = joined[:, width:]
    near = padded(keys_values, (("ctx", 0),), rim)

    def block_scores(index):
        begin = index * block
        query_block = lax.dynamic_slice_in_dim(query, begin, block).reshape(block, HEADS, HEAD)
        near_block = lax.dynamic_slice_in_dim(near, begin, span)
        key_block = near_block[:, :width].reshape(span, HEADS, HEAD)
        value_block = near_block[:, width:].reshape(span, HEADS, HEAD)
        seen = (
            lax.dynamic_slice_in_dim(own_ids, begin, block)[:, None]
            == lax.dynamic_slice_in_dim(near_ids, begin, span)[None, :]
        )
        scores = (
            jnp.einsum("qhd,khd->hqk", query_block, key_block, preferred_element_type=jnp.float32)
            * scale
        )
        scores = jnp.where(seen[None], scores, masked_score)
        return (query_block, key_block, value_block, scores)

    def forward_block(index):
        query_block, key_block, value_block, scores = block_scores(index)
        top = jnp.max(scores, axis=-1, keepdims=True)
        weights = jnp.exp(scores - top)
        total = jnp.sum(weights, axis=-1, keepdims=True)
        probs = weights / total
        mixed = jnp.einsum(
            "hqk,khd->qhd",
            probs.astype(jnp.bfloat16),
            value_block,
            preferred_element_type=jnp.float32,
        )
        return (mixed.reshape(block, width).astype(jnp.bfloat16), (top + jnp.log(total))[..., 0])

    context_blocks, log_totals = lax.map(forward_block, jnp.arange(count_blocks, dtype=jnp.int32))
    context = context_blocks.reshape(rows, width)
    attn_out = product(context, w_proj) + b_proj.astype(jnp.float32)
    resid_one = tokens.astype(jnp.float32) + attn_out
    normed, norm_one_back = jax.vjp(
        norm_rows, resid_one, g_attn.astype(jnp.float32), s_attn.astype(jnp.float32)
    )
    normed_low = normed.astype(jnp.bfloat16)
    pre_act = product(normed_low, w_inner) + b_inner.astype(jnp.float32)
    activated, gelu_back = jax.vjp(exact_gelu, pre_act)
    act_low = activated.astype(jnp.bfloat16)
    branch = product(act_low, w_outer) + b_outer.astype(jnp.float32)
    final, norm_two_back = jax.vjp(
        norm_rows, normed + branch, g_final.astype(jnp.float32), s_final.astype(jnp.float32)
    )
    flags = valid_flag[0].astype(jnp.float32)
    error = final - teacher_states[0].astype(jnp.float32)
    count, sq_err = lax.psum(
        (jnp.sum(flags), jnp.sum(flags[:, None] * error * error)), ("ctx", "fsdp")
    )
    mse = sq_err / (count * width)
    all_tokens = n_fsdp * n_ctx * rows
    d_final = out_cotangent[0].astype(jnp.float32) + all_tokens / count * flags[:, None] * error
    d_sum_two, final_gain_grad, final_shift_grad = norm_two_back(d_final)
    d_branch = d_sum_two.astype(jnp.bfloat16)
    outer_weight_grad = gram_rows(act_low, d_branch)
    outer_bias_grad = column_sum(d_branch)
    (d_pre_full,) = gelu_back(back_product(d_branch, w_outer))
    d_pre = d_pre_full.astype(jnp.bfloat16)
    inner_weight_grad = gram_rows(normed_low, d_pre)
    inner_bias_grad = column_sum(d_pre)
    d_normed = d_sum_two + back_product(d_pre, w_inner)
    d_sum_one, attn_gain_grad, attn_shift_grad = norm_one_back(d_normed)
    d_attn = d_sum_one.astype(jnp.bfloat16)
    proj_weight_grad = gram_rows(context, d_attn)
    proj_bias_grad = column_sum(d_attn)
    d_context = back_product(d_attn, w_proj).astype(jnp.bfloat16)

    def backward_block(carry, index):
        query_block, key_block, value_block, scores = block_scores(index)
        log_total = lax.dynamic_index_in_dim(log_totals, index, 0, keepdims=False)
        probs = jnp.exp(scores - log_total[..., None])
        begin = index * block
        grad_block = lax.dynamic_slice_in_dim(d_context, begin, block).reshape(block, HEADS, HEAD)
        d_probs = jnp.einsum(
            "qhd,khd->hqk", grad_block, value_block, preferred_element_type=jnp.float32
        )
        d_scores = (probs * (d_probs - jnp.sum(probs * d_probs, axis=-1, keepdims=True))).astype(
            jnp.bfloat16
        )
        d_query = (
            jnp.einsum("hqk,khd->qhd", d_scores, key_block, preferred_element_type=jnp.float32)
            * scale
        )
        d_keys = (
            jnp.einsum("hqk,qhd->khd", d_scores, query_block, preferred_element_type=jnp.float32)
            * scale
        )
        d_values = jnp.einsum(
            "hqk,qhd->khd",
            probs.astype(jnp.bfloat16),
            grad_block,
            preferred_element_type=jnp.float32,
        )
        update = jnp.concatenate(
            [d_keys.reshape(span, width), d_values.reshape(span, width)], axis=1
        )
        current = lax.dynamic_slice_in_dim(carry, begin, span)
        carry = lax.dynamic_update_slice_in_dim(carry, current + update, begin, 0)
        return (carry, d_query.reshape(block, width))

    near_grads, query_grad_blocks = lax.scan(
        backward_block,
        jnp.zeros((rows + 2 * rim, 2 * width), jnp.float32),
        jnp.arange(count_blocks, dtype=jnp.int32),
    )
    from_above = from_behind(near_grads[:rim].astype(jnp.bfloat16), "ctx", -1).astype(jnp.float32)
    from_below = from_behind(near_grads[rows + rim :].astype(jnp.bfloat16), "ctx", 1).astype(
        jnp.float32
    )
    own_grads = near_grads[rim : rim + rows]
    own_grads = own_grads.at[:rim].add(from_below)
    own_grads = own_grads.at[rows - rim :].add(from_above)
    d_joined = jnp.concatenate(
        [
            query_grad_blocks.reshape(rows, width).astype(jnp.bfloat16),
            own_grads.astype(jnp.bfloat16),
        ],
        axis=1,
    )
    joined_weight_grad = gram_rows(tokens, d_joined)
    joined_sums = column_sum(d_joined)
    input_grad = d_sum_one + back_product(d_joined, w_joined)
    grads = (
        joined_weight_grad[:, :width],
        joined_sums[:width],
        joined_weight_grad[:, width : 2 * width],
        joined_weight_grad[:, 2 * width :],
        joined_sums[2 * width :],
        proj_weight_grad,
        proj_bias_grad,
        attn_gain_grad,
        attn_shift_grad,
        inner_weight_grad,
        inner_bias_grad,
        outer_weight_grad,
        outer_bias_grad,
        final_gain_grad,
        final_shift_grad,
    )
    sectioned = [split_rows(grad, n_fsdp, n_ctx) for grad in grads]
    by_ctx = (
        lax.psum_scatter(
            sectioned[0].astype(jnp.bfloat16), "ctx", scatter_dimension=1, tiled=True
        ).astype(jnp.float32),
        lax.psum_scatter(
            sectioned[1].astype(jnp.bfloat16), "ctx", scatter_dimension=1, tiled=True
        ).astype(jnp.float32),
        lax.psum_scatter(
            sectioned[2].astype(jnp.bfloat16), "ctx", scatter_dimension=1, tiled=True
        ).astype(jnp.float32),
        lax.psum_scatter(
            sectioned[3].astype(jnp.bfloat16), "ctx", scatter_dimension=1, tiled=True
        ).astype(jnp.float32),
        lax.psum_scatter(
            sectioned[4].astype(jnp.bfloat16), "ctx", scatter_dimension=1, tiled=True
        ).astype(jnp.float32),
        lax.psum_scatter(
            sectioned[5].astype(jnp.bfloat16), "ctx", scatter_dimension=1, tiled=True
        ).astype(jnp.float32),
        lax.psum_scatter(
            sectioned[6].astype(jnp.bfloat16), "ctx", scatter_dimension=1, tiled=True
        ).astype(jnp.float32),
        lax.psum_scatter(
            sectioned[7].astype(jnp.bfloat16), "ctx", scatter_dimension=1, tiled=True
        ).astype(jnp.float32),
        lax.psum_scatter(
            sectioned[8].astype(jnp.bfloat16), "ctx", scatter_dimension=1, tiled=True
        ).astype(jnp.float32),
        lax.psum_scatter(
            sectioned[9].astype(jnp.bfloat16), "ctx", scatter_dimension=1, tiled=True
        ).astype(jnp.float32),
        lax.psum_scatter(
            sectioned[10].astype(jnp.bfloat16), "ctx", scatter_dimension=1, tiled=True
        ).astype(jnp.float32),
        lax.psum_scatter(
            sectioned[11].astype(jnp.bfloat16), "ctx", scatter_dimension=1, tiled=True
        ).astype(jnp.float32),
        lax.psum_scatter(
            sectioned[12].astype(jnp.bfloat16), "ctx", scatter_dimension=1, tiled=True
        ).astype(jnp.float32),
        lax.psum_scatter(
            sectioned[13].astype(jnp.bfloat16), "ctx", scatter_dimension=1, tiled=True
        ).astype(jnp.float32),
        lax.psum_scatter(
            sectioned[14].astype(jnp.bfloat16), "ctx", scatter_dimension=1, tiled=True
        ).astype(jnp.float32),
    )
    by_both = (
        lax.psum_scatter(
            by_ctx[0].astype(jnp.bfloat16), "fsdp", scatter_dimension=0, tiled=True
        ).astype(jnp.float32),
        lax.psum_scatter(
            by_ctx[1].astype(jnp.bfloat16), "fsdp", scatter_dimension=0, tiled=True
        ).astype(jnp.float32),
        lax.psum_scatter(
            by_ctx[2].astype(jnp.bfloat16), "fsdp", scatter_dimension=0, tiled=True
        ).astype(jnp.float32),
        lax.psum_scatter(
            by_ctx[3].astype(jnp.bfloat16), "fsdp", scatter_dimension=0, tiled=True
        ).astype(jnp.float32),
        lax.psum_scatter(
            by_ctx[4].astype(jnp.bfloat16), "fsdp", scatter_dimension=0, tiled=True
        ).astype(jnp.float32),
        lax.psum_scatter(
            by_ctx[5].astype(jnp.bfloat16), "fsdp", scatter_dimension=0, tiled=True
        ).astype(jnp.float32),
        lax.psum_scatter(
            by_ctx[6].astype(jnp.bfloat16), "fsdp", scatter_dimension=0, tiled=True
        ).astype(jnp.float32),
        lax.psum_scatter(
            by_ctx[7].astype(jnp.bfloat16), "fsdp", scatter_dimension=0, tiled=True
        ).astype(jnp.float32),
        lax.psum_scatter(
            by_ctx[8].astype(jnp.bfloat16), "fsdp", scatter_dimension=0, tiled=True
        ).astype(jnp.float32),
        lax.psum_scatter(
            by_ctx[9].astype(jnp.bfloat16), "fsdp", scatter_dimension=0, tiled=True
        ).astype(jnp.float32),
        lax.psum_scatter(
            by_ctx[10].astype(jnp.bfloat16), "fsdp", scatter_dimension=0, tiled=True
        ).astype(jnp.float32),
        lax.psum_scatter(
            by_ctx[11].astype(jnp.bfloat16), "fsdp", scatter_dimension=0, tiled=True
        ).astype(jnp.float32),
        lax.psum_scatter(
            by_ctx[12].astype(jnp.bfloat16), "fsdp", scatter_dimension=0, tiled=True
        ).astype(jnp.float32),
        lax.psum_scatter(
            by_ctx[13].astype(jnp.bfloat16), "fsdp", scatter_dimension=0, tiled=True
        ).astype(jnp.float32),
        lax.psum_scatter(
            by_ctx[14].astype(jnp.bfloat16), "fsdp", scatter_dimension=0, tiled=True
        ).astype(jnp.float32),
    )
    gathered = (
        lax.all_gather(by_both[0].astype(jnp.bfloat16), "ctx", axis=1, tiled=True).astype(
            jnp.float32
        ),
        lax.all_gather(by_both[1].astype(jnp.bfloat16), "ctx", axis=1, tiled=True).astype(
            jnp.float32
        ),
        lax.all_gather(by_both[2].astype(jnp.bfloat16), "ctx", axis=1, tiled=True).astype(
            jnp.float32
        ),
        lax.all_gather(by_both[3].astype(jnp.bfloat16), "ctx", axis=1, tiled=True).astype(
            jnp.float32
        ),
        lax.all_gather(by_both[4].astype(jnp.bfloat16), "ctx", axis=1, tiled=True).astype(
            jnp.float32
        ),
        lax.all_gather(by_both[5].astype(jnp.bfloat16), "ctx", axis=1, tiled=True).astype(
            jnp.float32
        ),
        lax.all_gather(by_both[6].astype(jnp.bfloat16), "ctx", axis=1, tiled=True).astype(
            jnp.float32
        ),
        lax.all_gather(by_both[7].astype(jnp.bfloat16), "ctx", axis=1, tiled=True).astype(
            jnp.float32
        ),
        lax.all_gather(by_both[8].astype(jnp.bfloat16), "ctx", axis=1, tiled=True).astype(
            jnp.float32
        ),
        lax.all_gather(by_both[9].astype(jnp.bfloat16), "ctx", axis=1, tiled=True).astype(
            jnp.float32
        ),
        lax.all_gather(by_both[10].astype(jnp.bfloat16), "ctx", axis=1, tiled=True).astype(
            jnp.float32
        ),
        lax.all_gather(by_both[11].astype(jnp.bfloat16), "ctx", axis=1, tiled=True).astype(
            jnp.float32
        ),
        lax.all_gather(by_both[12].astype(jnp.bfloat16), "ctx", axis=1, tiled=True).astype(
            jnp.float32
        ),
        lax.all_gather(by_both[13].astype(jnp.bfloat16), "ctx", axis=1, tiled=True).astype(
            jnp.float32
        ),
        lax.all_gather(by_both[14].astype(jnp.bfloat16), "ctx", axis=1, tiled=True).astype(
            jnp.float32
        ),
    )
    reduced = [join_rows(grad) for grad in gathered]
    layer_out = final.astype(jnp.bfloat16)[None]
    return (
        layer_out,
        input_grad[None],
        mse,
        reduced[0],
        reduced[1],
        reduced[2],
        reduced[3],
        reduced[4],
        reduced[5],
        reduced[6],
        reduced[7],
        reduced[8],
        reduced[9],
        reduced[10],
        reduced[11],
        reduced[12],
        reduced[13],
        reduced[14],
    )


def solution(mesh):
    return jax.shard_map(
        body,
        mesh=mesh,
        in_specs=(
            P("fsdp", "ctx", None),
            P("fsdp", "ctx", None),
            P("fsdp", "ctx", None),
            P("fsdp", None),
            P("fsdp", "ctx"),
            P("fsdp", None),
            P("fsdp"),
            P("fsdp", None),
            P("fsdp", None),
            P("fsdp"),
            P("fsdp", None),
            P("fsdp"),
            P("fsdp"),
            P("fsdp"),
            P("fsdp", None),
            P("fsdp"),
            P("fsdp", None),
            P("fsdp"),
            P("fsdp"),
            P("fsdp"),
        ),
        out_specs=(
            P("fsdp", "ctx", None),
            P("fsdp", "ctx", None),
            P(),
            P("fsdp", None),
            P("fsdp"),
            P("fsdp", None),
            P("fsdp", None),
            P("fsdp"),
            P("fsdp", None),
            P("fsdp"),
            P("fsdp"),
            P("fsdp"),
            P("fsdp", None),
            P("fsdp"),
            P("fsdp", None),
            P("fsdp"),
            P("fsdp"),
            P("fsdp"),
        ),
        check_vma=False,
    )
```

profile of v0, /device:TPU:0, one launch (start us, length us, event | category | flops | bytes accessed | tf_op | source)
XLA Modules:
  0.0 1761.1 jit_solution(16351387774469154030)
XLA Ops:
  12.0 9.5 all-gather
  21.5 8.0 all-gather.1
  33.6 7.1 all-gather.2
  41.3 8.0 all-gather.3
  49.9 7.1 all-gather.4
  57.6 8.0 all_gather.100
  66.3 7.1 all-gather.5
  73.9 39.9 %psum.14 = f32[]{:T(128)} all-reduce(f32[]{:T(128)} %convert_reduce_fusion.8), channel_id=1, replica_groups=mesh['ctx'=8,'fsdp'=4] {'ctx','fsdp'}, use_global_device_ids=true, to_apply=%region_9.10 | all-reduce | flops 1 | bytes 8 | tf_op jit(solution)/shard_map/psum | solution.py:200
  120.3 9.1 all-gather.6
  129.9 8.0 all-gather.7
  149.3 9.7 fusion.19
  171.6 7.2 pad_maximum_fusion
  178.8 11.9 copy.131
  190.6 151.8 %while.26 = (s32[]{:T(128)}, bf16[2,512,1024]{2,1,0:T(8,128)(2,1)}, f32[2,16,512]{2,1,0:T(8,128)S(1)}, s32[2]{0:T(128)S(1)}, bf16[2048,2048]{0,1:T(8,128)(2,1)},...) while((s32[]{:T(128)}, bf16[2,512,1024]{2,1,0:T(8,128)(2,1)}, ...), condition=%wide.region_3.4_spmd, body=%wide.region_0.3_spmd.sunk | while | flops 3373522944 | bytes 193225536 | solution.py:183
  199.5 20.6 %fusion.120 = (f32[16,512]{1,0:T(8,128)S(1)}, f32[16,512,1536]{2,1,0:T(8,128)}) fusion(pred[512,1536]{1,0:T(8,128)(4,1)} %broadcast_compare_fusion.4, bf16[512,16,64]{0,2,1:T(8,128)(2,1)} %bitcast.273, bf16[1536,16,64]{0,2,1:T(8,128)(2,1)S(1)} %bitcast.267), kind=kOutput, calls=%fused_computation.3.clone.1 | convolution fusion | flops 1648353280 | bytes 55345152 | tf_op jit(solution)/shard_map/while/body/eval_jaxpr/qhd,khd->hqk/dot_general | solution.py:163
  220.1 22.2 %fusion.121 = f32[16,512]{1,0:T(8,128)S(1)} fusion(f32[16,512,1536]{2,1,0:T(8,128)} %get-tuple-element.543, f32[16,512]{1,0:T(8,128)S(1)} %get-tuple-element.544, pred[512,1536]{1,0:T(8,128)(4,1)} %broadcast_compare_fusion.4), kind=kLoop, calls=%fused_computation.4.clone.1 | loop fusion | flops 50323456 | bytes 51183616 | tf_op jit(solution)/shard_map/while/body/eval_jaxpr/reduce_sum | solution.py:173
  242.4 22.6 %fusion.122 = bf16[16,64,512]{2,1,0:T(8,128)(2,1)S(1)} fusion(bf16[1536,16,64]{0,2,1:T(8,128)(2,1)} %bitcast.276, f32[16,512,1536]{2,1,0:T(8,128)} %get-tuple-element.543, f32[16,512]{1,0:T(8,128)S(1)} %fusion.121, f32[16,512]{1,0:T(8,128)S(1)} %get-tuple-element.544, pred[512,1536]{1,0:T(8,128)(4,1)S(1)} %copy-done.1), kind=kOutput, calls=%fused_computation.7.clone.1 | convolution fusion | flops 1674051584 | bytes 55377920 | tf_op jit(solution)/shard_map/while/body/eval_jaxpr/hqk,khd->qhd/dot_general | solution.py:175
  275.5 21.7 %fusion.120 = (f32[16,512]{1,0:T(8,128)S(1)}, f32[16,512,1536]{2,1,0:T(8,128)}) fusion(pred[512,1536]{1,0:T(8,128)(4,1)} %broadcast_compare_fusion.4, bf16[512,16,64]{0,2,1:T(8,128)(2,1)} %bitcast.273, bf16[1536,16,64]{0,2,1:T(8,128)(2,1)S(1)} %bitcast.267), kind=kOutput, calls=%fused_computation.3.clone.1 | convolution fusion | flops 1648353280 | bytes 55345152 | tf_op jit(solution)/shard_map/while/body/eval_jaxpr/qhd,khd->hqk/dot_general | solution.py:163
  297.1 22.2 %fusion.121 = f32[16,512]{1,0:T(8,128)S(1)} fusion(f32[16,512,1536]{2,1,0:T(8,128)} %get-tuple-element.543, f32[16,512]{1,0:T(8,128)S(1)} %get-tuple-element.544, pred[512,1536]{1,0:T(8,128)(4,1)} %broadcast_compare_fusion.4), kind=kLoop, calls=%fused_computation.4.clone.1 | loop fusion | flops 50323456 | bytes 51183616 | tf_op jit(solution)/shard_map/while/body/eval_jaxpr/reduce_sum | solution.py:173
  319.4 21.4 %fusion.122 = bf16[16,64,512]{2,1,0:T(8,128)(2,1)S(1)} fusion(bf16[1536,16,64]{0,2,1:T(8,128)(2,1)} %bitcast.276, f32[16,512,1536]{2,1,0:T(8,128)} %get-tuple-element.543, f32[16,512]{1,0:T(8,128)S(1)} %fusion.121, f32[16,512]{1,0:T(8,128)S(1)} %get-tuple-element.544, pred[512,1536]{1,0:T(8,128)(4,1)S(1)} %copy-done.1), kind=kOutput, calls=%fused_computation.7.clone.1 | convolution fusion | flops 1674051584 | bytes 55377920 | tf_op jit(solution)/shard_map/while/body/eval_jaxpr/hqk,khd->qhd/dot_general | solution.py:175
  355.0 47.8 %multiply_convert_fusion.1 = (bf16[1024,4096]{1,0:T(8,128)(2,1)}, f32[1024,4096]{1,0:T(8,128)}, f32[1024,4096]{1,0:T(8,128)}) fusion(f32[4096]{0:T(1024)S(1)} %copy-done.37, bf16[1024,4096]{1,0:T(8,128)(2,1)} %all-gather.25.cloned.1.call-done, bf16[1024,1024]{0,1:T(8,128)(2,1)S(1)} %fusion.51.clone.4), kind=kOutput, calls=%fused_computation.35 | convolution fusion | flops 8866758656 | bytes 52445184 | tf_op jit(solution)/shard_map/dot_general | solution.py:47
  402.9 15.1 fusion.64
  430.2 24.8 %fusion.53 = (bf16[4096]{0:T(1024)(128)(2,1)}, bf16[1024,4096]{1,0:T(8,128)(2,1)}) fusion(f32[1024,4096]{1,0:T(8,128)} %get-tuple-element.400, f32[1024,4096]{1,0:T(8,128)} %get-tuple-element.421, f32[4096]{0:T(1024)S(1)} %copy-done.37, bf16[1024,1024]{0,1:T(8,128)(2,1)S(1)} %get-tuple-element.390, bf16[4096,1024]{1,0:T(8,128)(2,1)} %all-gather.27.cloned.1.call-done), kind=kOutput, calls=%fused_computation.164 | convolution fusion | flops 8657039360 | bytes 52453376 | tf_op jit(solution)/shard_map/dot_general | solution.py:57
  454.9 15.1 convolution_convert_fusion.1
  470.0 15.7 multiply_reduce_fusion.2
  493.7 7.9 broadcast_in_dim.97
  501.6 356.5 %while.27 = (s32[]{:T(128)}, f32[2048,2048]{0,1:T(8,128)}, bf16[2,512,1024]{2,1,0:T(8,128)(2,1)}, s32[2]{0:T(128)S(1)}, bf16[1024,1024]{0,1:T(8,128)(2,1)}, /*in...) while((s32[]{:T(128)}, f32[2048,2048]{0,1:T(8,128)}, ...), condition=%wide.region_16.17_spmd, body=%wide.region_14.16_spmd.sunk | while | flops 8251498496 | bytes 476308320 | solution.py:254
  510.2 20.7 %fusion.134 = f32[16,512,1536]{2,1,0:T(8,128)} fusion(bf16[512,16,64]{0,2,1:T(8,128)(2,1)} %bitcast.269, bf16[1536,16,64]{0,2,1:T(8,128)(2,1)S(1)} %bitcast.262), kind=kOutput, calls=%fused_computation.175.clone.1 | convolution fusion | flops 1610612736 | bytes 54525952 | tf_op jit(solution)/shard_map/while/body/eval_jaxpr/qhd,khd->hqk/dot_general | solution.py:163
  538.9 37.1 %multiply_reduce_fusion.8 = (f32[16,512]{1,0:T(8,128)S(1)}, f32[16,512,1536]{2,1,0:T(8,128)}) fusion(f32[16,512,1536]{2,1,0:T(8,128)} %fusion.134, f32[16,512]{1,0:T(8,128)S(1)} %dynamic-slice_bitcast_fusion.2, pred[512,1536]{1,0:T(8,128)(4,1)} %broadcast_compare_fusion.5, bf16[512,16,64]{0,2,1:T(8,128)(2,1)} %bitcast.274, ...), kind=kOutput, calls=%fused_computation.15.clone.1 | convolution fusion | flops 1673519104 | bytes 105709568 | tf_op jit(solution)/shard_map/while/body/eval_jaxpr/qhd,khd->hqk/dot_general | solution.py:227
  576.0 41.2 %multiply_convert_fusion.3 = bf16[16,512,1536]{2,1,0:T(8,128)(2,1)} fusion(f32[16,512,1536]{2,1,0:T(8,128)} %get-tuple-element.557, f32[16,512,1536]{2,1,0:T(8,128)} %fusion.134, f32[16,512]{1,0:T(8,128)S(1)} %get-tuple-element.558, f32[16,512]{1,0:T(8,128)S(1)} %dynamic-slice_bitcast_fusion.2, pred[512,1536]{1,0:T(8,128)(4,1)} %broadcast_compare_fusion.5), kind=kLoop, calls=%fused_computation.14.clone.1 | loop fusion | flops 75497472 | bytes 126681088 | tf_op jit(solution)/shard_map/while/body/eval_jaxpr/convert_element_type | solution.py:230
  617.2 10.8 convolution_multiply_fusion.4
  628.0 22.9 %fusion.135 = f32[16,64,1536]{2,1,0:T(8,128)} fusion(bf16[512,16,64]{0,2,1:T(8,128)(2,1)S(1)} %bitcast.275, f32[16,512,1536]{2,1,0:T(8,128)} %fusion.134, f32[16,512]{1,0:T(8,128)S(1)} %dynamic-slice_bitcast_fusion.2, pred[512,1536]{1,0:T(8,128)(4,1)S(1)} %copy-done), kind=kOutput, calls=%fused_computation.18.clone.1 | convolution fusion | flops 1660944384 | bytes 58490880 | tf_op jit(solution)/shard_map/while/body/eval_jaxpr/hqk,qhd->khd/dot_general | solution.py:241
  650.9 12.9 fusion.136
  663.8 13.4 convolution_multiply_fusion.5
  688.2 20.7 %fusion.134 = f32[16,512,1536]{2,1,0:T(8,128)} fusion(bf16[512,16,64]{0,2,1:T(8,128)(2,1)} %bitcast.269, bf16[1536,16,64]{0,2,1:T(8,128)(2,1)S(1)} %bitcast.262), kind=kOutput, calls=%fused_computation.175.clone.1 | convolution fusion | flops 1610612736 | bytes 54525952 | tf_op jit(solution)/shard_map/while/body/eval_jaxpr/qhd,khd->hqk/dot_general | solution.py:163
  716.9 37.1 %multiply_reduce_fusion.8 = (f32[16,512]{1,0:T(8,128)S(1)}, f32[16,512,1536]{2,1,0:T(8,128)}) fusion(f32[16,512,1536]{2,1,0:T(8,128)} %fusion.134, f32[16,512]{1,0:T(8,128)S(1)} %dynamic-slice_bitcast_fusion.2, pred[512,1536]{1,0:T(8,128)(4,1)} %broadcast_compare_fusion.5, bf16[512,16,64]{0,2,1:T(8,128)(2,1)} %bitcast.274, ...), kind=kOutput, calls=%fused_computation.15.clone.1 | convolution fusion | flops 1673519104 | bytes 105709568 | tf_op jit(solution)/shard_map/while/body/eval_jaxpr/qhd,khd->hqk/dot_general | solution.py:227
  753.9 41.2 %multiply_convert_fusion.3 = bf16[16,512,1536]{2,1,0:T(8,128)(2,1)} fusion(f32[16,512,1536]{2,1,0:T(8,128)} %get-tuple-element.557, f32[16,512,1536]{2,1,0:T(8,128)} %fusion.134, f32[16,512]{1,0:T(8,128)S(1)} %get-tuple-element.558, f32[16,512]{1,0:T(8,128)S(1)} %dynamic-slice_bitcast_fusion.2, pred[512,1536]{1,0:T(8,128)(4,1)} %broadcast_compare_fusion.5), kind=kLoop, calls=%fused_computation.14.clone.1 | loop fusion | flops 75497472 | bytes 126681088 | tf_op jit(solution)/shard_map/while/body/eval_jaxpr/convert_element_type | solution.py:230
  795.1 10.8 convolution_multiply_fusion.4
  806.0 22.9 %fusion.135 = f32[16,64,1536]{2,1,0:T(8,128)} fusion(bf16[512,16,64]{0,2,1:T(8,128)(2,1)S(1)} %bitcast.275, f32[16,512,1536]{2,1,0:T(8,128)} %fusion.134, f32[16,512]{1,0:T(8,128)S(1)} %dynamic-slice_bitcast_fusion.2, pred[512,1536]{1,0:T(8,128)(4,1)S(1)} %copy-done), kind=kOutput, calls=%fused_computation.18.clone.1 | convolution fusion | flops 1660944384 | bytes 58490880 | tf_op jit(solution)/shard_map/while/body/eval_jaxpr/hqk,qhd->khd/dot_general | solution.py:241
  828.9 12.8 fusion.136
  841.7 13.4 convolution_multiply_fusion.5
  858.1 7.9 convert.33
  868.4 23.2 %collective-permute-start.2 = (bf16[512,2048]{0,1:T(8,128)(2,1)}, bf16[512,2048]{0,1:T(8,128)(2,1)}, u32[]{:S(2)}, u32[]{:S(2)}) collective-permute-start(bf16[512,2048]{0,1:T(8,128)(2,1)} %get-tuple-element.410), channel_id=1, source_target_pairs={{0,4},{4,8},{8,12},{12,16},{16,20},{20,24},{24,28},{1,5},{5,9},{9,... | collective-permute-start | bytes 6291464 | tf_op jit(solution)/shard_map/ppermute | solution.py:33
  903.9 15.1 convolution_convert_fusion
  925.9 12.9 convert_bitcast_fusion
  942.9 495.1 %all-reduce.35.cloned.1.call-done = (bf16[4,8,32,1024]{3,2,1,0:T(8,128)(2,1)}, bf16[4,8,32,1024]{3,2,1,0:T(8,128)(2,1)}, bf16[4,8,32,1024]{3,2,1,0:T(8,128)(2,1)...) async-done(((bf16[4,8,32,1024]{3,2,1,0:T(8,128)(2,1)}, bf16[4,8,32,1024]{3,2,1,0:T(8,128)(2,1)}, ...) | async-done | bytes 25165840
  1453.7 15.6 reduce-scatter.47.cloned.1.call-done
  1470.6 39.6 %psum.15 = f32[]{:T(128)} all-reduce(f32[]{:T(128)} %get-tuple-element.327), channel_id=1, replica_groups=mesh['ctx'=8,'fsdp'=4] {'ctx','fsdp'}, use_global_device_ids=true, to_apply=%region_18.19 | all-reduce | flops 1 | bytes 8 | tf_op jit(solution)/shard_map/psum | solution.py:200
  1518.7 27.8 %all-reduce.30 = (bf16[4,8,32]{2,0,1:T(4,128)(2,1)S(1)}, bf16[4,8,32]{2,0,1:T(4,128)(2,1)S(1)}, bf16[4,8,32]{2,0,1:T(4,128)(2,1)S(1)}, bf16[4,8,32]{2,0,1:T(4,12...) all-reduce(bf16[4,8,32]{2,0,1:T(4,128)(2,1)S(1)} %copy.145, ...), channel_id=4, replica_groups=mesh['ctx'=8,'fsdp'=4] {'ctx'}, use_global_device_ids=true, to_apply=%region_22.23.clone | all-reduce | flops 12288 | bytes 49152
  1549.9 16.4 all-reduce.32
  1566.9 8.4 all_gather.109
  1576.6 10.3 all_gather.111
  1588.3 8.6 all_gather.112
  1598.2 10.1 all_gather.113
  1609.6 8.6 all_gather.117
  1619.6 10.2 all_gather.118
  1631.0 8.8 all_gather.119
  1641.2 9.9 all_gather.115
  1652.3 8.8 all_gather.106
  1661.8 12.0 add_bitcast_fusion
  1679.1 16.6 all_gather.110
  1695.7 14.9 all_gather.108
  1710.7 14.9 all_gather.107
  1725.6 15.0 all_gather.105
  (372 shorter events, 209.7 us)
Async XLA Ops:
  7.2 14.3 copy-start.51
  7.2 26.3 %copy-start.52 = (bf16[256]{0:T(256)(128)(2,1)S(1)}, bf16[256]{0:T(256)(128)(2,1)}, u32[]{:S(2)}) copy-start(bf16[256]{0:T(256)(128)(2,1)} %param.39) | copy-start | bytes 1540
  7.2 34.0 %copy-start.53 = (bf16[256]{0:T(256)(128)(2,1)S(1)}, bf16[256]{0:T(256)(128)(2,1)}, u32[]{:S(2)}) copy-start(bf16[256]{0:T(256)(128)(2,1)} %param.40) | copy-start | bytes 1540
  7.2 42.7 %copy-start.54 = (bf16[256]{0:T(256)(128)(2,1)S(1)}, bf16[256]{0:T(256)(128)(2,1)}, u32[]{:S(2)}) copy-start(bf16[256]{0:T(256)(128)(2,1)} %param.41) | copy-start | bytes 1540
  7.3 50.3 %copy-start.46 = (bf16[1024]{0:T(1024)(128)(2,1)S(1)}, bf16[1024]{0:T(1024)(128)(2,1)}, u32[]{:S(2)}) copy-start(bf16[1024]{0:T(1024)(128)(2,1)} %param.43) | copy-start | bytes 6148
  7.3 59.0 %copy-start.55 = (bf16[256]{0:T(256)(128)(2,1)S(1)}, bf16[256]{0:T(256)(128)(2,1)}, u32[]{:S(2)}) copy-start(bf16[256]{0:T(256)(128)(2,1)} %param.45) | copy-start | bytes 1540
  7.3 106.5 %copy-start.16 = (bf16[1,1024,1024]{2,1,0:T(8,128)(2,1)S(1)}, bf16[1,1024,1024]{2,1,0:T(8,128)(2,1)}, u32[]{:S(2)}) copy-start(bf16[1,1024,1024]{2,1,0:T(8,128)(2,1)} %param.30) | copy-start | bytes 6291460
  7.3 132.0 %all-gather.17.cloned.1.call-start = ((), (), s32[]{:S(2)}) async-start(), calls=%async_computation.6 | async-start | bytes 2621440 | tf_op jit(solution)/shard_map/all_gather | solution.py:113
  8.0 134.6 %all-gather.19.cloned.1.call-start = ((), (), s32[]{:S(2)}) async-start(), calls=%async_computation.7 | async-start | bytes 2621440 | tf_op jit(solution)/shard_map/all_gather | solution.py:115
  8.8 137.0 %all-gather.21.cloned.1.call-start = ((), (), s32[]{:S(2)}) async-start(), calls=%async_computation.8 | async-start | bytes 2621440 | tf_op jit(solution)/shard_map/all_gather | solution.py:116
  9.5 337.1 %all-gather.23.cloned.1.call-start = ((), (), s32[]{:S(2)}) async-start(), calls=%async_computation.9 | async-start | bytes 2621440 | tf_op jit(solution)/shard_map/all_gather | solution.py:118
  10.1 344.9 %all-gather.25.cloned.1.call-start = ((), (), s32[]{:S(2)}) async-start(), calls=%async_computation.10 | async-start | bytes 10485760 | tf_op jit(solution)/shard_map/all_gather | solution.py:122
  10.7 392.1 %all-gather.27.cloned.1.call-start = ((), (), s32[]{:S(2)}) async-start(), calls=%async_computation.11 | async-start | bytes 10485760 | tf_op jit(solution)/shard_map/all_gather | solution.py:124
  11.2 1426.7 %all-reduce.35.cloned.1.call-start = ((), (), s32[]{:S(2)}) async-start(), calls=%async_computation.20 | async-start | bytes 50331648
  11.3 154.5 %copy-start.29 = (f32[1,1024]{1,0:T(1,128)}, f32[1,1024]{1,0:T(1,128)S(1)}, u32[]{:S(2)}) copy-start(f32[1,1024]{1,0:T(1,128)S(1)} %convert_element_type.293) | copy-start | bytes 12292
  29.6 90.7 %copy-start.56 = (bf16[256]{0:T(256)(128)(2,1)S(1)}, bf16[256]{0:T(256)(128)(2,1)}, u32[]{:S(2)}) copy-start(bf16[256]{0:T(256)(128)(2,1)} %param.46) | copy-start | bytes 1540
  29.6 100.3 %copy-start.57 = (bf16[256]{0:T(256)(128)(2,1)S(1)}, bf16[256]{0:T(256)(128)(2,1)}, u32[]{:S(2)}) copy-start(bf16[256]{0:T(256)(128)(2,1)} %param.47) | copy-start | bytes 1540
  139.3 10.1 copy-start.17
  161.3 10.3 collective-permute-start
  163.9 7.6 collective-permute-start.1
  190.6 156.0 %copy-start.45 = (f32[4,1,256]{2,1,0:T(1,128)S(1)}, f32[4,1,256]{2,1,0:T(1,128)}, u32[]{:S(2)}) copy-start(f32[4,1,256]{2,1,0:T(1,128)} %convert_element_type.330) | copy-start | bytes 12292
  220.1 22.2 %copy-start.1 = (pred[512,1536]{1,0:T(8,128)(4,1)S(1)}, pred[512,1536]{1,0:T(8,128)(4,1)}, u32[]{:S(2)}) copy-start(pred[512,1536]{1,0:T(8,128)(4,1)} %broadcast_compare_fusion.4) | copy-start | bytes 2359300 | tf_op jit(solution)/shard_map/while
  297.1 22.2 %copy-start.1 = (pred[512,1536]{1,0:T(8,128)(4,1)S(1)}, pred[512,1536]{1,0:T(8,128)(4,1)}, u32[]{:S(2)}) copy-start(pred[512,1536]{1,0:T(8,128)(4,1)} %broadcast_compare_fusion.4) | copy-start | bytes 2359300 | tf_op jit(solution)/shard_map/while
  342.4 9.9 copy-start.23
  352.8 50.0 %copy-start.31 = (f32[1024]{0:T(1024)}, f32[1024]{0:T(1024)S(1)}, u32[]{:S(2)}) copy-start(f32[1024]{0:T(1024)S(1)} %multiply_reduce_fusion.6) | copy-start | bytes 12292
  355.0 47.8 %copy-start.44 = (f32[4,1,256]{2,1,0:T(1,128)S(1)}, f32[4,1,256]{2,1,0:T(1,128)}, u32[]{:S(2)}) copy-start(f32[4,1,256]{2,1,0:T(1,128)} %convert_element_type.333) | copy-start | bytes 12292
  402.8 15.7 copy-start.26
  402.8 15.7 copy-start.27
  402.8 15.7 copy-start.28
  402.9 15.7 copy-start.30
  429.5 25.4 %copy-start.13 = (bf16[1024,1024]{0,1:T(8,128)(2,1)}, bf16[1024,1024]{0,1:T(8,128)(2,1)S(1)}, u32[]{:S(2)}) copy-start(bf16[1024,1024]{0,1:T(8,128)(2,1)S(1)} %get-tuple-element.390) | copy-start | bytes 6291460
  430.2 24.8 %copy-start.6 = (f32[1024,1024]{0,1:T(8,128)S(1)}, f32[1024,1024]{0,1:T(8,128)}, u32[]{:S(2)}) copy-start(f32[1024,1024]{0,1:T(8,128)} %copy-done.5) | copy-start | bytes 12582916
  454.9 15.1 copy-start.12
  470.0 15.7 copy-start.32
  617.2 10.8 copy-start
  617.2 10.8 copy-start.2
  795.1 10.8 copy-start
  795.1 10.8 copy-start.2
  858.1 37.3 %slice-start = ((s8[16777216]{0:T(1024)(128)(4,1)}), s8[4194304]{0:T(1024)(128)(4,1)S(1)}, s32[]{:S(2)}) async-start(s8[16777216]{0:T(1024)(128)(4,1)} %bitcast.265), calls=%async_computation.21 | async-start | bytes 8388608
  858.1 37.3 %slice-start.1 = ((s8[16777216]{0:T(1024)(128)(4,1)}), s8[4194304]{0:T(1024)(128)(4,1)S(1)}, s32[]{:S(2)}) async-start(s8[16777216]{0:T(1024)(128)(4,1)} %bitcast.265), calls=%async_computation.22 | async-start | bytes 8388608
  858.1 37.3 %slice-start.2 = ((s8[16777216]{0:T(1024)(128)(4,1)}), s8[4194304]{0:T(1024)(128)(4,1)S(1)}, s32[]{:S(2)}) async-start(s8[16777216]{0:T(1024)(128)(4,1)} %bitcast.265), calls=%async_computation.23 | async-start | bytes 8388608
  866.0 25.6 %copy-start.15 = (bf16[1024,1024]{0,1:T(8,128)(2,1)S(1)}, bf16[1024,1024]{0,1:T(8,128)(2,1)}, u32[]{:S(2)}) copy-start(bf16[1024,1024]{0,1:T(8,128)(2,1)} %copy-done.14) | copy-start | bytes 6291460
  866.0 25.6 %copy-start.18 = (bf16[1024,1024]{1,0:T(8,128)(2,1)S(1)}, bf16[1024,1024]{1,0:T(8,128)(2,1)}, u32[]{:S(2)}) copy-start(bf16[1024,1024]{1,0:T(8,128)(2,1)} %copy.153) | copy-start | bytes 6291460
  868.4 50.5 %collective-permute-start.2 = (bf16[512,2048]{0,1:T(8,128)(2,1)}, bf16[512,2048]{0,1:T(8,128)(2,1)}, u32[]{:S(2)}, u32[]{:S(2)}) collective-permute-start(bf16[512,2048]{0,1:T(8,128)(2,1)} %get-tuple-element.410), channel_id=1, source_target_pairs={{0,4},{4,8},{8,12},{12,16},{16,20},{20,24},{24,28},{1,5},{5,9},{9,... | collective-permute-start | bytes 6291464 | tf_op jit(solution)/shard_map/ppermute | solution.py:33
  899.7 22.8 %collective-permute-start.3 = (bf16[512,2048]{0,1:T(8,128)(2,1)}, bf16[512,2048]{0,1:T(8,128)(2,1)}, u32[]{:S(2)}, u32[]{:S(2)}) collective-permute-start(bf16[512,2048]{0,1:T(8,128)(2,1)} %get-tuple-element.409), channel_id=1, source_target_pairs={{4,0},{8,4},{12,8},{16,12},{20,16},{24,20},{28,24},{5,1},{9,5},{13... | collective-permute-start | bytes 6291464 | tf_op jit(solution)/shard_map/ppermute | solution.py:33
  903.9 15.1 copy-start.4
  925.9 12.9 copy-start.10
  941.7 527.7 %copy-start.58 = (u32[32]{0:T(128)S(1)}, u32[32]{0:T(128)}, u32[]{:S(2)}) copy-start(u32[32]{0:T(128)} %constant.227) | copy-start | bytes 388
  941.7 568.6 %copy-start.40 = (bf16[1024]{0:T(1024)(128)(2,1)S(1)}, bf16[1024]{0:T(1024)(128)(2,1)}, u32[]{:S(2)}) copy-start(bf16[1024]{0:T(1024)(128)(2,1)} %get-tuple-element.393) | copy-start | bytes 6148
  941.7 568.6 %copy-start.48 = (bf16[1024]{0:T(1024)(128)(2,1)S(1)}, bf16[1024]{0:T(1024)(128)(2,1)}, u32[]{:S(2)}) copy-start(bf16[1024]{0:T(1024)(128)(2,1)} %get-tuple-element.325) | copy-start | bytes 6148
  941.7 568.7 %copy-start.47 = (bf16[1024]{0:T(1024)(128)(2,1)S(1)}, bf16[1024]{0:T(1024)(128)(2,1)}, u32[]{:S(2)}) copy-start(bf16[1024]{0:T(1024)(128)(2,1)} %get-tuple-element.328) | copy-start | bytes 6148
  941.7 568.8 %copy-start.43 = (bf16[4096]{0:T(1024)(128)(2,1)S(1)}, bf16[4096]{0:T(1024)(128)(2,1)}, u32[]{:S(2)}) copy-start(bf16[4096]{0:T(1024)(128)(2,1)} %get-tuple-element.391) | copy-start | bytes 24580
  941.7 568.8 %copy-start.39 = (bf16[1024]{0:T(1024)(128)(2,1)S(1)}, bf16[1024]{0:T(1024)(128)(2,1)}, u32[]{:S(2)}) copy-start(bf16[1024]{0:T(1024)(128)(2,1)} %get-tuple-element.389) | copy-start | bytes 6148
  941.8 568.9 %copy-start.42 = (bf16[1024]{0:T(1024)(128)(2,1)S(1)}, bf16[1024]{0:T(1024)(128)(2,1)}, u32[]{:S(2)}) copy-start(bf16[1024]{0:T(1024)(128)(2,1)} %get-tuple-element.323) | copy-start | bytes 6148
  941.8 569.0 %copy-start.41 = (bf16[1024]{0:T(1024)(128)(2,1)S(1)}, bf16[1024]{0:T(1024)(128)(2,1)}, u32[]{:S(2)}) copy-start(bf16[1024]{0:T(1024)(128)(2,1)} %get-tuple-element.322) | copy-start | bytes 6148
  941.8 527.5 %reduce-scatter.47.cloned.1.call-start = ((), (), s32[]{:S(2)}) async-start(), calls=%async_computation.19 | async-start | bytes 1310720
  1440.9 220.9 %reduce-scatter.45.cloned.1.call-start = ((), (), s32[]{:S(2)}) async-start(), calls=%async_computation.18 | async-start | bytes 1310720
  1443.9 235.2 %reduce-scatter.43.cloned.1.call-start = ((), (), s32[]{:S(2)}) async-start(), calls=%async_computation.17 | async-start | bytes 327680
  1446.3 249.4 %reduce-scatter.41.cloned.1.call-start = ((), (), s32[]{:S(2)}) async-start(), calls=%async_computation.16 | async-start | bytes 327680
  1448.7 261.9 %reduce-scatter.39.cloned.1.call-start = ((), (), s32[]{:S(2)}) async-start(), calls=%async_computation.15 | async-start | bytes 327680
  1451.1 210.7 %copy-start.35 = (f32[1024]{0:T(1024)S(1)}, f32[1024]{0:T(1024)}, u32[]{:S(2)}) copy-start(f32[1024]{0:T(1024)} %copy-done.34) | copy-start | bytes 12292
  1451.1 274.5 %reduce-scatter.37.cloned.1.call-start = ((), (), s32[]{:S(2)}) async-start(), calls=%async_computation.14 | async-start | bytes 327680
  1453.5 291.5 %all-gather.31.cloned.1.call-start = ((), (), s32[]{:S(2)}) async-start(), calls=%async_computation.13 | async-start | bytes 2359296 | tf_op jit(solution)/shard_map/all_gather | solution.py:422
  1469.3 279.8 %all-gather.29.cloned.1.call-start = ((), (), s32[]{:S(2)}) async-start(), calls=%async_computation.12 | async-start | bytes 2359296 | tf_op jit(solution)/shard_map/all_gather | solution.py:416
  (23 other events, 131.7 us)
Sparse Core Ops, SparseCore 0:
  10.0 38.0 all-gather.16
  49.9 35.8 all-gather.18
  87.7 35.8 all-gather.20
  125.2 35.1 all-gather.22
  162.1 87.5 all-gather.24
  251.5 87.5 all-gather.26
  941.8 496.0 all-reduce.34
  1441.4 27.8 reduce-scatter.46
  1473.0 27.8 reduce-scatter.44
  1503.5 24.0 reduce-scatter.42
  1530.6 24.0 reduce-scatter.40
  1558.0 24.1 reduce-scatter.38
  1585.7 24.0 reduce-scatter.36
  1611.2 29.1 all-gather.30
  1661.9 30.7 all-gather.28
where the time goes:
time: 1770 us; the launch traced here: 1760 us
  waiting for transfers between devices  514 us (29%)
  matrix products  477 us (27%)
  blocking collectives  341 us (19%)
  other arithmetic  217 us (12%)
  local copies, waits for them, and re-layouts  157 us (9%)
  starting transfers between devices  29.6 us (2%)
  between operations  18.4 us (1%)
    unnamed x22, waiting for transfers between devices  514 us
    dot_general x4, matrix products, block_scores(): jnp.einsum('qhd,khd->hqk', query_block, key_block, preferred_element_type...  83.6 us
    convert_element_type x2, other arithmetic, backward_block(): (probs * (d_probs - jnp.sum(probs * d_probs, axis=-1, keepdims=True))).as...  82.4 us
    psum x2, blocking collectives, body(): lax.psum((jnp.sum(flags), jnp.sum(flags[:, None] * error * error)), ('ctx...  79.5 us
    dot_general x4, matrix products, product(): return jnp.dot(left, right, preferred_element_type=jnp.float32)  78.2 us
    dot_general x2, matrix products, backward_block(): jnp.einsum('qhd,khd->hqk', grad_block, value_block, preferred_element_typ...  74.1 us
    dot_general x4, matrix products, back_product(): lax.dot_general(left, right, (((1,), (1,)), ((), ())), preferred_element_...  56.1 us
    unnamed x150, local copies, waits for them, and re-layouts  50.9 us
  transfers between devices with their start and end apart: 19, of which 2 were waited for; matrix products, arithmetic and copies ran while one was open for 21% of the time, Pallas kernels for 0%

commit v1 on v0

v1 whole, which is shorter than its diff:
```python
import functools

import jax
import jax.numpy as jnp
from jax import lax
from jax.experimental import pallas as pl
from jax.experimental.pallas import tpu as pltpu
from jax.sharding import PartitionSpec as P

D = 1024
FF = 4096
HEAD = 64
DOC_MAX = 512
TILE = 256
NEG = -1e30
NORM_EPS = 1e-05
VMEM_BYTES = 56 * 2**20
bf16 = jnp.bfloat16
f32 = jnp.float32


def nn(a, b):
    return jnp.dot(a, b, preferred_element_type=f32)


def nt(a, b):
    return lax.dot_general(a, b, (((1,), (1,)), ((), ())), preferred_element_type=f32)


def tn(a, b):
    return lax.dot_general(a, b, (((0,), (0,)), ((), ())), preferred_element_type=f32)


def params():
    return pltpu.CompilerParams(vmem_limit_bytes=VMEM_BYTES)


def cost(flops, bytes_accessed):
    return pl.CostEstimate(flops=int(flops), bytes_accessed=int(bytes_accessed), transcendentals=0)


def sds(shape, dtype):
    return jax.ShapeDtypeStruct(shape, dtype)


def weight_copies(where_ref, pieces, full, out, sem):
    shard, mine, other = pieces
    f, parity = where_ref[0], where_ref[1]
    rows = shard.shape[0]
    half, quarter = rows // 2, rows // 4
    copies = []

    def add(source, begin):
        begin = pl.multiple_of(begin, 16)
        copies.append(pltpu.make_async_copy(source, full.at[pl.ds(begin, source.shape[0])], sem.at[len(copies)]))

    add(shard, f * rows)
    at = 0
    for r in range(1, full.shape[0] // rows):
        base = jnp.bitwise_xor(f, r) * rows
        for offset, length in ((0, half),) if r & (r - 1) == 0 else ((0, quarter), (quarter, quarter)):
            add(mine.at[pl.ds(at, length)], base + offset + parity * half)
            add(other.at[pl.ds(at, length)], base + offset + (1 - parity) * half)
            at += length
    return copies, pltpu.make_async_copy(full, out, sem.at[len(copies)])


def join_weight(where_ref, pieces, full, out, sem):
    copies, save = weight_copies(where_ref, pieces, full, out, sem)

    @pl.when(pl.program_id(0) == 0)
    def _():
        for copy in copies:
            copy.start()
        for copy in copies:
            copy.wait()
        save.start()

    @pl.when(pl.program_id(0) == pl.num_programs(0) - 1)
    def _():
        save.wait()


WEIGHT_SPECS = [pl.BlockSpec(memory_space=pltpu.SMEM)] + [pl.BlockSpec(memory_space=pl.ANY)] * 3


def weight_scratch(rows, columns):
    return [pltpu.VMEM((rows, columns), bf16), pltpu.SemaphoreType.DMA((64,))]


def qkv_kernel(
    where_ref, shard, mine, other, x_ref, bq_ref, bv_ref, q_ref, k_ref, v_ref, kt_ref, vt_ref, full_ref, w_ref, sem
):
    join_weight(where_ref, (shard, mine, other), w_ref, full_ref, sem)
    i = pl.program_id(0)
    x = x_ref[...]

    @pl.when((i > 0) & (i < pl.num_programs(0) - 1))
    def _():
        query = (nn(x, w_ref[:, :D]) + bq_ref[...]).astype(bf16)
        q_ref[...] = query * jnp.asarray(HEAD**-0.5, bf16)

    keys = nn(x, w_ref[:, D : 2 * D]).astype(bf16)
    k_ref[...] = keys
    kt_ref[...] = jnp.transpose(keys)
    values = (nn(x, w_ref[:, 2 * D :]) + bv_ref[...]).astype(bf16)
    v_ref[...] = values
    vt_ref[...] = jnp.transpose(values)


def project_qkv(where, pieces, x_near, bq, bv):
    span = x_near.shape[0]
    rows = span - 2 * DOC_MAX
    row = pl.BlockSpec((1, D), lambda i: (0, 0))
    tall = pl.BlockSpec((512, D), lambda i: (i, 0))
    wide = pl.BlockSpec((D, 512), lambda i: (0, i))
    return pl.pallas_call(
        qkv_kernel,
        grid=(span // 512,),
        in_specs=WEIGHT_SPECS + [tall, row, row],
        out_specs=[
            pl.BlockSpec((512, D), lambda i: (jnp.clip(i - 1, 0, rows // 512 - 1), 0)),
            tall,
            tall,
            wide,
            wide,
            pl.BlockSpec(memory_space=pl.ANY),
        ],
        scratch_shapes=weight_scratch(D, 3 * D),
        out_shape=[
            sds((rows, D), bf16),
            sds((span, D), bf16),
            sds((span, D), bf16),
            sds((D, span), bf16),
            sds((D, span), bf16),
            sds((D, 3 * D), bf16),
        ],
        compiler_params=params(),
        cost_estimate=cost(2 * D * D * (rows + 2 * span), 30 * 2**20),
        name="project_qkv",
    )(where, *pieces, x_near, bq, bv)


def stack_rows(block, stack):
    lanes = lax.broadcasted_iota(jnp.int32, block.shape, 1)
    for h in range(4):
        stack[h*TILE:(h+1)*TILE, :] = jnp.where(lanes//HEAD==h, block, jnp.zeros_like(block))

def stack_columns(turned, stack):
    for h in range(4):
        hr = slice(h*HEAD,(h+1)*HEAD)
        stack[hr, h*TILE:(h+1)*TILE] = turned[hr, :]

def attn_fwd_kernel(lo_ref, hi_ref, q_ref, k_ref, vt_ref, idq_ref, idk_ref, out_ref, lse_ref, qs, acc, top, tot):
    t = pl.program_id(1)
    @pl.when((t==0)&(pl.program_id(0)==0))
    def _():
        qs[...] = jnp.zeros_like(qs)
    stack_columns(jnp.transpose(q_ref[...]), qs)
    acc[...] = jnp.zeros_like(acc)
    top[...] = jnp.full_like(top, NEG)
    tot[...] = jnp.zeros_like(tot)
    def step(kt, carry):
        rows = pl.ds(pl.multiple_of(kt*TILE, TILE), TILE)
        bias = jnp.where(idk_ref[rows,:] == idq_ref[0], 0.0, NEG)
        vt_tile = vt_ref[:, rows]
        s = nn(k_ref[rows,:], qs[...])
        for h in range(4):
            cols = slice(h*TILE,(h+1)*TILE)
            hr = slice(h*HEAD,(h+1)*HEAD)
            sh = s[:, cols] + bias
            old = top[h:h+1,:]
            new = jnp.maximum(old, jnp.max(sh, axis=0, keepdims=True))
            top[h:h+1,:] = new
            p = jnp.exp(sh - new)
            fade = jnp.exp(old-new)
            tot[h:h+1,:] = tot[h:h+1,:]*fade + jnp.sum(p, axis=0, keepdims=True)
            acc[hr,:] = acc[hr,:]*fade + nn(vt_tile[hr,:], p.astype(bf16))
        return carry
    lax.fori_loop(lo_ref[t], hi_ref[t], step, 0)
    total = tot[...]
    inv = 1.0/total
    for h in range(4):
        hr = slice(h*HEAD,(h+1)*HEAD)
        acc[hr,:] = acc[hr,:]*inv[h:h+1,:]
    out_ref[...] = jnp.transpose(acc[...]).astype(bf16)
    lse_ref[0] = top[...] + jnp.log(total)

def attn_fwd(lo, hi, q, k_near, vt_near, idq_rows, idk_col):
    rows=q.shape[0]; span=k_near.shape[0]
    return pl.pallas_call(attn_fwd_kernel,
        grid_spec=pltpu.PrefetchScalarGridSpec(num_scalar_prefetch=2, grid=(D//256, rows//TILE),
            in_specs=[pl.BlockSpec((TILE,256),lambda g,t,*_:(t,g)),
                pl.BlockSpec((span,256),lambda g,t,*_:(0,g)),
                pl.BlockSpec((256,span),lambda g,t,*_:(g,0)),
                pl.BlockSpec((1,1,TILE),lambda g,t,*_:(t,0,0)),
                pl.BlockSpec((span,1),lambda g,t,*_:(0,0))],
            out_specs=[pl.BlockSpec((TILE,256),lambda g,t,*_:(t,g)),
                pl.BlockSpec((1,8,TILE),lambda g,t,*_:(g,0,t))],
            scratch_shapes=[pltpu.VMEM((256,4*TILE),bf16),
                pltpu.VMEM((256,TILE),f32),pltpu.VMEM((8,TILE),f32),pltpu.VMEM((8,TILE),f32)]),
        out_shape=[jax.ShapeDtypeStruct((rows,D),bf16),jax.ShapeDtypeStruct((D//256,8,rows),f32)],
        compiler_params=pltpu.CompilerParams(vmem_limit_bytes=VMEM_BYTES),
        name="attn_forward",
    )(lo,hi,q,k_near,vt_near,idq_rows,idk_col)

def attn_bwd_kernel(lo_ref, hi_ref, q_ref, do_ref, ctx_ref, k_ref, kt_ref, v_ref, lse_ref, idq_ref, idk_ref,
        dq_ref, dk_ref, dv_ref, qs, dos, qst, dost, dk_acc, dv_acc, dq_acc):
    t = pl.program_id(1)
    @pl.when((t==0)&(pl.program_id(0)==0))
    def _():
        qst[...] = jnp.zeros_like(qst)
        dost[...] = jnp.zeros_like(dost)
    @pl.when(t==0)
    def _():
        dk_acc[...] = jnp.zeros_like(dk_acc)
        dv_acc[...] = jnp.zeros_like(dv_acc)
    stack_rows(q_ref[...], qs)
    stack_rows(do_ref[...], dos)
    stack_columns(jnp.transpose(q_ref[...]), qst)
    stack_columns(jnp.transpose(do_ref[...]), dost)
    prod = do_ref[...].astype(f32)*ctx_ref[...].astype(f32)
    high = prod.astype(bf16)
    low = (prod-high.astype(f32)).astype(bf16)
    sel = (lax.broadcasted_iota(jnp.int32,(8,256),1)//HEAD == lax.broadcasted_iota(jnp.int32,(8,256),0)).astype(bf16)
    delta = nt(sel, high)+nt(sel, low)
    lse = lse_ref[0]
    delta_row = jnp.concatenate([delta[h:h+1] for h in range(4)],axis=1)
    lse_row = jnp.concatenate([lse[h:h+1] for h in range(4)],axis=1)
    dq_acc[...] = jnp.zeros_like(dq_acc)
    def step(kt, carry):
        rows = pl.ds(pl.multiple_of(kt*TILE, TILE), TILE)
        seen = idk_ref[rows,:] == idq_ref[0]
        bias = jnp.where(seen, 0.0, NEG)
        s = nn(k_ref[rows,:], qst[...])
        dp = nn(v_ref[rows,:], dost[...])
        p = jnp.exp(s + jnp.concatenate([bias]*4,axis=1) - lse_row)
        ds = (p*(dp-delta_row)).astype(bf16)
        dv_acc[rows,:] += nn(p.astype(bf16), dos[...])
        dk_acc[rows,:] += nn(ds, qs[...])
        kt_tile = kt_ref[:, rows]
        for h in range(4):
            hr=slice(h*HEAD,(h+1)*HEAD)
            dq_acc[hr,:] += nn(kt_tile[hr,:], ds[:, h*TILE:(h+1)*TILE])
        return carry
    lax.fori_loop(lo_ref[t], hi_ref[t], step, 0)
    dq_ref[...] = (jnp.transpose(dq_acc[...])*(HEAD**-0.5)).astype(bf16)
    @pl.when(t==pl.num_programs(1)-1)
    def _():
        dk_ref[...] = dk_acc[...].astype(bf16)
        dv_ref[...] = dv_acc[...].astype(bf16)

def attn_bwd(lo, hi, q, do, ctx, k_near, kt_near, v_near, lse, idq_rows, idk_col, g0=0, ng=4):
    rows=q.shape[0]; span=k_near.shape[0]
    return pl.pallas_call(attn_bwd_kernel,
        grid_spec=pltpu.PrefetchScalarGridSpec(num_scalar_prefetch=2, grid=(ng, rows//TILE),
            in_specs=[pl.BlockSpec((TILE,256),lambda g,t,*_:(t,g+g0)),
                pl.BlockSpec((TILE,256),lambda g,t,*_:(t,g+g0)),
                pl.BlockSpec((TILE,256),lambda g,t,*_:(t,g+g0)),
                pl.BlockSpec((span,256),lambda g,t,*_:(0,g+g0)),
                pl.BlockSpec((256,span),lambda g,t,*_:(g+g0,0)),
                pl.BlockSpec((span,256),lambda g,t,*_:(0,g+g0)),
                pl.BlockSpec((1,8,TILE),lambda g,t,*_:(g+g0,0,t)),
                pl.BlockSpec((1,1,TILE),lambda g,t,*_:(t,0,0)),
                pl.BlockSpec((span,1),lambda g,t,*_:(0,0))],
            out_specs=[pl.BlockSpec((TILE,256),lambda g,t,*_:(t,g)),
                pl.BlockSpec((span,256),lambda g,t,*_:(0,g)),
                pl.BlockSpec((span,256),lambda g,t,*_:(0,g))],
            scratch_shapes=[pltpu.VMEM((4*TILE,256),bf16),pltpu.VMEM((4*TILE,256),bf16),
                pltpu.VMEM((256,4*TILE),bf16),pltpu.VMEM((256,4*TILE),bf16),
                pltpu.VMEM((span,256),f32),pltpu.VMEM((span,256),f32),pltpu.VMEM((256,TILE),f32)]),
        out_shape=[jax.ShapeDtypeStruct((rows,ng*256),bf16),jax.ShapeDtypeStruct((span,ng*256),bf16),jax.ShapeDtypeStruct((span,ng*256),bf16)],
        compiler_params=pltpu.CompilerParams(vmem_limit_bytes=VMEM_BYTES),
        name="attn_backward",
    )(lo,hi,q,do,ctx,k_near,kt_near,v_near,lse,idq_rows,idk_col)


def norm_stats(hidden):
    center = hidden - jnp.mean(hidden, axis=1, keepdims=True)
    rate = lax.rsqrt(jnp.mean(center * center, axis=1, keepdims=True) + NORM_EPS)
    return center * rate, rate


def norm_back(grad, unit, rate):
    return rate * (
        grad - jnp.mean(grad, axis=1, keepdims=True) - unit * jnp.mean(grad * unit, axis=1, keepdims=True)
    )


def mix_kernel(
    where_ref, shard, mine, other, c_ref, b_ref, x_ref, g_ref, s_ref, normed_ref, low_ref, rate_ref, full_ref, w_ref, sem
):
    join_weight(where_ref, (shard, mine, other), w_ref, full_ref, sem)
    hidden = x_ref[...].astype(f32) + (nn(c_ref[...], w_ref[...]) + b_ref[...])
    unit, rate = norm_stats(hidden)
    normed = unit * g_ref[...] + s_ref[...]
    normed_ref[...] = normed
    low_ref[...] = normed.astype(bf16)
    rate_ref[...] = rate


def mix_and_norm(where, pieces, context, b, tokens, gain, shift):
    rows = context.shape[0]
    tile = pl.BlockSpec((TILE, D), lambda i: (i, 0))
    row = pl.BlockSpec((1, D), lambda i: (0, 0))
    return pl.pallas_call(
        mix_kernel,
        grid=(rows // TILE,),
        in_specs=WEIGHT_SPECS + [tile, row, tile, row, row],
        out_specs=[tile, tile, pl.BlockSpec((TILE, 1), lambda i: (i, 0)), pl.BlockSpec(memory_space=pl.ANY)],
        out_shape=[sds((rows, D), f32), sds((rows, D), bf16), sds((rows, 1), f32), sds((D, D), bf16)],
        scratch_shapes=weight_scratch(D, D),
        compiler_params=params(),
        cost_estimate=cost(2 * D * D * rows, 14 * 2**20),
        name="mix_and_norm",
    )(where, *pieces, context, b, tokens, gain, shift)


def gelu_parts(u):
    t = 1.0 / (1.0 + (0.3275911 * 0.7071067811865476) * jnp.abs(u))
    poly = t * (0.254829592 + t * (-0.284496736 + t * (1.421413741 + t * (-1.453152027 + t * 1.061405429))))
    bell = jnp.exp(-0.5 * u * u)
    tail = 0.5 * poly * bell
    share = jnp.where(u >= 0, 1.0 - tail, tail)
    return u * share, share + u * bell * 0.3989422804014327


def inner_kernel(where_ref, shard, mine, other, x_ref, b_ref, act_ref, slope_ref, full_ref, w_ref, sem):
    join_weight(where_ref, (shard, mine, other), w_ref, full_ref, sem)
    wide = act_ref.shape[1]
    columns = pl.ds(pl.multiple_of(pl.program_id(0) * wide, wide), wide)
    for i in range(x_ref.shape[0] // TILE):
        rows = slice(i * TILE, (i + 1) * TILE)
        act, slope = gelu_parts(nn(x_ref[rows, :], w_ref[:, columns]) + b_ref[...])
        act_ref[rows, :] = act.astype(bf16)
        slope_ref[rows, :] = slope.astype(bf16)


def inner_forward(where, pieces, x, b):
    rows, wide = x.shape[0], 512
    block = pl.BlockSpec((rows, wide), lambda j: (0, j))
    return pl.pallas_call(
        inner_kernel,
        grid=(FF // wide,),
        in_specs=WEIGHT_SPECS
        + [pl.BlockSpec((rows, D), lambda j: (0, 0)), pl.BlockSpec((1, wide), lambda j: (0, j))],
        out_specs=[block, block, pl.BlockSpec(memory_space=pl.ANY)],
        out_shape=[sds((rows, FF), bf16), sds((rows, FF), bf16), sds((D, FF), bf16)],
        scratch_shapes=weight_scratch(D, FF),
        compiler_params=params(),
        cost_estimate=cost(2 * D * FF * rows, 26 * 2**20),
        name="inner_forward",
    )(where, *pieces, x, b)


def outer_kernel(
    where_ref, shard, mine, other, coef_ref, act_ref, b_ref, normed_ref, g_ref, s_ref, teach_ref, cot_ref, flag_ref,
    out_ref, dsum_ref, dlow_ref, sums_ref, full_ref, w_ref, sem,
):
    join_weight(where_ref, (shard, mine, other), w_ref, full_ref, sem)
    hidden = normed_ref[...] + (nn(act_ref[...], w_ref[...]) + b_ref[...])
    unit, rate = norm_stats(hidden)
    gain = g_ref[...]
    final = unit * gain + s_ref[...]
    out_ref[...] = final.astype(bf16)
    error = final - teach_ref[...].astype(f32)
    marked = flag_ref[...] * error
    grad = cot_ref[...].astype(f32) + coef_ref[0] * marked
    dsum = norm_back(grad * gain, unit, rate)
    dsum_ref[...] = dsum
    low = dsum.astype(bf16)
    dlow_ref[...] = low

    @pl.when(pl.program_id(0) == 0)
    def _():
        sums_ref[...] = jnp.zeros_like(sums_ref)

    sums_ref[0:1, :] += jnp.sum(grad * unit, axis=0, keepdims=True)
    sums_ref[1:2, :] += jnp.sum(grad, axis=0, keepdims=True)
    sums_ref[2:3, :] += jnp.sum(low.astype(f32), axis=0, keepdims=True)
    sums_ref[3:4, :] += jnp.sum(marked * error, axis=0, keepdims=True)


def outer_forward(where, pieces, coef, act, b, normed, gain, shift, teacher, cotangent, flags):
    rows = act.shape[0]
    tile = pl.BlockSpec((TILE, D), lambda i: (i, 0))
    row = pl.BlockSpec((1, D), lambda i: (0, 0))
    return pl.pallas_call(
        outer_kernel,
        grid=(rows // TILE,),
        in_specs=WEIGHT_SPECS
        + [
            pl.BlockSpec(memory_space=pltpu.SMEM),
            pl.BlockSpec((TILE, FF), lambda i: (i, 0)),
            row, tile, row, row, tile, tile,
            pl.BlockSpec((TILE, 1), lambda i: (i, 0)),
        ],
        out_specs=[
            tile, tile, tile, pl.BlockSpec((8, D), lambda i: (0, 0)), pl.BlockSpec(memory_space=pl.ANY),
        ],
        out_shape=[
            sds((rows, D), bf16), sds((rows, D), f32), sds((rows, D), bf16), sds((8, D), f32), sds((FF, D), bf16),
        ],
        scratch_shapes=weight_scratch(FF, D),
        compiler_params=params(),
        cost_estimate=cost(2 * D * FF * rows, 32 * 2**20),
        name="outer_forward",
    )(where, *pieces, coef, act, b, normed, gain, shift, teacher, cotangent, flags)


def gram_kernel(order_ref, left_ref, right_ref, keep_ref, send_ref):
    half = keep_ref.shape[1]
    grad = tn(left_ref[...], right_ref[...])
    first = order_ref[pl.num_programs(1)] == 0
    low, high = grad[:half], grad[half:]
    keep_ref[0] = jnp.where(first, low, high).astype(bf16)
    send_ref[0] = jnp.where(first, high, low).astype(bf16)


def gram(order, left, right, shards, wide):
    tokens, height = left.shape
    columns = right.shape[1]
    part = height // shards
    out = pl.BlockSpec((1, part // 2, wide), lambda j, r, order_ref: (r, 0, j))
    return pl.pallas_call(
        gram_kernel,
        grid_spec=pltpu.PrefetchScalarGridSpec(
            num_scalar_prefetch=1,
            grid=(columns // wide, shards),
            in_specs=[
                pl.BlockSpec((tokens, part), lambda j, r, order_ref: (0, order_ref[r])),
                pl.BlockSpec((tokens, wide), lambda j, r, order_ref: (0, j)),
            ],
            out_specs=[out, out],
        ),
        out_shape=[sds((shards, part // 2, columns), bf16)] * 2,
        compiler_params=params(),
        cost_estimate=cost(2 * tokens * height * columns, 2 * (tokens * (height + columns) + height * columns)),
        name="gram",
    )(order, left, right)


def feed_back_kernel(
    db_ref, wo_ref, slope_ref, wi_ref, dsum_ref, normed_ref, rate_ref, g_ref, s_ref,
    dpre_ref, bias_ref, done_ref, dattn_ref, sums_ref, total,
):
    j = pl.program_id(0)

    @pl.when(j == 0)
    def _():
        total[...] = dsum_ref[...]

    ones = jnp.ones((8, TILE), bf16)
    bias = jnp.zeros(bias_ref.shape, f32)
    for i in range(db_ref.shape[0] // TILE):
        rows = slice(i * TILE, (i + 1) * TILE)
        pre = (nt(db_ref[rows, :], wo_ref[...]) * slope_ref[rows, :].astype(f32)).astype(bf16)
        dpre_ref[rows, :] = pre
        bias += nn(ones, pre)
        total[rows, :] += nt(pre, wi_ref[...])
    bias_ref[...] = bias

    @pl.when(j == pl.num_programs(0) - 1)
    def _():
        gain = g_ref[...]
        sums_ref[...] = jnp.zeros_like(sums_ref)
        for i in range(db_ref.shape[0] // TILE):
            rows = slice(i * TILE, (i + 1) * TILE)
            grad = total[rows, :]
            unit = (normed_ref[rows, :] - s_ref[...]) / gain
            done = norm_back(grad * gain, unit, rate_ref[rows, :])
            done_ref[rows, :] = done
            low = done.astype(bf16)
            dattn_ref[rows, :] = low
            sums_ref[0:1, :] += jnp.sum(grad * unit, axis=0, keepdims=True)
            sums_ref[1:2, :] += jnp.sum(grad, axis=0, keepdims=True)
            sums_ref[2:3, :] += jnp.sum(low.astype(f32), axis=0, keepdims=True)


def feed_back(d_branch, w_outer, slope, w_inner, d_sum_two, normed, rate, gain, shift):
    rows, wide = d_branch.shape[0], 512
    whole = pl.BlockSpec((rows, D), lambda j: (0, 0))
    row = pl.BlockSpec((1, D), lambda j: (0, 0))
    tall = pl.BlockSpec((rows, wide), lambda j: (0, j))
    return pl.pallas_call(
        feed_back_kernel,
        grid=(FF // wide,),
        in_specs=[
            whole,
            pl.BlockSpec((wide, D), lambda j: (j, 0)),
            tall,
            pl.BlockSpec((D, wide), lambda j: (0, j)),
            whole, whole,
            pl.BlockSpec((rows, 1), lambda j: (0, 0)),
            row, row,
        ],
        out_specs=[tall, pl.BlockSpec((8, wide), lambda j: (0, j)), whole, whole, pl.BlockSpec((8, D), lambda j: (0, 0))],
        out_shape=[sds((rows, FF), bf16), sds((8, FF), f32), sds((rows, D), f32), sds((rows, D), bf16), sds((8, D), f32)],
        scratch_shapes=[pltpu.VMEM((rows, D), f32)],
        compiler_params=params(),
        cost_estimate=cost(4 * D * FF * rows, 50 * 2**20),
        name="feed_back",
    )(d_branch, w_outer, slope, w_inner, d_sum_two, normed, rate, gain, shift)


def turn_kernel(d_ref, w_ref, out_ref):
    out_ref[...] = nt(d_ref[...], w_ref[...]).astype(bf16)


def turned_product(d, w):
    rows = d.shape[0]
    tile = pl.BlockSpec((TILE, D), lambda i: (i, 0))
    return pl.pallas_call(
        turn_kernel,
        grid=(rows // TILE,),
        in_specs=[tile, pl.BlockSpec((D, D), lambda i: (0, 0))],
        out_specs=tile,
        out_shape=sds((rows, D), bf16),
        compiler_params=params(),
        cost_estimate=cost(2 * D * D * rows, 6 * 2**20),
        name="turned_product",
    )(d, w)


def input_kernel(base_ref, d_ref, w_ref, out_ref):
    out_ref[...] = base_ref[...] + nt(d_ref[...], w_ref[...])


def input_back(base, d, w):
    rows = base.shape[0]
    tile = pl.BlockSpec((TILE, D), lambda i: (i, 0))
    return pl.pallas_call(
        input_kernel,
        grid=(rows // TILE,),
        in_specs=[tile, pl.BlockSpec((TILE, 3 * D), lambda i: (i, 0)), pl.BlockSpec((D, 3 * D), lambda i: (0, 0))],
        out_specs=tile,
        out_shape=sds((rows, D), f32),
        compiler_params=params(),
        cost_estimate=cost(6 * D * D * rows, 20 * 2**20),
        name="input_back",
    )(base, d, w)


def swap(value, axis, bit):
    return lax.ppermute(value, axis, [(i, i ^ bit) for i in range(lax.axis_size(axis))])


def after(value, *others):
    return lax.optimization_barrier((value,) + others)[0]


def gather_weight(shard, own):
    n = lax.axis_size("fsdp")
    rows = shard.shape[0]
    half, quarter = rows // 2, rows // 4
    held, whole = {}, {}
    for r in range(1, n):
        if r & (r - 1) == 0:
            whole[r] = swap(own, "fsdp", r)
            for s in (0, 1):
                held[r, s] = whole[r][s * quarter : (s + 1) * quarter]
        else:
            for s, bit in ((0, 1 << (r.bit_length() - 1)), (1, r & -r)):
                held[r, s] = swap(held[r ^ bit, s], "fsdp", bit)
    found = []
    for r in range(1, n):
        found += [whole[r]] if r in whole else [held[r, 0], held[r, 1]]
    mine = jnp.concatenate(found, axis=0)
    other = swap(mine, "ctx", 1)
    return (shard, mine, other), [whole[r] for r in whole], mine


def half_sets(value, bit):
    shape = value.shape
    split = value.reshape((shape[0] // (2 * bit), 2, bit) + shape[1:])
    rest = (shape[0] // 2,) + shape[1:]
    return split[:, 0].reshape(rest), split[:, 1].reshape(rest)


def add_low(a, b):
    return (a.astype(f32) + b.astype(f32)).astype(bf16)


def scatter_sum(keep, send):
    n = lax.axis_size("fsdp")
    got = swap(send, "ctx", 1)
    quarter = keep.shape[1] // 2
    bits = [1 << b for b in range(n.bit_length() - 1)]
    parts = []
    for s, order in ((0, bits), (1, bits[::-1])):
        rows = slice(s * quarter, (s + 1) * quarter)
        current = add_low(keep[:, rows], got[:, rows])
        ids = list(range(n))
        for bit in order:
            where = [i for i, r in enumerate(ids) if not r & bit]
            away = [i for i, r in enumerate(ids) if r & bit]
            step = away[0] - where[0]
            mine, theirs = half_sets(current, step)
            ids = [ids[i] for i in where]
            current = add_low(mine, swap(theirs, "fsdp", bit))
        parts.append(current[0])
    return parts


def chain_sum(value):
    count = lax.axis_size("ctx") // 2
    position = lax.axis_index("ctx") // 2
    half = count // 2

    def move(value, chip_pairs):
        pairs = [(2 * a + c, 2 * b + c) for a, b in chip_pairs for c in (0, 1)]
        return lax.ppermute(value, "ctx", pairs)

    for s in range(half - 1):
        value = add_low(value, move(value, [(s, s + 1), (count - 1 - s, count - 2 - s)]))
    inner = (position == half - 1) | (position == half)
    across = move(value, [(half - 1, half), (half, half - 1)])
    value = jnp.where(inner, add_low(value, across), value)
    for s in reversed(range(half - 1)):
        back = move(value, [(s + 1, s), (count - 2 - s, count - 1 - s)])
        value = jnp.where((position == s) | (position == count - 1 - s), back, value)
    return value


def gather_small(vector, f):
    n = lax.axis_size("fsdp")
    value = vector.reshape(1, -1)
    bit = 1
    while bit < n:
        value = jnp.concatenate([value, swap(value, "fsdp", bit)], axis=0)
        bit *= 2
    bit = 1
    while bit < n:
        split = value.reshape(n // (2 * bit), 2, bit, -1)
        value = jnp.where(f & bit > 0, split[:, ::-1], split).reshape(n, -1)
        bit *= 2
    return value


def sum_everywhere(value):
    for axis in ("ctx", "fsdp"):
        bit = 1
        while bit < lax.axis_size(axis):
            value = value + swap(value, axis, bit)
            bit *= 2
    return value


def body(
    layer_input,
    teacher_states,
    out_cotangent,
    doc_start,
    valid_flag,
    query_weight,
    query_bias,
    key_weight,
    value_weight,
    value_bias,
    proj_weight,
    proj_bias,
    attn_gain,
    attn_shift,
    inner_weight,
    inner_bias,
    outer_weight,
    outer_bias,
    final_gain,
    final_shift,
):
    n_ctx, n_fsdp = lax.axis_size("ctx"), lax.axis_size("fsdp")
    c, f = lax.axis_index("ctx"), lax.axis_index("fsdp")
    parity = c % 2
    tokens = layer_input[0]
    rows = tokens.shape[0]
    part = query_weight.shape[0]
    where = jnp.stack([f, parity]).astype(jnp.int32)
    order = jnp.concatenate([f ^ jnp.arange(n_fsdp, dtype=jnp.int32), parity[None].astype(jnp.int32)])

    up = [(i, i + 1) for i in range(n_ctx - 1)]
    down = [(b, a) for a, b in up]
    before = lax.ppermute(tokens[rows - DOC_MAX :], "ctx", up)
    behind = lax.ppermute(tokens[:DOC_MAX], "ctx", down)
    x_near = jnp.concatenate([before, tokens, behind], axis=0)

    small = jnp.concatenate(
        [query_bias, value_bias, proj_bias, attn_gain, attn_shift, outer_bias, final_gain, final_shift, inner_bias]
    )
    small = gather_small(small, f).astype(f32)
    vectors = [small[:, i * part : (i + 1) * part].reshape(1, D) for i in range(8)]
    b_query, b_value, b_proj, g_attn, s_attn, b_outer, g_final, s_final = vectors
    b_inner = small[:, 8 * part :].reshape(1, FF)

    flags = valid_flag[0].astype(f32)[:, None]

    def own_half(shard):
        half = shard.shape[0] // 2
        return lax.dynamic_slice_in_dim(shard, parity * half, half)

    qkv_shard = jnp.concatenate([query_weight, key_weight, value_weight], axis=1)
    qkv_pieces, qkv_first, qkv_last = gather_weight(qkv_shard, own_half(qkv_shard))
    proj_own = after(own_half(proj_weight), *qkv_first)
    proj_pieces, proj_first, proj_last = gather_weight(proj_weight, proj_own)
    inner_own = after(own_half(inner_weight), *qkv_first)
    inner_pieces, inner_first, inner_last = gather_weight(inner_weight, inner_own)
    outer_own = after(own_half(outer_weight), *proj_first, qkv_last)
    outer_pieces, outer_first, outer_last = gather_weight(outer_weight, outer_own)

    count = sum_everywhere(after(jnp.full((8, 128), jnp.sum(flags), f32), *qkv_first))[0, 0]

    position = c * rows
    starts = doc_start[0]
    near_starts = lax.dynamic_slice_in_dim(
        jnp.concatenate(
            [jnp.full((DOC_MAX,), -1, jnp.int32), starts, jnp.full((DOC_MAX,), 2**30, jnp.int32)]
        ),
        position,
        rows + 2 * DOC_MAX,
    )
    own_starts = near_starts[DOC_MAX : DOC_MAX + rows]
    count_tiles = rows // TILE
    low_tile = (own_starts[::TILE] - position + DOC_MAX) // TILE
    last = position + TILE * (1 + jnp.arange(count_tiles, dtype=jnp.int32)) - 1
    ends = jnp.sum((near_starts[None, :] <= last[:, None]).astype(jnp.int32), axis=1)
    high_tile = (ends + TILE - 1) // TILE
    idq = own_starts.reshape(count_tiles, 1, TILE)
    idk = near_starts[:, None]

    query, keys, values, keys_t, values_t, w_qkv = project_qkv(where, qkv_pieces, x_near, b_query, b_value)
    context, log_totals = attn_fwd(low_tile, high_tile, query, keys, values_t, idq, idk)
    normed, normed_low, rate, w_proj = mix_and_norm(where, proj_pieces, context, b_proj, tokens, g_attn, s_attn)
    act, slope, w_inner = inner_forward(where, inner_pieces, normed_low, b_inner)
    coef = (n_fsdp * n_ctx * rows / count).reshape(1)
    layer_out, d_sum_two, d_branch, final_sums, w_outer = outer_forward(
        where, outer_pieces, coef, act, b_outer, normed, g_final, s_final, teacher_states[0], out_cotangent[0], flags
    )

    outer_parts = scatter_sum(*gram(order, act, d_branch, n_fsdp, 512))
    d_pre, inner_bias_sum, d_sum_one, d_attn, attn_sums = feed_back(
        d_branch, w_outer, slope, w_inner, d_sum_two, normed, rate, g_attn, s_attn
    )
    inner_parts = scatter_sum(*gram(order, normed_low, d_pre, n_fsdp, 2048))
    d_context = turned_product(d_attn, w_proj)
    proj_parts = scatter_sum(*gram(order, context, d_attn, n_fsdp, D))
    outer_total = chain_sum(jnp.concatenate(outer_parts, axis=0))
    inner_total = chain_sum(jnp.concatenate(inner_parts, axis=0))
    proj_total = chain_sum(jnp.concatenate(proj_parts, axis=0))
    d_query, near_dk, near_dv = attn_bwd(
        low_tile, high_tile, query, d_context, context, keys, keys_t, values, log_totals, idq, idk
    )
    near_d = jnp.concatenate([near_dk, near_dv], axis=1)
    from_above = lax.ppermute(near_d[:DOC_MAX], "ctx", down)
    from_below = lax.ppermute(near_d[rows + DOC_MAX :], "ctx", up)
    own = near_d[DOC_MAX : DOC_MAX + rows].astype(f32)
    rest = jnp.zeros((rows - DOC_MAX, 2 * D), f32)
    own = (
        own
        + jnp.concatenate([from_below.astype(f32), rest], axis=0)
        + jnp.concatenate([rest, from_above.astype(f32)], axis=0)
    ).astype(bf16)
    d_keys, d_values = own[:, :D], own[:, D:]
    d_joined = jnp.concatenate([d_query, own], axis=1)
    qkv_parts = scatter_sum(*gram(order, tokens, d_joined, n_fsdp, 3 * D // 2))
    input_grad = input_back(d_sum_one, d_joined, w_qkv)
    qkv_total = chain_sum(jnp.concatenate(qkv_parts, axis=0))

    def finish(mine):
        quarter = mine.shape[0] // 2
        other = swap(mine, "ctx", 1)
        first = parity == 0
        return jnp.concatenate([jnp.where(first, mine, other), jnp.where(first, other, mine)], axis=0).astype(f32)

    outer_grad, inner_grad, proj_grad, qkv_grad = (
        finish(outer_total), finish(inner_total), finish(proj_total), finish(qkv_total)
    )

    early = jnp.concatenate([final_sums[:4], attn_sums[:3], inner_bias_sum[:1].reshape(4, D)], axis=0)
    early = sum_everywhere(jnp.concatenate([early, jnp.zeros((5, D), f32)], axis=0))
    late = jnp.sum(jnp.stack([d_query, d_values]).astype(f32), axis=1)
    late = sum_everywhere(jnp.concatenate([late, jnp.zeros((6, D), f32)], axis=0))
    mse = jnp.sum(early[3]) / (count * D)

    def mine(vector):
        length = vector.shape[0] // n_fsdp
        return lax.dynamic_slice_in_dim(vector, f * length, length)

    return (
        layer_out[None],
        input_grad[None],
        mse,
        qkv_grad[:, :D],
        mine(late[0]),
        qkv_grad[:, D : 2 * D],
        qkv_grad[:, 2 * D :],
        mine(late[1]),
        proj_grad,
        mine(early[6]),
        mine(early[4]),
        mine(early[5]),
        inner_grad,
        mine(early[7:11].reshape(FF)),
        outer_grad,
        mine(early[2]),
        mine(early[0]),
        mine(early[1]),
    )


def solution(mesh):
    tokens = P("fsdp", "ctx", None)
    matrix, vector = P("fsdp", None), P("fsdp")
    weights = (
        matrix, vector, matrix, matrix, vector, matrix, vector, vector, vector, matrix, vector, matrix, vector, vector, vector,
    )
    return jax.shard_map(
        body,
        mesh=mesh,
        in_specs=(tokens, tokens, tokens, matrix, P("fsdp", "ctx")) + weights,
        out_specs=(tokens, tokens, P()) + weights,
        check_vma=False,
    )
```

time: 1770 us -> 759 us (0.43)
  matrix products: 477 us -> 0 us
  blocking collectives: 341 us -> 0 us
  Pallas kernels: 0 us -> 269 us
  waiting for transfers between devices: 514 us -> 260 us
  other arithmetic: 217 us -> 35.5 us
  local copies, waits for them, and re-layouts: 157 us -> 59.1 us
  starting transfers between devices: 29.6 us -> 123 us
    unnamed x22 -> x0, waiting for transfers between devices: 514 us -> none
    dot_general x26 -> x0, matrix products: 477 us -> none  [the longest x4 83.6 us: block_scores(): jnp.einsum('qhd,khd->hqk', query_block, key_block, preferred_element_type...]
    pallas_call x0 -> x13, Pallas kernels: none -> 269 us  [the longest x4 54.8 us: gram(): pl.pallas_call(gram_kernel, grid_spec=pltpu.PrefetchScalarGridSpec(num_sc...]
    ppermute x4 -> x77, waiting for transfers between devices: 0.01 us -> 260 us  [the longest x61 170 us: swap(): lax.ppermute(value, axis, [(i, i ^ bit) for i in range(lax.axis_size(axis...]
    all_gather x22 -> x0, blocking collectives: 217 us -> none  [the longest x1 16.6 us: body(): lax.all_gather(by_both[5].astype(jnp.bfloat16), 'ctx', axis=1, tiled=True)]
    ppermute x4 -> x77, starting transfers between devices: 28.9 us -> 123 us  [the longest x61 96.1 us: swap(): lax.ppermute(value, axis, [(i, i ^ bit) for i in range(lax.axis_size(axis...]
    psum x2 -> x0, blocking collectives: 79.5 us -> none  [body(): lax.psum((jnp.sum(flags), jnp.sum(flags[:, None] * error * error)), ('ctx...]
    convert_element_type x13 -> x15, other arithmetic: 87.9 us -> 19.5 us  [the longest x8 9.04 us: add_low(): return (a.astype(f32) + b.astype(f32)).astype(bf16)]
  transfers between devices with their start and end apart: 19 -> 77, of which waited for: 2 -> 32; matrix products, arithmetic and copies ran while one was open for 21% -> 11% of each run, Pallas kernels for 0% -> 31%
where the time goes in v1:
time: 759 us; the launch traced here: 752 us
  Pallas kernels  269 us (35%)
  waiting for transfers between devices  260 us (34%)
  starting transfers between devices  123 us (16%)
  local copies, waits for them, and re-layouts  59.1 us (8%)
  other arithmetic  35.5 us (5%)
    ppermute x61, waiting for transfers between devices, swap(): lax.ppermute(value, axis, [(i, i ^ bit) for i in range(lax.axis_size(axis...  170 us
    ppermute x61, starting transfers between devices, swap(): lax.ppermute(value, axis, [(i, i ^ bit) for i in range(lax.axis_size(axis...  96.1 us
    ppermute x12, waiting for transfers between devices, move(): return lax.ppermute(value, 'ctx', pairs)  90.2 us
    pallas_call x4, Pallas kernels, gram(): pl.pallas_call(gram_kernel, grid_spec=pltpu.PrefetchScalarGridSpec(num_sc...  54.8 us
    pallas_call x1, Pallas kernels, attn_bwd(): pl.pallas_call(attn_bwd_kernel, grid_spec=pltpu.PrefetchScalarGridSpec(nu...  45 us
    pallas_call x1, Pallas kernels, feed_back(): pl.pallas_call(feed_back_kernel, grid=(FF // wide,), in_specs=[whole, pl....  36.9 us
    pallas_call x1, Pallas kernels, inner_forward(): pl.pallas_call(inner_kernel, grid=(FF // wide,), in_specs=WEIGHT_SPECS +...  31.5 us
    pallas_call x1, Pallas kernels, attn_fwd(): pl.pallas_call(attn_fwd_kernel, grid_spec=pltpu.PrefetchScalarGridSpec(nu...  31.2 us
  transfers between devices with their start and end apart: 77, of which 32 were waited for; matrix products, arithmetic and copies ran while one was open for 11% of the time, Pallas kernels for 31%

profile of v1, /device:TPU:0, one launch (start us, length us, event | category | flops | bytes accessed | tf_op | source)
XLA Modules:
  0.0 752.3 jit_solution(10668634966418748230)
XLA Ops:
  0.8 2.0 constant_dynamic-update-slice_fusion.2
  5.5 2.1 constant_dynamic-slice_fusion.9
  7.6 2.9 collective-permute-start
  17.9 2.3 constant_dynamic-slice_fusion.8
  20.7 2.3 constant_dynamic-slice_fusion.11
  23.5 5.0 collective-permute-done.27
  40.4 2.1 constant_dynamic-update-slice_fusion.6
  47.7 3.4 collective-permute-done.4
  52.4 2.6 collective-permute-start.13
  58.0 2.3 collective-permute-start.25
  60.3 13.5 %collective-permute-done.16 = bf16[128,4096]{1,0:T(8,128)(2,1)S(1)} collective-permute-done((bf16[128,4096]{1,0:T(8,128)(2,1)S(1)}, bf16[128,4096]{1,0:T(8,128)(2,1)S(1)}, u32[]{:S(2)}, u32[]{:S(2)}) %collective-permute-start.16) | collective-permute-done | bytes 1048608 | tf_op jit(solution)/shard_map/ppermute | solution.py:545
  74.5 2.7 collective-permute-done.17
  80.0 16.3 %collective-permute-done.6 = bf16[512,1024]{1,0:T(8,128)(2,1)S(1)} collective-permute-done((bf16[512,1024]{1,0:T(8,128)(2,1)S(1)}, bf16[512,1024]{1,0:T(8,128)(2,1)S(1)}, u32[]{:S(2)}, u32[]{:S(2)}) %collective-permute-start.6) | collective-permute-done | bytes 1048608 | tf_op jit(solution)/shard_map/ppermute | solution.py:545
  97.6 2.1 collective-permute-done.7
  101.5 6.7 collective-permute-done.18
  110.9 7.9 %collective-permute-done.8 = bf16[256,1024]{1,0:T(8,128)(2,1)} collective-permute-done((bf16[256,1024]{1,0:T(8,128)(2,1)S(1)}, bf16[256,1024]{1,0:T(8,128)(2,1)}, u32[]{:S(2)}, u32[]{:S(2)}) %collective-permute-start.8) | collective-permute-done | bytes 524320 | tf_op jit(solution)/shard_map/ppermute | solution.py:545
  121.3 3.7 collective-permute-done.9
  138.9 3.6 pad_maximum_fusion.1.x_ref
  144.1 19.2 %project_qkv.1 = (bf16[1024,1024]{1,0:T(8,128)(2,1)}, bf16[2048,1024]{1,0:T(8,128)(2,1)}, bf16[2048,1024]{1,0:T(8,128)(2,1)}, bf16[1024,2048]{1,0:T(8,128)(2,1)}...) custom-call(s32[2]{0:T(128)} %pad_add_fusion.1.where_ref, ...), custom_call_target="tpu_custom_call" | custom-call | flops 10737418240 | bytes 31457280 | tf_op jit(solution)/shard_map/project_qkv/pallas_call | solution.py:117
  163.3 31.2 %attn_forward.1 = (bf16[1024,1024]{1,0:T(8,128)(2,1)}, f32[4,8,1024]{2,1,0:T(8,128)}) custom-call(s32[4]{0:T(128)} %get-tuple-element.139.lo_ref, s32[4]{0:T(128)} %get-tuple-element.138.hi_ref, bf16[1024,1024]{1,0:T(8,128)(2,1)} %get-tuple-element.62.q_ref, bf16[2048,1024]{1,0:T(8,128)(2,1)} %get-tuple-element.63.k_ref, ...), custom_call_target="tpu_custom_call" | custom-call | tf_op jit(solution)/shard_map/attn_forward/pallas_call | solution.py:191
  195.4 9.6 %mix_and_norm.1 = (f32[1024,1024]{1,0:T(8,128)}, bf16[1024,1024]{1,0:T(8,128)(2,1)}, f32[1024,1]{1,0:T(8,128)}, bf16[1024,1024]{1,0:T(8,128)(2,1)}) custom-call(s32[2]{0:T(128)} %pad_add_fusion.1.where_ref, bf16[256,1024]{1,0:T(8,128)(2,1)} %shard.3, bf16[384,1024]{1,0:T(8,128)(2,1)} %copy-done.14, bf16[384,1024]{1,0:T(8,128)(2,1)} %copy-done.29, ...), custom_call_target="tpu_custom_call" | custom-call | flops 2147483648 | bytes 14680064 | tf_op jit(solution)/shard_map/mix_and_norm/pallas_call | solution.py:306
  205.0 31.5 %inner_forward.1 = (bf16[1024,4096]{1,0:T(8,128)(2,1)}, bf16[1024,4096]{1,0:T(8,128)(2,1)}, bf16[1024,4096]{1,0:T(8,128)(2,1)}) custom-call(s32[2]{0:T(128)} %pad_add_fusion.1.where_ref, bf16[256,4096]{1,0:T(8,128)(2,1)} %shard.4, bf16[384,4096]{1,0:T(8,128)(2,1)} %constant_dynamic-update-slice_fusion.11.mine, ...), custom_call_target="tpu_custom_call" | custom-call | flops 8589934592 | bytes 27262976 | tf_op jit(solution)/shard_map/inner_forward/pallas_call | solution.py:342
  236.6 22.4 %outer_forward.1 = (bf16[1024,1024]{1,0:T(8,128)(2,1)}, f32[1024,1024]{1,0:T(8,128)}, bf16[1024,1024]{1,0:T(8,128)(2,1)}, f32[8,1024]{1,0:T(8,128)}, bf16[4096,1024]{1,0:T(8,128)(2,1)}) custom-call(s32[2]{0:T(128)} %pad_add_fusion.1.where_ref, bf16[1024,1024]{1,0:T(8,128)(2,1)} %shard.5, bf16[1536,1024]{1,0:T(8,128)(2,1)} %copy-done.13, ...), custom_call_target="tpu_custom_call" | custom-call | flops 8589934592 | bytes 33554432 | tf_op jit(solution)/shard_map/outer_forward/pallas_call | solution.py:388
  259.0 17.0 %gram.7 = (bf16[4,512,1024]{2,1,0:T(8,128)(2,1)}, bf16[4,512,1024]{2,1,0:T(8,128)(2,1)}) custom-call(s32[5]{0:T(128)} %pad_add_fusion.2.order_ref, bf16[1024,4096]{1,0:T(8,128)(2,1)} %get-tuple-element.67.act_ref.left_ref, bf16[1024,1024]{1,0:T(8,128)(2,1)} %get-tuple-element.70.db_ref.right_ref), custom_call_target="tpu_custom_call" | custom-call | flops 8589934592 | bytes 18874368 | tf_op jit(solution)/shard_map/gram/pallas_call | solution.py:425
  276.0 16.2 %collective-permute-start.68 = (bf16[4,512,1024]{2,1,0:T(8,128)(2,1)}, bf16[4,512,1024]{2,1,0:T(8,128)(2,1)}, u32[]{:S(2)}, u32[]{:S(2)}) collective-permute-start(bf16[4,512,1024]{2,1,0:T(8,128)(2,1)} %get-tuple-element.97), channel_id=1, source_target_pairs={{0,4},{4,0},{8,12},{12,8},{16,20},{20,16},{24,28},{28,24},{1,5},{5... | collective-permute-start | bytes 12582920 | tf_op jit(solution)/shard_map/ppermute | solution.py:545
  292.1 36.9 %feed_back.1 = (bf16[1024,4096]{1,0:T(8,128)(2,1)}, f32[8,4096]{1,0:T(8,128)}, f32[1024,1024]{1,0:T(8,128)}, bf16[1024,1024]{1,0:T(8,128)(2,1)}, f32[8,1024]{1,0:T(8,128)}) custom-call(bf16[1024,1024]{1,0:T(8,128)(2,1)} %get-tuple-element.70.db_ref.right_ref, bf16[4096,1024]{1,0:T(8,128)(2,1)} %get-tuple-element.71.wo_ref, ...), custom_call_target="tpu_custom_call" | custom-call | flops 17179869184 | bytes 52428800 | tf_op jit(solution)/shard_map/feed_back/pallas_call | solution.py:485
  329.1 16.7 %gram.6 = (bf16[4,128,4096]{2,1,0:T(8,128)(2,1)}, bf16[4,128,4096]{2,1,0:T(8,128)(2,1)}) custom-call(s32[5]{0:T(128)} %pad_add_fusion.2.order_ref, bf16[1024,1024]{1,0:T(8,128)(2,1)} %get-tuple-element.66.x_ref.left_ref, bf16[1024,4096]{1,0:T(8,128)(2,1)} %get-tuple-element.93.right_ref), custom_call_target="tpu_custom_call" | custom-call | flops 8589934592 | bytes 18874368 | tf_op jit(solution)/shard_map/gram/pallas_call | solution.py:425
  347.4 6.8 gram.5
  356.1 6.1 turned_product.1.do_ref
  362.3 45.0 %attn_backward.1 = (bf16[1024,1024]{1,0:T(8,128)(2,1)}, bf16[2048,1024]{1,0:T(8,128)(2,1)}, bf16[2048,1024]{1,0:T(8,128)(2,1)}) custom-call(s32[4]{0:T(128)} %get-tuple-element.139.lo_ref, s32[4]{0:T(128)} %get-tuple-element.138.hi_ref, bf16[1024,1024]{1,0:T(8,128)(2,1)} %get-tuple-element.62.q_ref, bf16[1024,1024]{1,0:T(8,128)(2,1)} %turned_product.1.do_ref, ...), custom_call_target="tpu_custom_call" | custom-call | tf_op jit(solution)/shard_map/attn_backward/pallas_call | solution.py:255
  407.3 22.1 %collective-permute-start.33 = (f32[16,1024]{1,0:T(8,128)S(1)}, f32[16,1024]{1,0:T(8,128)S(1)}, u32[]{:S(2)}, u32[]{:S(2)}) collective-permute-start(f32[16,1024]{1,0:T(8,128)S(1)} %add.226), channel_id=1, source_target_pairs={{0,16},{4,20},{8,24},{12,28},{16,0},{20,4},{24,8},{28,12},{1,17},{... | collective-permute-start | bytes 196616 | tf_op jit(solution)/shard_map/ppermute | solution.py:545
  429.4 2.8 constant_dynamic-update-slice_fusion.20
  433.5 3.1 collective-permute-done.34
  436.6 3.1 collective-permute-start.35
  439.7 2.3 fusion.41
  442.0 4.6 collective-permute-start.29
  451.6 7.7 %collective-permute-done.51 = bf16[2,64,1024]{2,1,0:T(8,128)(2,1)S(1)} collective-permute-done((bf16[2,64,1024]{2,1,0:T(8,128)(2,1)S(1)}, bf16[2,64,1024]{2,1,0:T(8,128)(2,1)S(1)}, u32[]{:S(2)}, u32[]{:S(2)}) %collective-permute-start.51) | collective-permute-done | bytes 262176 | tf_op jit(solution)/shard_map/ppermute | solution.py:545
  459.8 7.9 %collective-permute-done.53 = bf16[2,64,1024]{2,1,0:T(8,128)(2,1)S(1)} collective-permute-done((bf16[2,64,1024]{2,1,0:T(8,128)(2,1)S(1)}, bf16[2,64,1024]{2,1,0:T(8,128)(2,1)S(1)}, u32[]{:S(2)}, u32[]{:S(2)}) %collective-permute-start.53) | collective-permute-done | bytes 262176 | tf_op jit(solution)/shard_map/ppermute | solution.py:545
  468.1 4.5 collective-permute-done.52
  473.4 4.2 collective-permute-done.54
  483.6 4.0 add_convert_fusion
  491.6 6.2 collective-permute-start.46
  497.8 3.2 pad_maximum_fusion.d_ref.right_ref
  501.0 4.4 collective-permute-done.46
  505.3 14.3 %gram.4 = (bf16[4,128,3072]{2,1,0:T(8,128)(2,1)}, bf16[4,128,3072]{2,1,0:T(8,128)(2,1)}) custom-call(s32[5]{0:T(128)} %pad_add_fusion.2.order_ref, bf16[1024,1024]{1,0:T(8,128)(2,1)} %bitcast.249, bf16[1024,3072]{1,0:T(8,128)(2,1)} %pad_maximum_fusion.d_ref.right_ref), custom_call_target="tpu_custom_call" | custom-call | flops 6442450944 | bytes 14680064 | tf_op jit(solution)/shard_map/gram/pallas_call | solution.py:425
  520.4 12.4 %input_back.1 = f32[1024,1024]{1,0:T(8,128)} custom-call(f32[1024,1024]{1,0:T(8,128)} %get-tuple-element.76.base_ref, bf16[1024,3072]{1,0:T(8,128)(2,1)} %pad_maximum_fusion.d_ref.right_ref, bf16[1024,3072]{1,0:T(8,128)(2,1)} %get-tuple-element.85.w_ref), custom_call_target="tpu_custom_call" | custom-call | flops 6442450944 | bytes 20971520 | tf_op jit(solution)/shard_map/input_back/pallas_call | solution.py:532
  534.7 2.0 collective-permute-done.49
  537.4 3.5 add_convert_fusion.2
  543.4 3.0 add_convert_fusion.4
  548.2 18.9 %collective-permute-done.69 = bf16[2,256,1024]{2,1,0:T(8,128)(2,1)S(1)} collective-permute-done((bf16[2,256,1024]{2,1,0:T(8,128)(2,1)S(1)}, bf16[2,256,1024]{2,1,0:T(8,128)(2,1)S(1)}, u32[]{:S(2)}, u32[]{:S(2)}) %collective-permute-start.69) | collective-permute-done | bytes 1048608 | tf_op jit(solution)/shard_map/ppermute | solution.py:545
  570.2 17.5 %collective-permute-done.60 = bf16[2,64,4096]{2,1,0:T(8,128)(2,1)S(1)} collective-permute-done((bf16[2,64,4096]{2,1,0:T(8,128)(2,1)S(1)}, bf16[2,64,4096]{2,1,0:T(8,128)(2,1)S(1)}, u32[]{:S(2)}, u32[]{:S(2)}) %collective-permute-start.60) | collective-permute-done | bytes 1048608 | tf_op jit(solution)/shard_map/ppermute | solution.py:545
  589.3 4.0 collective-permute-done.62
  597.2 7.3 collective-permute-done.70
  607.3 8.5 %collective-permute-done.61 = bf16[1,64,4096]{2,1,0:T(8,128)(2,1)S(1)} collective-permute-done((bf16[1,64,4096]{2,1,0:T(8,128)(2,1)S(1)}, bf16[1,64,4096]{2,1,0:T(8,128)(2,1)S(1)}, u32[]{:S(2)}, u32[]{:S(2)}) %collective-permute-start.61) | collective-permute-done | bytes 524320 | tf_op jit(solution)/shard_map/ppermute | solution.py:545
  615.7 3.4 collective-permute-start.73
  619.4 8.3 %collective-permute-done.37 = bf16[2,64,3072]{2,1,0:T(8,128)(2,1)S(1)} collective-permute-done((bf16[2,64,3072]{2,1,0:T(8,128)(2,1)S(1)}, bf16[2,64,3072]{2,1,0:T(8,128)(2,1)S(1)}, u32[]{:S(2)}, u32[]{:S(2)}) %collective-permute-start.37) | collective-permute-done | bytes 786464 | tf_op jit(solution)/shard_map/ppermute | solution.py:545
  630.6 6.0 collective-permute-done.38
  638.2 3.4 collective-permute-start.41
  644.8 14.7 %collective-permute-done.41 = bf16[128,3072]{1,0:T(8,128)(2,1)S(1)} collective-permute-done((bf16[128,3072]{1,0:T(8,128)(2,1)S(1)}, bf16[128,3072]{1,0:T(8,128)(2,1)S(1)}, u32[]{:S(2)}, u32[]{:S(2)}) %collective-permute-start.41) | collective-permute-done | bytes 786464 | tf_op jit(solution)/shard_map/ppermute | solution.py:612
  660.5 16.5 %collective-permute-done.64 = bf16[128,4096]{1,0:T(8,128)(2,1)S(1)} collective-permute-done((bf16[128,4096]{1,0:T(8,128)(2,1)S(1)}, bf16[128,4096]{1,0:T(8,128)(2,1)S(1)}, u32[]{:S(2)}, u32[]{:S(2)}) %collective-permute-start.64) | collective-permute-done | bytes 1048608 | tf_op jit(solution)/shard_map/ppermute | solution.py:612
  684.3 42.3 %collective-permute-done.43 = bf16[128,3072]{1,0:T(8,128)(2,1)S(1)} collective-permute-done((bf16[128,3072]{1,0:T(8,128)(2,1)S(1)}, bf16[128,3072]{1,0:T(8,128)(2,1)S(1)}, u32[]{:S(2)}, u32[]{:S(2)}) %collective-permute-start.43) | collective-permute-done | bytes 786464 | tf_op jit(solution)/shard_map/ppermute | solution.py:612
  727.5 15.7 %collective-permute-done.66 = bf16[128,4096]{1,0:T(8,128)(2,1)S(1)} collective-permute-done((bf16[128,4096]{1,0:T(8,128)(2,1)S(1)}, bf16[128,4096]{1,0:T(8,128)(2,1)S(1)}, u32[]{:S(2)}, u32[]{:S(2)}) %collective-permute-start.66) | collective-permute-done | bytes 1048608 | tf_op jit(solution)/shard_map/ppermute | solution.py:612
  745.8 2.4 maximum_convert_fusion.1
  748.4 2.5 maximum_convert_fusion
  (346 shorter events, 117.7 us)
Async XLA Ops:
  7.6 26.8 %collective-permute-start = (bf16[128,3072]{1,0:T(8,128)(2,1)}, bf16[128,3072]{1,0:T(8,128)(2,1)}, u32[]{:S(2)}, u32[]{:S(2)}) collective-permute-start(bf16[128,3072]{1,0:T(8,128)(2,1)} %constant_dynamic-slice_fusion.9), channel_id=1, source_target_pairs={{0,1},{1,0},{2,3},{3,2},{4,5},{5,4},{6,7},{7,6},{8,9},{9,8},{10,11... | collective-permute-start | bytes 2359304 | tf_op jit(solution)/shard_map/ppermute | solution.py:545
  10.5 23.9 %collective-permute-start.1 = (bf16[128,3072]{1,0:T(8,128)(2,1)}, bf16[128,3072]{1,0:T(8,128)(2,1)S(1)}, u32[]{:S(2)}, u32[]{:S(2)}) collective-permute-start(bf16[128,3072]{1,0:T(8,128)(2,1)} %constant_dynamic-slice_fusion.9), channel_id=1, source_target_pairs={{0,2},{1,3},{2,0},{3,1},{4,6},{5,7},{6,4},{7,5},{8,10},{9,11},{10,... | collective-permute-start | bytes 2359304 | tf_op jit(solution)/shard_map/ppermute | solution.py:545
  13.8 14.7 %collective-permute-start.27 = (bf16[1,3072]{1,0:T(2,128)(2,1)S(1)}, bf16[1,3072]{1,0:T(2,128)(2,1)S(1)}, u32[]{:S(2)}, u32[]{:S(2)}) collective-permute-start(bf16[1,3072]{1,0:T(2,128)(2,1)S(1)} %reshape.301), channel_id=1, source_target_pairs={{0,1},{1,0},{2,3},{3,2},{4,5},{5,4},{6,7},{7,6},{8,9},{9,8},{10,11... | collective-permute-start | bytes 18440 | tf_op jit(solution)/shard_map/ppermute | solution.py:545
  34.4 21.4 %collective-permute-start.2 = (bf16[128,1024]{1,0:T(8,128)(2,1)S(1)}, bf16[128,1024]{1,0:T(8,128)(2,1)S(1)}, u32[]{:S(2)}, u32[]{:S(2)}) collective-permute-start(bf16[128,1024]{1,0:T(8,128)(2,1)S(1)} %constant_dynamic-slice_fusion.10), channel_id=1, source_target_pairs={{0,1},{1,0},{2,3},{3,2},{4,5},{5,4},{6,7},{7,6},{8,9},{9,8},{10,11... | collective-permute-start | bytes 786440 | tf_op jit(solution)/shard_map/ppermute | solution.py:545
  36.0 19.9 %collective-permute-start.3 = (bf16[128,1024]{1,0:T(8,128)(2,1)S(1)}, bf16[128,1024]{1,0:T(8,128)(2,1)}, u32[]{:S(2)}, u32[]{:S(2)}) collective-permute-start(bf16[128,1024]{1,0:T(8,128)(2,1)S(1)} %constant_dynamic-slice_fusion.10), channel_id=1, source_target_pairs={{0,2},{1,3},{2,0},{3,1},{4,6},{5,7},{6,4},{7,5},{8,10},{9,11},{10,... | collective-permute-start | bytes 786440 | tf_op jit(solution)/shard_map/ppermute | solution.py:545
  37.5 13.6 %collective-permute-start.4 = (bf16[64,3072]{1,0:T(8,128)(2,1)S(1)}, bf16[64,3072]{1,0:T(8,128)(2,1)S(1)}, u32[]{:S(2)}, u32[]{:S(2)}) collective-permute-start(bf16[64,3072]{1,0:T(8,128)(2,1)S(1)} %slice.379), channel_id=1, source_target_pairs={{0,2},{1,3},{2,0},{3,1},{4,6},{5,7},{6,4},{7,5},{8,10},{9,11},{10,... | collective-permute-start | bytes 1179656 | tf_op jit(solution)/shard_map/ppermute | solution.py:545
  39.1 13.3 %collective-permute-start.5 = (bf16[64,3072]{1,0:T(8,128)(2,1)S(1)}, bf16[64,3072]{1,0:T(8,128)(2,1)S(1)}, u32[]{:S(2)}, u32[]{:S(2)}) collective-permute-start(bf16[64,3072]{1,0:T(8,128)(2,1)S(1)} %slice.380), channel_id=1, source_target_pairs={{0,1},{1,0},{2,3},{3,2},{4,5},{5,4},{6,7},{7,6},{8,9},{9,8},{10,11... | collective-permute-start | bytes 1179656 | tf_op jit(solution)/shard_map/ppermute | solution.py:545
  46.2 27.6 %collective-permute-start.16 = (bf16[128,4096]{1,0:T(8,128)(2,1)S(1)}, bf16[128,4096]{1,0:T(8,128)(2,1)S(1)}, u32[]{:S(2)}, u32[]{:S(2)}) collective-permute-start(bf16[128,4096]{1,0:T(8,128)(2,1)S(1)} %copy-done.11), channel_id=1, source_target_pairs={{0,1},{1,0},{2,3},{3,2},{4,5},{5,4},{6,7},{7,6},{8,9},{9,8},{10,11... | collective-permute-start | bytes 3145736 | tf_op jit(solution)/shard_map/ppermute | solution.py:545
  51.1 26.1 %collective-permute-start.17 = (bf16[128,4096]{1,0:T(8,128)(2,1)S(1)}, bf16[128,4096]{1,0:T(8,128)(2,1)S(1)}, u32[]{:S(2)}, u32[]{:S(2)}) collective-permute-start(bf16[128,4096]{1,0:T(8,128)(2,1)S(1)} %copy-done.11), channel_id=1, source_target_pairs={{0,2},{1,3},{2,0},{3,1},{4,6},{5,7},{6,4},{7,5},{8,10},{9,11},{10,... | collective-permute-start | bytes 3145736 | tf_op jit(solution)/shard_map/ppermute | solution.py:545
  55.8 40.5 %collective-permute-start.6 = (bf16[512,1024]{1,0:T(8,128)(2,1)S(1)}, bf16[512,1024]{1,0:T(8,128)(2,1)S(1)}, u32[]{:S(2)}, u32[]{:S(2)}) collective-permute-start(bf16[512,1024]{1,0:T(8,128)(2,1)S(1)} %copy-done.10), channel_id=1, source_target_pairs={{0,1},{1,0},{2,3},{3,2},{4,5},{5,4},{6,7},{7,6},{8,9},{9,8},{10,11... | collective-permute-start | bytes 3145736 | tf_op jit(solution)/shard_map/ppermute | solution.py:545
  56.4 43.3 %collective-permute-start.7 = (bf16[512,1024]{1,0:T(8,128)(2,1)S(1)}, bf16[512,1024]{1,0:T(8,128)(2,1)S(1)}, u32[]{:S(2)}, u32[]{:S(2)}) collective-permute-start(bf16[512,1024]{1,0:T(8,128)(2,1)S(1)} %copy-done.10), channel_id=1, source_target_pairs={{0,2},{1,3},{2,0},{3,1},{4,6},{5,7},{6,4},{7,5},{8,10},{9,11},{10,... | collective-permute-start | bytes 3145736 | tf_op jit(solution)/shard_map/ppermute | solution.py:545
  58.0 78.8 %collective-permute-start.25 = (bf16[512,1024]{1,0:T(8,128)(2,1)}, bf16[512,1024]{1,0:T(8,128)(2,1)}, u32[]{:S(2)}, u32[]{:S(2)}) collective-permute-start(bf16[512,1024]{1,0:T(8,128)(2,1)} %get-tuple-element.115), channel_id=1, source_target_pairs={{0,4},{4,8},{8,12},{12,16},{16,20},{20,24},{24,28},{1,5},{5,9},{9,... | collective-permute-start | bytes 3145736 | tf_op jit(solution)/shard_map/ppermute | solution.py:682
  73.8 34.3 %collective-permute-start.18 = (bf16[64,4096]{1,0:T(8,128)(2,1)S(1)}, bf16[64,4096]{1,0:T(8,128)(2,1)S(1)}, u32[]{:S(2)}, u32[]{:S(2)}) collective-permute-start(bf16[64,4096]{1,0:T(8,128)(2,1)S(1)} %slice.383), channel_id=1, source_target_pairs={{0,2},{1,3},{2,0},{3,1},{4,6},{5,7},{6,4},{7,5},{8,10},{9,11},{10,... | collective-permute-start | bytes 1572872 | tf_op jit(solution)/shard_map/ppermute | solution.py:545
  77.2 32.2 %collective-permute-start.19 = (bf16[64,4096]{1,0:T(8,128)(2,1)S(1)}, bf16[64,4096]{1,0:T(8,128)(2,1)S(1)}, u32[]{:S(2)}, u32[]{:S(2)}) collective-permute-start(bf16[64,4096]{1,0:T(8,128)(2,1)S(1)} %slice.384), channel_id=1, source_target_pairs={{0,1},{1,0},{2,3},{3,2},{4,5},{5,4},{6,7},{7,6},{8,9},{9,8},{10,11... | collective-permute-start | bytes 1572872 | tf_op jit(solution)/shard_map/ppermute | solution.py:545
  96.3 42.1 %collective-permute-start.26 = (bf16[512,1024]{1,0:T(8,128)(2,1)}, bf16[512,1024]{1,0:T(8,128)(2,1)}, u32[]{:S(2)}, u32[]{:S(2)}) collective-permute-start(bf16[512,1024]{1,0:T(8,128)(2,1)} %get-tuple-element.116), channel_id=1, source_target_pairs={{4,0},{8,4},{12,8},{16,12},{20,16},{24,20},{28,24},{5,1},{9,5},{13... | collective-permute-start | bytes 3145736 | tf_op jit(solution)/shard_map/ppermute | solution.py:683
  99.7 10.6 %collective-permute-start.14 = (f32[8,128]{1,0:T(8,128)S(1)}, f32[8,128]{1,0:T(8,128)S(1)}, u32[]{:S(2)}, u32[]{:S(2)}) collective-permute-start(f32[8,128]{1,0:T(8,128)S(1)} %add.216), channel_id=1, source_target_pairs={{0,1},{1,0},{2,3},{3,2},{4,5},{5,4},{6,7},{7,6},{8,9},{9,8},{10,11... | collective-permute-start | bytes 12296 | tf_op jit(solution)/shard_map/ppermute | solution.py:545
  108.1 10.7 %collective-permute-start.8 = (bf16[256,1024]{1,0:T(8,128)(2,1)S(1)}, bf16[256,1024]{1,0:T(8,128)(2,1)}, u32[]{:S(2)}, u32[]{:S(2)}) collective-permute-start(bf16[256,1024]{1,0:T(8,128)(2,1)S(1)} %slice.381), channel_id=1, source_target_pairs={{0,2},{1,3},{2,0},{3,1},{4,6},{5,7},{6,4},{7,5},{8,10},{9,11},{10,... | collective-permute-start | bytes 1572872 | tf_op jit(solution)/shard_map/ppermute | solution.py:545
  109.5 34.6 %collective-permute-start.24 = (bf16[384,3072]{1,0:T(8,128)(2,1)}, bf16[384,3072]{1,0:T(8,128)(2,1)}, u32[]{:S(2)}, u32[]{:S(2)}) collective-permute-start(bf16[384,3072]{1,0:T(8,128)(2,1)} %constant_dynamic-update-slice_fusion.3.mine), channel_id=1, source_target_pairs={{0,4},{4,0},{8,12},{12,8},{16,20},{20,16},{24,28},{28,24},{1,5},{5... | collective-permute-start | bytes 7077896 | tf_op jit(solution)/shard_map/ppermute | solution.py:545
  110.3 14.7 %collective-permute-start.9 = (bf16[256,1024]{1,0:T(8,128)(2,1)}, bf16[256,1024]{1,0:T(8,128)(2,1)}, u32[]{:S(2)}, u32[]{:S(2)}) collective-permute-start(bf16[256,1024]{1,0:T(8,128)(2,1)} %slice.382), channel_id=1, source_target_pairs={{0,1},{1,0},{2,3},{3,2},{4,5},{5,4},{6,7},{7,6},{8,9},{9,8},{10,11... | collective-permute-start | bytes 1572872 | tf_op jit(solution)/shard_map/ppermute | solution.py:545
  118.8 86.2 %collective-permute-start.20 = (bf16[384,4096]{1,0:T(8,128)(2,1)}, bf16[384,4096]{1,0:T(8,128)(2,1)}, u32[]{:S(2)}, u32[]{:S(2)}) collective-permute-start(bf16[384,4096]{1,0:T(8,128)(2,1)} %constant_dynamic-update-slice_fusion.11.mine), channel_id=1, source_target_pairs={{0,4},{4,0},{8,12},{12,8},{16,20},{20,16},{24,28},{28,24},{1,5},{5... | collective-permute-start | bytes 9437192 | tf_op jit(solution)/shard_map/ppermute | solution.py:545
  128.6 108.0 %collective-permute-start.10 = (bf16[1536,1024]{1,0:T(8,128)(2,1)S(1)}, bf16[1536,1024]{1,0:T(8,128)(2,1)}, u32[]{:S(2)}, u32[]{:S(2)}) collective-permute-start(bf16[1536,1024]{1,0:T(8,128)(2,1)S(1)} %constant_dynamic-update-slice_fusion.7.mine), channel_id=1, source_target_pairs={{0,4},{4,0},{8,12},{12,8},{16,20},{20,16},{24,28},{28,24},{1,5},{5... | collective-permute-start | bytes 9437192 | tf_op jit(solution)/shard_map/ppermute | solution.py:545
  136.8 6.7 collective-permute-start.21
  138.4 5.6 collective-permute-start.22
  144.0 50.5 %collective-permute-start.23 = (bf16[384,1024]{1,0:T(8,128)(2,1)S(1)}, bf16[384,1024]{1,0:T(8,128)(2,1)S(1)}, u32[]{:S(2)}, u32[]{:S(2)}) collective-permute-start(bf16[384,1024]{1,0:T(8,128)(2,1)S(1)} %constant_dynamic-update-slice_fusion.15.mine), channel_id=1, source_target_pairs={{0,4},{4,0},{8,12},{12,8},{16,20},{20,16},{24,28},{28,24},{1,5},{5... | collective-permute-start | bytes 2359304 | tf_op jit(solution)/shard_map/ppermute | solution.py:545
  276.0 261.4 %collective-permute-start.68 = (bf16[4,512,1024]{2,1,0:T(8,128)(2,1)}, bf16[4,512,1024]{2,1,0:T(8,128)(2,1)}, u32[]{:S(2)}, u32[]{:S(2)}) collective-permute-start(bf16[4,512,1024]{2,1,0:T(8,128)(2,1)} %get-tuple-element.97), channel_id=1, source_target_pairs={{0,4},{4,0},{8,12},{12,8},{16,20},{20,16},{24,28},{28,24},{1,5},{5... | collective-permute-start | bytes 12582920 | tf_op jit(solution)/shard_map/ppermute | solution.py:545
  345.8 197.6 %collective-permute-start.59 = (bf16[4,128,4096]{2,1,0:T(8,128)(2,1)}, bf16[4,128,4096]{2,1,0:T(8,128)(2,1)}, u32[]{:S(2)}, u32[]{:S(2)}) collective-permute-start(bf16[4,128,4096]{2,1,0:T(8,128)(2,1)} %get-tuple-element.95), channel_id=1, source_target_pairs={{0,4},{4,0},{8,12},{12,8},{16,20},{20,16},{24,28},{28,24},{1,5},{5... | collective-permute-start | bytes 12582920 | tf_op jit(solution)/shard_map/ppermute | solution.py:545
  346.9 7.4 collective-permute-start.31
  354.3 95.5 %collective-permute-start.50 = (bf16[4,128,1024]{2,1,0:T(8,128)(2,1)}, bf16[4,128,1024]{2,1,0:T(8,128)(2,1)S(1)}, u32[]{:S(2)}, u32[]{:S(2)}) collective-permute-start(bf16[4,128,1024]{2,1,0:T(8,128)(2,1)} %get-tuple-element.92), channel_id=1, source_target_pairs={{0,4},{4,0},{8,12},{12,8},{16,20},{20,16},{24,28},{28,24},{1,5},{5... | collective-permute-start | bytes 3145736 | tf_op jit(solution)/shard_map/ppermute | solution.py:545
  354.4 52.9 %collective-permute-start.32 = (f32[16,1024]{1,0:T(8,128)S(1)}, f32[16,1024]{1,0:T(8,128)S(1)}, u32[]{:S(2)}, u32[]{:S(2)}) collective-permute-start(f32[16,1024]{1,0:T(8,128)S(1)} %fusion.40), channel_id=1, source_target_pairs={{0,8},{4,12},{8,0},{12,4},{16,24},{20,28},{24,16},{28,20},{1,9},{5... | collective-permute-start | bytes 196616 | tf_op jit(solution)/shard_map/ppermute | solution.py:545
  407.3 24.9 %collective-permute-start.33 = (f32[16,1024]{1,0:T(8,128)S(1)}, f32[16,1024]{1,0:T(8,128)S(1)}, u32[]{:S(2)}, u32[]{:S(2)}) collective-permute-start(f32[16,1024]{1,0:T(8,128)S(1)} %add.226), channel_id=1, source_target_pairs={{0,16},{4,20},{8,24},{12,28},{16,0},{20,4},{24,8},{28,12},{1,17},{... | collective-permute-start | bytes 196616 | tf_op jit(solution)/shard_map/ppermute | solution.py:545
  436.6 10.1 %collective-permute-start.35 = (f32[16,1024]{1,0:T(8,128)S(1)}, f32[16,1024]{1,0:T(8,128)S(1)}, u32[]{:S(2)}, u32[]{:S(2)}) collective-permute-start(f32[16,1024]{1,0:T(8,128)S(1)} %add.228), channel_id=1, source_target_pairs={{0,2},{1,3},{2,0},{3,1},{4,6},{5,7},{6,4},{7,5},{8,10},{9,11},{10,... | collective-permute-start | bytes 196616 | tf_op jit(solution)/shard_map/ppermute | solution.py:545
  442.0 41.6 %collective-permute-start.29 = (bf16[512,2048]{1,0:T(8,128)(2,1)}, bf16[512,2048]{1,0:T(8,128)(2,1)S(1)}, u32[]{:S(2)}, u32[]{:S(2)}) collective-permute-start(bf16[512,2048]{1,0:T(8,128)(2,1)} %get-tuple-element.102), channel_id=1, source_target_pairs={{0,4},{4,8},{8,12},{12,16},{16,20},{20,24},{24,28},{1,5},{5,9},{9,... | collective-permute-start | bytes 6291464 | tf_op jit(solution)/shard_map/ppermute | solution.py:753
  446.7 36.9 %collective-permute-start.30 = (bf16[512,2048]{1,0:T(8,128)(2,1)}, bf16[512,2048]{1,0:T(8,128)(2,1)}, u32[]{:S(2)}, u32[]{:S(2)}) collective-permute-start(bf16[512,2048]{1,0:T(8,128)(2,1)} %get-tuple-element.103), channel_id=1, source_target_pairs={{4,0},{8,4},{12,8},{16,12},{20,16},{24,20},{28,24},{5,1},{9,5},{13... | collective-permute-start | bytes 6291464 | tf_op jit(solution)/shard_map/ppermute | solution.py:752
  450.3 9.1 %collective-permute-start.51 = (bf16[2,64,1024]{2,1,0:T(8,128)(2,1)S(1)}, bf16[2,64,1024]{2,1,0:T(8,128)(2,1)S(1)}, u32[]{:S(2)}, u32[]{:S(2)}) collective-permute-start(bf16[2,64,1024]{2,1,0:T(8,128)(2,1)S(1)} %slice_bitcast_fusion.29), channel_id=1, source_target_pairs={{0,1},{1,0},{2,3},{3,2},{4,5},{5,4},{6,7},{7,6},{8,9},{9,8},{10,11... | collective-permute-start | bytes 786440 | tf_op jit(solution)/shard_map/ppermute | solution.py:545
  459.3 8.3 %collective-permute-start.53 = (bf16[2,64,1024]{2,1,0:T(8,128)(2,1)S(1)}, bf16[2,64,1024]{2,1,0:T(8,128)(2,1)S(1)}, u32[]{:S(2)}, u32[]{:S(2)}) collective-permute-start(bf16[2,64,1024]{2,1,0:T(8,128)(2,1)S(1)} %slice_bitcast_fusion.27), channel_id=1, source_target_pairs={{0,2},{1,3},{2,0},{3,1},{4,6},{5,7},{6,4},{7,5},{8,10},{9,11},{10,... | collective-permute-start | bytes 786440 | tf_op jit(solution)/shard_map/ppermute | solution.py:545
  482.9 7.2 collective-permute-start.56
  490.2 44.4 %collective-permute-start.57 = (bf16[128,1024]{1,0:T(8,128)(2,1)S(1)}, bf16[128,1024]{1,0:T(8,128)(2,1)S(1)}, u32[]{:S(2)}, u32[]{:S(2)}) collective-permute-start(bf16[128,1024]{1,0:T(8,128)(2,1)S(1)} %fusion.27), channel_id=1, source_target_pairs={{8,0},{12,4},{16,24},{20,28},{9,1},{13,5},{17,25},{21,29},{10,2},{... | collective-permute-start | bytes 786440 | tf_op jit(solution)/shard_map/ppermute | solution.py:612
  491.6 13.8 %collective-permute-start.46 = (f32[8,1024]{1,0:T(8,128)S(1)}, f32[8,1024]{1,0:T(8,128)S(1)}, u32[]{:S(2)}, u32[]{:S(2)}) collective-permute-start(f32[8,1024]{1,0:T(8,128)S(1)} %pad_add_fusion), channel_id=1, source_target_pairs={{0,8},{4,12},{8,0},{12,4},{16,24},{20,28},{24,16},{28,20},{1,9},{5... | collective-permute-start | bytes 98312 | tf_op jit(solution)/shard_map/ppermute | solution.py:545
  505.3 14.3 %collective-permute-start.47 = (f32[8,1024]{1,0:T(8,128)S(1)}, f32[8,1024]{1,0:T(8,128)S(1)}, u32[]{:S(2)}, u32[]{:S(2)}) collective-permute-start(f32[8,1024]{1,0:T(8,128)S(1)} %add.239), channel_id=1, source_target_pairs={{0,16},{4,20},{8,24},{12,28},{16,0},{20,4},{24,8},{28,12},{1,17},{... | collective-permute-start | bytes 98312 | tf_op jit(solution)/shard_map/ppermute | solution.py:545
  519.6 75.7 %collective-permute-start.36 = (bf16[4,128,3072]{2,1,0:T(8,128)(2,1)}, bf16[4,128,3072]{2,1,0:T(8,128)(2,1)S(1)}, u32[]{:S(2)}, u32[]{:S(2)}) collective-permute-start(bf16[4,128,3072]{2,1,0:T(8,128)(2,1)} %get-tuple-element.90), channel_id=1, source_target_pairs={{0,4},{4,0},{8,12},{12,8},{16,20},{20,16},{24,28},{28,24},{1,5},{5... | collective-permute-start | bytes 9437192 | tf_op jit(solution)/shard_map/ppermute | solution.py:545
  519.6 13.2 %collective-permute-start.48 = (f32[8,1024]{1,0:T(8,128)S(1)}, f32[8,1024]{1,0:T(8,128)S(1)}, u32[]{:S(2)}, u32[]{:S(2)}) collective-permute-start(f32[8,1024]{1,0:T(8,128)S(1)} %add.240), channel_id=1, source_target_pairs={{0,1},{1,0},{2,3},{3,2},{4,5},{5,4},{6,7},{7,6},{8,9},{9,8},{10,11... | collective-permute-start | bytes 98312 | tf_op jit(solution)/shard_map/ppermute | solution.py:545
  534.7 143.6 %collective-permute-start.58 = (bf16[128,1024]{1,0:T(8,128)(2,1)S(1)}, bf16[128,1024]{1,0:T(8,128)(2,1)S(1)}, u32[]{:S(2)}, u32[]{:S(2)}) collective-permute-start(bf16[128,1024]{1,0:T(8,128)(2,1)S(1)} %broadcast_select_fusion.9), channel_id=1, source_target_pairs={{0,4},{4,0},{8,12},{12,8},{16,20},{20,16},{24,28},{28,24},{1,5},{5... | collective-permute-start | bytes 786440 | tf_op jit(solution)/shard_map/ppermute | solution.py:545
  541.0 26.2 %collective-permute-start.69 = (bf16[2,256,1024]{2,1,0:T(8,128)(2,1)S(1)}, bf16[2,256,1024]{2,1,0:T(8,128)(2,1)S(1)}, u32[]{:S(2)}, u32[]{:S(2)}) collective-permute-start(bf16[2,256,1024]{2,1,0:T(8,128)(2,1)S(1)} %slice_bitcast_fusion.3), channel_id=1, source_target_pairs={{0,1},{1,0},{2,3},{3,2},{4,5},{5,4},{6,7},{7,6},{8,9},{9,8},{10,11... | collective-permute-start | bytes 3145736 | tf_op jit(solution)/shard_map/ppermute | solution.py:545
  542.5 26.9 %collective-permute-start.71 = (bf16[2,256,1024]{2,1,0:T(8,128)(2,1)S(1)}, bf16[2,256,1024]{2,1,0:T(8,128)(2,1)S(1)}, u32[]{:S(2)}, u32[]{:S(2)}) collective-permute-start(bf16[2,256,1024]{2,1,0:T(8,128)(2,1)S(1)} %slice_bitcast_fusion.1), channel_id=1, source_target_pairs={{0,2},{1,3},{2,0},{3,1},{4,6},{5,7},{6,4},{7,5},{8,10},{9,11},{10,... | collective-permute-start | bytes 3145736 | tf_op jit(solution)/shard_map/ppermute | solution.py:545
  546.5 41.2 %collective-permute-start.60 = (bf16[2,64,4096]{2,1,0:T(8,128)(2,1)S(1)}, bf16[2,64,4096]{2,1,0:T(8,128)(2,1)S(1)}, u32[]{:S(2)}, u32[]{:S(2)}) collective-permute-start(bf16[2,64,4096]{2,1,0:T(8,128)(2,1)S(1)} %slice_bitcast_fusion.7), channel_id=1, source_target_pairs={{0,1},{1,0},{2,3},{3,2},{4,5},{5,4},{6,7},{7,6},{8,9},{9,8},{10,11... | collective-permute-start | bytes 3145736 | tf_op jit(solution)/shard_map/ppermute | solution.py:545
  567.2 26.1 %collective-permute-start.62 = (bf16[2,64,4096]{2,1,0:T(8,128)(2,1)S(1)}, bf16[2,64,4096]{2,1,0:T(8,128)(2,1)S(1)}, u32[]{:S(2)}, u32[]{:S(2)}) collective-permute-start(bf16[2,64,4096]{2,1,0:T(8,128)(2,1)S(1)} %slice_bitcast_fusion.5), channel_id=1, source_target_pairs={{0,2},{1,3},{2,0},{3,1},{4,6},{5,7},{6,4},{7,5},{8,10},{9,11},{10,... | collective-permute-start | bytes 3145736 | tf_op jit(solution)/shard_map/ppermute | solution.py:545
  569.4 35.1 %collective-permute-start.70 = (bf16[1,256,1024]{2,1,0:T(8,128)(2,1)S(1)}, bf16[1,256,1024]{2,1,0:T(8,128)(2,1)S(1)}, u32[]{:S(2)}, u32[]{:S(2)}) collective-permute-start(bf16[1,256,1024]{2,1,0:T(8,128)(2,1)S(1)} %slice_bitcast_fusion.17), channel_id=1, source_target_pairs={{0,2},{1,3},{2,0},{3,1},{4,6},{5,7},{6,4},{7,5},{8,10},{9,11},{10,... | collective-permute-start | bytes 1572872 | tf_op jit(solution)/shard_map/ppermute | solution.py:545
  587.7 18.3 %collective-permute-start.72 = (bf16[1,256,1024]{2,1,0:T(8,128)(2,1)S(1)}, bf16[1,256,1024]{2,1,0:T(8,128)(2,1)S(1)}, u32[]{:S(2)}, u32[]{:S(2)}) collective-permute-start(bf16[1,256,1024]{2,1,0:T(8,128)(2,1)S(1)} %slice_bitcast_fusion.15), channel_id=1, source_target_pairs={{0,1},{1,0},{2,3},{3,2},{4,5},{5,4},{6,7},{7,6},{8,9},{9,8},{10,11... | collective-permute-start | bytes 1572872 | tf_op jit(solution)/shard_map/ppermute | solution.py:545
  593.3 22.5 %collective-permute-start.61 = (bf16[1,64,4096]{2,1,0:T(8,128)(2,1)S(1)}, bf16[1,64,4096]{2,1,0:T(8,128)(2,1)S(1)}, u32[]{:S(2)}, u32[]{:S(2)}) collective-permute-start(bf16[1,64,4096]{2,1,0:T(8,128)(2,1)S(1)} %slice_bitcast_fusion.21), channel_id=1, source_target_pairs={{0,2},{1,3},{2,0},{3,1},{4,6},{5,7},{6,4},{7,5},{8,10},{9,11},{10,... | collective-permute-start | bytes 1572872 | tf_op jit(solution)/shard_map/ppermute | solution.py:545
  595.3 24.0 %collective-permute-start.63 = (bf16[1,64,4096]{2,1,0:T(8,128)(2,1)S(1)}, bf16[1,64,4096]{2,1,0:T(8,128)(2,1)S(1)}, u32[]{:S(2)}, u32[]{:S(2)}) collective-permute-start(bf16[1,64,4096]{2,1,0:T(8,128)(2,1)S(1)} %slice_bitcast_fusion.19), channel_id=1, source_target_pairs={{0,1},{1,0},{2,3},{3,2},{4,5},{5,4},{6,7},{7,6},{8,9},{9,8},{10,11... | collective-permute-start | bytes 1572872 | tf_op jit(solution)/shard_map/ppermute | solution.py:545
  604.5 23.3 %collective-permute-start.37 = (bf16[2,64,3072]{2,1,0:T(8,128)(2,1)S(1)}, bf16[2,64,3072]{2,1,0:T(8,128)(2,1)S(1)}, u32[]{:S(2)}, u32[]{:S(2)}) collective-permute-start(bf16[2,64,3072]{2,1,0:T(8,128)(2,1)S(1)} %slice_bitcast_fusion.13), channel_id=1, source_target_pairs={{0,1},{1,0},{2,3},{3,2},{4,5},{5,4},{6,7},{7,6},{8,9},{9,8},{10,11... | collective-permute-start | bytes 2359304 | tf_op jit(solution)/shard_map/ppermute | solution.py:545
  606.0 23.8 %collective-permute-start.39 = (bf16[2,64,3072]{2,1,0:T(8,128)(2,1)S(1)}, bf16[2,64,3072]{2,1,0:T(8,128)(2,1)S(1)}, u32[]{:S(2)}, u32[]{:S(2)}) collective-permute-start(bf16[2,64,3072]{2,1,0:T(8,128)(2,1)S(1)} %slice_bitcast_fusion.11), channel_id=1, source_target_pairs={{0,2},{1,3},{2,0},{3,1},{4,6},{5,7},{6,4},{7,5},{8,10},{9,11},{10,... | collective-permute-start | bytes 2359304 | tf_op jit(solution)/shard_map/ppermute | solution.py:545
  615.7 27.9 %collective-permute-start.73 = (bf16[512,1024]{1,0:T(8,128)(2,1)S(1)}, bf16[512,1024]{1,0:T(8,128)(2,1)S(1)}, u32[]{:S(2)}, u32[]{:S(2)}) collective-permute-start(bf16[512,1024]{1,0:T(8,128)(2,1)S(1)} %pad_maximum_fusion.3), channel_id=1, source_target_pairs={{0,8},{4,12},{24,16},{28,20},{1,9},{5,13},{25,17},{29,21},{2,10},{... | collective-permute-start | bytes 3145736 | tf_op jit(solution)/shard_map/ppermute | solution.py:612
  628.0 8.6 %collective-permute-start.38 = (bf16[1,64,3072]{2,1,0:T(8,128)(2,1)S(1)}, bf16[1,64,3072]{2,1,0:T(8,128)(2,1)S(1)}, u32[]{:S(2)}, u32[]{:S(2)}) collective-permute-start(bf16[1,64,3072]{2,1,0:T(8,128)(2,1)S(1)} %slice_bitcast_fusion.25), channel_id=1, source_target_pairs={{0,2},{1,3},{2,0},{3,1},{4,6},{5,7},{6,4},{7,5},{8,10},{9,11},{10,... | collective-permute-start | bytes 1179656 | tf_op jit(solution)/shard_map/ppermute | solution.py:545
  630.0 8.0 %collective-permute-start.40 = (bf16[1,64,3072]{2,1,0:T(8,128)(2,1)S(1)}, bf16[1,64,3072]{2,1,0:T(8,128)(2,1)S(1)}, u32[]{:S(2)}, u32[]{:S(2)}) collective-permute-start(bf16[1,64,3072]{2,1,0:T(8,128)(2,1)S(1)} %slice_bitcast_fusion.23), channel_id=1, source_target_pairs={{0,1},{1,0},{2,3},{3,2},{4,5},{5,4},{6,7},{7,6},{8,9},{9,8},{10,11... | collective-permute-start | bytes 1179656 | tf_op jit(solution)/shard_map/ppermute | solution.py:545
  638.2 21.3 %collective-permute-start.41 = (bf16[128,3072]{1,0:T(8,128)(2,1)S(1)}, bf16[128,3072]{1,0:T(8,128)(2,1)S(1)}, u32[]{:S(2)}, u32[]{:S(2)}) collective-permute-start(bf16[128,3072]{1,0:T(8,128)(2,1)S(1)} %pad_maximum_fusion.4), channel_id=1, source_target_pairs={{0,8},{4,12},{24,16},{28,20},{1,9},{5,13},{25,17},{29,21},{2,10},{... | collective-permute-start | bytes 2359304 | tf_op jit(solution)/shard_map/ppermute | solution.py:612
  641.7 35.3 %collective-permute-start.64 = (bf16[128,4096]{1,0:T(8,128)(2,1)S(1)}, bf16[128,4096]{1,0:T(8,128)(2,1)S(1)}, u32[]{:S(2)}, u32[]{:S(2)}) collective-permute-start(bf16[128,4096]{1,0:T(8,128)(2,1)S(1)} %pad_maximum_fusion.2), channel_id=1, source_target_pairs={{0,8},{4,12},{24,16},{28,20},{1,9},{5,13},{25,17},{29,21},{2,10},{... | collective-permute-start | bytes 3145736 | tf_op jit(solution)/shard_map/ppermute | solution.py:612
  644.1 34.2 %collective-permute-start.74 = (bf16[512,1024]{1,0:T(8,128)(2,1)S(1)}, bf16[512,1024]{1,0:T(8,128)(2,1)S(1)}, u32[]{:S(2)}, u32[]{:S(2)}) collective-permute-start(bf16[512,1024]{1,0:T(8,128)(2,1)S(1)} %add_convert_fusion.8), channel_id=1, source_target_pairs={{8,16},{12,20},{16,8},{20,12},{9,17},{13,21},{17,9},{21,13},{10,18... | collective-permute-start | bytes 3145736 | tf_op jit(solution)/shard_map/ppermute | solution.py:612
  659.7 20.3 %collective-permute-start.42 = (bf16[128,3072]{1,0:T(8,128)(2,1)S(1)}, bf16[128,3072]{1,0:T(8,128)(2,1)S(1)}, u32[]{:S(2)}, u32[]{:S(2)}) collective-permute-start(bf16[128,3072]{1,0:T(8,128)(2,1)S(1)} %add_convert_fusion.12), channel_id=1, source_target_pairs={{8,16},{12,20},{16,8},{20,12},{9,17},{13,21},{17,9},{21,13},{10,18... | collective-permute-start | bytes 2359304 | tf_op jit(solution)/shard_map/ppermute | solution.py:612
  678.7 48.1 %collective-permute-start.75 = (bf16[512,1024]{1,0:T(8,128)(2,1)S(1)}, bf16[512,1024]{1,0:T(8,128)(2,1)S(1)}, u32[]{:S(2)}, u32[]{:S(2)}) collective-permute-start(bf16[512,1024]{1,0:T(8,128)(2,1)S(1)} %fusion.5), channel_id=1, source_target_pairs={{8,0},{12,4},{16,24},{20,28},{9,1},{13,5},{17,25},{21,29},{10,2},{... | collective-permute-start | bytes 3145736 | tf_op jit(solution)/shard_map/ppermute | solution.py:612
  680.3 46.3 %collective-permute-start.43 = (bf16[128,3072]{1,0:T(8,128)(2,1)S(1)}, bf16[128,3072]{1,0:T(8,128)(2,1)S(1)}, u32[]{:S(2)}, u32[]{:S(2)}) collective-permute-start(bf16[128,3072]{1,0:T(8,128)(2,1)S(1)} %fusion.8), channel_id=1, source_target_pairs={{8,0},{12,4},{16,24},{20,28},{9,1},{13,5},{17,25},{21,29},{10,2},{... | collective-permute-start | bytes 2359304 | tf_op jit(solution)/shard_map/ppermute | solution.py:612
  681.9 61.2 %collective-permute-start.66 = (bf16[128,4096]{1,0:T(8,128)(2,1)S(1)}, bf16[128,4096]{1,0:T(8,128)(2,1)S(1)}, u32[]{:S(2)}, u32[]{:S(2)}) collective-permute-start(bf16[128,4096]{1,0:T(8,128)(2,1)S(1)} %fusion.4), channel_id=1, source_target_pairs={{8,0},{12,4},{16,24},{20,28},{9,1},{13,5},{17,25},{21,29},{10,2},{... | collective-permute-start | bytes 3145736 | tf_op jit(solution)/shard_map/ppermute | solution.py:612
  726.7 16.7 %collective-permute-start.44 = (bf16[128,3072]{1,0:T(8,128)(2,1)S(1)}, bf16[128,3072]{1,0:T(8,128)(2,1)S(1)}, u32[]{:S(2)}, u32[]{:S(2)}) collective-permute-start(bf16[128,3072]{1,0:T(8,128)(2,1)S(1)} %broadcast_select_fusion.6), channel_id=1, source_target_pairs={{0,4},{4,0},{8,12},{12,8},{16,20},{20,16},{24,28},{28,24},{1,5},{5... | collective-permute-start | bytes 2359304 | tf_op jit(solution)/shard_map/ppermute | solution.py:545
  726.9 18.7 %collective-permute-start.76 = (bf16[512,1024]{1,0:T(8,128)(2,1)S(1)}, bf16[512,1024]{1,0:T(8,128)(2,1)S(1)}, u32[]{:S(2)}, u32[]{:S(2)}) collective-permute-start(bf16[512,1024]{1,0:T(8,128)(2,1)S(1)} %broadcast_select_fusion), channel_id=1, source_target_pairs={{0,4},{4,0},{8,12},{12,8},{16,20},{20,16},{24,28},{28,24},{1,5},{5... | collective-permute-start | bytes 3145736 | tf_op jit(solution)/shard_map/ppermute | solution.py:545
  (43 other events, 363.8 us)

commit v2 on v1

--- a/solution.py
+++ b/solution.py
@@ -88,38 +88,73 @@
     return [pltpu.VMEM((rows, columns), bf16), pltpu.SemaphoreType.DMA((64,))]
 
 
+def pack_kernel(where_ref, q_ref, k_ref, v_ref, shard_ref, own_ref):
+    half = own_ref.shape[0]
+    first = where_ref[1] == 0
+    for side in (0, 1):
+        for which, ref in enumerate((q_ref, k_ref, v_ref)):
+            columns = qkv_columns(which, side)
+            block = ref[:, side * D // 2 : (side + 1) * D // 2]
+            shard_ref[:, columns] = block
+            own_ref[:, columns] = jnp.where(first, block[:half], block[half:])
+
+
+def pack_qkv(where, q, k, v):
+    part = q.shape[0]
+    return pl.pallas_call(
+        pack_kernel,
+        in_specs=[pl.BlockSpec(memory_space=pltpu.SMEM)] + [pl.BlockSpec(memory_space=pltpu.VMEM)] * 3,
+        out_specs=[pl.BlockSpec(memory_space=pltpu.VMEM)] * 2,
+        out_shape=[sds((part, 3 * D), bf16), sds((part // 2, 3 * D), bf16)],
+        compiler_params=params(),
+        cost_estimate=cost(0, 4 * 2**20),
+        name="pack_qkv",
+    )(where, q, k, v)
+
+
+def qkv_columns(which, side):
+    begin = (3 * side + which) * D // 2
+    return slice(begin, begin + D // 2)
+
+
 def qkv_kernel(
-    where_ref, shard, mine, other, x_ref, bq_ref, bv_ref, q_ref, k_ref, v_ref, kt_ref, vt_ref, full_ref, w_ref, sem
+    where_ref, shard, mine, other, before_ref, x_ref, behind_ref, bq_ref, bv_ref, q_ref, k_ref, v_ref, kt_ref, vt_ref, full_ref, w_ref, sem
 ):
     join_weight(where_ref, (shard, mine, other), w_ref, full_ref, sem)
     i = pl.program_id(0)
-    x = x_ref[...]
+    x = jnp.where(i == 0, before_ref[...], jnp.where(i == pl.num_programs(0) - 1, behind_ref[...], x_ref[...]))
 
     @pl.when((i > 0) & (i < pl.num_programs(0) - 1))
     def _():
-        query = (nn(x, w_ref[:, :D]) + bq_ref[...]).astype(bf16)
-        q_ref[...] = query * jnp.asarray(HEAD**-0.5, bf16)
-
-    keys = nn(x, w_ref[:, D : 2 * D]).astype(bf16)
-    k_ref[...] = keys
-    kt_ref[...] = jnp.transpose(keys)
-    values = (nn(x, w_ref[:, 2 * D :]) + bv_ref[...]).astype(bf16)
-    v_ref[...] = values
-    vt_ref[...] = jnp.transpose(values)
-
-
-def project_qkv(where, pieces, x_near, bq, bv):
-    span = x_near.shape[0]
-    rows = span - 2 * DOC_MAX
+        for s in (0, 1):
+            half = slice(s * D // 2, (s + 1) * D // 2)
+            query = (nn(x, w_ref[:, qkv_columns(0, s)]) + bq_ref[:, half]).astype(bf16)
+            q_ref[:, half] = query * jnp.asarray(HEAD**-0.5, bf16)
+
+    for s in (0, 1):
+        half = slice(s * D // 2, (s + 1) * D // 2)
+        keys = nn(x, w_ref[:, qkv_columns(1, s)]).astype(bf16)
+        k_ref[:, half] = keys
+        kt_ref[half, :] = jnp.transpose(keys)
+        values = (nn(x, w_ref[:, qkv_columns(2, s)]) + bv_ref[:, half]).astype(bf16)
+        v_ref[:, half] = values
+        vt_ref[half, :] = jnp.transpose(values)
+
+
+def project_qkv(where, pieces, before, tokens, behind, bq, bv):
+    rows = tokens.shape[0]
+    span = rows + 2 * DOC_MAX
+    rim = pl.BlockSpec((512, D), lambda i: (0, 0))
+    inside = pl.BlockSpec((512, D), lambda i: (jnp.clip(i - 1, 0, rows // 512 - 1), 0))
     row = pl.BlockSpec((1, D), lambda i: (0, 0))
     tall = pl.BlockSpec((512, D), lambda i: (i, 0))
     wide = pl.BlockSpec((D, 512), lambda i: (0, i))
     return pl.pallas_call(
         qkv_kernel,
         grid=(span // 512,),
-        in_specs=WEIGHT_SPECS + [tall, row, row],
+        in_specs=WEIGHT_SPECS + [rim, inside, rim, row, row],
         out_specs=[
-            pl.BlockSpec((512, D), lambda i: (jnp.clip(i - 1, 0, rows // 512 - 1), 0)),
+            inside,
             tall,
             tall,
             wide,
@@ -138,7 +173,7 @@
         compiler_params=params(),
         cost_estimate=cost(2 * D * D * (rows + 2 * span), 30 * 2**20),
         name="project_qkv",
-    )(where, *pieces, x_near, bq, bv)
+    )(where, *pieces, before, tokens, behind, bq, bv)
 
 
 def stack_rows(block, stack):
@@ -151,7 +186,8 @@
         hr = slice(h*HEAD,(h+1)*HEAD)
         stack[hr, h*TILE:(h+1)*TILE] = turned[hr, :]
 
-def attn_fwd_kernel(lo_ref, hi_ref, q_ref, k_ref, vt_ref, idq_ref, idk_ref, out_ref, lse_ref, qs, acc, top, tot):
+def attn_fwd_kernel(lo_ref, hi_ref, q_ref, k_ref, vt_ref, idq_ref, idk_ref, *refs):
+    out_ref, lse_ref, qs, acc, top, tot = refs[-6:]
     t = pl.program_id(1)
     @pl.when((t==0)&(pl.program_id(0)==0))
     def _():
@@ -186,26 +222,28 @@
     out_ref[...] = jnp.transpose(acc[...]).astype(bf16)
     lse_ref[0] = top[...] + jnp.log(total)
 
-def attn_fwd(lo, hi, q, k_near, vt_near, idq_rows, idk_col):
+def attn_fwd(lo, hi, q, k_near, vt_near, idq_rows, idk_col, g0, ng, so_far=()):
     rows=q.shape[0]; span=k_near.shape[0]
     return pl.pallas_call(attn_fwd_kernel,
-        grid_spec=pltpu.PrefetchScalarGridSpec(num_scalar_prefetch=2, grid=(D//256, rows//TILE),
-            in_specs=[pl.BlockSpec((TILE,256),lambda g,t,*_:(t,g)),
-                pl.BlockSpec((span,256),lambda g,t,*_:(0,g)),
-                pl.BlockSpec((256,span),lambda g,t,*_:(g,0)),
+        grid_spec=pltpu.PrefetchScalarGridSpec(num_scalar_prefetch=2, grid=(ng, rows//TILE),
+            in_specs=[pl.BlockSpec((TILE,256),lambda g,t,*_:(t,g+g0)),
+                pl.BlockSpec((span,256),lambda g,t,*_:(0,g+g0)),
+                pl.BlockSpec((256,span),lambda g,t,*_:(g+g0,0)),
                 pl.BlockSpec((1,1,TILE),lambda g,t,*_:(t,0,0)),
-                pl.BlockSpec((span,1),lambda g,t,*_:(0,0))],
-            out_specs=[pl.BlockSpec((TILE,256),lambda g,t,*_:(t,g)),
-                pl.BlockSpec((1,8,TILE),lambda g,t,*_:(g,0,t))],
+                pl.BlockSpec((span,1),lambda g,t,*_:(0,0))] + [pl.BlockSpec(memory_space=pl.ANY)] * len(so_far),
+            out_specs=[pl.BlockSpec((TILE,256),lambda g,t,*_:(t,g+g0)),
+                pl.BlockSpec((1,8,TILE),lambda g,t,*_:(g+g0,0,t))],
             scratch_shapes=[pltpu.VMEM((256,4*TILE),bf16),
                 pltpu.VMEM((256,TILE),f32),pltpu.VMEM((8,TILE),f32),pltpu.VMEM((8,TILE),f32)]),
-        out_shape=[jax.ShapeDtypeStruct((rows,D),bf16),jax.ShapeDtypeStruct((D//256,8,rows),f32)],
-        compiler_params=pltpu.CompilerParams(vmem_limit_bytes=VMEM_BYTES),
+        out_shape=[sds((rows,D),bf16),sds((D//256,8,rows),f32)],
+        input_output_aliases={7+i: i for i in range(len(so_far))},
+        compiler_params=params(),
+        cost_estimate=cost(ng * 10**10, 2**21),
         name="attn_forward",
-    )(lo,hi,q,k_near,vt_near,idq_rows,idk_col)
+    )(lo,hi,q,k_near,vt_near,idq_rows,idk_col,*so_far)
 
 def attn_bwd_kernel(lo_ref, hi_ref, q_ref, do_ref, ctx_ref, k_ref, kt_ref, v_ref, lse_ref, idq_ref, idk_ref,
-        dq_ref, dk_ref, dv_ref, qs, dos, qst, dost, dk_acc, dv_acc, dq_acc):
+        dq_ref, own_ref, low_ref, high_ref, qs, dos, qst, dost, dk_acc, dv_acc, dq_acc):
     t = pl.program_id(1)
     @pl.when((t==0)&(pl.program_id(0)==0))
     def _():
@@ -247,10 +285,12 @@
     dq_ref[...] = (jnp.transpose(dq_acc[...])*(HEAD**-0.5)).astype(bf16)
     @pl.when(t==pl.num_programs(1)-1)
     def _():
-        dk_ref[...] = dk_acc[...].astype(bf16)
-        dv_ref[...] = dv_acc[...].astype(bf16)
-
-def attn_bwd(lo, hi, q, do, ctx, k_near, kt_near, v_near, lse, idq_rows, idk_col, g0=0, ng=4):
+        for s, sums in ((0, dk_acc), (1, dv_acc)):
+            low_ref[s] = sums[:DOC_MAX].astype(bf16)
+            own_ref[s] = sums[DOC_MAX:-DOC_MAX].astype(bf16)
+            high_ref[s] = sums[-DOC_MAX:].astype(bf16)
+
+def attn_bwd(lo, hi, q, do, ctx, k_near, kt_near, v_near, lse, idq_rows, idk_col, g0, ng):
     rows=q.shape[0]; span=k_near.shape[0]
     return pl.pallas_call(attn_bwd_kernel,
         grid_spec=pltpu.PrefetchScalarGridSpec(num_scalar_prefetch=2, grid=(ng, rows//TILE),
@@ -264,13 +304,15 @@
                 pl.BlockSpec((1,1,TILE),lambda g,t,*_:(t,0,0)),
                 pl.BlockSpec((span,1),lambda g,t,*_:(0,0))],
             out_specs=[pl.BlockSpec((TILE,256),lambda g,t,*_:(t,g)),
-                pl.BlockSpec((span,256),lambda g,t,*_:(0,g)),
-                pl.BlockSpec((span,256),lambda g,t,*_:(0,g))],
+                pl.BlockSpec((2,rows,256),lambda g,t,*_:(0,0,g)),
+                pl.BlockSpec((2,DOC_MAX,256),lambda g,t,*_:(0,0,g)),
+                pl.BlockSpec((2,DOC_MAX,256),lambda g,t,*_:(0,0,g))],
             scratch_shapes=[pltpu.VMEM((4*TILE,256),bf16),pltpu.VMEM((4*TILE,256),bf16),
                 pltpu.VMEM((256,4*TILE),bf16),pltpu.VMEM((256,4*TILE),bf16),
                 pltpu.VMEM((span,256),f32),pltpu.VMEM((span,256),f32),pltpu.VMEM((256,TILE),f32)]),
-        out_shape=[jax.ShapeDtypeStruct((rows,ng*256),bf16),jax.ShapeDtypeStruct((span,ng*256),bf16),jax.ShapeDtypeStruct((span,ng*256),bf16)],
-        compiler_params=pltpu.CompilerParams(vmem_limit_bytes=VMEM_BYTES),
+        out_shape=[sds((rows,ng*256),bf16),sds((2,rows,ng*256),bf16),sds((2,DOC_MAX,ng*256),bf16),sds((2,DOC_MAX,ng*256),bf16)],
+        compiler_params=params(),
+        cost_estimate=cost(ng * 15 * 10**9, 2**22),
         name="attn_backward",
     )(lo,hi,q,do,ctx,k_near,kt_near,v_near,lse,idq_rows,idk_col)
 
@@ -288,7 +330,8 @@
 
 
 def mix_kernel(
-    where_ref, shard, mine, other, c_ref, b_ref, x_ref, g_ref, s_ref, normed_ref, low_ref, rate_ref, full_ref, w_ref, sem
+    where_ref, shard, mine, other, c_ref, b_ref, x_ref, g_ref, s_ref,
+    normed_ref, low_ref, rate_ref, full_ref, w_ref, sem,
 ):
     join_weight(where_ref, (shard, mine, other), w_ref, full_ref, sem)
     hidden = x_ref[...].astype(f32) + (nn(c_ref[...], w_ref[...]) + b_ref[...])
@@ -300,7 +343,7 @@
 
 
 def mix_and_norm(where, pieces, context, b, tokens, gain, shift):
-    rows = context.shape[0]
+    rows = tokens.shape[0]
     tile = pl.BlockSpec((TILE, D), lambda i: (i, 0))
     row = pl.BlockSpec((1, D), lambda i: (0, 0))
     return pl.pallas_call(
@@ -408,48 +451,43 @@
     )(where, *pieces, coef, act, b, normed, gain, shift, teacher, cotangent, flags)
 
 
-def gram_kernel(order_ref, left_ref, right_ref, keep_ref, send_ref):
+def gram_kernel(order_ref, left_ref, *refs):
+    rights, keep_ref, send_ref = refs[:-2], refs[-2], refs[-1]
     half = keep_ref.shape[1]
-    grad = tn(left_ref[...], right_ref[...])
     first = order_ref[pl.num_programs(1)] == 0
-    low, high = grad[:half], grad[half:]
-    keep_ref[0] = jnp.where(first, low, high).astype(bf16)
-    send_ref[0] = jnp.where(first, high, low).astype(bf16)
-
-
-def gram(order, left, right, shards, wide):
+    at = 0
+    for right_ref in rights:
+        grad = tn(left_ref[...], right_ref[...])
+        columns = slice(at, at + right_ref.shape[1])
+        at += right_ref.shape[1]
+        low, high = grad[:half], grad[half:]
+        keep_ref[0, :, columns] = jnp.where(first, low, high).astype(bf16)
+        send_ref[0, :, columns] = jnp.where(first, high, low).astype(bf16)
+
+
+def gram(order, left, rights, shards, wide=D):
     tokens, height = left.shape
-    columns = right.shape[1]
+    columns = sum(right.shape[1] for right in rights)
     part = height // shards
-    out = pl.BlockSpec((1, part // 2, wide), lambda j, r, order_ref: (r, 0, j))
+    steps = columns // wide if len(rights) == 1 else 1
+    out = pl.BlockSpec((1, part // 2, columns // steps), lambda j, r, order_ref: (r, 0, j))
     return pl.pallas_call(
         gram_kernel,
         grid_spec=pltpu.PrefetchScalarGridSpec(
             num_scalar_prefetch=1,
-            grid=(columns // wide, shards),
-            in_specs=[
-                pl.BlockSpec((tokens, part), lambda j, r, order_ref: (0, order_ref[r])),
-                pl.BlockSpec((tokens, wide), lambda j, r, order_ref: (0, j)),
-            ],
+            grid=(steps, shards),
+            in_specs=[pl.BlockSpec((tokens, part), lambda j, r, order_ref: (0, order_ref[r]))]
+            + [pl.BlockSpec((tokens, right.shape[1] // steps), lambda j, r, order_ref: (0, j)) for right in rights],
             out_specs=[out, out],
         ),
         out_shape=[sds((shards, part // 2, columns), bf16)] * 2,
         compiler_params=params(),
         cost_estimate=cost(2 * tokens * height * columns, 2 * (tokens * (height + columns) + height * columns)),
         name="gram",
-    )(order, left, right)
-
-
-def feed_back_kernel(
-    db_ref, wo_ref, slope_ref, wi_ref, dsum_ref, normed_ref, rate_ref, g_ref, s_ref,
-    dpre_ref, bias_ref, done_ref, dattn_ref, sums_ref, total,
-):
-    j = pl.program_id(0)
-
-    @pl.when(j == 0)
-    def _():
-        total[...] = dsum_ref[...]
-
+    )(order, left, *rights)
+
+
+def feed_back_columns(db_ref, wo_ref, slope_ref, wi_ref, dpre_ref, bias_ref, total):
     ones = jnp.ones((8, TILE), bf16)
     bias = jnp.zeros(bias_ref.shape, f32)
     for i in range(db_ref.shape[0] // TILE):
@@ -460,7 +498,26 @@
         total[rows, :] += nt(pre, wi_ref[...])
     bias_ref[...] = bias
 
-    @pl.when(j == pl.num_programs(0) - 1)
+
+def feed_back_first_kernel(tie_ref, db_ref, wo_ref, slope_ref, wi_ref, dsum_ref, dpre_ref, bias_ref, total):
+    @pl.when(pl.program_id(0) == 0)
+    def _():
+        total[...] = dsum_ref[...]
+
+    feed_back_columns(db_ref, wo_ref, slope_ref, wi_ref, dpre_ref, bias_ref, total)
+
+
+def feed_back_last_kernel(
+    tie_ref, db_ref, wo_ref, slope_ref, wi_ref, dsum_ref, normed_ref, rate_ref, g_ref, s_ref,
+    dpre_ref, bias_ref, done_ref, dattn_ref, sums_ref, total,
+):
+    @pl.when(pl.program_id(0) == 0)
+    def _():
+        total[...] = dsum_ref[...]
+
+    feed_back_columns(db_ref, wo_ref, slope_ref, wi_ref, dpre_ref, bias_ref, total)
+
+    @pl.when(pl.program_id(0) == pl.num_programs(0) - 1)
     def _():
         gain = g_ref[...]
         sums_ref[...] = jnp.zeros_like(sums_ref)
@@ -477,30 +534,42 @@
             sums_ref[2:3, :] += jnp.sum(low.astype(f32), axis=0, keepdims=True)
 
 
-def feed_back(d_branch, w_outer, slope, w_inner, d_sum_two, normed, rate, gain, shift):
+def feed_back(tie, side, d_branch, w_outer, slope, w_inner, so_far, norm=None):
     rows, wide = d_branch.shape[0], 512
+    steps = FF // wide // 2
+    begin = side * steps
     whole = pl.BlockSpec((rows, D), lambda j: (0, 0))
     row = pl.BlockSpec((1, D), lambda j: (0, 0))
-    tall = pl.BlockSpec((rows, wide), lambda j: (0, j))
+    in_specs = [
+        pl.BlockSpec(memory_space=pltpu.SMEM),
+        whole,
+        pl.BlockSpec((wide, D), lambda j: (j + begin, 0)),
+        pl.BlockSpec((rows, wide), lambda j: (0, j + begin)),
+        pl.BlockSpec((D, wide), lambda j: (0, j + begin)),
+        whole,
+    ]
+    out_specs = [pl.BlockSpec((rows, wide), lambda j: (0, j)), pl.BlockSpec((8, wide), lambda j: (0, j)), whole]
+    out_shape = [sds((rows, FF // 2), bf16), sds((8, FF // 2), f32), sds((rows, D), f32)]
+    args = (tie, d_branch, w_outer, slope, w_inner, so_far)
+    common = dict(grid=(steps,), compiler_params=params(), cost_estimate=cost(2 * D * FF * rows, 30 * 2**20))
+    if norm is None:
+        return pl.pallas_call(
+            feed_back_first_kernel,
+            in_specs=in_specs,
+            out_specs=out_specs,
+            out_shape=out_shape,
+            name="feed_back_first",
+            **common,
+        )(*args)
     return pl.pallas_call(
-        feed_back_kernel,
-        grid=(FF // wide,),
-        in_specs=[
-            whole,
-            pl.BlockSpec((wide, D), lambda j: (j, 0)),
-            tall,
-            pl.BlockSpec((D, wide), lambda j: (0, j)),
-            whole, whole,
-            pl.BlockSpec((rows, 1), lambda j: (0, 0)),
-            row, row,
-        ],
-        out_specs=[tall, pl.BlockSpec((8, wide), lambda j: (0, j)), whole, whole, pl.BlockSpec((8, D), lambda j: (0, 0))],
-        out_shape=[sds((rows, FF), bf16), sds((8, FF), f32), sds((rows, D), f32), sds((rows, D), bf16), sds((8, D), f32)],
+        feed_back_last_kernel,
+        in_specs=in_specs + [whole, pl.BlockSpec((rows, 1), lambda j: (0, 0)), row, row],
+        out_specs=out_specs + [whole, pl.BlockSpec((8, D), lambda j: (0, 0))],
+        out_shape=out_shape + [sds((rows, D), bf16), sds((8, D), f32)],
         scratch_shapes=[pltpu.VMEM((rows, D), f32)],
-        compiler_params=params(),
-        cost_estimate=cost(4 * D * FF * rows, 50 * 2**20),
-        name="feed_back",
-    )(d_branch, w_outer, slope, w_inner, d_sum_two, normed, rate, gain, shift)
+        name="feed_back_last",
+        **common,
+    )(*args, *norm)
 
 
 def turn_kernel(d_ref, w_ref, out_ref):
@@ -522,23 +591,89 @@
     )(d, w)
 
 
-def input_kernel(base_ref, d_ref, w_ref, out_ref):
-    out_ref[...] = base_ref[...] + nt(d_ref[...], w_ref[...])
-
-
-def input_back(base, d, w):
-    rows = base.shape[0]
+def qkv_gradient_kernel(order_ref, x_ref, dq_ref, own_ref, before_ref, behind_ref, *refs):
+    mixing, (keep_ref, send_ref, joined_ref, sums_ref) = refs[:-4], refs[-4:]
+    rows, wide = dq_ref.shape
+    half = keep_ref.shape[1]
+    first = order_ref[pl.num_programs(0)] == 0
+
+    @pl.when(pl.program_id(0) == 0)
+    def _():
+        ones = jnp.ones((8, rows), bf16)
+        if rows > 2 * DOC_MAX:
+            joined_ref[:, DOC_MAX:-DOC_MAX] = own_ref[:, DOC_MAX:-DOC_MAX]
+        for s in (0, 1):
+            for edge, part_ref in ((slice(0, DOC_MAX), before_ref), (slice(rows - DOC_MAX, rows), behind_ref)):
+                joined_ref[s, edge] = (own_ref[s, edge].astype(f32) + part_ref[s].astype(f32)).astype(bf16)
+        sums_ref[:, :wide] = nn(ones, dq_ref[...])
+        sums_ref[:, wide:] = nn(ones, joined_ref[1])
+
+    def put(begin, grad):
+        columns = slice(begin, begin + grad.shape[1])
+        low, high = grad[:half], grad[half:]
+        keep_ref[0, :, columns] = jnp.where(first, low, high).astype(bf16)
+        send_ref[0, :, columns] = jnp.where(first, high, low).astype(bf16)
+
+    x = x_ref[...]
+    put(0, tn(x, dq_ref[...]))
+    put(wide, tn(x, joined_ref[0]))
+    put(2 * wide, tn(x, joined_ref[1]))
+    if mixing:
+        context_ref, d_attn_ref = mixing
+        put(3 * wide, tn(context_ref[...], d_attn_ref[...]))
+
+
+def qkv_gradient(order, tokens, dq, own, before, behind, shards, mixing=()):
+    rows, wide = dq.shape
+    part = D // shards
+    columns = 3 * wide + (D if mixing else 0)
+    out = pl.BlockSpec((1, part // 2, columns), lambda r, order_ref: (r, 0, 0))
+    left = pl.BlockSpec((rows, part), lambda r, order_ref: (0, order_ref[r]))
+    whole = pl.BlockSpec((rows, wide), lambda r, order_ref: (0, 0))
+    both = pl.BlockSpec((2, rows, wide), lambda r, order_ref: (0, 0, 0))
+    rim = pl.BlockSpec((2, DOC_MAX, wide), lambda r, order_ref: (0, 0, 0))
+    return pl.pallas_call(
+        qkv_gradient_kernel,
+        grid_spec=pltpu.PrefetchScalarGridSpec(
+            num_scalar_prefetch=1,
+            grid=(shards,),
+            in_specs=[left, whole, both, rim, rim]
+            + ([left, pl.BlockSpec((rows, D), lambda r, order_ref: (0, 0))] if mixing else []),
+            out_specs=[out, out, both, pl.BlockSpec((8, 2 * wide), lambda r, order_ref: (0, 0))],
+        ),
+        out_shape=[sds((shards, part // 2, columns), bf16)] * 2 + [sds((2, rows, wide), bf16), sds((8, 2 * wide), f32)],
+        compiler_params=params(),
+        cost_estimate=cost(2 * rows * D * columns, 16 * 2**20),
+        name="qkv_gradient",
+    )(order, tokens, dq, own, before, behind, *mixing)
+
+
+def input_kernel(base_ref, dq_ref, joined_ref, w_ref, out_ref):
+    wide = dq_ref.shape[1]
+    total = base_ref[...] + nt(dq_ref[...], w_ref[:, :wide])
+    for s in (0, 1):
+        total += nt(joined_ref[s], w_ref[:, (1 + s) * wide : (2 + s) * wide])
+    out_ref[...] = total
+
+
+def input_back(base, dq, joined, w, side):
+    rows, wide = dq.shape
     tile = pl.BlockSpec((TILE, D), lambda i: (i, 0))
     return pl.pallas_call(
         input_kernel,
         grid=(rows // TILE,),
-        in_specs=[tile, pl.BlockSpec((TILE, 3 * D), lambda i: (i, 0)), pl.BlockSpec((D, 3 * D), lambda i: (0, 0))],
+        in_specs=[
+            tile,
+            pl.BlockSpec((TILE, wide), lambda i: (i, 0)),
+            pl.BlockSpec((2, TILE, wide), lambda i: (0, i, 0)),
+            pl.BlockSpec((D, 3 * wide), lambda i: (0, side)),
+        ],
         out_specs=tile,
         out_shape=sds((rows, D), f32),
         compiler_params=params(),
-        cost_estimate=cost(6 * D * D * rows, 20 * 2**20),
+        cost_estimate=cost(6 * D * wide * rows, 14 * 2**20),
         name="input_back",
-    )(base, d, w)
+    )(base, dq, joined, w)
 
 
 def swap(value, axis, bit):
@@ -549,25 +684,26 @@
     return lax.optimization_barrier((value,) + others)[0]
 
 
-def gather_weight(shard, own):
+def arrive(gate, value):
+    return value if gate[0] is None else after(value, gate[0])
+
+
+def gathering(gate, shard, own):
     n = lax.axis_size("fsdp")
-    rows = shard.shape[0]
-    half, quarter = rows // 2, rows // 4
-    held, whole = {}, {}
+    quarter = shard.shape[0] // 4
+    near = [1 << b for b in range(n.bit_length() - 1)]
+    whole = dict(zip(near, (yield [arrive(gate, swap(own, "fsdp", r)) for r in near])))
+    held = {(r, s): value[s * quarter : (s + 1) * quarter] for r, value in whole.items() for s in (0, 1)}
+    found = []
     for r in range(1, n):
-        if r & (r - 1) == 0:
-            whole[r] = swap(own, "fsdp", r)
-            for s in (0, 1):
-                held[r, s] = whole[r][s * quarter : (s + 1) * quarter]
+        if r in whole:
+            found.append(whole[r])
         else:
             for s, bit in ((0, 1 << (r.bit_length() - 1)), (1, r & -r)):
-                held[r, s] = swap(held[r ^ bit, s], "fsdp", bit)
-    found = []
-    for r in range(1, n):
-        found += [whole[r]] if r in whole else [held[r, 0], held[r, 1]]
-    mine = jnp.concatenate(found, axis=0)
-    other = swap(mine, "ctx", 1)
-    return (shard, mine, other), [whole[r] for r in whole], mine
+                held[r, s] = arrive(gate, swap(held[r ^ bit, s], "fsdp", bit))
+                found.append(held[r, s])
+    (mine,) = yield [jnp.concatenate(found, axis=0)]
+    yield [shard, mine, arrive(gate, swap(mine, "ctx", 1))]
 
 
 def half_sets(value, bit):
@@ -581,45 +717,103 @@
     return (a.astype(f32) + b.astype(f32)).astype(bf16)
 
 
-def scatter_sum(keep, send):
+def reduction(gate, keep, send, parity):
+    got = arrive(gate, swap(send, "ctx", 1))
     n = lax.axis_size("fsdp")
-    got = swap(send, "ctx", 1)
     quarter = keep.shape[1] // 2
     bits = [1 << b for b in range(n.bit_length() - 1)]
-    parts = []
-    for s, order in ((0, bits), (1, bits[::-1])):
-        rows = slice(s * quarter, (s + 1) * quarter)
-        current = add_low(keep[:, rows], got[:, rows])
-        ids = list(range(n))
-        for bit in order:
-            where = [i for i, r in enumerate(ids) if not r & bit]
-            away = [i for i, r in enumerate(ids) if r & bit]
-            step = away[0] - where[0]
-            mine, theirs = half_sets(current, step)
-            ids = [ids[i] for i in where]
-            current = add_low(mine, swap(theirs, "fsdp", bit))
-        parts.append(current[0])
-    return parts
-
-
-def chain_sum(value):
+    streams = [(order, list(range(n))) for order in (bits, bits[::-1])]
+    parts = [add_low(keep[:, s * quarter : (s + 1) * quarter], got[:, s * quarter : (s + 1) * quarter]) for s in (0, 1)]
+    parts = list((yield parts))
+    for k in range(len(bits)):
+        for s, (order, ids) in enumerate(streams):
+            bit = order[k]
+            step = [i for i, r in enumerate(ids) if r & bit][0]
+            ids[:] = [r for r in ids if not r & bit]
+            mine, theirs = half_sets(parts[s], step)
+            parts[s] = add_low(mine, arrive(gate, swap(theirs, "fsdp", bit)))
+        if k < len(bits) - 1:
+            parts = list((yield parts))
+    value = jnp.concatenate([part[0] for part in parts], axis=0)
+    (value,) = yield [value]
     count = lax.axis_size("ctx") // 2
     position = lax.axis_index("ctx") // 2
     half = count // 2
 
     def move(value, chip_pairs):
         pairs = [(2 * a + c, 2 * b + c) for a, b in chip_pairs for c in (0, 1)]
-        return lax.ppermute(value, "ctx", pairs)
+        return arrive(gate, lax.ppermute(value, "ctx", pairs))
 
     for s in range(half - 1):
         value = add_low(value, move(value, [(s, s + 1), (count - 1 - s, count - 2 - s)]))
+        (value,) = yield [value]
     inner = (position == half - 1) | (position == half)
     across = move(value, [(half - 1, half), (half, half - 1)])
     value = jnp.where(inner, add_low(value, across), value)
+    (value,) = yield [value]
     for s in reversed(range(half - 1)):
         back = move(value, [(s + 1, s), (count - 2 - s, count - 1 - s)])
         value = jnp.where((position == s) | (position == count - 1 - s), back, value)
-    return value
+        (value,) = yield [value]
+    other = arrive(gate, swap(value, "ctx", 1))
+    first = parity == 0
+    yield [jnp.concatenate([jnp.where(first, value, other), jnp.where(first, other, value)], axis=0).astype(f32)]
+
+
+def chip_sum(gate, keep, send, pause=0):
+    value = add_low(keep, arrive(gate, swap(send, "ctx", 1)))
+    (value,) = yield [value]
+    (value,) = yield [lax.psum_scatter(value, "fsdp", scatter_dimension=0, tiled=True)[0]]
+    for _ in range(pause):
+        (value,) = yield [value]
+    groups = [list(range(k, lax.axis_size("ctx"), 2)) for k in (0, 1)]
+    yield [lax.psum(value, "ctx", axis_index_groups=groups)]
+
+
+def both_halves(value, parity):
+    other = swap(value, "ctx", 1)
+    first = parity == 0
+    return jnp.concatenate([jnp.where(first, value, other), jnp.where(first, other, value)], axis=0).astype(f32)
+
+
+def summed(gate, value):
+    (value,) = yield [value]
+    for axis in ("ctx", "fsdp"):
+        bit = 1
+        while bit < lax.axis_size(axis):
+            value = value + arrive(gate, swap(value, axis, bit))
+            bit *= 2
+            (value,) = yield [value]
+
+
+class Staged:
+    def __init__(self, stages, *args):
+        self.gate, self.values, self.done = [None], None, False
+        self.stages = stages(self.gate, *args)
+
+    def step(self):
+        try:
+            self.values = self.stages.send(self.values)
+        except StopIteration:
+            self.done = True
+        return not self.done
+
+    def result(self):
+        while self.step():
+            pass
+        return self.values
+
+
+def boundary(done, tie, *transfers):
+    moving = []
+    for transfer in transfers:
+        transfer.gate[0] = done
+        if transfer.step():
+            moving.append(transfer)
+    tie, values = lax.optimization_barrier((tie, [transfer.values for transfer in moving], done))[:2]
+    for transfer, value in zip(moving, values):
+        transfer.values = value
+    return tie
 
 
 def gather_small(vector, f):
@@ -634,15 +828,6 @@
         split = value.reshape(n // (2 * bit), 2, bit, -1)
         value = jnp.where(f & bit > 0, split[:, ::-1], split).reshape(n, -1)
         bit *= 2
-    return value
-
-
-def sum_everywhere(value):
-    for axis in ("ctx", "fsdp"):
-        bit = 1
-        while bit < lax.axis_size(axis):
-            value = value + swap(value, axis, bit)
-            bit *= 2
     return value
 
 
@@ -677,11 +862,21 @@
     where = jnp.stack([f, parity]).astype(jnp.int32)
     order = jnp.concatenate([f ^ jnp.arange(n_fsdp, dtype=jnp.int32), parity[None].astype(jnp.int32)])
 
+    def own_half(shard):
+        half = shard.shape[0] // 2
+        return lax.dynamic_slice_in_dim(shard, parity * half, half)
+
+    qkv_shard, own_qkv = pack_qkv(where, query_weight, key_weight, value_weight)
+    w_qkv = Staged(gathering, qkv_shard, own_qkv)
+    w_qkv.step()
+    own_proj, own_inner = after((own_half(proj_weight), own_half(inner_weight)), w_qkv.values)
+    w_proj = Staged(gathering, proj_weight, own_proj)
+    w_inner = Staged(gathering, inner_weight, own_inner)
+
     up = [(i, i + 1) for i in range(n_ctx - 1)]
     down = [(b, a) for a, b in up]
     before = lax.ppermute(tokens[rows - DOC_MAX :], "ctx", up)
     behind = lax.ppermute(tokens[:DOC_MAX], "ctx", down)
-    x_near = jnp.concatenate([before, tokens, behind], axis=0)
 
     small = jnp.concatenate(
         [query_bias, value_bias, proj_bias, attn_gain, attn_shift, outer_bias, final_gain, final_shift, inner_bias]
@@ -692,21 +887,7 @@
     b_inner = small[:, 8 * part :].reshape(1, FF)
 
     flags = valid_flag[0].astype(f32)[:, None]
-
-    def own_half(shard):
-        half = shard.shape[0] // 2
-        return lax.dynamic_slice_in_dim(shard, parity * half, half)
-
-    qkv_shard = jnp.concatenate([query_weight, key_weight, value_weight], axis=1)
-    qkv_pieces, qkv_first, qkv_last = gather_weight(qkv_shard, own_half(qkv_shard))
-    proj_own = after(own_half(proj_weight), *qkv_first)
-    proj_pieces, proj_first, proj_last = gather_weight(proj_weight, proj_own)
-    inner_own = after(own_half(inner_weight), *qkv_first)
-    inner_pieces, inner_first, inner_last = gather_weight(inner_weight, inner_own)
-    outer_own = after(own_half(outer_weight), *proj_first, qkv_last)
-    outer_pieces, outer_first, outer_last = gather_weight(outer_weight, outer_own)
-
-    count = sum_everywhere(after(jnp.full((8, 128), jnp.sum(flags), f32), *qkv_first))[0, 0]
+    counted = Staged(summed, after(jnp.full((8, 128), jnp.sum(flags), f32), w_qkv.values))
 
     position = c * rows
     starts = doc_start[0]
@@ -726,58 +907,79 @@
     idq = own_starts.reshape(count_tiles, 1, TILE)
     idk = near_starts[:, None]
 
-    query, keys, values, keys_t, values_t, w_qkv = project_qkv(where, qkv_pieces, x_near, b_query, b_value)
-    context, log_totals = attn_fwd(low_tile, high_tile, query, keys, values_t, idq, idk)
-    normed, normed_low, rate, w_proj = mix_and_norm(where, proj_pieces, context, b_proj, tokens, g_attn, s_attn)
-    act, slope, w_inner = inner_forward(where, inner_pieces, normed_low, b_inner)
+    w_qkv.step()
+    w_qkv.values, b_query, b_value, b_proj, g_attn, s_attn, b_inner, idq, idk, low_tile, high_tile = lax.optimization_barrier(
+        (w_qkv.values, b_query, b_value, b_proj, g_attn, s_attn, b_inner, idq, idk, low_tile, high_tile)
+    )
+
+    def attend(side, tie, *so_far):
+        return attn_fwd(tie, high_tile, query, keys, values_t, idq, idk, 2 * side, 2, so_far)
+
+    query, keys, values, keys_t, values_t, w_qkv = project_qkv(where, w_qkv.result(), before, tokens, behind, b_query, b_value)
+    context_a, log_a = attend(0, boundary(query, low_tile, w_proj, counted))
+    tie, own_outer = boundary(context_a, (low_tile, own_half(outer_weight)), w_proj, w_inner, counted)
+    w_outer = Staged(gathering, outer_weight, own_outer)
+    context, log_totals = attend(1, tie, context_a, log_a)
+    normed, normed_low, rate, w_proj = mix_and_norm(
+        boundary(context, where, w_proj, w_inner, counted), w_proj.values, context, b_proj, tokens, g_attn, s_attn
+    )
+    act, slope, w_inner = inner_forward(boundary(normed, where, w_inner, w_outer, counted), w_inner.values, normed_low, b_inner)
+    count = counted.result()[0][0, 0]
     coef = (n_fsdp * n_ctx * rows / count).reshape(1)
+    tie = boundary(act, where, w_outer)
     layer_out, d_sum_two, d_branch, final_sums, w_outer = outer_forward(
-        where, outer_pieces, coef, act, b_outer, normed, g_final, s_final, teacher_states[0], out_cotangent[0], flags
-    )
-
-    outer_parts = scatter_sum(*gram(order, act, d_branch, n_fsdp, 512))
-    d_pre, inner_bias_sum, d_sum_one, d_attn, attn_sums = feed_back(
-        d_branch, w_outer, slope, w_inner, d_sum_two, normed, rate, g_attn, s_attn
-    )
-    inner_parts = scatter_sum(*gram(order, normed_low, d_pre, n_fsdp, 2048))
-    d_context = turned_product(d_attn, w_proj)
-    proj_parts = scatter_sum(*gram(order, context, d_attn, n_fsdp, D))
-    outer_total = chain_sum(jnp.concatenate(outer_parts, axis=0))
-    inner_total = chain_sum(jnp.concatenate(inner_parts, axis=0))
-    proj_total = chain_sum(jnp.concatenate(proj_parts, axis=0))
-    d_query, near_dk, near_dv = attn_bwd(
-        low_tile, high_tile, query, d_context, context, keys, keys_t, values, log_totals, idq, idk
-    )
-    near_d = jnp.concatenate([near_dk, near_dv], axis=1)
-    from_above = lax.ppermute(near_d[:DOC_MAX], "ctx", down)
-    from_below = lax.ppermute(near_d[rows + DOC_MAX :], "ctx", up)
-    own = near_d[DOC_MAX : DOC_MAX + rows].astype(f32)
-    rest = jnp.zeros((rows - DOC_MAX, 2 * D), f32)
-    own = (
-        own
-        + jnp.concatenate([from_below.astype(f32), rest], axis=0)
-        + jnp.concatenate([rest, from_above.astype(f32)], axis=0)
-    ).astype(bf16)
-    d_keys, d_values = own[:, :D], own[:, D:]
-    d_joined = jnp.concatenate([d_query, own], axis=1)
-    qkv_parts = scatter_sum(*gram(order, tokens, d_joined, n_fsdp, 3 * D // 2))
-    input_grad = input_back(d_sum_one, d_joined, w_qkv)
-    qkv_total = chain_sum(jnp.concatenate(qkv_parts, axis=0))
-
-    def finish(mine):
-        quarter = mine.shape[0] // 2
-        other = swap(mine, "ctx", 1)
-        first = parity == 0
-        return jnp.concatenate([jnp.where(first, mine, other), jnp.where(first, other, mine)], axis=0).astype(f32)
-
-    outer_grad, inner_grad, proj_grad, qkv_grad = (
-        finish(outer_total), finish(inner_total), finish(proj_total), finish(qkv_total)
-    )
-
-    early = jnp.concatenate([final_sums[:4], attn_sums[:3], inner_bias_sum[:1].reshape(4, D)], axis=0)
-    early = sum_everywhere(jnp.concatenate([early, jnp.zeros((5, D), f32)], axis=0))
-    late = jnp.sum(jnp.stack([d_query, d_values]).astype(f32), axis=1)
-    late = sum_everywhere(jnp.concatenate([late, jnp.zeros((6, D), f32)], axis=0))
+        tie, w_outer.result(), coef, act, b_outer, normed, g_final, s_final, teacher_states[0], out_cotangent[0], flags
+    )
+
+    plain = jnp.concatenate([jnp.arange(n_fsdp, dtype=jnp.int32), order[n_fsdp:]])
+    outer = Staged(chip_sum, *gram(plain, act, [d_branch], n_fsdp))
+    d_pre_a, bias_a, so_far = feed_back(where, 0, d_branch, w_outer, slope, w_inner, d_sum_two)
+    d_pre_b, bias_b, d_sum_one, d_attn, attn_sums = feed_back(
+        boundary(d_pre_a, where, outer), 1, d_branch, w_outer, slope, w_inner, so_far, (normed, rate, g_attn, s_attn)
+    )
+    early = Staged(
+        summed,
+        jnp.concatenate(
+            [final_sums[:4], attn_sums[:3], bias_a[:1].reshape(2, D), bias_b[:1].reshape(2, D), jnp.zeros((5, D), f32)]
+        ),
+    )
+    inner_pair = gram(boundary(d_attn, plain), normed_low, [d_pre_a, d_pre_b], n_fsdp)
+    inner = Staged(chip_sum, *inner_pair, 1)
+    d_context = turned_product(d_attn, boundary(inner_pair[0], w_proj, early))
+
+    def attend_back(side, tie):
+        dq, own, low, high = attn_bwd(
+            tie, high_tile, query, d_context, context, keys, keys_t, values, log_totals, idq, idk, 2 * side, 2
+        )
+        return dq, own, lax.ppermute(high, "ctx", up), lax.ppermute(low, "ctx", down)
+
+    parts_a = attend_back(0, boundary(d_context, low_tile, outer, inner, early))
+    *first_pair, joined_a, sums_a = qkv_gradient(
+        boundary(parts_a[0], order, early), tokens, *parts_a, n_fsdp, (context, d_attn)
+    )
+    first = Staged(reduction, *first_pair, parity)
+    parts_b = attend_back(1, boundary(first_pair[0], low_tile, inner, early))
+    *last_pair, joined_b, sums_b = qkv_gradient(
+        boundary(parts_b[0], order, first, outer, inner, early), tokens, *parts_b, n_fsdp
+    )
+    last = Staged(reduction, *last_pair, parity)
+    late = jnp.stack([sums_a[0], sums_b[0]]).reshape(2, 2, D // 2).transpose(1, 0, 2).reshape(2, D)
+    late = Staged(summed, jnp.concatenate([late, jnp.zeros((6, D), f32)]))
+    input_a = input_back(
+        d_sum_one, parts_a[0], joined_a, boundary(last_pair[0], w_qkv, first, early, late), 0
+    )
+    input_grad = input_back(
+        input_a, parts_b[0], joined_b, boundary(input_a, w_qkv, last, first, early, late), 1
+    )
+    boundary(input_grad, where, last, first, late)
+    first, last, early, late = (transfer.result()[0] for transfer in (first, last, early, late))
+    outer_grad, inner_grad = both_halves(outer.result()[0], parity), both_halves(inner.result()[0], parity)
+    proj_grad = first[:, 3 * D // 2 :]
+    sixth = D // 2
+    query_grad, key_grad, value_grad = (
+        jnp.concatenate([grad[:, i * sixth : (i + 1) * sixth] for grad in (first, last)], axis=1)
+        for i in range(3)
+    )
     mse = jnp.sum(early[3]) / (count * D)
 
     def mine(vector):
@@ -788,10 +990,10 @@
         layer_out[None],
         input_grad[None],
         mse,
-        qkv_grad[:, :D],
+        query_grad,
         mine(late[0]),
-        qkv_grad[:, D : 2 * D],
-        qkv_grad[:, 2 * D :],
+        key_grad,
+        value_grad,
         mine(late[1]),
         proj_grad,
         mine(early[6]),

time: 759 us -> 615 us (0.81)
  waiting for transfers between devices: 260 us -> 83.3 us
  Pallas kernels: 269 us -> 315 us
  local copies, waits for them, and re-layouts: 59.1 us -> 39.3 us
  between operations: 5.4 us -> 18.3 us
  starting transfers between devices: 123 us -> 113 us
    ppermute x61 -> x53, waiting for transfers between devices: 170 us -> 54.2 us  [swap(): lax.ppermute(value, axis, [(i, i ^ bit) for i in range(lax.axis_size(axis...]
    ppermute x14 -> x10, waiting for transfers between devices: 90.2 us -> 23.5 us  [the longest x6 23.5 us: move(): return arrive(gate, lax.ppermute(value, 'ctx', pairs))]
    pallas_call x1 -> x5, Pallas kernels: 36.9 us -> 68.9 us  [the longest x1 24.5 us: feed_back(): pl.pallas_call(feed_back_last_kernel, in_specs=in_specs + [whole, pl.Bloc...]
    pallas_call x4 -> x2, Pallas kernels: 54.8 us -> 29.4 us  [gram(): pl.pallas_call(gram_kernel, grid_spec=pltpu.PrefetchScalarGridSpec(num_sc...]
    pallas_call x1 -> x2, Pallas kernels: 45 us -> 63.9 us  [attn_bwd(): pl.pallas_call(attn_bwd_kernel, grid_spec=pltpu.PrefetchScalarGridSpec(nu...]
    pallas_call x1 -> x2, Pallas kernels: 31.2 us -> 45.1 us  [attn_fwd(): pl.pallas_call(attn_fwd_kernel, grid_spec=pltpu.PrefetchScalarGridSpec(nu...]
    ppermute x61 -> x53, starting transfers between devices: 96.1 us -> 84 us  [swap(): lax.ppermute(value, axis, [(i, i ^ bit) for i in range(lax.axis_size(axis...]
    unnamed x96 -> x65, local copies, waits for them, and re-layouts: 27.2 us -> 16 us
  transfers between devices with their start and end apart: 77 -> 69, of which waited for: 32 -> 17; matrix products, arithmetic and copies ran while one was open for 11% -> 10% of each run, Pallas kernels for 31% -> 45%
where the time goes in v2:
time: 615 us; the launch traced here: 611 us
  Pallas kernels  315 us (51%)
  starting transfers between devices  113 us (18%)
  waiting for transfers between devices  83.3 us (14%)
  other arithmetic  42.6 us (7%)
  local copies, waits for them, and re-layouts  39.3 us (6%)
  between operations  18.3 us (3%)
    ppermute x53, starting transfers between devices, swap(): lax.ppermute(value, axis, [(i, i ^ bit) for i in range(lax.axis_size(axis...  84 us
    pallas_call x2, Pallas kernels, attn_bwd(): pl.pallas_call(attn_bwd_kernel, grid_spec=pltpu.PrefetchScalarGridSpec(nu...  63.9 us
    ppermute x53, waiting for transfers between devices, swap(): lax.ppermute(value, axis, [(i, i ^ bit) for i in range(lax.axis_size(axis...  54.2 us
    pallas_call x2, Pallas kernels, attn_fwd(): pl.pallas_call(attn_fwd_kernel, grid_spec=pltpu.PrefetchScalarGridSpec(nu...  45.1 us
    pallas_call x1, Pallas kernels, inner_forward(): pl.pallas_call(inner_kernel, grid=(FF // wide,), in_specs=WEIGHT_SPECS +...  31.5 us
    pallas_call x2, Pallas kernels, gram(): pl.pallas_call(gram_kernel, grid_spec=pltpu.PrefetchScalarGridSpec(num_sc...  29.4 us
    pallas_call x1, Pallas kernels, feed_back(): pl.pallas_call(feed_back_last_kernel, in_specs=in_specs + [whole, pl.Bloc...  24.5 us
    ppermute x6, waiting for transfers between devices, move(): return arrive(gate, lax.ppermute(value, 'ctx', pairs))  23.5 us
  transfers between devices with their start and end apart: 69, of which 17 were waited for; matrix products, arithmetic and copies ran while one was open for 10% of the time, Pallas kernels for 45%

profile of v2, /device:TPU:0, one launch (start us, length us, event | category | flops | bytes accessed | tf_op | source)
XLA Modules:
  0.0 611.1 jit_solution(18290021709539681578)
XLA Ops:
  7.8 2.9 pack_qkv.1
  10.8 3.0 collective-permute-start.1
  24.3 8.9 %collective-permute-done.4 = bf16[1,3072]{1,0:T(2,128)(2,1)S(1)} collective-permute-done((bf16[1,3072]{1,0:T(2,128)(2,1)S(1)}, bf16[1,3072]{1,0:T(2,128)(2,1)S(1)}, u32[]{:S(2)}, u32[]{:S(2)}) %collective-permute-start.4) | collective-permute-done | bytes 6176 | tf_op jit(solution)/shard_map/ppermute | solution.py:680
  34.1 2.9 collective-permute-done.5
  38.0 1.6 collective-permute-start.3
  43.8 2.8 collective-permute-done.3
  50.7 3.1 collective-permute-start.8
  53.8 1.8 collective-permute-start.9
  56.3 1.7 constant_dynamic-slice_fusion.9
  58.0 2.3 constant_dynamic-slice_fusion.10
  67.4 20.5 %project_qkv.1 = (bf16[1024,1024]{1,0:T(8,128)(2,1)}, bf16[2048,1024]{1,0:T(8,128)(2,1)}, bf16[2048,1024]{1,0:T(8,128)(2,1)}, bf16[1024,2048]{1,0:T(8,128)(2,1)}...) custom-call(s32[2]{0:T(128)} %pad_add_fusion.where_ref.tie_ref, bf16[256,3072]{1,0:T(8,128)(2,1)} %get-tuple-element.196.shard, ...), custom_call_target="tpu_custom_call" | custom-call | flops 10737418240 | bytes 31457280 | tf_op jit(solution)/shard_map/project_qkv/pallas_call | solution.py:152
  91.1 4.0 collective-permute-start.15
  95.0 22.5 %attn_forward.2 = (bf16[1024,1024]{1,0:T(8,128)(2,1)}, f32[4,8,1024]{2,1,0:T(8,128)}) custom-call(s32[4]{0:T(128)} %get-tuple-element.310.lo_ref, s32[4]{0:T(128)} %get-tuple-element.207.hi_ref, bf16[1024,1024]{1,0:T(8,128)(2,1)} %get-tuple-element.200.q_ref, bf16[2048,1024]{1,0:T(8,128)(2,1)} %get-tuple-element.208.k_ref, ...), custom_call_target="tpu_custom_call" | custom-call | flops 20000000000 | bytes 2097152 | tf_op jit(solution)/shard_map/attn_forward/pallas_call | solution.py:227
  120.2 1.5 collective-permute-start.18
  121.8 4.3 collective-permute-start.19
  126.1 22.5 %attn_forward.3 = (bf16[1024,1024]{1,0:T(8,128)(2,1)}, f32[4,8,1024]{2,1,0:T(8,128)}) custom-call(s32[4]{0:T(128)} %get-tuple-element.310.lo_ref, s32[4]{0:T(128)} %get-tuple-element.207.hi_ref, bf16[1024,1024]{1,0:T(8,128)(2,1)} %get-tuple-element.200.q_ref, ...), custom_call_target="tpu_custom_call", output_to_operand_aliasing={{0}: (7, {}), {1}: (8, {})} | custom-call | flops 20000000000 | bytes 2097152 | tf_op jit(solution)/shard_map/attn_forward/pallas_call | solution.py:227
  150.7 2.5 collective-permute-start.22
  153.2 4.4 collective-permute-start.23
  157.6 9.6 %mix_and_norm.1 = (f32[1024,1024]{1,0:T(8,128)}, bf16[1024,1024]{1,0:T(8,128)(2,1)}, f32[1024,1]{1,0:T(8,128)}, bf16[1024,1024]{1,0:T(8,128)(2,1)}) custom-call(s32[2]{0:T(128)} %pad_add_fusion.where_ref.tie_ref, bf16[256,1024]{1,0:T(8,128)(2,1)} %shard.1, bf16[384,1024]{1,0:T(8,128)(2,1)} %copy-done.14, bf16[384,1024]{1,0:T(8,128)(2,1)} %collective-permute-done.16.other, ...), custom_call_target="tpu_custom_call" | custom-call | flops 2147483648 | bytes 14680064 | tf_op jit(solution)/shard_map/mix_and_norm/pallas_call | solution.py:349
  167.3 9.0 %collective-permute-done.21 = bf16[512,1024]{1,0:T(8,128)(2,1)S(1)} collective-permute-done((bf16[512,1024]{1,0:T(8,128)(2,1)S(1)}, bf16[512,1024]{1,0:T(8,128)(2,1)S(1)}, u32[]{:S(2)}, u32[]{:S(2)}) %collective-permute-start.21) | collective-permute-done | bytes 1048608 | tf_op jit(solution)/shard_map/ppermute | solution.py:680
  176.3 1.8 collective-permute-start.25
  178.1 1.8 collective-permute-start.24
  180.0 31.5 %inner_forward.1 = (bf16[1024,4096]{1,0:T(8,128)(2,1)}, bf16[1024,4096]{1,0:T(8,128)(2,1)}, bf16[1024,4096]{1,0:T(8,128)(2,1)}) custom-call(s32[2]{0:T(128)} %pad_add_fusion.where_ref.tie_ref, bf16[256,4096]{1,0:T(8,128)(2,1)} %shard.2, bf16[384,4096]{1,0:T(8,128)(2,1)} %copy-done.2, bf16[384,4096]{1,0:T(8,128)(2,1)} %collective-permute-done.20.other, ...), custom_call_target="tpu_custom_call" | custom-call | flops 8589934592 | bytes 27262976 | tf_op jit(solution)/shard_map/inner_forward/pallas_call | solution.py:385
  213.5 3.3 collective-permute-done.27
  221.7 22.6 %outer_forward.1 = (bf16[1024,1024]{1,0:T(8,128)(2,1)}, f32[1024,1024]{1,0:T(8,128)}, bf16[1024,1024]{1,0:T(8,128)(2,1)}, f32[8,1024]{1,0:T(8,128)}, bf16[4096,1024]{1,0:T(8,128)(2,1)}) custom-call(s32[2]{0:T(128)} %pad_add_fusion.where_ref.tie_ref, bf16[1024,1024]{1,0:T(8,128)(2,1)} %shard.3, bf16[1536,1024]{1,0:T(8,128)(2,1)} %copy-done.3, ...), custom_call_target="tpu_custom_call" | custom-call | flops 8589934592 | bytes 33554432 | tf_op jit(solution)/shard_map/outer_forward/pallas_call | solution.py:431
  244.3 13.8 %gram.2 = (bf16[4,512,1024]{2,1,0:T(8,128)(2,1)}, bf16[4,512,1024]{2,1,0:T(8,128)(2,1)}) custom-call(s32[5]{0:T(128)} %pad_add_fusion.1.order_ref, bf16[1024,4096]{1,0:T(8,128)(2,1)} %get-tuple-element.254.act_ref.left_ref, bf16[1024,1024]{1,0:T(8,128)(2,1)} %get-tuple-element.264.refs_0_.db_ref), custom_call_target="tpu_custom_call" | custom-call | flops 8589934592 | bytes 18874368 | tf_op jit(solution)/shard_map/gram/pallas_call | solution.py:474
  258.1 19.1 %feed_back_first.1 = (bf16[1024,2048]{1,0:T(8,128)(2,1)}, f32[8,2048]{1,0:T(8,128)}, f32[1024,1024]{1,0:T(8,128)}) custom-call(s32[2]{0:T(128)} %pad_add_fusion.where_ref.tie_ref, bf16[1024,1024]{1,0:T(8,128)(2,1)} %get-tuple-element.264.refs_0_.db_ref, bf16[4096,1024]{1,0:T(8,128)(2,1)} %get-tuple-element.267.wo_ref, ...), custom_call_target="tpu_custom_call" | custom-call | flops 8589934592 | bytes 31457280 | tf_op jit(solution)/shard_map/feed_back_first/pallas_call | solution.py:556
  277.2 6.4 %add_convert_fusion.1 = bf16[4,512,1024]{2,1,0:T(8,128)(2,1)} fusion(bf16[4,512,1024]{2,1,0:T(8,128)(2,1)} %collective-permute-done.29, bf16[4,512,1024]{2,1,0:T(8,128)(2,1)S(1)} %copy-done.1), kind=kLoop, calls=%fused_computation.1 | loop fusion | flops 8388608 | bytes 12582912 | tf_op jit(solution)/shard_map/convert_element_type | solution.py:717
  283.7 24.5 %feed_back_last.1 = (bf16[1024,2048]{1,0:T(8,128)(2,1)}, f32[8,2048]{1,0:T(8,128)}, f32[1024,1024]{1,0:T(8,128)}, bf16[1024,1024]{1,0:T(8,128)(2,1)}, f32[8,1024]{1,0:T(8,128)}) custom-call(s32[2]{0:T(128)} %pad_add_fusion.where_ref.tie_ref, bf16[1024,1024]{1,0:T(8,128)(2,1)} %get-tuple-element.264.refs_0_.db_ref, ...), custom_call_target="tpu_custom_call" | custom-call | flops 8589934592 | bytes 31457280 | tf_op jit(solution)/shard_map/feed_back_last/pallas_call | solution.py:564
  308.2 15.6 %gram.3 = (bf16[4,128,4096]{2,1,0:T(8,128)(2,1)}, bf16[4,128,4096]{2,1,0:T(8,128)(2,1)}) custom-call(s32[5]{0:T(128)} %pad_add_fusion.1.order_ref, bf16[1024,1024]{1,0:T(8,128)(2,1)} %get-tuple-element.252.x_ref.left_ref, bf16[1024,2048]{1,0:T(8,128)(2,1)} %get-tuple-element.271.refs_0_, bf16[1024,2048]{1,0:T(8,128)(2,1)} %get-tuple-element.280.refs_1_), custom_call_target="tpu_custom_call" | custom-call | flops 8589934592 | bytes 18874368 | tf_op jit(solution)/shard_map/gram/pallas_call | solution.py:474
  326.4 6.3 %turned_product.1.do_ref = bf16[1024,1024]{1,0:T(8,128)(2,1)} custom-call(bf16[1024,1024]{1,0:T(8,128)(2,1)} %get-tuple-element.278.d_ref.refs_1_, bf16[1024,1024]{1,0:T(8,128)(2,1)} %get-tuple-element.288.w_ref), custom_call_target="tpu_custom_call" | custom-call | flops 2147483648 | bytes 6291456 | tf_op jit(solution)/shard_map/turned_product/pallas_call | solution.py:582
  332.7 6.0 add_convert_fusion
  338.7 31.8 %attn_backward.2 = (bf16[1024,512]{1,0:T(8,128)(2,1)}, bf16[2,1024,512]{2,1,0:T(8,128)(2,1)}, bf16[2,512,512]{2,1,0:T(8,128)(2,1)}, bf16[2,512,512]{2,1,0:T(8,128)(2,1)}) custom-call(s32[4]{0:T(128)} %get-tuple-element.310.lo_ref, s32[4]{0:T(128)} %get-tuple-element.207.hi_ref, bf16[1024,1024]{1,0:T(8,128)(2,1)} %get-tuple-element.200.q_ref, ...), custom_call_target="tpu_custom_call" | custom-call | flops 30000001024 | bytes 4194304 | tf_op jit(solution)/shard_map/attn_backward/pallas_call | solution.py:295
  370.5 4.4 collective-permute-start.33
  375.0 1.7 collective-permute-start.34
  376.7 2.4 collective-permute-start.32
  380.5 12.5 %collective-permute-done.32 = f32[16,1024]{1,0:T(8,128)S(1)} collective-permute-done((f32[16,1024]{1,0:T(8,128)S(1)}, f32[16,1024]{1,0:T(8,128)S(1)}, u32[]{:S(2)}, u32[]{:S(2)}) %collective-permute-start.32) | collective-permute-done | bytes 65568 | tf_op jit(solution)/shard_map/ppermute | solution.py:680
  393.0 9.3 %collective-permute-start.36 = (f32[16,1024]{1,0:T(8,128)S(1)}, f32[16,1024]{1,0:T(8,128)S(1)}, u32[]{:S(2)}, u32[]{:S(2)}) collective-permute-start(f32[16,1024]{1,0:T(8,128)S(1)} %add.181), channel_id=1, source_target_pairs={{0,16},{4,20},{8,24},{12,28},{16,0},{20,4},{24,8},{28,12},{1,17},{... | collective-permute-start | bytes 196616 | tf_op jit(solution)/shard_map/ppermute | solution.py:680
  403.6 12.7 %qkv_gradient.2 = (bf16[4,128,2560]{2,1,0:T(8,128)(2,1)}, bf16[4,128,2560]{2,1,0:T(8,128)(2,1)}, bf16[2,1024,512]{2,1,0:T(8,128)(2,1)}, f32[8,1024]{1,0:T(8,128)}) custom-call(s32[5]{0:T(128)} %pad_add_fusion.2.order_ref, bf16[1024,1024]{1,0:T(8,128)(2,1)} %bitcast.170, bf16[1024,512]{1,0:T(8,128)(2,1)} %get-tuple-element.296.dq_ref, ...), custom_call_target="tpu_custom_call" | custom-call | flops 5368709120 | bytes 16777216 | tf_op jit(solution)/shard_map/qkv_gradient/pallas_call | solution.py:635
  417.1 32.1 %attn_backward.3 = (bf16[1024,512]{1,0:T(8,128)(2,1)}, bf16[2,1024,512]{2,1,0:T(8,128)(2,1)}, bf16[2,512,512]{2,1,0:T(8,128)(2,1)}, bf16[2,512,512]{2,1,0:T(8,128)(2,1)}) custom-call(s32[4]{0:T(128)} %get-tuple-element.310.lo_ref, s32[4]{0:T(128)} %get-tuple-element.207.hi_ref, bf16[1024,1024]{1,0:T(8,128)(2,1)} %get-tuple-element.200.q_ref, ...), custom_call_target="tpu_custom_call" | custom-call | flops 30000001024 | bytes 4194304 | tf_op jit(solution)/shard_map/attn_backward/pallas_call | solution.py:295
  450.7 2.4 add_convert_fusion.2
  453.1 5.1 collective-permute-start.39
  459.6 1.8 collective-permute-start.38
  462.3 2.0 collective-permute-start.42
  464.4 4.9 collective-permute-start.64
  469.3 9.6 %qkv_gradient.3 = (bf16[4,128,1536]{2,1,0:T(8,128)(2,1)}, bf16[4,128,1536]{2,1,0:T(8,128)(2,1)}, bf16[2,1024,512]{2,1,0:T(8,128)(2,1)}, f32[8,1024]{1,0:T(8,128)}) custom-call(s32[5]{0:T(128)} %pad_add_fusion.2.order_ref, bf16[1024,1024]{1,0:T(8,128)(2,1)} %bitcast.171, bf16[1024,512]{1,0:T(8,128)(2,1)} %get-tuple-element.311.dq_ref, ...), custom_call_target="tpu_custom_call" | custom-call | flops 3221225472 | bytes 16777216 | tf_op jit(solution)/shard_map/qkv_gradient/pallas_call | solution.py:635
  482.3 13.6 %collective-permute-start.43 = (bf16[4,128,1536]{2,1,0:T(8,128)(2,1)}, bf16[4,128,1536]{2,1,0:T(8,128)(2,1)}, u32[]{:S(2)}, u32[]{:S(2)}) collective-permute-start(bf16[4,128,1536]{2,1,0:T(8,128)(2,1)} %get-tuple-element.332), channel_id=1, source_target_pairs={{0,4},{4,0},{8,12},{12,8},{16,20},{20,16},{24,28},{28,24},{1,5},{5... | collective-permute-start | bytes 4718600 | tf_op jit(solution)/shard_map/ppermute | solution.py:680
  495.9 2.9 collective-permute-start.45
  502.4 8.6 %input_back.2.base_ref = f32[1024,1024]{1,0:T(8,128)} custom-call(f32[1024,1024]{1,0:T(8,128)} %get-tuple-element.276.base_ref, bf16[1024,512]{1,0:T(8,128)(2,1)} %get-tuple-element.296.dq_ref, bf16[2,1024,512]{2,1,0:T(8,128)(2,1)} %get-tuple-element.303.joined_ref, bf16[1024,3072]{1,0:T(8,128)(2,1)} %get-tuple-element.340.w_ref), custom_call_target="tpu_custom_call" | custom-call | flops 3221225472 | bytes 14680064 | tf_op jit(solution)/shard_map/input_back/pallas_call | solution.py:662
  512.8 5.5 all-reduce.8.cloned.1.call-done
  519.7 2.4 maximum_convert_fusion.1
  525.8 1.8 add_convert_fusion.4
  530.7 3.4 collective-permute-start.49
  534.2 8.5 %input_back.3 = f32[1024,1024]{1,0:T(8,128)} custom-call(f32[1024,1024]{1,0:T(8,128)} %input_back.2.base_ref, bf16[1024,512]{1,0:T(8,128)(2,1)} %get-tuple-element.311.dq_ref, bf16[2,1024,512]{2,1,0:T(8,128)(2,1)} %get-tuple-element.331.joined_ref, bf16[1024,3072]{1,0:T(8,128)(2,1)} %get-tuple-element.340.w_ref), custom_call_target="tpu_custom_call" | custom-call | flops 3221225472 | bytes 14680064 | tf_op jit(solution)/shard_map/input_back/pallas_call | solution.py:662
  542.7 6.0 collective-permute-done.50
  549.1 3.0 collective-permute-start.60
  552.7 1.6 collective-permute-done.60
  556.2 2.3 collective-permute-done.61
  559.1 1.9 collective-permute-done.54
  561.1 3.9 collective-permute-start.56
  565.0 2.5 maximum_convert_fusion
  567.5 2.7 collective-permute-done.56
  575.1 16.5 %collective-permute-done.52 = bf16[128,2560]{1,0:T(8,128)(2,1)S(1)} collective-permute-done((bf16[128,2560]{1,0:T(8,128)(2,1)S(1)}, bf16[128,2560]{1,0:T(8,128)(2,1)S(1)}, u32[]{:S(2)}, u32[]{:S(2)}) %collective-permute-start.52) | collective-permute-done | bytes 655392 | tf_op jit(solution)/shard_map/ppermute | solution.py:745
  591.6 4.2 collective-permute-done.58
  (286 shorter events, 84.1 us)
Async XLA Ops:
  7.2 331.4 %reduce-scatter.7.cloned.1.call-start = ((), (), s32[]{:S(2)}) async-start(), calls=%async_computation.4 | async-start | bytes 5242880
  10.8 27.2 %collective-permute-start.1 = (bf16[128,3072]{1,0:T(8,128)(2,1)}, bf16[128,3072]{1,0:T(8,128)(2,1)S(1)}, u32[]{:S(2)}, u32[]{:S(2)}) collective-permute-start(bf16[128,3072]{1,0:T(8,128)(2,1)} %get-tuple-element.193), channel_id=1, source_target_pairs={{0,2},{1,3},{2,0},{3,1},{4,6},{5,7},{6,4},{7,5},{8,10},{9,11},{10,... | collective-permute-start | bytes 2359304 | tf_op jit(solution)/shard_map/ppermute | solution.py:680
  13.7 25.8 %collective-permute-start = (bf16[128,3072]{1,0:T(8,128)(2,1)}, bf16[128,3072]{1,0:T(8,128)(2,1)S(1)}, u32[]{:S(2)}, u32[]{:S(2)}) collective-permute-start(bf16[128,3072]{1,0:T(8,128)(2,1)} %get-tuple-element.193), channel_id=1, source_target_pairs={{0,1},{1,0},{2,3},{3,2},{4,5},{5,4},{6,7},{7,6},{8,9},{9,8},{10,11... | collective-permute-start | bytes 2359304 | tf_op jit(solution)/shard_map/ppermute | solution.py:680
  22.6 10.6 %collective-permute-start.4 = (bf16[1,3072]{1,0:T(2,128)(2,1)S(1)}, bf16[1,3072]{1,0:T(2,128)(2,1)S(1)}, u32[]{:S(2)}, u32[]{:S(2)}) collective-permute-start(bf16[1,3072]{1,0:T(2,128)(2,1)S(1)} %reshape.221), channel_id=1, source_target_pairs={{0,1},{1,0},{2,3},{3,2},{4,5},{5,4},{6,7},{7,6},{8,9},{9,8},{10,11... | collective-permute-start | bytes 18440 | tf_op jit(solution)/shard_map/ppermute | solution.py:680
  33.3 3.8 collective-permute-start.5
  38.0 8.6 %collective-permute-start.3 = (bf16[64,3072]{1,0:T(8,128)(2,1)S(1)}, bf16[64,3072]{1,0:T(8,128)(2,1)S(1)}, u32[]{:S(2)}, u32[]{:S(2)}) collective-permute-start(bf16[64,3072]{1,0:T(8,128)(2,1)S(1)} %slice.296), channel_id=1, source_target_pairs={{0,1},{1,0},{2,3},{3,2},{4,5},{5,4},{6,7},{7,6},{8,9},{9,8},{10,11... | collective-permute-start | bytes 1179656 | tf_op jit(solution)/shard_map/ppermute | solution.py:680
  39.6 8.3 %collective-permute-start.2 = (bf16[64,3072]{1,0:T(8,128)(2,1)S(1)}, bf16[64,3072]{1,0:T(8,128)(2,1)S(1)}, u32[]{:S(2)}, u32[]{:S(2)}) collective-permute-start(bf16[64,3072]{1,0:T(8,128)(2,1)S(1)} %slice.295), channel_id=1, source_target_pairs={{0,2},{1,3},{2,0},{3,1},{4,6},{5,7},{6,4},{7,5},{8,10},{9,11},{10,... | collective-permute-start | bytes 1179656 | tf_op jit(solution)/shard_map/ppermute | solution.py:680
  49.2 18.2 %collective-permute-start.7 = (bf16[384,3072]{1,0:T(8,128)(2,1)S(1)}, bf16[384,3072]{1,0:T(8,128)(2,1)}, u32[]{:S(2)}, u32[]{:S(2)}) collective-permute-start(bf16[384,3072]{1,0:T(8,128)(2,1)S(1)} %pad_maximum_fusion.2.mine), channel_id=1, source_target_pairs={{0,4},{4,0},{8,12},{12,8},{16,20},{20,16},{24,28},{28,24},{1,5},{5... | collective-permute-start | bytes 7077896 | tf_op jit(solution)/shard_map/ppermute | solution.py:680
  50.7 13.8 %collective-permute-start.8 = (bf16[512,1024]{1,0:T(8,128)(2,1)}, bf16[512,1024]{1,0:T(8,128)(2,1)}, u32[]{:S(2)}, u32[]{:S(2)}) collective-permute-start(bf16[512,1024]{1,0:T(8,128)(2,1)} %get-tuple-element.377), channel_id=1, source_target_pairs={{0,4},{4,8},{8,12},{12,16},{16,20},{20,24},{24,28},{1,5},{5,9},{9,... | collective-permute-start | bytes 3145736 | tf_op jit(solution)/shard_map/ppermute | solution.py:878
  53.8 12.0 %collective-permute-start.9 = (bf16[512,1024]{1,0:T(8,128)(2,1)S(1)}, bf16[512,1024]{1,0:T(8,128)(2,1)}, u32[]{:S(2)}, u32[]{:S(2)}) collective-permute-start(bf16[512,1024]{1,0:T(8,128)(2,1)S(1)} %get-tuple-element.376), channel_id=1, source_target_pairs={{4,0},{8,4},{12,8},{16,12},{20,16},{24,20},{28,24},{5,1},{9,5},{13... | collective-permute-start | bytes 3145736 | tf_op jit(solution)/shard_map/ppermute | solution.py:879
  61.3 26.6 %collective-permute-start.6 = (bf16[128,1024]{1,0:T(8,128)(2,1)}, bf16[128,1024]{1,0:T(8,128)(2,1)}, u32[]{:S(2)}, u32[]{:S(2)}) collective-permute-start(bf16[128,1024]{1,0:T(8,128)(2,1)} %constant_dynamic-slice_fusion.9), channel_id=1, source_target_pairs={{0,1},{1,0},{2,3},{3,2},{4,5},{5,4},{6,7},{7,6},{8,9},{9,8},{10,11... | collective-permute-start | bytes 786440 | tf_op jit(solution)/shard_map/ppermute | solution.py:680
  61.8 26.1 %collective-permute-start.10 = (bf16[128,1024]{1,0:T(8,128)(2,1)}, bf16[128,1024]{1,0:T(8,128)(2,1)}, u32[]{:S(2)}, u32[]{:S(2)}) collective-permute-start(bf16[128,1024]{1,0:T(8,128)(2,1)} %constant_dynamic-slice_fusion.9), channel_id=1, source_target_pairs={{0,2},{1,3},{2,0},{3,1},{4,6},{5,7},{6,4},{7,5},{8,10},{9,11},{10,... | collective-permute-start | bytes 786440 | tf_op jit(solution)/shard_map/ppermute | solution.py:680
  64.5 53.1 %collective-permute-start.13 = (bf16[128,4096]{1,0:T(8,128)(2,1)}, bf16[128,4096]{1,0:T(8,128)(2,1)S(1)}, u32[]{:S(2)}, u32[]{:S(2)}) collective-permute-start(bf16[128,4096]{1,0:T(8,128)(2,1)} %constant_dynamic-slice_fusion.8), channel_id=1, source_target_pairs={{0,1},{1,0},{2,3},{3,2},{4,5},{5,4},{6,7},{7,6},{8,9},{9,8},{10,11... | collective-permute-start | bytes 3145736 | tf_op jit(solution)/shard_map/ppermute | solution.py:680
  65.9 51.7 %collective-permute-start.14 = (bf16[128,4096]{1,0:T(8,128)(2,1)}, bf16[128,4096]{1,0:T(8,128)(2,1)S(1)}, u32[]{:S(2)}, u32[]{:S(2)}) collective-permute-start(bf16[128,4096]{1,0:T(8,128)(2,1)} %constant_dynamic-slice_fusion.8), channel_id=1, source_target_pairs={{0,2},{1,3},{2,0},{3,1},{4,6},{5,7},{6,4},{7,5},{8,10},{9,11},{10,... | collective-permute-start | bytes 3145736 | tf_op jit(solution)/shard_map/ppermute | solution.py:680
  88.9 28.8 %collective-permute-start.12 = (bf16[64,1024]{1,0:T(8,128)(2,1)S(1)}, bf16[64,1024]{1,0:T(8,128)(2,1)S(1)}, u32[]{:S(2)}, u32[]{:S(2)}) collective-permute-start(bf16[64,1024]{1,0:T(8,128)(2,1)S(1)} %slice.239), channel_id=1, source_target_pairs={{0,1},{1,0},{2,3},{3,2},{4,5},{5,4},{6,7},{7,6},{8,9},{9,8},{10,11... | collective-permute-start | bytes 393224 | tf_op jit(solution)/shard_map/ppermute | solution.py:680
  90.4 27.2 %collective-permute-start.11 = (bf16[64,1024]{1,0:T(8,128)(2,1)S(1)}, bf16[64,1024]{1,0:T(8,128)(2,1)S(1)}, u32[]{:S(2)}, u32[]{:S(2)}) collective-permute-start(bf16[64,1024]{1,0:T(8,128)(2,1)S(1)} %slice.238), channel_id=1, source_target_pairs={{0,2},{1,3},{2,0},{3,1},{4,6},{5,7},{6,4},{7,5},{8,10},{9,11},{10,... | collective-permute-start | bytes 393224 | tf_op jit(solution)/shard_map/ppermute | solution.py:680
  91.1 26.5 %collective-permute-start.15 = (f32[8,128]{1,0:T(8,128)S(1)}, f32[8,128]{1,0:T(8,128)S(1)}, u32[]{:S(2)}, u32[]{:S(2)}) collective-permute-start(f32[8,128]{1,0:T(8,128)S(1)} %broadcast_in_dim.29), channel_id=1, source_target_pairs={{0,4},{4,0},{8,12},{12,8},{16,20},{20,16},{24,28},{28,24},{1,5},{5... | collective-permute-start | bytes 12296 | tf_op jit(solution)/shard_map/ppermute | solution.py:680
  118.7 30.3 %collective-permute-start.16 = (bf16[384,1024]{1,0:T(8,128)(2,1)S(1)}, bf16[384,1024]{1,0:T(8,128)(2,1)}, u32[]{:S(2)}, u32[]{:S(2)}) collective-permute-start(bf16[384,1024]{1,0:T(8,128)(2,1)S(1)} %pad_maximum_fusion.6.mine), channel_id=1, source_target_pairs={{0,4},{4,0},{8,12},{12,8},{16,20},{20,16},{24,28},{28,24},{1,5},{5... | collective-permute-start | bytes 2359304 | tf_op jit(solution)/shard_map/ppermute | solution.py:680
  120.2 28.6 %collective-permute-start.18 = (bf16[64,4096]{1,0:T(8,128)(2,1)S(1)}, bf16[64,4096]{1,0:T(8,128)(2,1)S(1)}, u32[]{:S(2)}, u32[]{:S(2)}) collective-permute-start(bf16[64,4096]{1,0:T(8,128)(2,1)S(1)} %slice.241), channel_id=1, source_target_pairs={{0,1},{1,0},{2,3},{3,2},{4,5},{5,4},{6,7},{7,6},{8,9},{9,8},{10,11... | collective-permute-start | bytes 1572872 | tf_op jit(solution)/shard_map/ppermute | solution.py:680
  121.7 27.0 %collective-permute-start.17 = (bf16[64,4096]{1,0:T(8,128)(2,1)S(1)}, bf16[64,4096]{1,0:T(8,128)(2,1)S(1)}, u32[]{:S(2)}, u32[]{:S(2)}) collective-permute-start(bf16[64,4096]{1,0:T(8,128)(2,1)S(1)} %slice.240), channel_id=1, source_target_pairs={{0,2},{1,3},{2,0},{3,1},{4,6},{5,7},{6,4},{7,5},{8,10},{9,11},{10,... | collective-permute-start | bytes 1572872 | tf_op jit(solution)/shard_map/ppermute | solution.py:680
  121.8 26.9 %collective-permute-start.19 = (f32[8,128]{1,0:T(8,128)S(1)}, f32[8,128]{1,0:T(8,128)S(1)}, u32[]{:S(2)}, u32[]{:S(2)}) collective-permute-start(f32[8,128]{1,0:T(8,128)S(1)} %add.173), channel_id=1, source_target_pairs={{0,8},{4,12},{8,0},{12,4},{16,24},{20,28},{24,16},{28,20},{1,9},{5... | collective-permute-start | bytes 12296 | tf_op jit(solution)/shard_map/ppermute | solution.py:680
  149.1 27.2 %collective-permute-start.20 = (bf16[384,4096]{1,0:T(8,128)(2,1)S(1)}, bf16[384,4096]{1,0:T(8,128)(2,1)}, u32[]{:S(2)}, u32[]{:S(2)}) collective-permute-start(bf16[384,4096]{1,0:T(8,128)(2,1)S(1)} %pad_maximum_fusion.mine), channel_id=1, source_target_pairs={{0,4},{4,0},{8,12},{12,8},{16,20},{20,16},{24,28},{28,24},{1,5},{5... | collective-permute-start | bytes 9437192 | tf_op jit(solution)/shard_map/ppermute | solution.py:680
  150.4 25.8 %collective-permute-start.21 = (bf16[512,1024]{1,0:T(8,128)(2,1)S(1)}, bf16[512,1024]{1,0:T(8,128)(2,1)S(1)}, u32[]{:S(2)}, u32[]{:S(2)}) collective-permute-start(bf16[512,1024]{1,0:T(8,128)(2,1)S(1)} %copy-done.13), channel_id=1, source_target_pairs={{0,1},{1,0},{2,3},{3,2},{4,5},{5,4},{6,7},{7,6},{8,9},{9,8},{10,11... | collective-permute-start | bytes 3145736 | tf_op jit(solution)/shard_map/ppermute | solution.py:680
  150.7 25.6 %collective-permute-start.22 = (bf16[512,1024]{1,0:T(8,128)(2,1)S(1)}, bf16[512,1024]{1,0:T(8,128)(2,1)S(1)}, u32[]{:S(2)}, u32[]{:S(2)}) collective-permute-start(bf16[512,1024]{1,0:T(8,128)(2,1)S(1)} %copy-done.13), channel_id=1, source_target_pairs={{0,2},{1,3},{2,0},{3,1},{4,6},{5,7},{6,4},{7,5},{8,10},{9,11},{10,... | collective-permute-start | bytes 3145736 | tf_op jit(solution)/shard_map/ppermute | solution.py:680
  153.2 14.0 %collective-permute-start.23 = (f32[8,128]{1,0:T(8,128)S(1)}, f32[8,128]{1,0:T(8,128)S(1)}, u32[]{:S(2)}, u32[]{:S(2)}) collective-permute-start(f32[8,128]{1,0:T(8,128)S(1)} %add.174), channel_id=1, source_target_pairs={{0,16},{4,20},{8,24},{12,28},{16,0},{20,4},{24,8},{28,12},{1,17},{... | collective-permute-start | bytes 12296 | tf_op jit(solution)/shard_map/ppermute | solution.py:680
  176.3 35.2 %collective-permute-start.25 = (bf16[256,1024]{1,0:T(8,128)(2,1)S(1)}, bf16[256,1024]{1,0:T(8,128)(2,1)S(1)}, u32[]{:S(2)}, u32[]{:S(2)}) collective-permute-start(bf16[256,1024]{1,0:T(8,128)(2,1)S(1)} %slice.243), channel_id=1, source_target_pairs={{0,1},{1,0},{2,3},{3,2},{4,5},{5,4},{6,7},{7,6},{8,9},{9,8},{10,11... | collective-permute-start | bytes 1572872 | tf_op jit(solution)/shard_map/ppermute | solution.py:680
  178.1 33.3 %collective-permute-start.24 = (bf16[256,1024]{1,0:T(8,128)(2,1)S(1)}, bf16[256,1024]{1,0:T(8,128)(2,1)S(1)}, u32[]{:S(2)}, u32[]{:S(2)}) collective-permute-start(bf16[256,1024]{1,0:T(8,128)(2,1)S(1)} %slice.242), channel_id=1, source_target_pairs={{0,2},{1,3},{2,0},{3,1},{4,6},{5,7},{6,4},{7,5},{8,10},{9,11},{10,... | collective-permute-start | bytes 1572872 | tf_op jit(solution)/shard_map/ppermute | solution.py:680
  213.0 8.7 %collective-permute-start.26 = (bf16[1536,1024]{1,0:T(8,128)(2,1)S(1)}, bf16[1536,1024]{1,0:T(8,128)(2,1)}, u32[]{:S(2)}, u32[]{:S(2)}) collective-permute-start(bf16[1536,1024]{1,0:T(8,128)(2,1)S(1)} %pad_maximum_fusion.1.mine), channel_id=1, source_target_pairs={{0,4},{4,0},{8,12},{12,8},{16,20},{20,16},{24,28},{28,24},{1,5},{5... | collective-permute-start | bytes 9437192 | tf_op jit(solution)/shard_map/ppermute | solution.py:680
  258.1 19.1 %collective-permute-start.29 = (bf16[4,512,1024]{2,1,0:T(8,128)(2,1)}, bf16[4,512,1024]{2,1,0:T(8,128)(2,1)}, u32[]{:S(2)}, u32[]{:S(2)}) collective-permute-start(bf16[4,512,1024]{2,1,0:T(8,128)(2,1)} %get-tuple-element.266), channel_id=1, source_target_pairs={{0,4},{4,0},{8,12},{12,8},{16,20},{20,16},{24,28},{28,24},{1,5},{5... | collective-permute-start | bytes 12582920 | tf_op jit(solution)/shard_map/ppermute | solution.py:680
  283.7 133.4 %reduce-scatter.9.cloned.1.call-start = ((), (), s32[]{:S(2)}) async-start(), calls=%async_computation.5 | async-start | bytes 5242880
  323.8 8.8 %collective-permute-start.30 = (bf16[4,128,4096]{2,1,0:T(8,128)(2,1)}, bf16[4,128,4096]{2,1,0:T(8,128)(2,1)}, u32[]{:S(2)}, u32[]{:S(2)}) collective-permute-start(bf16[4,128,4096]{2,1,0:T(8,128)(2,1)} %get-tuple-element.282), channel_id=1, source_target_pairs={{0,4},{4,0},{8,12},{12,8},{16,20},{20,16},{24,28},{28,24},{1,5},{5... | collective-permute-start | bytes 12582920 | tf_op jit(solution)/shard_map/ppermute | solution.py:680
  326.3 6.3 %collective-permute-start.31 = (f32[16,1024]{1,0:T(8,128)S(1)}, f32[16,1024]{1,0:T(8,128)S(1)}, u32[]{:S(2)}, u32[]{:S(2)}) collective-permute-start(f32[16,1024]{1,0:T(8,128)S(1)} %concatenate.73), channel_id=1, source_target_pairs={{0,4},{4,0},{8,12},{12,8},{16,20},{20,16},{24,28},{28,24},{1,5},{5... | collective-permute-start | bytes 196616 | tf_op jit(solution)/shard_map/ppermute | solution.py:680
  338.7 120.9 %all-reduce.6.cloned.1.call-start = ((), (), s32[]{:S(2)}) async-start(), calls=%async_computation.2 | async-start | bytes 2097152 | tf_op jit(solution)/shard_map/psum | solution.py:770
  370.5 31.8 %collective-permute-start.33 = (bf16[2,512,512]{2,1,0:T(8,128)(2,1)}, bf16[2,512,512]{2,1,0:T(8,128)(2,1)S(1)}, u32[]{:S(2)}, u32[]{:S(2)}) collective-permute-start(bf16[2,512,512]{2,1,0:T(8,128)(2,1)} %get-tuple-element.301), channel_id=1, source_target_pairs={{0,4},{4,8},{8,12},{12,16},{16,20},{20,24},{24,28},{1,5},{5,9},{9,... | collective-permute-start | bytes 3145736 | tf_op jit(solution)/shard_map/ppermute | solution.py:954
  375.0 27.3 %collective-permute-start.34 = (bf16[2,512,512]{2,1,0:T(8,128)(2,1)}, bf16[2,512,512]{2,1,0:T(8,128)(2,1)S(1)}, u32[]{:S(2)}, u32[]{:S(2)}) collective-permute-start(bf16[2,512,512]{2,1,0:T(8,128)(2,1)} %get-tuple-element.302), channel_id=1, source_target_pairs={{4,0},{8,4},{12,8},{16,12},{20,16},{24,20},{28,24},{5,1},{9,5},{13... | collective-permute-start | bytes 3145736 | tf_op jit(solution)/shard_map/ppermute | solution.py:954
  376.7 16.3 %collective-permute-start.32 = (f32[16,1024]{1,0:T(8,128)S(1)}, f32[16,1024]{1,0:T(8,128)S(1)}, u32[]{:S(2)}, u32[]{:S(2)}) collective-permute-start(f32[16,1024]{1,0:T(8,128)S(1)} %add.180), channel_id=1, source_target_pairs={{0,8},{4,12},{8,0},{12,4},{16,24},{20,28},{24,16},{28,20},{1,9},{5... | collective-permute-start | bytes 196616 | tf_op jit(solution)/shard_map/ppermute | solution.py:680
  380.4 137.8 %all-reduce.8.cloned.1.call-start = ((), (), s32[]{:S(2)}) async-start(), calls=%async_computation.3 | async-start | bytes 2097152 | tf_op jit(solution)/shard_map/psum | solution.py:770
  393.0 23.3 %collective-permute-start.36 = (f32[16,1024]{1,0:T(8,128)S(1)}, f32[16,1024]{1,0:T(8,128)S(1)}, u32[]{:S(2)}, u32[]{:S(2)}) collective-permute-start(f32[16,1024]{1,0:T(8,128)S(1)} %add.181), channel_id=1, source_target_pairs={{0,16},{4,20},{8,24},{12,28},{16,0},{20,4},{24,8},{28,12},{1,17},{... | collective-permute-start | bytes 196616 | tf_op jit(solution)/shard_map/ppermute | solution.py:680
  416.3 32.9 %collective-permute-start.35 = (bf16[4,128,2560]{2,1,0:T(8,128)(2,1)}, bf16[4,128,2560]{2,1,0:T(8,128)(2,1)S(1)}, u32[]{:S(2)}, u32[]{:S(2)}) collective-permute-start(bf16[4,128,2560]{2,1,0:T(8,128)(2,1)} %get-tuple-element.306), channel_id=1, source_target_pairs={{0,4},{4,0},{8,12},{12,8},{16,20},{20,16},{24,28},{28,24},{1,5},{5... | collective-permute-start | bytes 7864328 | tf_op jit(solution)/shard_map/ppermute | solution.py:680
  450.7 8.8 %collective-permute-start.37 = (f32[16,1024]{1,0:T(8,128)S(1)}, f32[16,1024]{1,0:T(8,128)S(1)}, u32[]{:S(2)}, u32[]{:S(2)}) collective-permute-start(f32[16,1024]{1,0:T(8,128)S(1)} %add.182), channel_id=1, source_target_pairs={{0,1},{1,0},{2,3},{3,2},{4,5},{5,4},{6,7},{7,6},{8,9},{9,8},{10,11... | collective-permute-start | bytes 196616 | tf_op jit(solution)/shard_map/ppermute | solution.py:680
  453.1 11.3 %collective-permute-start.39 = (bf16[2,512,512]{2,1,0:T(8,128)(2,1)}, bf16[2,512,512]{2,1,0:T(8,128)(2,1)}, u32[]{:S(2)}, u32[]{:S(2)}) collective-permute-start(bf16[2,512,512]{2,1,0:T(8,128)(2,1)} %get-tuple-element.320), channel_id=1, source_target_pairs={{0,4},{4,8},{8,12},{12,16},{16,20},{20,24},{24,28},{1,5},{5,9},{9,... | collective-permute-start | bytes 3145736 | tf_op jit(solution)/shard_map/ppermute | solution.py:954
  458.2 11.1 %collective-permute-start.40 = (bf16[2,512,512]{2,1,0:T(8,128)(2,1)}, bf16[2,512,512]{2,1,0:T(8,128)(2,1)}, u32[]{:S(2)}, u32[]{:S(2)}) collective-permute-start(bf16[2,512,512]{2,1,0:T(8,128)(2,1)} %get-tuple-element.321), channel_id=1, source_target_pairs={{4,0},{8,4},{12,8},{16,12},{20,16},{24,20},{28,24},{5,1},{9,5},{13... | collective-permute-start | bytes 3145736 | tf_op jit(solution)/shard_map/ppermute | solution.py:954
  459.6 19.3 %collective-permute-start.38 = (bf16[2,64,2560]{2,1,0:T(8,128)(2,1)S(1)}, bf16[2,64,2560]{2,1,0:T(8,128)(2,1)}, u32[]{:S(2)}, u32[]{:S(2)}) collective-permute-start(bf16[2,64,2560]{2,1,0:T(8,128)(2,1)S(1)} %slice_bitcast_fusion.4), channel_id=1, source_target_pairs={{0,1},{1,0},{2,3},{3,2},{4,5},{5,4},{6,7},{7,6},{8,9},{9,8},{10,11... | collective-permute-start | bytes 1966088 | tf_op jit(solution)/shard_map/ppermute | solution.py:680
  462.3 17.9 %collective-permute-start.41 = (bf16[2,64,2560]{2,1,0:T(8,128)(2,1)}, bf16[2,64,2560]{2,1,0:T(8,128)(2,1)}, u32[]{:S(2)}, u32[]{:S(2)}) collective-permute-start(bf16[2,64,2560]{2,1,0:T(8,128)(2,1)} %slice_bitcast_fusion.2), channel_id=1, source_target_pairs={{0,2},{1,3},{2,0},{3,1},{4,6},{5,7},{6,4},{7,5},{8,10},{9,11},{10,... | collective-permute-start | bytes 1966088 | tf_op jit(solution)/shard_map/ppermute | solution.py:680
  462.3 19.2 %collective-permute-start.42 = (f32[16,1024]{1,0:T(8,128)S(1)}, f32[16,1024]{1,0:T(8,128)S(1)}, u32[]{:S(2)}, u32[]{:S(2)}) collective-permute-start(f32[16,1024]{1,0:T(8,128)S(1)} %add.185), channel_id=1, source_target_pairs={{0,2},{1,3},{2,0},{3,1},{4,6},{5,7},{6,4},{7,5},{8,10},{9,11},{10,... | collective-permute-start | bytes 196616 | tf_op jit(solution)/shard_map/ppermute | solution.py:680
  464.4 54.0 %collective-permute-start.64 = (bf16[512,1024]{1,0:T(8,128)(2,1)}, bf16[512,1024]{1,0:T(8,128)(2,1)}, u32[]{:S(2)}, u32[]{:S(2)}) collective-permute-start(bf16[512,1024]{1,0:T(8,128)(2,1)} %all-reduce.6.cloned.1.call-done), channel_id=1, source_target_pairs={{0,4},{4,0},{8,12},{12,8},{16,20},{20,16},{24,28},{28,24},{1,5},{5... | collective-permute-start | bytes 3145736 | tf_op jit(solution)/shard_map/ppermute | solution.py:680
  482.3 42.4 %collective-permute-start.43 = (bf16[4,128,1536]{2,1,0:T(8,128)(2,1)}, bf16[4,128,1536]{2,1,0:T(8,128)(2,1)}, u32[]{:S(2)}, u32[]{:S(2)}) collective-permute-start(bf16[4,128,1536]{2,1,0:T(8,128)(2,1)} %get-tuple-element.332), channel_id=1, source_target_pairs={{0,4},{4,0},{8,12},{12,8},{16,20},{20,16},{24,28},{28,24},{1,5},{5... | collective-permute-start | bytes 4718600 | tf_op jit(solution)/shard_map/ppermute | solution.py:680
  495.9 26.3 %collective-permute-start.45 = (bf16[1,64,2560]{2,1,0:T(8,128)(2,1)S(1)}, bf16[1,64,2560]{2,1,0:T(8,128)(2,1)}, u32[]{:S(2)}, u32[]{:S(2)}) collective-permute-start(bf16[1,64,2560]{2,1,0:T(8,128)(2,1)S(1)} %slice_bitcast_fusion.10), channel_id=1, source_target_pairs={{0,1},{1,0},{2,3},{3,2},{4,5},{5,4},{6,7},{7,6},{8,9},{9,8},{10,11... | collective-permute-start | bytes 983048 | tf_op jit(solution)/shard_map/ppermute | solution.py:680
  498.8 24.5 %collective-permute-start.44 = (bf16[1,64,2560]{2,1,0:T(8,128)(2,1)S(1)}, bf16[1,64,2560]{2,1,0:T(8,128)(2,1)}, u32[]{:S(2)}, u32[]{:S(2)}) collective-permute-start(bf16[1,64,2560]{2,1,0:T(8,128)(2,1)S(1)} %slice_bitcast_fusion.12), channel_id=1, source_target_pairs={{0,2},{1,3},{2,0},{3,1},{4,6},{5,7},{6,4},{7,5},{8,10},{9,11},{10,... | collective-permute-start | bytes 983048 | tf_op jit(solution)/shard_map/ppermute | solution.py:680
  498.9 13.9 %collective-permute-start.46 = (f32[8,1024]{1,0:T(8,128)S(1)}, f32[8,1024]{1,0:T(8,128)S(1)}, u32[]{:S(2)}, u32[]{:S(2)}) collective-permute-start(f32[8,1024]{1,0:T(8,128)S(1)} %concatenate.75), channel_id=1, source_target_pairs={{0,4},{4,0},{8,12},{12,8},{16,20},{20,16},{24,28},{28,24},{1,5},{5... | collective-permute-start | bytes 98312 | tf_op jit(solution)/shard_map/ppermute | solution.py:680
  518.3 6.1 %collective-permute-start.63 = (bf16[128,4096]{1,0:T(8,128)(2,1)}, bf16[128,4096]{1,0:T(8,128)(2,1)S(1)}, u32[]{:S(2)}, u32[]{:S(2)}) collective-permute-start(bf16[128,4096]{1,0:T(8,128)(2,1)} %all-reduce.8.cloned.1.call-done), channel_id=1, source_target_pairs={{0,4},{4,0},{8,12},{12,8},{16,20},{20,16},{24,28},{28,24},{1,5},{5... | collective-permute-start | bytes 3145736 | tf_op jit(solution)/shard_map/ppermute | solution.py:680
  527.6 21.1 %collective-permute-start.47 = (bf16[2,64,1536]{2,1,0:T(8,128)(2,1)S(1)}, bf16[2,64,1536]{2,1,0:T(8,128)(2,1)S(1)}, u32[]{:S(2)}, u32[]{:S(2)}) collective-permute-start(bf16[2,64,1536]{2,1,0:T(8,128)(2,1)S(1)} %slice_bitcast_fusion.8), channel_id=1, source_target_pairs={{0,1},{1,0},{2,3},{3,2},{4,5},{5,4},{6,7},{7,6},{8,9},{9,8},{10,11... | collective-permute-start | bytes 1179656 | tf_op jit(solution)/shard_map/ppermute | solution.py:680
  529.2 19.6 %collective-permute-start.48 = (bf16[2,64,1536]{2,1,0:T(8,128)(2,1)S(1)}, bf16[2,64,1536]{2,1,0:T(8,128)(2,1)S(1)}, u32[]{:S(2)}, u32[]{:S(2)}) collective-permute-start(bf16[2,64,1536]{2,1,0:T(8,128)(2,1)S(1)} %slice_bitcast_fusion.6), channel_id=1, source_target_pairs={{0,2},{1,3},{2,0},{3,1},{4,6},{5,7},{6,4},{7,5},{8,10},{9,11},{10,... | collective-permute-start | bytes 1179656 | tf_op jit(solution)/shard_map/ppermute | solution.py:680
  530.7 18.2 %collective-permute-start.49 = (bf16[128,2560]{1,0:T(8,128)(2,1)S(1)}, bf16[128,2560]{1,0:T(8,128)(2,1)S(1)}, u32[]{:S(2)}, u32[]{:S(2)}) collective-permute-start(bf16[128,2560]{1,0:T(8,128)(2,1)S(1)} %pad_maximum_fusion.7), channel_id=1, source_target_pairs={{0,8},{4,12},{24,16},{28,20},{1,9},{5,13},{25,17},{29,21},{2,10},{... | collective-permute-start | bytes 1966088 | tf_op jit(solution)/shard_map/ppermute | solution.py:745
  534.1 14.6 %collective-permute-start.50 = (f32[8,1024]{1,0:T(8,128)S(1)}, f32[8,1024]{1,0:T(8,128)S(1)}, u32[]{:S(2)}, u32[]{:S(2)}) collective-permute-start(f32[8,1024]{1,0:T(8,128)S(1)} %add.193), channel_id=1, source_target_pairs={{0,8},{4,12},{8,0},{12,4},{16,24},{20,28},{24,16},{28,20},{1,9},{5... | collective-permute-start | bytes 98312 | tf_op jit(solution)/shard_map/ppermute | solution.py:680
  549.1 5.3 collective-permute-start.60
  552.1 6.9 %collective-permute-start.55 = (bf16[1,64,1536]{2,1,0:T(8,128)(2,1)S(1)}, bf16[1,64,1536]{2,1,0:T(8,128)(2,1)S(1)}, u32[]{:S(2)}, u32[]{:S(2)}) collective-permute-start(bf16[1,64,1536]{2,1,0:T(8,128)(2,1)S(1)} %slice_bitcast_fusion.14), channel_id=1, source_target_pairs={{0,1},{1,0},{2,3},{3,2},{4,5},{5,4},{6,7},{7,6},{8,9},{9,8},{10,11... | collective-permute-start | bytes 589832 | tf_op jit(solution)/shard_map/ppermute | solution.py:680
  554.3 4.1 collective-permute-start.61
  554.9 6.1 collective-permute-start.54
  555.5 15.5 %collective-permute-start.51 = (bf16[128,2560]{1,0:T(8,128)(2,1)S(1)}, bf16[128,2560]{1,0:T(8,128)(2,1)S(1)}, u32[]{:S(2)}, u32[]{:S(2)}) collective-permute-start(bf16[128,2560]{1,0:T(8,128)(2,1)S(1)} %add_convert_fusion.7), channel_id=1, source_target_pairs={{8,16},{12,20},{16,8},{20,12},{9,17},{13,21},{17,9},{21,13},{10,18... | collective-permute-start | bytes 1966088 | tf_op jit(solution)/shard_map/ppermute | solution.py:745
  558.5 9.0 %collective-permute-start.62 = (f32[8,1024]{1,0:T(8,128)S(1)}, f32[8,1024]{1,0:T(8,128)S(1)}, u32[]{:S(2)}, u32[]{:S(2)}) collective-permute-start(f32[8,1024]{1,0:T(8,128)S(1)} %add.204), channel_id=1, source_target_pairs={{0,2},{1,3},{2,0},{3,1},{4,6},{5,7},{6,4},{7,5},{8,10},{9,11},{10,... | collective-permute-start | bytes 98312 | tf_op jit(solution)/shard_map/ppermute | solution.py:680
  561.1 9.1 %collective-permute-start.56 = (bf16[128,1536]{1,0:T(8,128)(2,1)S(1)}, bf16[128,1536]{1,0:T(8,128)(2,1)S(1)}, u32[]{:S(2)}, u32[]{:S(2)}) collective-permute-start(bf16[128,1536]{1,0:T(8,128)(2,1)S(1)} %pad_maximum_fusion.9), channel_id=1, source_target_pairs={{0,8},{4,12},{24,16},{28,20},{1,9},{5,13},{25,17},{29,21},{2,10},{... | collective-permute-start | bytes 1179656 | tf_op jit(solution)/shard_map/ppermute | solution.py:745
  571.2 20.4 %collective-permute-start.52 = (bf16[128,2560]{1,0:T(8,128)(2,1)S(1)}, bf16[128,2560]{1,0:T(8,128)(2,1)S(1)}, u32[]{:S(2)}, u32[]{:S(2)}) collective-permute-start(bf16[128,2560]{1,0:T(8,128)(2,1)S(1)} %fusion.2), channel_id=1, source_target_pairs={{8,0},{12,4},{16,24},{20,28},{9,1},{13,5},{17,25},{21,29},{10,2},{... | collective-permute-start | bytes 1966088 | tf_op jit(solution)/shard_map/ppermute | solution.py:745
  572.7 23.2 %collective-permute-start.58 = (bf16[128,1536]{1,0:T(8,128)(2,1)S(1)}, bf16[128,1536]{1,0:T(8,128)(2,1)S(1)}, u32[]{:S(2)}, u32[]{:S(2)}) collective-permute-start(bf16[128,1536]{1,0:T(8,128)(2,1)S(1)} %fusion.7), channel_id=1, source_target_pairs={{8,0},{12,4},{16,24},{20,28},{9,1},{13,5},{17,25},{21,29},{10,2},{... | collective-permute-start | bytes 1179656 | tf_op jit(solution)/shard_map/ppermute | solution.py:745
  (27 other events, 287.0 us)
Sparse Core Ops, SparseCore 0:
  283.8 53.9 reduce-scatter.6
  341.0 52.6 reduce-scatter.8
  396.1 51.7 all-reduce.5
  464.5 53.7 all-reduce.7

commit v3 on v2

v3 whole, which is shorter than its diff:
```python
import functools

import jax
import jax.numpy as jnp
from jax import lax
from jax.experimental import pallas as pl
from jax.experimental.pallas import tpu as pltpu
from jax.sharding import PartitionSpec as P

D = 1024
FF = 4096
HEAD = 64
DOC_MAX = 512
TILE = 256
RIM = DOC_MAX // TILE
NEG = -1e30
NORM_EPS = 1e-05
VMEM_BYTES = 56 * 2**20
bf16 = jnp.bfloat16
f32 = jnp.float32


def nn(a, b):
    return jnp.dot(a, b, preferred_element_type=f32)


def nt(a, b):
    return lax.dot_general(a, b, (((1,), (1,)), ((), ())), preferred_element_type=f32)


def tn(a, b):
    return lax.dot_general(a, b, (((0,), (0,)), ((), ())), preferred_element_type=f32)


def params():
    return pltpu.CompilerParams(vmem_limit_bytes=VMEM_BYTES)


def cost(flops, bytes_accessed):
    return pl.CostEstimate(flops=int(flops), bytes_accessed=int(bytes_accessed), transcendentals=0)


def sds(shape, dtype):
    return jax.ShapeDtypeStruct(shape, dtype)


def weight_copies(where_ref, pieces, full, out, sem):
    shard, mine, other = pieces[0], pieces[1 : len(pieces) // 2 + 1], pieces[len(pieces) // 2 + 1 :]
    f, parity = where_ref[0], where_ref[1]
    rows = shard.shape[0]
    half, quarter = rows // 2, rows // 4
    copies = []

    def add(source, begin):
        begin = pl.multiple_of(begin, 16)
        copies.append(pltpu.make_async_copy(source, full.at[pl.ds(begin, source.shape[0])], sem.at[len(copies)]))

    add(shard, f * rows)
    at = 0
    for r in range(1, full.shape[0] // rows):
        base = jnp.bitwise_xor(f, r) * rows
        for offset in (0,) if r & (r - 1) == 0 else (0, quarter):
            add(mine[at], base + offset + parity * half)
            add(other[at], base + offset + (1 - parity) * half)
            at += 1
    return copies, pltpu.make_async_copy(full, out, sem.at[len(copies)])


def join_weight(where_ref, pieces, full, out, sem):
    copies, save = weight_copies(where_ref, pieces, full, out, sem)

    @pl.when(pl.program_id(0) == 0)
    def _():
        for copy in copies:
            copy.start()
        for copy in copies:
            copy.wait()
        save.start()

    @pl.when(pl.program_id(0) == pl.num_programs(0) - 1)
    def _():
        save.wait()


def weight_specs(pieces):
    return [pl.BlockSpec(memory_space=pltpu.SMEM)] + [pl.BlockSpec(memory_space=pl.ANY)] * len(pieces)


def weight_scratch(rows, columns):
    return [pltpu.VMEM((rows, columns), bf16), pltpu.SemaphoreType.DMA((64,))]


def pack_kernel(where_ref, q_ref, k_ref, v_ref, shard_ref, own_ref):
    half = own_ref.shape[0]
    first = where_ref[1] == 0
    for side in (0, 1):
        for which, ref in enumerate((q_ref, k_ref, v_ref)):
            columns = qkv_columns(which, side)
            block = ref[:, side * D // 2 : (side + 1) * D // 2]
            shard_ref[:, columns] = block
            own_ref[:, columns] = jnp.where(first, block[:half], block[half:])


def pack_shards(where, q, k, v):
    part = q.shape[0]
    return pl.pallas_call(
        pack_kernel,
        in_specs=[pl.BlockSpec(memory_space=pltpu.SMEM)] + [pl.BlockSpec(memory_space=pltpu.VMEM)] * 3,
        out_specs=[pl.BlockSpec(memory_space=pltpu.VMEM)] * 2,
        out_shape=[sds((part, 3 * D), bf16), sds((part // 2, 3 * D), bf16)],
        compiler_params=params(),
        cost_estimate=cost(0, 4 * 2**20),
        name="pack_shards",
    )(where, q, k, v)


def unpack_kernel(where_ref, packed_ref, *outs):
    packed = packed_ref[...].astype(f32)
    shards = packed.shape[0]
    at = 0
    for out in outs:
        part = out.shape[1] // shards
        for r in range(shards):
            begin = pl.multiple_of(jnp.bitwise_xor(where_ref[0], r) * part, part)
            out[:, pl.ds(begin, part)] = packed[r : r + 1, at : at + part]
        at += part


def unpack_vectors(where, packed):
    return pl.pallas_call(
        unpack_kernel,
        in_specs=[pl.BlockSpec(memory_space=pltpu.SMEM), pl.BlockSpec(memory_space=pltpu.VMEM)],
        out_specs=[pl.BlockSpec(memory_space=pltpu.VMEM)] * 9,
        out_shape=[sds((1, D), f32)] * 8 + [sds((1, FF), f32)],
        compiler_params=params(),
        cost_estimate=cost(0, 2**17),
        name="unpack_vectors",
    )(where, packed)


def qkv_columns(which, side):
    begin = (3 * side + which) * D // 2
    return slice(begin, begin + D // 2)


def qkv_kernel(count, where_ref, *refs):
    pieces, refs = refs[:count], refs[count:]
    before_ref, x_ref, behind_ref, bq_ref, bv_ref, q_ref, k_ref, v_ref, kt_ref, vt_ref, full_ref, w_ref, sem = refs
    join_weight(where_ref, pieces, w_ref, full_ref, sem)
    i = pl.program_id(0)
    x = jnp.where(i == 0, before_ref[...], jnp.where(i == pl.num_programs(0) - 1, behind_ref[...], x_ref[...]))

    for s in (0, 1):
        half = slice(s * D // 2, (s + 1) * D // 2)
        query = (nn(x, w_ref[:, qkv_columns(0, s)]) + bq_ref[:, half]).astype(bf16)
        q_ref[:, half] = query * jnp.asarray(HEAD**-0.5, bf16)
        keys = nn(x, w_ref[:, qkv_columns(1, s)]).astype(bf16)
        k_ref[:, half] = keys
        kt_ref[half, :] = jnp.transpose(keys)
        values = (nn(x, w_ref[:, qkv_columns(2, s)]) + bv_ref[:, half]).astype(bf16)
        v_ref[:, half] = values
        vt_ref[half, :] = jnp.transpose(values)


def project_qkv(where, pieces, before, tokens, behind, bq, bv):
    rows = tokens.shape[0]
    span = rows + 2 * DOC_MAX
    rim = pl.BlockSpec((512, D), lambda i: (0, 0))
    inside = pl.BlockSpec((512, D), lambda i: (jnp.clip(i - 1, 0, rows // 512 - 1), 0))
    row = pl.BlockSpec((1, D), lambda i: (0, 0))
    tall = pl.BlockSpec((512, D), lambda i: (i, 0))
    wide = pl.BlockSpec((D, 512), lambda i: (0, i))
    return pl.pallas_call(
        functools.partial(qkv_kernel, len(pieces)),
        grid=(span // 512,),
        in_specs=weight_specs(pieces) + [rim, inside, rim, row, row],
        out_specs=[
            tall,
            tall,
            tall,
            wide,
            wide,
            pl.BlockSpec(memory_space=pl.ANY),
        ],
        scratch_shapes=weight_scratch(D, 3 * D),
        out_shape=[
            sds((span, D), bf16),
            sds((span, D), bf16),
            sds((span, D), bf16),
            sds((D, span), bf16),
            sds((D, span), bf16),
            sds((D, 3 * D), bf16),
        ],
        compiler_params=params(),
        cost_estimate=cost(2 * D * D * (rows + 2 * span), 30 * 2**20),
        name="project_qkv",
    )(where, *pieces, before, tokens, behind, bq, bv)


def stack_rows(block, stack):
    lanes = lax.broadcasted_iota(jnp.int32, block.shape, 1)
    for h in range(4):
        stack[h * TILE : (h + 1) * TILE, :] = jnp.where(lanes // HEAD == h, block, jnp.zeros_like(block))


def stack_columns(turned, stack):
    for h in range(4):
        heads = slice(h * HEAD, (h + 1) * HEAD)
        stack[heads, h * TILE : (h + 1) * TILE] = turned[heads, :]


def attn_fwd_kernel(lo_ref, hi_ref, q_ref, k_ref, vt_ref, idq_ref, idk_ref, *refs):
    out_ref, lse_ref, qs, acc, top, tot = refs[-6:]
    quads = qs.shape[0]
    t = pl.program_id(0)

    @pl.when(t == 0)
    def _():
        qs[...] = jnp.zeros_like(qs)

    turned = jnp.transpose(q_ref[...])
    for g in range(quads):
        stack_columns(turned[g * 256 : (g + 1) * 256], qs.at[g])
    acc[...] = jnp.zeros_like(acc)
    top[...] = jnp.full_like(top, NEG)
    tot[...] = jnp.zeros_like(tot)

    def step(kt, carry):
        rows = pl.ds(pl.multiple_of(kt * TILE, TILE), TILE)
        bias = jnp.where(idk_ref[rows, :] == idq_ref[0], 0.0, NEG)
        scores = [nn(k_ref[rows, g * 256 : (g + 1) * 256], qs[g]) for g in range(quads)]
        for g in range(quads):
            vt_tile = vt_ref[g * 256 : (g + 1) * 256, rows]
            for h in range(4):
                heads = slice(h * HEAD, (h + 1) * HEAD)
                own = scores[g][:, h * TILE : (h + 1) * TILE] + bias
                old = top[g, h : h + 1, :]
                new = jnp.maximum(old, jnp.max(own, axis=0, keepdims=True))
                top[g, h : h + 1, :] = new
                p = jnp.exp(own - new)
                fade = jnp.exp(old - new)
                tot[g, h : h + 1, :] = tot[g, h : h + 1, :] * fade + jnp.sum(p, axis=0, keepdims=True)
                acc[g, heads, :] = acc[g, heads, :] * fade + nn(vt_tile[heads, :], p.astype(bf16))
        return carry

    lax.fori_loop(lo_ref[t + RIM], hi_ref[t + RIM], step, 0)
    for g in range(quads):
        total = tot[g]
        inverse = 1.0 / total
        for h in range(4):
            heads = slice(h * HEAD, (h + 1) * HEAD)
            acc[g, heads, :] = acc[g, heads, :] * inverse[h : h + 1, :]
        out_ref[:, g * 256 : (g + 1) * 256] = jnp.transpose(acc[g]).astype(bf16)
        lse_ref[g] = top[g] + jnp.log(total)


def attn_fwd(lo, hi, q, k_near, vt_near, idq_rows, idk_col, side, quads, so_far=()):
    span, wide = k_near.shape[0], quads * 256
    rows = span - 2 * DOC_MAX
    return pl.pallas_call(
        attn_fwd_kernel,
        grid_spec=pltpu.PrefetchScalarGridSpec(
            num_scalar_prefetch=2,
            grid=(rows // TILE,),
            in_specs=[
                pl.BlockSpec((TILE, wide), lambda t, *_: (t + RIM, side)),
                pl.BlockSpec((span, wide), lambda t, *_: (0, side)),
                pl.BlockSpec((wide, span), lambda t, *_: (side, 0)),
                pl.BlockSpec((1, 1, TILE), lambda t, *_: (t + RIM, 0, 0)),
                pl.BlockSpec((span, 1), lambda t, *_: (0, 0)),
            ]
            + [pl.BlockSpec(memory_space=pl.ANY)] * len(so_far),
            out_specs=[
                pl.BlockSpec((TILE, wide), lambda t, *_: (t, side)),
                pl.BlockSpec((quads, 8, TILE), lambda t, *_: (side, 0, t)),
            ],
            scratch_shapes=[
                pltpu.VMEM((quads, 256, 4 * TILE), bf16),
                pltpu.VMEM((quads, 256, TILE), f32),
                pltpu.VMEM((quads, 8, TILE), f32),
                pltpu.VMEM((quads, 8, TILE), f32),
            ],
        ),
        out_shape=[sds((rows, D), bf16), sds((D // 256, 8, rows), f32)],
        input_output_aliases={7 + i: i for i in range(len(so_far))},
        compiler_params=params(),
        cost_estimate=cost(quads * 10**10, 2**21),
        name="attn_forward",
    )(lo, hi, q, k_near, vt_near, idq_rows, idk_col, *so_far)


def attn_bwd_kernel(
    lo_ref, hi_ref, q_ref, before_ref, do_ref, behind_ref, k_ref, kt_ref, v_ref, stats_ref, idq_ref, idk_ref,
    dq_ref, joined_ref, qs, dos, qst, dost, dk_acc, dv_acc, dq_acc,
):
    t = pl.program_id(1)
    low, high = lo_ref[t], hi_ref[t]
    end = pl.num_programs(1) - RIM
    own_low, own_high = jnp.maximum(low, RIM), jnp.minimum(high, end)

    @pl.when((t == 0) & (pl.program_id(0) == 0))
    def _():
        qst[...] = jnp.zeros_like(qst)
        dost[...] = jnp.zeros_like(dost)

    @pl.when(t == 0)
    def _():
        dk_acc[...] = jnp.zeros_like(dk_acc)
        dv_acc[...] = jnp.zeros_like(dv_acc)

    @pl.when(low < high)
    def _():
        q = q_ref[...]
        do = jnp.where(t < RIM, before_ref[...], jnp.where(t >= end, behind_ref[...], do_ref[...]))
        stack_rows(q, qs)
        stack_rows(do, dos)
        stack_columns(jnp.transpose(q), qst)
        stack_columns(jnp.transpose(do), dost)
        lse_row, delta_row = (
            jnp.concatenate([stats_ref[s, 0, h : h + 1] for h in range(4)], axis=1) for s in (0, 1)
        )
        dq_acc[...] = jnp.zeros_like(dq_acc)

        def step(own, kt, carry):
            rows = pl.ds(pl.multiple_of(kt * TILE, TILE), TILE)
            bias = jnp.where(idk_ref[rows, :] == idq_ref[0], 0.0, NEG)
            s = nn(k_ref[rows, :], qst[...])
            dp = nn(v_ref[rows, :], dost[...])
            p = jnp.exp(s + jnp.concatenate([bias] * 4, axis=1) - lse_row)
            ds = (p * (dp - delta_row)).astype(bf16)
            if own:
                inside = pl.ds(pl.multiple_of((kt - RIM) * TILE, TILE), TILE)
                dv_acc[inside, :] += nn(p.astype(bf16), dos[...])
                dk_acc[inside, :] += nn(ds, qs[...])
            kt_tile = kt_ref[:, rows]
            for h in range(4):
                heads = slice(h * HEAD, (h + 1) * HEAD)
                dq_acc[heads, :] += nn(kt_tile[heads, :], ds[:, h * TILE : (h + 1) * TILE])
            return carry

        lax.fori_loop(low, jnp.minimum(high, RIM), functools.partial(step, False), 0)
        lax.fori_loop(own_low, own_high, functools.partial(step, True), 0)
        lax.fori_loop(jnp.maximum(low, end), high, functools.partial(step, False), 0)

        @pl.when((t >= RIM) & (t < end))
        def _():
            dq_ref[...] = (jnp.transpose(dq_acc[...]) * (HEAD**-0.5)).astype(bf16)

    @pl.when(t == pl.num_programs(1) - 1)
    def _():
        joined_ref[0] = dk_acc[...].astype(bf16)
        joined_ref[1] = dv_acc[...].astype(bf16)


def attn_bwd(lo, hi, q_near, before, do, behind, k_near, kt_near, v_near, stats, idq_rows, idk_col, side, quads):
    rows, span = do.shape[0], k_near.shape[0]
    tiles, first = rows // TILE, side * quads
    near = pl.BlockSpec((span, 256), lambda g, t, *_: (0, g + first))
    return pl.pallas_call(
        attn_bwd_kernel,
        grid_spec=pltpu.PrefetchScalarGridSpec(
            num_scalar_prefetch=2,
            grid=(quads, span // TILE),
            in_specs=[
                pl.BlockSpec((TILE, 256), lambda g, t, *_: (t, g + first)),
                pl.BlockSpec((TILE, 256), lambda g, t, *_: (jnp.clip(t, 0, RIM - 1), g + first)),
                pl.BlockSpec((TILE, 256), lambda g, t, *_: (jnp.clip(t - RIM, 0, tiles - 1), g + first)),
                pl.BlockSpec((TILE, 256), lambda g, t, *_: (jnp.clip(t - RIM - tiles, 0, RIM - 1), g + first)),
                near,
                pl.BlockSpec((256, span), lambda g, t, *_: (g + first, 0)),
                near,
                pl.BlockSpec((2, 1, 8, TILE), lambda g, t, *_: (0, g + first, 0, t)),
                pl.BlockSpec((1, 1, TILE), lambda g, t, *_: (t, 0, 0)),
                pl.BlockSpec((span, 1), lambda g, t, *_: (0, 0)),
            ],
            out_specs=[
                pl.BlockSpec((TILE, 256), lambda g, t, *_: (jnp.clip(t - RIM, 0, tiles - 1), g)),
                pl.BlockSpec((2, rows, 256), lambda g, t, *_: (0, 0, g)),
            ],
            scratch_shapes=[
                pltpu.VMEM((4 * TILE, 256), bf16),
                pltpu.VMEM((4 * TILE, 256), bf16),
                pltpu.VMEM((256, 4 * TILE), bf16),
                pltpu.VMEM((256, 4 * TILE), bf16),
                pltpu.VMEM((rows, 256), f32),
                pltpu.VMEM((rows, 256), f32),
                pltpu.VMEM((256, TILE), f32),
            ],
        ),
        out_shape=[sds((rows, quads * 256), bf16), sds((2, rows, quads * 256), bf16)],
        compiler_params=params(),
        cost_estimate=cost(quads * 15 * 10**9, 2**22),
        name="attn_backward",
    )(lo, hi, q_near, before, do, behind, k_near, kt_near, v_near, stats, idq_rows, idk_col)


def norm_stats(hidden):
    center = hidden - jnp.mean(hidden, axis=1, keepdims=True)
    rate = lax.rsqrt(jnp.mean(center * center, axis=1, keepdims=True) + NORM_EPS)
    return center * rate, rate


def norm_back(grad, unit, rate):
    return rate * (
        grad - jnp.mean(grad, axis=1, keepdims=True) - unit * jnp.mean(grad * unit, axis=1, keepdims=True)
    )


def mix_kernel(count, where_ref, *refs):
    pieces, refs = refs[:count], refs[count:]
    c_ref, b_ref, x_ref, g_ref, s_ref, normed_ref, low_ref, rate_ref, full_ref, w_ref, sem = refs
    join_weight(where_ref, pieces, w_ref, full_ref, sem)
    hidden = x_ref[...].astype(f32) + (nn(c_ref[...], w_ref[...]) + b_ref[...])
    unit, rate = norm_stats(hidden)
    normed = unit * g_ref[...] + s_ref[...]
    normed_ref[...] = normed
    low_ref[...] = normed.astype(bf16)
    rate_ref[...] = rate


def mix_and_norm(where, pieces, context, b, tokens, gain, shift):
    rows = tokens.shape[0]
    tile = pl.BlockSpec((TILE, D), lambda i: (i, 0))
    row = pl.BlockSpec((1, D), lambda i: (0, 0))
    return pl.pallas_call(
        functools.partial(mix_kernel, len(pieces)),
        grid=(rows // TILE,),
        in_specs=weight_specs(pieces) + [tile, row, tile, row, row],
        out_specs=[tile, tile, pl.BlockSpec((TILE, 1), lambda i: (i, 0)), pl.BlockSpec(memory_space=pl.ANY)],
        out_shape=[sds((rows, D), f32), sds((rows, D), bf16), sds((rows, 1), f32), sds((D, D), bf16)],
        scratch_shapes=weight_scratch(D, D),
        compiler_params=params(),
        cost_estimate=cost(2 * D * D * rows, 14 * 2**20),
        name="mix_and_norm",
    )(where, *pieces, context, b, tokens, gain, shift)


def gelu_parts(u):
    t = 1.0 / (1.0 + (0.3275911 * 0.7071067811865476) * jnp.abs(u))
    poly = t * (0.254829592 + t * (-0.284496736 + t * (1.421413741 + t * (-1.453152027 + t * 1.061405429))))
    bell = jnp.exp(-0.5 * u * u)
    tail = 0.5 * poly * bell
    share = jnp.where(u >= 0, 1.0 - tail, tail)
    return u * share, share + u * bell * 0.3989422804014327


def inner_kernel(count, where_ref, *refs):
    pieces, (x_ref, b_ref, act_ref, slope_ref, full_ref, w_ref, sem) = refs[:count], refs[count:]
    join_weight(where_ref, pieces, w_ref, full_ref, sem)
    wide = act_ref.shape[1]
    columns = pl.ds(pl.multiple_of(pl.program_id(0) * wide, wide), wide)
    weight = w_ref[:, columns]
    parts = [slice(i, i + 128) for i in range(0, x_ref.shape[0], 128)]
    ahead = nn(x_ref[parts[0], :], weight)
    for i, rows in enumerate(parts):
        pre = ahead
        if i + 1 < len(parts):
            ahead = nn(x_ref[parts[i + 1], :], weight)
        act, slope = gelu_parts(pre + b_ref[...])
        act_ref[rows, :] = act.astype(bf16)
        slope_ref[rows, :] = slope.astype(bf16)


def inner_forward(where, pieces, x, b):
    rows, wide = x.shape[0], 512
    block = pl.BlockSpec((rows, wide), lambda j: (0, j))
    return pl.pallas_call(
        functools.partial(inner_kernel, len(pieces)),
        grid=(FF // wide,),
        in_specs=weight_specs(pieces)
        + [pl.BlockSpec((rows, D), lambda j: (0, 0)), pl.BlockSpec((1, wide), lambda j: (0, j))],
        out_specs=[block, block, pl.BlockSpec(memory_space=pl.ANY)],
        out_shape=[sds((rows, FF), bf16), sds((rows, FF), bf16), sds((D, FF), bf16)],
        scratch_shapes=weight_scratch(D, FF),
        compiler_params=params(),
        cost_estimate=cost(2 * D * FF * rows, 26 * 2**20),
        name="inner_forward",
    )(where, *pieces, x, b)


def outer_kernel(count, where_ref, *refs):
    pieces, refs = refs[:count], refs[count:]
    coef_ref, act_ref, b_ref, normed_ref, g_ref, s_ref, teach_ref, cot_ref, flag_ref = refs[:9]
    out_ref, dsum_ref, dlow_ref, sums_ref, full_ref, w_ref, sem = refs[9:]
    join_weight(where_ref, pieces, w_ref, full_ref, sem)
    hidden = normed_ref[...] + (nn(act_ref[...], w_ref[...]) + b_ref[...])
    unit, rate = norm_stats(hidden)
    gain = g_ref[...]
    final = unit * gain + s_ref[...]
    out_ref[...] = final.astype(bf16)
    error = final - teach_ref[...].astype(f32)
    marked = flag_ref[...] * error
    grad = cot_ref[...].astype(f32) + coef_ref[0] * marked
    dsum = norm_back(grad * gain, unit, rate)
    dsum_ref[...] = dsum
    low = dsum.astype(bf16)
    dlow_ref[...] = low

    @pl.when(pl.program_id(0) == 0)
    def _():
        sums_ref[...] = jnp.zeros_like(sums_ref)

    sums_ref[0:1, :] += jnp.sum(grad * unit, axis=0, keepdims=True)
    sums_ref[1:2, :] += jnp.sum(grad, axis=0, keepdims=True)
    sums_ref[2:3, :] += jnp.sum(low.astype(f32), axis=0, keepdims=True)
    sums_ref[3:4, :] += jnp.sum(marked * error, axis=0, keepdims=True)


def outer_forward(where, pieces, coef, act, b, normed, gain, shift, teacher, cotangent, flags):
    rows = act.shape[0]
    tile = pl.BlockSpec((TILE, D), lambda i: (i, 0))
    row = pl.BlockSpec((1, D), lambda i: (0, 0))
    return pl.pallas_call(
        functools.partial(outer_kernel, len(pieces)),
        grid=(rows // TILE,),
        in_specs=weight_specs(pieces)
        + [
            pl.BlockSpec(memory_space=pltpu.SMEM),
            pl.BlockSpec((TILE, FF), lambda i: (i, 0)),
            row, tile, row, row, tile, tile,
            pl.BlockSpec((TILE, 1), lambda i: (i, 0)),
        ],
        out_specs=[
            tile, tile, tile, pl.BlockSpec((8, D), lambda i: (0, 0)), pl.BlockSpec(memory_space=pl.ANY),
        ],
        out_shape=[
            sds((rows, D), bf16), sds((rows, D), f32), sds((rows, D), bf16), sds((8, D), f32), sds((FF, D), bf16),
        ],
        scratch_shapes=weight_scratch(FF, D),
        compiler_params=params(),
        cost_estimate=cost(2 * D * FF * rows, 32 * 2**20),
        name="outer_forward",
    )(where, *pieces, coef, act, b, normed, gain, shift, teacher, cotangent, flags)


def put_halves(keep_ref, send_ref, first, begin, grad):
    half = keep_ref.shape[1]
    columns = slice(begin, begin + grad.shape[1])
    low, high = grad[:half], grad[half:]
    keep_ref[0, :, columns] = jnp.where(first, low, high).astype(bf16)
    send_ref[0, :, columns] = jnp.where(first, high, low).astype(bf16)


def gram_kernel(counts, order_ref, *refs):
    operands, keep_ref, send_ref = list(refs[:-2]), refs[-2], refs[-1]
    first = order_ref[pl.num_programs(0)] == 0
    at = 0
    for count in counts:
        left = operands.pop(0)[...]
        for _ in range(count):
            right_ref = operands.pop(0)
            put_halves(keep_ref, send_ref, first, at, tn(left, right_ref[...]))
            at += right_ref.shape[1]


def gram(order, shards, *groups):
    tokens, height = groups[0][0].shape
    part = height // shards
    columns = sum(right.shape[1] for group in groups for right in group[1:])
    out = pl.BlockSpec((1, part // 2, columns), lambda r, order_ref: (r, 0, 0))
    in_specs = []
    for group in groups:
        in_specs.append(pl.BlockSpec((tokens, part), lambda r, order_ref: (0, order_ref[r])))
        in_specs += [pl.BlockSpec((tokens, right.shape[1]), lambda r, order_ref: (0, 0)) for right in group[1:]]
    return pl.pallas_call(
        functools.partial(gram_kernel, [len(group) - 1 for group in groups]),
        grid_spec=pltpu.PrefetchScalarGridSpec(
            num_scalar_prefetch=1, grid=(shards,), in_specs=in_specs, out_specs=[out, out]
        ),
        out_shape=[sds((shards, part // 2, columns), bf16)] * 2,
        compiler_params=params(),
        cost_estimate=cost(2 * tokens * height * columns, 2 * (tokens * (height + columns) + height * columns)),
        name="gram",
    )(order, *[operand for group in groups for operand in group])


def feed_back_columns(db_ref, wo_ref, slope_ref, wi_ref, dpre_ref, bias_ref, total):
    ones = jnp.ones((8, TILE), bf16)
    bias = jnp.zeros(bias_ref.shape, f32)
    for i in range(db_ref.shape[0] // TILE):
        rows = slice(i * TILE, (i + 1) * TILE)
        pre = (nt(db_ref[rows, :], wo_ref[...]) * slope_ref[rows, :].astype(f32)).astype(bf16)
        dpre_ref[rows, :] = pre
        bias += nn(ones, pre)
        total[rows, :] += nt(pre, wi_ref[...])
    bias_ref[...] = bias


def feed_back_first_kernel(tie_ref, db_ref, wo_ref, slope_ref, wi_ref, dsum_ref, dpre_ref, bias_ref, total):
    @pl.when(pl.program_id(0) == 0)
    def _():
        total[...] = dsum_ref[...]

    feed_back_columns(db_ref, wo_ref, slope_ref, wi_ref, dpre_ref, bias_ref, total)


def feed_back_last_kernel(
    tie_ref, db_ref, wo_ref, slope_ref, wi_ref, dsum_ref, normed_ref, rate_ref, g_ref, s_ref,
    dpre_ref, bias_ref, done_ref, dattn_ref, sums_ref, total,
):
    @pl.when(pl.program_id(0) == 0)
    def _():
        total[...] = dsum_ref[...]

    feed_back_columns(db_ref, wo_ref, slope_ref, wi_ref, dpre_ref, bias_ref, total)

    @pl.when(pl.program_id(0) == pl.num_programs(0) - 1)
    def _():
        gain = g_ref[...]
        sums_ref[...] = jnp.zeros_like(sums_ref)
        for i in range(db_ref.shape[0] // TILE):
            rows = slice(i * TILE, (i + 1) * TILE)
            grad = total[rows, :]
            unit = (normed_ref[rows, :] - s_ref[...]) / gain
            done = norm_back(grad * gain, unit, rate_ref[rows, :])
            done_ref[rows, :] = done
            low = done.astype(bf16)
            dattn_ref[rows, :] = low
            sums_ref[0:1, :] += jnp.sum(grad * unit, axis=0, keepdims=True)
            sums_ref[1:2, :] += jnp.sum(grad, axis=0, keepdims=True)
            sums_ref[2:3, :] += jnp.sum(low.astype(f32), axis=0, keepdims=True)


def feed_back(tie, side, d_branch, w_outer, slope, w_inner, so_far, norm=None):
    rows, wide = d_branch.shape[0], 512
    steps = FF // wide // 2
    begin = side * steps
    whole = pl.BlockSpec((rows, D), lambda j: (0, 0))
    row = pl.BlockSpec((1, D), lambda j: (0, 0))
    in_specs = [
        pl.BlockSpec(memory_space=pltpu.SMEM),
        whole,
        pl.BlockSpec((wide, D), lambda j: (j + begin, 0)),
        pl.BlockSpec((rows, wide), lambda j: (0, j + begin)),
        pl.BlockSpec((D, wide), lambda j: (0, j + begin)),
        whole,
    ]
    out_specs = [pl.BlockSpec((rows, wide), lambda j: (0, j)), pl.BlockSpec((8, wide), lambda j: (0, j)), whole]
    out_shape = [sds((rows, FF // 2), bf16), sds((8, FF // 2), f32), sds((rows, D), f32)]
    args = (tie, d_branch, w_outer, slope, w_inner, so_far)
    common = dict(grid=(steps,), compiler_params=params(), cost_estimate=cost(2 * D * FF * rows, 30 * 2**20))
    if norm is None:
        return pl.pallas_call(
            feed_back_first_kernel,
            in_specs=in_specs,
            out_specs=out_specs,
            out_shape=out_shape,
            name="feed_back_first",
            **common,
        )(*args)
    return pl.pallas_call(
        feed_back_last_kernel,
        in_specs=in_specs + [whole, pl.BlockSpec((rows, 1), lambda j: (0, 0)), row, row],
        out_specs=out_specs + [whole, pl.BlockSpec((8, D), lambda j: (0, 0))],
        out_shape=out_shape + [sds((rows, D), bf16), sds((8, D), f32)],
        scratch_shapes=[pltpu.VMEM((rows, D), f32)],
        name="feed_back_last",
        **common,
    )(*args, *norm)


def turn_kernel(d_ref, w_ref, context_ref, out_ref, delta_ref):
    out = nt(d_ref[...], w_ref[...]).astype(bf16)
    out_ref[...] = out
    select = (
        lax.broadcasted_iota(jnp.int32, (8, 256), 1) // HEAD == lax.broadcasted_iota(jnp.int32, (8, 256), 0)
    ).astype(bf16)
    for g in range(D // 256):
        lanes = slice(g * 256, (g + 1) * 256)
        product = out[:, lanes].astype(f32) * context_ref[:, lanes].astype(f32)
        high = product.astype(bf16)
        low = (product - high.astype(f32)).astype(bf16)
        delta_ref[g] = nt(select, high) + nt(select, low)


def context_back(d, w, context):
    rows = d.shape[0]
    tile = pl.BlockSpec((TILE, D), lambda i: (i, 0))
    return pl.pallas_call(
        turn_kernel,
        grid=(rows // TILE,),
        in_specs=[tile, pl.BlockSpec((D, D), lambda i: (0, 0)), tile],
        out_specs=[tile, pl.BlockSpec((D // 256, 8, TILE), lambda i: (0, 0, i))],
        out_shape=[sds((rows, D), bf16), sds((D // 256, 8, rows), f32)],
        compiler_params=params(),
        cost_estimate=cost(2 * D * D * rows, 8 * 2**20),
        name="context_back",
    )(d, w, context)


def qkv_gradient_kernel(used, order_ref, x_ref, dq_ref, joined_ref, *refs):
    riders, (keep_ref, send_ref, sums_ref, rider) = refs[:-4], refs[-4:]
    rows, wide = dq_ref.shape
    first = order_ref[pl.num_programs(0)] == 0

    @pl.when(pl.program_id(0) == 0)
    def _():
        ones = jnp.ones((8, rows), bf16)
        sums_ref[:, :wide] = nn(ones, dq_ref[...])
        sums_ref[:, wide:] = nn(ones, joined_ref[1])

    x = x_ref[...]
    for i, grad in enumerate((dq_ref[...], joined_ref[0], joined_ref[1])):
        put_halves(keep_ref, send_ref, first, i * wide, tn(x, grad))
    if keep_ref.shape[2] > 3 * wide:
        lanes = rider.shape[1]

        @pl.when(pl.program_id(0) == 0)
        def _():
            rider[...] = jnp.zeros_like(rider)
            at = 0
            for ref, height in zip((*riders, sums_ref), (*used, 1)):
                for i in range(height):
                    for begin in range(0, ref.shape[1], lanes):
                        rider[at : at + 1, :] = ref[i : i + 1, begin : begin + lanes]
                        at += 1

        low = rider[...].astype(bf16)
        keep_ref[0, :, 3 * wide :] = low
        send_ref[0, :, 3 * wide :] = low


def qkv_gradient(order, tokens, dq, joined, shards, riders=()):
    rows, wide = dq.shape
    part = D // shards
    lanes = 16 * D // (part // 2)
    columns = 3 * wide + (lanes if riders else 0)
    sums = [array for array, _ in riders]
    out = pl.BlockSpec((1, part // 2, columns), lambda r, order_ref: (r, 0, 0))
    left = pl.BlockSpec((rows, part), lambda r, order_ref: (0, order_ref[r]))
    whole = pl.BlockSpec((rows, wide), lambda r, order_ref: (0, 0))
    both = pl.BlockSpec((2, rows, wide), lambda r, order_ref: (0, 0, 0))
    return pl.pallas_call(
        functools.partial(qkv_gradient_kernel, [height for _, height in riders]),
        grid_spec=pltpu.PrefetchScalarGridSpec(
            num_scalar_prefetch=1,
            grid=(shards,),
            in_specs=[left, whole, both]
            + [pl.BlockSpec(array.shape, lambda r, order_ref: (0, 0)) for array in sums],
            out_specs=[out, out, pl.BlockSpec((8, 2 * wide), lambda r, order_ref: (0, 0))],
            scratch_shapes=[pltpu.VMEM((part // 2, lanes), f32)],
        ),
        out_shape=[sds((shards, part // 2, columns), bf16)] * 2 + [sds((8, 2 * wide), f32)],
        compiler_params=params(),
        cost_estimate=cost(2 * rows * D * columns, 16 * 2**20),
        name="qkv_gradient",
    )(order, tokens, dq, joined, *sums)


def input_kernel(base_ref, *refs):
    grads, w_ref, out_ref = refs[:-2], refs[-2], refs[-1]
    total = base_ref[...]
    for side in (0, 1):
        dq_ref, joined_ref = grads[2 * side : 2 * side + 2]
        for which, grad in enumerate((dq_ref[...], joined_ref[0], joined_ref[1])):
            total += nt(grad, w_ref[:, qkv_columns(which, side)])
    out_ref[...] = total


def input_back(base, grads, w):
    rows = base.shape[0]
    tile = pl.BlockSpec((TILE, D), lambda i: (i, 0))
    side = [pl.BlockSpec((TILE, D // 2), lambda i: (i, 0)), pl.BlockSpec((2, TILE, D // 2), lambda i: (0, i, 0))]
    return pl.pallas_call(
        input_kernel,
        grid=(rows // TILE,),
        in_specs=[tile, *side, *side, pl.BlockSpec((D, 3 * D), lambda i: (0, 0))],
        out_specs=tile,
        out_shape=sds((rows, D), f32),
        compiler_params=params(),
        cost_estimate=cost(6 * D * D * rows, 20 * 2**20),
        name="input_back",
    )(base, *grads, w)


def swap(value, axis, bit):
    return lax.ppermute(value, axis, [(i, i ^ bit) for i in range(lax.axis_size(axis))])


def after(value, *others):
    return lax.optimization_barrier((value,) + others)[0]


def arrive(gate, value):
    return value if gate[0] is None else after(value, gate[0])


def gathering(gate, shard, own):
    n = lax.axis_size("fsdp")
    quarter = shard.shape[0] // 4
    near = [1 << b for b in range(n.bit_length() - 1)]
    whole = dict(zip(near, (yield [arrive(gate, swap(own, "fsdp", r)) for r in near])))
    held = {(r, s): value[s * quarter : (s + 1) * quarter] for r, value in whole.items() for s in (0, 1)}
    found = []
    for r in range(1, n):
        if r in whole:
            found.append(whole[r])
        else:
            for s, bit in ((0, 1 << (r.bit_length() - 1)), (1, r & -r)):
                held[r, s] = arrive(gate, swap(held[r ^ bit, s], "fsdp", bit))
                found.append(held[r, s])
    found = yield found
    yield [shard, *found, *[arrive(gate, swap(value, "ctx", 1)) for value in found]]


def half_sets(value, bit):
    shape = value.shape
    split = value.reshape((shape[0] // (2 * bit), 2, bit) + shape[1:])
    rest = (shape[0] // 2,) + shape[1:]
    return split[:, 0].reshape(rest), split[:, 1].reshape(rest)


def add_low(a, b):
    return (a.astype(f32) + b.astype(f32)).astype(bf16)


def reduction(gate, keep, send, parity, short=False):
    got = arrive(gate, swap(send, "ctx", 1))
    n = lax.axis_size("fsdp")
    quarter = keep.shape[1] // 2
    bits = [1 << b for b in range(n.bit_length() - 1)]
    streams = [(order, list(range(n))) for order in (bits, bits[::-1])]
    parts = [add_low(keep[:, s * quarter : (s + 1) * quarter], got[:, s * quarter : (s + 1) * quarter]) for s in (0, 1)]
    parts = list((yield parts))
    for k in range(len(bits)):
        for s, (order, ids) in enumerate(streams):
            bit = order[k]
            step = [i for i, r in enumerate(ids) if r & bit][0]
            ids[:] = [r for r in ids if not r & bit]
            mine, theirs = half_sets(parts[s], step)
            parts[s] = add_low(mine, arrive(gate, swap(theirs, "fsdp", bit)))
        if k < len(bits) - 1:
            parts = list((yield parts))
    value = jnp.concatenate([part[0] for part in parts], axis=0)
    (value,) = yield [value]
    if short:
        bit = 2
        while bit < lax.axis_size("ctx"):
            value = add_low(value, arrive(gate, swap(value, "ctx", bit)))
            (value,) = yield [value]
            bit *= 2
        yield from both_halves(gate, value, parity)
    else:
        yield from chain(gate, value, parity)


def chain(gate, value, parity):
    count = lax.axis_size("ctx") // 2
    position = lax.axis_index("ctx") // 2
    half = count // 2

    def move(value, chip_pairs):
        pairs = [(2 * a + c, 2 * b + c) for a, b in chip_pairs for c in (0, 1)]
        return arrive(gate, lax.ppermute(value, "ctx", pairs))

    for s in range(half - 1):
        value = add_low(value, move(value, [(s, s + 1), (count - 1 - s, count - 2 - s)]))
        (value,) = yield [value]
    inner = (position == half - 1) | (position == half)
    across = move(value, [(half - 1, half), (half, half - 1)])
    value = jnp.where(inner, add_low(value, across), value)
    (value,) = yield [value]
    for s in reversed(range(half - 1)):
        back = move(value, [(s + 1, s), (count - 2 - s, count - 1 - s)])
        value = jnp.where((position == s) | (position == count - 1 - s), back, value)
        (value,) = yield [value]
    yield from both_halves(gate, value, parity)


def wide_reduction(gate, keep, send, parity):
    value = add_low(keep, arrive(gate, swap(send, "ctx", 1)))
    (value,) = yield [value]
    (value,) = yield [lax.psum_scatter(value, "fsdp", scatter_dimension=0, tiled=True)[0]]
    yield from chain(gate, value, parity)


def both_halves(gate, value, parity):
    other = arrive(gate, swap(value, "ctx", 1))
    first = parity == 0
    yield [jnp.concatenate([jnp.where(first, value, other), jnp.where(first, other, value)], axis=0).astype(f32)]


def whole_reduction(gate, keep, send, parity):
    value = add_low(keep, arrive(gate, swap(send, "ctx", 1)))
    (value,) = yield [value]
    (value,) = yield [lax.psum_scatter(value, "fsdp", scatter_dimension=0, tiled=True)[0]]
    groups = [list(range(k, lax.axis_size("ctx"), 2)) for k in (0, 1)]
    (value,) = yield [lax.psum(value, "ctx", axis_index_groups=groups)]
    yield from both_halves(gate, value, parity)


class Staged:
    def __init__(self, stages, *args):
        self.gate, self.values, self.done = [None], None, False
        self.stages = stages(self.gate, *args)

    def step(self):
        try:
            self.values = self.stages.send(self.values)
        except StopIteration:
            self.done = True
        return not self.done

    def result(self):
        while self.step():
            pass
        return self.values


def boundary(done, tie, *transfers, hold=()):
    moving = list(hold)
    for transfer in transfers:
        transfer.gate[0] = done
        if transfer.step():
            moving.append(transfer)
    gates = () if done is None else (done,)
    tie, values = lax.optimization_barrier((tie, [transfer.values for transfer in moving], gates))[:2]
    for transfer, value in zip(moving, values):
        transfer.values = value
    return tie


def gathering_rows(gate, row):
    (value,) = yield [row]
    bit = 1
    while bit < lax.axis_size("fsdp"):
        value = jnp.concatenate([value, swap(value, "fsdp", bit)], axis=0)
        bit *= 2
        (value,) = yield [value]


def body(
    layer_input,
    teacher_states,
    out_cotangent,
    doc_start,
    valid_flag,
    query_weight,
    query_bias,
    key_weight,
    value_weight,
    value_bias,
    proj_weight,
    proj_bias,
    attn_gain,
    attn_shift,
    inner_weight,
    inner_bias,
    outer_weight,
    outer_bias,
    final_gain,
    final_shift,
):
    n_ctx, n_fsdp = lax.axis_size("ctx"), lax.axis_size("fsdp")
    c, f = lax.axis_index("ctx"), lax.axis_index("fsdp")
    parity = c % 2
    tokens = layer_input[0]
    rows = tokens.shape[0]
    part = query_weight.shape[0]
    where = jnp.stack([f, parity]).astype(jnp.int32)
    order = jnp.concatenate([f ^ jnp.arange(n_fsdp, dtype=jnp.int32), parity[None].astype(jnp.int32)])

    def own_half(shard):
        half = shard.shape[0] // 2
        return lax.dynamic_slice_in_dim(shard, parity * half, half)

    qkv_shard, own_qkv = pack_shards(where, query_weight, key_weight, value_weight)
    w_qkv = Staged(gathering, qkv_shard, own_qkv)

    up = [(i, i + 1) for i in range(n_ctx - 1)]
    down = [(b, a) for a, b in up]
    before = lax.ppermute(tokens[rows - DOC_MAX :], "ctx", up)
    behind = lax.ppermute(tokens[:DOC_MAX], "ctx", down)
    flags = valid_flag[0]
    valid = jnp.sum(flags)
    valid = jnp.pad(jnp.stack([valid // 64, valid % 64]).astype(bf16), (0, 126))
    flags = flags.astype(f32)[:, None]
    small = jnp.concatenate(
        [query_bias, value_bias, proj_bias, attn_gain, attn_shift, outer_bias, final_gain, final_shift, inner_bias, valid]
    )
    small = Staged(gathering_rows, small.reshape(1, -1))
    small.step()
    small.step()
    position = c * rows
    starts = doc_start[0]
    near_starts = lax.dynamic_slice_in_dim(
        jnp.concatenate(
            [jnp.full((DOC_MAX,), -1, jnp.int32), starts, jnp.full((DOC_MAX,), 2**30, jnp.int32)]
        ),
        position,
        rows + 2 * DOC_MAX,
    )
    tiles = near_starts.shape[0] // TILE
    low_tile = (near_starts[::TILE] - position + DOC_MAX) // TILE
    last = position - DOC_MAX + TILE * (1 + jnp.arange(tiles, dtype=jnp.int32)) - 1
    ends = jnp.sum((near_starts[None, :] <= last[:, None]).astype(jnp.int32), axis=1)
    high_tile = (ends + TILE - 1) // TILE
    inside = (jnp.arange(tiles) >= RIM) & (jnp.arange(tiles) < tiles - RIM)
    low_tile = jnp.where(inside, low_tile, jnp.maximum(low_tile, RIM))
    high_tile = jnp.where(inside, high_tile, jnp.minimum(high_tile, tiles - RIM))
    idq = near_starts.reshape(tiles, 1, TILE)
    idk = near_starts[:, None]

    before, behind, idq, idk, low_tile, high_tile, flags, own_proj, own_inner = boundary(
        None, (before, behind, idq, idk, low_tile, high_tile, flags, own_half(proj_weight), own_half(inner_weight)),
        w_qkv, small,
    )
    w_proj = Staged(gathering, proj_weight, own_proj)
    w_inner = Staged(gathering, inner_weight, own_inner)
    boundary(None, where, w_qkv)
    small = small.result()[0]
    valid = jnp.sum(small[:, -128:].astype(f32), axis=0)
    counted = valid[0] * 64 + valid[1]
    bit = 1
    while bit < n_ctx:
        counted = jnp.full((8, 128), counted, f32) if counted.ndim == 0 else counted
        counted = counted + swap(counted, "ctx", bit)
        bit *= 2
    count = counted[0, 0]
    b_query, b_value, b_proj, g_attn, s_attn, b_outer, g_final, s_final, b_inner = unpack_vectors(where, small)
    w_qkv.values, b_query, b_value, count = lax.optimization_barrier((w_qkv.values, b_query, b_value, count))

    def attend(side, tie, *so_far):
        return attn_fwd(tie, high_tile, query, keys, values_t, idq, idk, side, 2, so_far)

    query, keys, values, keys_t, values_t, w_qkv = project_qkv(where, w_qkv.result(), before, tokens, behind, b_query, b_value)
    tie, own_outer = boundary(query, (low_tile, own_half(outer_weight)), w_proj)
    w_outer = Staged(gathering, outer_weight, own_outer)
    context_a, log_a = attend(0, tie)
    context, log_totals = attend(1, boundary(context_a, low_tile, w_proj, w_inner, w_outer), context_a, log_a)
    normed, normed_low, rate, w_proj = mix_and_norm(
        boundary(context, where, w_proj, w_inner, w_outer), w_proj.values, context, b_proj, tokens, g_attn, s_attn
    )
    tie = boundary(normed, where, w_inner, w_outer)
    act, slope, w_inner = inner_forward(tie, w_inner.values, normed_low, b_inner)
    coef = (n_fsdp * n_ctx * rows / count).reshape(1)
    layer_out, d_sum_two, d_branch, final_sums, w_outer = outer_forward(
        where, w_outer.result(), coef, act, b_outer, normed, g_final, s_final, teacher_states[0], out_cotangent[0], flags
    )

    plain = jnp.concatenate([jnp.arange(n_fsdp, dtype=jnp.int32), order[n_fsdp:]])
    outer = Staged(wide_reduction, *gram(plain, n_fsdp, (act, d_branch)), parity)
    d_pre_a, bias_a, so_far = feed_back(where, 0, d_branch, w_outer, slope, w_inner, d_sum_two)
    d_pre_b, bias_b, d_sum_one, d_attn, attn_sums = feed_back(
        boundary(d_pre_a, where, outer), 1, d_branch, w_outer, slope, w_inner, so_far, (normed, rate, g_attn, s_attn)
    )
    inner_pair = gram(
        after(plain, d_attn), n_fsdp, (normed_low, d_pre_a, d_pre_b), (context, d_attn)
    )
    inner = Staged(whole_reduction, *inner_pair, parity)

    d_context, delta = context_back(after(d_attn, inner_pair[0]), w_proj, context)
    stats = jnp.stack([log_totals, delta])

    def rims(value, axis):
        size = value.shape[axis]
        before = lax.ppermute(lax.slice_in_dim(value, size - DOC_MAX, size, axis=axis), "ctx", up)
        behind = lax.ppermute(lax.slice_in_dim(value, 0, DOC_MAX, axis=axis), "ctx", down)
        return before, behind

    do_before, do_behind = rims(d_context, 0)
    stats_before, stats_behind = rims(stats, 3)
    stats = jnp.concatenate([stats_before, stats, stats_behind], axis=3)
    def attend_back(side, tie):
        return attn_bwd(
            tie, high_tile, query, do_before, d_context, do_behind, keys, keys_t, values, stats, idq, idk, side, 2
        )

    parts_a = attend_back(0, boundary(d_context, low_tile, outer, inner))
    *first_pair, sums_a = qkv_gradient(boundary(parts_a[0], order, outer), tokens, *parts_a, n_fsdp)
    first = Staged(reduction, *first_pair, parity)
    parts_b = attend_back(1, boundary(first_pair[0], low_tile, outer, inner))
    riders = [(final_sums, 4), (attn_sums, 3), (bias_a, 1), (bias_b, 1), (sums_a, 1)]
    *last_pair, sums_b = qkv_gradient(
        boundary(parts_b[0], order, first, hold=[outer]), tokens, *parts_b, n_fsdp, riders
    )
    last = Staged(reduction, *last_pair, parity, True)
    input_grad = input_back(d_sum_one, (*parts_a, *parts_b), boundary(last_pair[0], w_qkv, first))
    boundary(input_grad, where, last, first)
    boundary(last.values[0], where, last, first)
    boundary(last.values[0], where, last, first, outer, inner)
    outer_grad, inner_grad, first, last = (transfer.result()[0] for transfer in (outer, inner, first, last))
    vectors = last[: part // 2, 3 * D // 2 :].reshape(16, D)
    query_sum, value_sum = vectors[11:13].reshape(2, 2, D // 2).transpose(1, 0, 2).reshape(2, D)
    inner_grad, proj_grad = inner_grad[:, :FF], inner_grad[:, FF:]
    sixth = D // 2
    query_grad, key_grad, value_grad = (
        jnp.concatenate([grad[:, i * sixth : (i + 1) * sixth] for grad in (first, last)], axis=1)
        for i in range(3)
    )
    mse = jnp.sum(vectors[3]) / (count * D)

    def mine(vector):
        length = vector.shape[0] // n_fsdp
        return lax.dynamic_slice_in_dim(vector, f * length, length)

    return (
        layer_out[None],
        input_grad[None],
        mse,
        query_grad,
        mine(query_sum),
        key_grad,
        value_grad,
        mine(value_sum),
        proj_grad,
        mine(vectors[6]),
        mine(vectors[4]),
        mine(vectors[5]),
        inner_grad,
        mine(vectors[7:11].reshape(FF)),
        outer_grad,
        mine(vectors[2]),
        mine(vectors[0]),
        mine(vectors[1]),
    )


def solution(mesh):
    tokens = P("fsdp", "ctx", None)
    matrix, vector = P("fsdp", None), P("fsdp")
    weights = (
        matrix, vector, matrix, matrix, vector, matrix, vector, vector, vector, matrix, vector, matrix, vector, vector, vector,
    )
    return jax.shard_map(
        body,
        mesh=mesh,
        in_specs=(tokens, tokens, tokens, matrix, P("fsdp", "ctx")) + weights,
        out_specs=(tokens, tokens, P()) + weights,
        check_vma=False,
    )
```

time: 615 us -> 593 us (0.964)
  waiting for transfers between devices: 83.3 us -> 69.8 us
  other arithmetic: 42.6 us -> 34.3 us
  local copies, waits for them, and re-layouts: 39.3 us -> 32.8 us
    ppermute x6, starting transfers between devices: 11.2 us -> 35 us  [move(): return arrive(gate, lax.ppermute(value, 'ctx', pairs))]
    ppermute x53 -> x55, starting transfers between devices: 84 us -> 65.1 us  [swap(): lax.ppermute(value, axis, [(i, i ^ bit) for i in range(lax.axis_size(axis...]
    pallas_call x2, Pallas kernels: 63.9 us -> 74.9 us  [attn_bwd(): pl.pallas_call(attn_bwd_kernel, grid_spec=pltpu.PrefetchScalarGridSpec(nu...]
    ppermute x6, waiting for transfers between devices: 23.5 us -> 13 us  [move(): return arrive(gate, lax.ppermute(value, 'ctx', pairs))]
    pallas_call x2, Pallas kernels: 45.1 us -> 36.4 us  [attn_fwd(): pl.pallas_call(attn_fwd_kernel, grid_spec=pltpu.PrefetchScalarGridSpec(nu...]
    unnamed x65 -> x71, local copies, waits for them, and re-layouts: 16 us -> 12.2 us
    convert_element_type x10 -> x12, other arithmetic: 19.5 us -> 16.4 us  [add_low(): return (a.astype(f32) + b.astype(f32)).astype(bf16)]
    ppermute x53 -> x55, waiting for transfers between devices: 54.2 us -> 55.4 us  [swap(): lax.ppermute(value, axis, [(i, i ^ bit) for i in range(lax.axis_size(axis...]
  transfers between devices with their start and end apart: 69 -> 70, of which waited for: 17 -> 22; matrix products, arithmetic and copies ran while one was open for 10% -> 8% of each run, Pallas kernels for 45% -> 41%
where the time goes in v3:
time: 593 us; the launch traced here: 587 us
  Pallas kernels  313 us (53%)
  starting transfers between devices  116 us (20%)
  waiting for transfers between devices  69.8 us (12%)
  other arithmetic  34.3 us (6%)
  local copies, waits for them, and re-layouts  32.8 us (6%)
  between operations  22.1 us (4%)
    pallas_call x2, Pallas kernels, attn_bwd(): pl.pallas_call(attn_bwd_kernel, grid_spec=pltpu.PrefetchScalarGridSpec(nu...  74.9 us
    ppermute x55, starting transfers between devices, swap(): lax.ppermute(value, axis, [(i, i ^ bit) for i in range(lax.axis_size(axis...  65.1 us
    ppermute x55, waiting for transfers between devices, swap(): lax.ppermute(value, axis, [(i, i ^ bit) for i in range(lax.axis_size(axis...  55.4 us
    pallas_call x2, Pallas kernels, attn_fwd(): pl.pallas_call(attn_fwd_kernel, grid_spec=pltpu.PrefetchScalarGridSpec(nu...  36.4 us
    ppermute x6, starting transfers between devices, move(): return arrive(gate, lax.ppermute(value, 'ctx', pairs))  35 us
    pallas_call x2, Pallas kernels, gram(): pl.pallas_call(functools.partial(gram_kernel, [len(group) - 1 for group i...  32.5 us
    pallas_call x1, Pallas kernels, inner_forward(): pl.pallas_call(functools.partial(inner_kernel, len(pieces)), grid=(FF //...  30.1 us
    pallas_call x1, Pallas kernels, feed_back(): pl.pallas_call(feed_back_last_kernel, in_specs=in_specs + [whole, pl.Bloc...  24.6 us
  transfers between devices with their start and end apart: 70, of which 22 were waited for; matrix products, arithmetic and copies ran while one was open for 8% of the time, Pallas kernels for 41%

profile of v3, /device:TPU:0, one launch (start us, length us, event | category | flops | bytes accessed | tf_op | source)
XLA Modules:
  0.0 587.2 jit_solution(14738603449750217639)
XLA Ops:
  7.8 2.9 pack_shards.1
  10.8 3.0 collective-permute-start.3
  13.7 1.5 collective-permute-start.2
  27.4 1.7 slice_bitcast_fusion
  30.4 4.0 collective-permute-start
  37.8 2.7 collective-permute-done.5
  42.5 5.8 collective-permute-start.9
  50.4 1.6 collective-permute-start.8
  52.5 2.5 collective-permute-start.10
  54.9 1.6 collective-permute-done.10
  56.5 3.0 collective-permute-start.11
  69.1 1.5 collective-permute-start.19
  70.6 21.9 %project_qkv.1 = (bf16[2048,1024]{1,0:T(8,128)(2,1)}, bf16[2048,1024]{1,0:T(8,128)(2,1)}, bf16[2048,1024]{1,0:T(8,128)(2,1)}, bf16[1024,2048]{1,0:T(8,128)(2,1)}...) custom-call(s32[2]{0:T(128)} %pad_add_fusion.where_ref.tie_ref, bf16[256,3072]{1,0:T(8,128)(2,1)} %get-tuple-element.227.refs_0_, ...), custom_call_target="tpu_custom_call" | custom-call | flops 10737418240 | bytes 31457280 | tf_op jit(solution)/shard_map/project_qkv/pallas_call | solution.py:173
  92.5 2.0 collective-permute-done.16.refs_2_
  95.7 1.6 collective-permute-start.18
  97.2 1.5 collective-permute-start.17
  98.7 18.3 %attn_forward.2 = (bf16[1024,1024]{1,0:T(8,128)(2,1)}, f32[4,8,1024]{2,1,0:T(8,128)}) custom-call(s32[8]{0:T(128)} %get-tuple-element.379.lo_ref, s32[8]{0:T(128)} %get-tuple-element.251.hi_ref, bf16[2048,1024]{1,0:T(8,128)(2,1)} %get-tuple-element.245.q_ref, bf16[2048,1024]{1,0:T(8,128)(2,1)} %get-tuple-element.252.k_ref, ...), custom_call_target="tpu_custom_call" | custom-call | flops 20000000000 | bytes 2097152 | tf_op jit(solution)/shard_map/attn_forward/pallas_call | solution.py:260
  117.0 6.9 %collective-permute-done.18.refs_4_ = bf16[64,1024]{1,0:T(8,128)(2,1)S(1)} collective-permute-done((bf16[64,1024]{1,0:T(8,128)(2,1)S(1)}, bf16[64,1024]{1,0:T(8,128)(2,1)S(1)}, u32[]{:S(2)}, u32[]{:S(2)}) %collective-permute-start.18) | collective-permute-done | bytes 131104 | tf_op jit(solution)/shard_map/ppermute | solution.py:777
  130.0 1.5 collective-permute-start.28
  132.5 18.2 %attn_forward.3 = (bf16[1024,1024]{1,0:T(8,128)(2,1)}, f32[4,8,1024]{2,1,0:T(8,128)}) custom-call(s32[8]{0:T(128)} %get-tuple-element.379.lo_ref, s32[8]{0:T(128)} %get-tuple-element.251.hi_ref, bf16[2048,1024]{1,0:T(8,128)(2,1)} %get-tuple-element.245.q_ref, ...), custom_call_target="tpu_custom_call", output_to_operand_aliasing={{0}: (7, {}), {1}: (8, {})} | custom-call | flops 20000000000 | bytes 2097152 | tf_op jit(solution)/shard_map/attn_forward/pallas_call | solution.py:260
  150.8 2.8 collective-permute-done.28.refs_4_
  157.5 2.1 collective-permute-done.38.refs_8_
  162.7 9.6 %mix_and_norm.1 = (f32[1024,1024]{1,0:T(8,128)}, bf16[1024,1024]{1,0:T(8,128)(2,1)}, f32[1024,1]{1,0:T(8,128)}, bf16[1024,1024]{1,0:T(8,128)(2,1)}) custom-call(s32[2]{0:T(128)} %pad_add_fusion.where_ref.tie_ref, bf16[256,1024]{1,0:T(8,128)(2,1)} %refs_0_, bf16[128,1024]{1,0:T(8,128)(2,1)} %copy-done.13, bf16[128,1024]{1,0:T(8,128)(2,1)} %copy-done.12, ...), custom_call_target="tpu_custom_call" | custom-call | flops 2147483648 | bytes 14680064 | tf_op jit(solution)/shard_map/mix_and_norm/pallas_call | solution.py:425
  172.5 30.1 %inner_forward.1 = (bf16[1024,4096]{1,0:T(8,128)(2,1)}, bf16[1024,4096]{1,0:T(8,128)(2,1)}, bf16[1024,4096]{1,0:T(8,128)(2,1)}) custom-call(s32[2]{0:T(128)} %pad_add_fusion.where_ref.tie_ref, bf16[256,4096]{1,0:T(8,128)(2,1)} %refs_0_.1, bf16[128,4096]{1,0:T(8,128)(2,1)} %collective-permute-done.19.refs_1_, bf16[128,4096]{1,0:T(8,128)(2,1)} %copy-done.9, ...), custom_call_target="tpu_custom_call" | custom-call | flops 8589934592 | bytes 27262976 | tf_op jit(solution)/shard_map/inner_forward/pallas_call | solution.py:467
  202.6 22.6 %outer_forward.1 = (bf16[1024,1024]{1,0:T(8,128)(2,1)}, f32[1024,1024]{1,0:T(8,128)}, bf16[1024,1024]{1,0:T(8,128)(2,1)}, f32[8,1024]{1,0:T(8,128)}, bf16[4096,1024]{1,0:T(8,128)(2,1)}) custom-call(s32[2]{0:T(128)} %pad_add_fusion.where_ref.tie_ref, bf16[1024,1024]{1,0:T(8,128)(2,1)} %refs_0_.2, bf16[512,1024]{1,0:T(8,128)(2,1)} %collective-permute-done.21.refs_1_, ...), custom_call_target="tpu_custom_call" | custom-call | flops 8589934592 | bytes 33554432 | tf_op jit(solution)/shard_map/outer_forward/pallas_call | solution.py:513
  225.2 13.9 %gram.2 = (bf16[4,512,1024]{2,1,0:T(8,128)(2,1)}, bf16[4,512,1024]{2,1,0:T(8,128)(2,1)}) custom-call(s32[5]{0:T(128)} %pad_add_fusion.1.order_ref, bf16[1024,4096]{1,0:T(8,128)(2,1)} %get-tuple-element.336.refs_10_.refs_0_, bf16[1024,1024]{1,0:T(8,128)(2,1)} %get-tuple-element.342.refs_1_.db_ref), custom_call_target="tpu_custom_call" | custom-call | flops 8589934592 | bytes 18874368 | tf_op jit(solution)/shard_map/gram/pallas_call | solution.py:565
  239.2 19.0 %feed_back_first.1 = (bf16[1024,2048]{1,0:T(8,128)(2,1)}, f32[8,2048]{1,0:T(8,128)}, f32[1024,1024]{1,0:T(8,128)}) custom-call(s32[2]{0:T(128)} %pad_add_fusion.where_ref.tie_ref, bf16[1024,1024]{1,0:T(8,128)(2,1)} %get-tuple-element.342.refs_1_.db_ref, bf16[4096,1024]{1,0:T(8,128)(2,1)} %get-tuple-element.345.wo_ref, ...), custom_call_target="tpu_custom_call" | custom-call | flops 8589934592 | bytes 31457280 | tf_op jit(solution)/shard_map/feed_back_first/pallas_call | solution.py:643
  258.3 6.3 %add_convert_fusion.1 = bf16[4,512,1024]{2,1,0:T(8,128)(2,1)} fusion(bf16[4,512,1024]{2,1,0:T(8,128)(2,1)} %collective-permute-done.39, bf16[4,512,1024]{2,1,0:T(8,128)(2,1)S(1)} %copy-done.1), kind=kLoop, calls=%fused_computation.1 | loop fusion | flops 8388608 | bytes 12582912 | tf_op jit(solution)/shard_map/convert_element_type | solution.py:814
  264.6 24.6 %feed_back_last.1 = (bf16[1024,2048]{1,0:T(8,128)(2,1)}, f32[8,2048]{1,0:T(8,128)}, f32[1024,1024]{1,0:T(8,128)}, bf16[1024,1024]{1,0:T(8,128)(2,1)}, f32[8,1024]{1,0:T(8,128)}) custom-call(s32[2]{0:T(128)} %pad_add_fusion.where_ref.tie_ref, bf16[1024,1024]{1,0:T(8,128)(2,1)} %get-tuple-element.342.refs_1_.db_ref, ...), custom_call_target="tpu_custom_call" | custom-call | flops 8589934592 | bytes 31457280 | tf_op jit(solution)/shard_map/feed_back_last/pallas_call | solution.py:651
  289.2 18.7 %gram.3 = (bf16[4,128,5120]{2,1,0:T(8,128)(2,1)}, bf16[4,128,5120]{2,1,0:T(8,128)(2,1)}) custom-call(s32[5]{0:T(128)} %pad_add_fusion.1.order_ref, bf16[1024,1024]{1,0:T(8,128)(2,1)} %get-tuple-element.334.refs_9_.refs_0_, bf16[1024,2048]{1,0:T(8,128)(2,1)} %get-tuple-element.349.refs_1_, bf16[1024,2048]{1,0:T(8,128)(2,1)} %get-tuple-element.358.refs_2_, ...), custom_call_target="tpu_custom_call" | custom-call | flops 10737418240 | bytes 23068672 | tf_op jit(solution)/shard_map/gram/pallas_call | solution.py:565
  308.3 7.0 %context_back.1 = (bf16[1024,1024]{1,0:T(8,128)(2,1)}, f32[4,8,1024]{2,1,0:T(8,128)}) custom-call(bf16[1024,1024]{1,0:T(8,128)(2,1)} %get-tuple-element.361.refs_4_.d_ref, bf16[1024,1024]{1,0:T(8,128)(2,1)} %get-tuple-element.362.w_ref, bf16[1024,1024]{1,0:T(8,128)(2,1)} %get-tuple-element.271.refs_9_.refs_3_.context_ref), custom_call_target="tpu_custom_call" | custom-call | flops 2147483648 | bytes 8388608 | tf_op jit(solution)/shard_map/context_back/pallas_call | solution.py:679
  315.3 1.6 collective-permute-done.40
  317.0 6.8 %add_convert_fusion = bf16[4,128,5120]{2,1,0:T(8,128)(2,1)} fusion(bf16[4,128,5120]{2,1,0:T(8,128)(2,1)} %collective-permute-done.40, bf16[4,128,5120]{2,1,0:T(8,128)(2,1)S(1)} %copy-done), kind=kLoop, calls=%fused_computation | loop fusion | flops 10485760 | bytes 15728640 | tf_op jit(solution)/shard_map/convert_element_type | solution.py:814
  323.9 1.5 copy-done.2
  326.9 3.1 collective-permute-start.41
  330.0 4.4 collective-permute-start.43
  338.5 12.2 %collective-permute-start.45 = (bf16[512,1024]{1,0:T(8,128)(2,1)S(1)}, bf16[512,1024]{1,0:T(8,128)(2,1)S(1)}, u32[]{:S(2)}, u32[]{:S(2)}) collective-permute-start(bf16[512,1024]{1,0:T(8,128)(2,1)S(1)} %bitcast.144), channel_id=1, source_target_pairs={{0,8},{4,12},{24,16},{28,20},{1,9},{5,13},{25,17},{29,21},{2,10},{... | collective-permute-start | bytes 3145736 | tf_op jit(solution)/shard_map/ppermute | solution.py:854
  352.1 37.5 %attn_backward.2 = (bf16[1024,512]{1,0:T(8,128)(2,1)}, bf16[2,1024,512]{2,1,0:T(8,128)(2,1)}) custom-call(s32[8]{0:T(128)} %get-tuple-element.379.lo_ref, s32[8]{0:T(128)} %get-tuple-element.251.hi_ref, bf16[2048,1024]{1,0:T(8,128)(2,1)} %get-tuple-element.245.q_ref, bf16[512,1024]{1,0:T(8,128)(2,1)} %copy-done.16, ...), custom_call_target="tpu_custom_call" | custom-call | flops 30000001024 | bytes 4194304 | tf_op jit(solution)/shard_map/attn_backward/pallas_call | solution.py:359
  390.8 8.5 %qkv_gradient.2 = (bf16[4,128,1536]{2,1,0:T(8,128)(2,1)}, bf16[4,128,1536]{2,1,0:T(8,128)(2,1)}, f32[8,1024]{1,0:T(8,128)}) custom-call(s32[5]{0:T(128)} %pad_add_fusion.2.order_ref, bf16[1024,1024]{1,0:T(8,128)(2,1)} %bitcast.133, bf16[1024,512]{1,0:T(8,128)(2,1)} %get-tuple-element.370.dq_ref.refs_0_, ...), custom_call_target="tpu_custom_call" | custom-call | flops 3221225472 | bytes 16777216 | tf_op jit(solution)/shard_map/qkv_gradient/pallas_call | solution.py:733
  399.3 5.2 collective-permute-start.47
  405.0 37.4 %attn_backward.3 = (bf16[1024,512]{1,0:T(8,128)(2,1)}, bf16[2,1024,512]{2,1,0:T(8,128)(2,1)}) custom-call(s32[8]{0:T(128)} %get-tuple-element.379.lo_ref, s32[8]{0:T(128)} %get-tuple-element.251.hi_ref, bf16[2048,1024]{1,0:T(8,128)(2,1)} %get-tuple-element.245.q_ref, bf16[512,1024]{1,0:T(8,128)(2,1)} %copy-done.16, ...), custom_call_target="tpu_custom_call" | custom-call | flops 30000001024 | bytes 4194304 | tf_op jit(solution)/shard_map/attn_backward/pallas_call | solution.py:359
  442.4 1.8 add_convert_fusion.6
  444.2 4.2 collective-permute-start.49
  449.9 8.6 %qkv_gradient.3 = (bf16[4,128,1664]{2,1,0:T(8,128)(2,1)}, bf16[4,128,1664]{2,1,0:T(8,128)(2,1)}, f32[8,1024]{1,0:T(8,128)}) custom-call(s32[5]{0:T(128)} %pad_add_fusion.2.order_ref, bf16[1024,1024]{1,0:T(8,128)(2,1)} %bitcast.134, bf16[1024,512]{1,0:T(8,128)(2,1)} %get-tuple-element.380.dq_ref.refs_2_, ...), custom_call_target="tpu_custom_call" | custom-call | flops 3489660928 | bytes 16777216 | tf_op jit(solution)/shard_map/qkv_gradient/pallas_call | solution.py:733
  458.5 2.0 collective-permute-start.50
  460.7 1.8 collective-permute-start.52
  462.5 1.6 collective-permute-start.51
  464.1 12.2 %input_back.1 = f32[1024,1024]{1,0:T(8,128)} custom-call(f32[1024,1024]{1,0:T(8,128)} %get-tuple-element.354.base_ref, bf16[1024,512]{1,0:T(8,128)(2,1)} %get-tuple-element.370.dq_ref.refs_0_, bf16[2,1024,512]{2,1,0:T(8,128)(2,1)} %get-tuple-element.371.joined_ref.refs_1_, bf16[1024,512]{1,0:T(8,128)(2,1)} %get-tuple-element.380.dq_ref.refs_2_, ...), custom_call_target="tpu_custom_call" | custom-call | flops 6442450944 | bytes 20971520 | tf_op jit(solution)/shard_map/input_back/pallas_call | solution.py:764
  478.2 18.7 %collective-permute-start.55 = (bf16[128,1536]{1,0:T(8,128)(2,1)S(1)}, bf16[128,1536]{1,0:T(8,128)(2,1)S(1)}, u32[]{:S(2)}, u32[]{:S(2)}) collective-permute-start(bf16[128,1536]{1,0:T(8,128)(2,1)S(1)} %pad_maximum_fusion.6), channel_id=1, source_target_pairs={{0,8},{4,12},{24,16},{28,20},{1,9},{5,13},{25,17},{29,21},{2,10},{... | collective-permute-start | bytes 1179656 | tf_op jit(solution)/shard_map/ppermute | solution.py:854
  497.0 1.8 collective-permute-start.53
  498.8 1.8 collective-permute-start.54
  500.6 4.2 collective-permute-done.55
  504.9 3.1 collective-permute-done.53
  508.0 1.5 collective-permute-done.54
  509.8 1.8 collective-permute-start.56
  512.7 3.0 collective-permute-done.56
  515.8 1.7 collective-permute-done.57
  519.6 8.5 %collective-permute-start.60 = (bf16[128,1664]{1,0:T(8,128)(2,1)S(1)}, bf16[128,1664]{1,0:T(8,128)(2,1)S(1)}, u32[]{:S(2)}, u32[]{:S(2)}) collective-permute-start(bf16[128,1664]{1,0:T(8,128)(2,1)S(1)} %pad_maximum_fusion.5), channel_id=1, source_target_pairs={{0,8},{4,12},{8,0},{12,4},{16,24},{20,28},{24,16},{28,20},{1,9},{5... | collective-permute-start | bytes 1277960 | tf_op jit(solution)/shard_map/ppermute | solution.py:777
  528.6 8.7 %collective-permute-done.63 = bf16[128,1536]{1,0:T(8,128)(2,1)S(1)} collective-permute-done((bf16[128,1536]{1,0:T(8,128)(2,1)S(1)}, bf16[128,1536]{1,0:T(8,128)(2,1)S(1)}, u32[]{:S(2)}, u32[]{:S(2)}) %collective-permute-start.63) | collective-permute-done | bytes 393248 | tf_op jit(solution)/shard_map/ppermute | solution.py:854
  537.5 5.4 collective-permute-done.60
  543.9 16.9 %collective-permute-done.61 = bf16[128,1664]{1,0:T(8,128)(2,1)S(1)} collective-permute-done((bf16[128,1664]{1,0:T(8,128)(2,1)S(1)}, bf16[128,1664]{1,0:T(8,128)(2,1)S(1)}, u32[]{:S(2)}, u32[]{:S(2)}) %collective-permute-start.61) | collective-permute-done | bytes 426016 | tf_op jit(solution)/shard_map/ppermute | solution.py:777
  561.2 2.5 maximum_convert_fusion
  574.2 1.5 broadcast_select_fusion.1
  576.8 2.5 fusion
  (269 shorter events, 70.6 us)
Async XLA Ops:
  7.2 316.6 %reduce-scatter.7.cloned.1.call-start = ((), (), s32[]{:S(2)}) async-start(), calls=%async_computation.3 | async-start | bytes 5242880
  10.8 29.8 %collective-permute-start.3 = (bf16[128,3072]{1,0:T(8,128)(2,1)}, bf16[128,3072]{1,0:T(8,128)(2,1)}, u32[]{:S(2)}, u32[]{:S(2)}) collective-permute-start(bf16[128,3072]{1,0:T(8,128)(2,1)} %get-tuple-element.224), channel_id=1, source_target_pairs={{0,2},{1,3},{2,0},{3,1},{4,6},{5,7},{6,4},{7,5},{8,10},{9,11},{10,... | collective-permute-start | bytes 2359304 | tf_op jit(solution)/shard_map/ppermute | solution.py:777
  13.7 26.8 %collective-permute-start.2 = (bf16[128,3072]{1,0:T(8,128)(2,1)}, bf16[128,3072]{1,0:T(8,128)(2,1)}, u32[]{:S(2)}, u32[]{:S(2)}) collective-permute-start(bf16[128,3072]{1,0:T(8,128)(2,1)} %get-tuple-element.224), channel_id=1, source_target_pairs={{0,1},{1,0},{2,3},{3,2},{4,5},{5,4},{6,7},{7,6},{8,9},{9,8},{10,11... | collective-permute-start | bytes 2359304 | tf_op jit(solution)/shard_map/ppermute | solution.py:777
  26.8 9.9 %collective-permute-start.4 = (bf16[1,3200]{1,0:T(2,128)(2,1)S(1)}, bf16[1,3200]{1,0:T(2,128)(2,1)S(1)}, u32[]{:S(2)}, u32[]{:S(2)}) collective-permute-start(bf16[1,3200]{1,0:T(2,128)(2,1)S(1)} %reshape.188), channel_id=1, source_target_pairs={{0,1},{1,0},{2,3},{3,2},{4,5},{5,4},{6,7},{7,6},{8,9},{9,8},{10,11... | collective-permute-start | bytes 19208 | tf_op jit(solution)/shard_map/ppermute | solution.py:777
  29.1 11.5 %collective-permute-start.1 = (bf16[512,1024]{1,0:T(8,128)(2,1)S(1)}, bf16[512,1024]{1,0:T(8,128)(2,1)}, u32[]{:S(2)}, u32[]{:S(2)}) collective-permute-start(bf16[512,1024]{1,0:T(8,128)(2,1)S(1)} %get-tuple-element.440), channel_id=1, source_target_pairs={{4,0},{8,4},{12,8},{16,12},{20,16},{24,20},{28,24},{5,1},{9,5},{13... | collective-permute-start | bytes 3145736 | tf_op jit(solution)/shard_map/ppermute | solution.py:973
  30.4 10.2 %collective-permute-start = (bf16[512,1024]{1,0:T(8,128)(2,1)S(1)}, bf16[512,1024]{1,0:T(8,128)(2,1)}, u32[]{:S(2)}, u32[]{:S(2)}) collective-permute-start(bf16[512,1024]{1,0:T(8,128)(2,1)S(1)} %get-tuple-element.441), channel_id=1, source_target_pairs={{0,4},{4,8},{8,12},{12,16},{16,20},{20,24},{24,28},{1,5},{5,9},{9,... | collective-permute-start | bytes 3145736 | tf_op jit(solution)/shard_map/ppermute | solution.py:972
  42.5 10.0 %collective-permute-start.9 = (f32[8,128]{1,0:T(8,128)S(1)}, f32[8,128]{1,0:T(8,128)S(1)}, u32[]{:S(2)}, u32[]{:S(2)}) collective-permute-start(f32[8,128]{1,0:T(8,128)S(1)} %broadcast_in_dim.25), channel_id=1, source_target_pairs={{0,4},{4,0},{8,12},{12,8},{16,20},{20,16},{24,28},{28,24},{1,5},{5... | collective-permute-start | bytes 12296 | tf_op jit(solution)/shard_map/ppermute | solution.py:777
  50.4 11.3 %collective-permute-start.8 = (bf16[64,3072]{1,0:T(8,128)(2,1)S(1)}, bf16[64,3072]{1,0:T(8,128)(2,1)}, u32[]{:S(2)}, u32[]{:S(2)}) collective-permute-start(bf16[64,3072]{1,0:T(8,128)(2,1)S(1)} %slice.213), channel_id=1, source_target_pairs={{0,1},{1,0},{2,3},{3,2},{4,5},{5,4},{6,7},{7,6},{8,9},{9,8},{10,11... | collective-permute-start | bytes 1179656 | tf_op jit(solution)/shard_map/ppermute | solution.py:777
  51.9 10.9 %collective-permute-start.7 = (bf16[64,3072]{1,0:T(8,128)(2,1)S(1)}, bf16[64,3072]{1,0:T(8,128)(2,1)}, u32[]{:S(2)}, u32[]{:S(2)}) collective-permute-start(bf16[64,3072]{1,0:T(8,128)(2,1)S(1)} %slice.212), channel_id=1, source_target_pairs={{0,2},{1,3},{2,0},{3,1},{4,6},{5,7},{6,4},{7,5},{8,10},{9,11},{10,... | collective-permute-start | bytes 1179656 | tf_op jit(solution)/shard_map/ppermute | solution.py:777
  52.5 4.1 collective-permute-start.10
  56.5 4.6 collective-permute-start.11
  62.8 6.2 %collective-permute-start.12 = (bf16[128,3072]{1,0:T(8,128)(2,1)}, bf16[128,3072]{1,0:T(8,128)(2,1)}, u32[]{:S(2)}, u32[]{:S(2)}) collective-permute-start(bf16[128,3072]{1,0:T(8,128)(2,1)} %collective-permute-done.2.refs_1_), channel_id=1, source_target_pairs={{0,4},{4,0},{8,12},{12,8},{16,20},{20,16},{24,28},{28,24},{1,5},{5... | collective-permute-start | bytes 2359304 | tf_op jit(solution)/shard_map/ppermute | solution.py:777
  62.8 7.7 %collective-permute-start.13 = (bf16[128,3072]{1,0:T(8,128)(2,1)}, bf16[128,3072]{1,0:T(8,128)(2,1)}, u32[]{:S(2)}, u32[]{:S(2)}) collective-permute-start(bf16[128,3072]{1,0:T(8,128)(2,1)} %collective-permute-done.3.refs_2_), channel_id=1, source_target_pairs={{0,4},{4,0},{8,12},{12,8},{16,20},{20,16},{24,28},{28,24},{1,5},{5... | collective-permute-start | bytes 2359304 | tf_op jit(solution)/shard_map/ppermute | solution.py:777
  63.3 5.2 collective-permute-start.15
  63.8 33.4 %collective-permute-start.20 = (bf16[128,4096]{1,0:T(8,128)(2,1)S(1)}, bf16[128,4096]{1,0:T(8,128)(2,1)S(1)}, u32[]{:S(2)}, u32[]{:S(2)}) collective-permute-start(bf16[128,4096]{1,0:T(8,128)(2,1)S(1)} %constant_dynamic-slice_fusion.1), channel_id=1, source_target_pairs={{0,2},{1,3},{2,0},{3,1},{4,6},{5,7},{6,4},{7,5},{8,10},{9,11},{10,... | collective-permute-start | bytes 3145736 | tf_op jit(solution)/shard_map/ppermute | solution.py:777
  67.1 27.4 %collective-permute-start.16 = (bf16[128,1024]{1,0:T(8,128)(2,1)S(1)}, bf16[128,1024]{1,0:T(8,128)(2,1)S(1)}, u32[]{:S(2)}, u32[]{:S(2)}) collective-permute-start(bf16[128,1024]{1,0:T(8,128)(2,1)S(1)} %constant_dynamic-slice_fusion.2), channel_id=1, source_target_pairs={{0,2},{1,3},{2,0},{3,1},{4,6},{5,7},{6,4},{7,5},{8,10},{9,11},{10,... | collective-permute-start | bytes 786440 | tf_op jit(solution)/shard_map/ppermute | solution.py:777
  68.5 26.0 %collective-permute-start.6 = (bf16[128,1024]{1,0:T(8,128)(2,1)S(1)}, bf16[128,1024]{1,0:T(8,128)(2,1)S(1)}, u32[]{:S(2)}, u32[]{:S(2)}) collective-permute-start(bf16[128,1024]{1,0:T(8,128)(2,1)S(1)} %constant_dynamic-slice_fusion.2), channel_id=1, source_target_pairs={{0,1},{1,0},{2,3},{3,2},{4,5},{5,4},{6,7},{7,6},{8,9},{9,8},{10,11... | collective-permute-start | bytes 786440 | tf_op jit(solution)/shard_map/ppermute | solution.py:777
  69.1 47.9 %collective-permute-start.19 = (bf16[128,4096]{1,0:T(8,128)(2,1)S(1)}, bf16[128,4096]{1,0:T(8,128)(2,1)}, u32[]{:S(2)}, u32[]{:S(2)}) collective-permute-start(bf16[128,4096]{1,0:T(8,128)(2,1)S(1)} %constant_dynamic-slice_fusion.1), channel_id=1, source_target_pairs={{0,1},{1,0},{2,3},{3,2},{4,5},{5,4},{6,7},{7,6},{8,9},{9,8},{10,11... | collective-permute-start | bytes 3145736 | tf_op jit(solution)/shard_map/ppermute | solution.py:777
  94.5 29.4 %collective-permute-start.22 = (bf16[512,1024]{1,0:T(8,128)(2,1)S(1)}, bf16[512,1024]{1,0:T(8,128)(2,1)}, u32[]{:S(2)}, u32[]{:S(2)}) collective-permute-start(bf16[512,1024]{1,0:T(8,128)(2,1)S(1)} %constant_dynamic-slice_fusion), channel_id=1, source_target_pairs={{0,2},{1,3},{2,0},{3,1},{4,6},{5,7},{6,4},{7,5},{8,10},{9,11},{10,... | collective-permute-start | bytes 3145736 | tf_op jit(solution)/shard_map/ppermute | solution.py:777
  95.1 28.8 %collective-permute-start.21 = (bf16[512,1024]{1,0:T(8,128)(2,1)S(1)}, bf16[512,1024]{1,0:T(8,128)(2,1)}, u32[]{:S(2)}, u32[]{:S(2)}) collective-permute-start(bf16[512,1024]{1,0:T(8,128)(2,1)S(1)} %constant_dynamic-slice_fusion), channel_id=1, source_target_pairs={{0,1},{1,0},{2,3},{3,2},{4,5},{5,4},{6,7},{7,6},{8,9},{9,8},{10,11... | collective-permute-start | bytes 3145736 | tf_op jit(solution)/shard_map/ppermute | solution.py:777
  95.7 28.3 %collective-permute-start.18 = (bf16[64,1024]{1,0:T(8,128)(2,1)S(1)}, bf16[64,1024]{1,0:T(8,128)(2,1)S(1)}, u32[]{:S(2)}, u32[]{:S(2)}) collective-permute-start(bf16[64,1024]{1,0:T(8,128)(2,1)S(1)} %slice.219), channel_id=1, source_target_pairs={{0,1},{1,0},{2,3},{3,2},{4,5},{5,4},{6,7},{7,6},{8,9},{9,8},{10,11... | collective-permute-start | bytes 393224 | tf_op jit(solution)/shard_map/ppermute | solution.py:777
  97.2 26.7 %collective-permute-start.17 = (bf16[64,1024]{1,0:T(8,128)(2,1)S(1)}, bf16[64,1024]{1,0:T(8,128)(2,1)S(1)}, u32[]{:S(2)}, u32[]{:S(2)}) collective-permute-start(bf16[64,1024]{1,0:T(8,128)(2,1)S(1)} %slice.218), channel_id=1, source_target_pairs={{0,2},{1,3},{2,0},{3,1},{4,6},{5,7},{6,4},{7,5},{8,10},{9,11},{10,... | collective-permute-start | bytes 393224 | tf_op jit(solution)/shard_map/ppermute | solution.py:777
  124.0 7.5 %collective-permute-start.23 = (bf16[128,1024]{1,0:T(8,128)(2,1)S(1)}, bf16[128,1024]{1,0:T(8,128)(2,1)S(1)}, u32[]{:S(2)}, u32[]{:S(2)}) collective-permute-start(bf16[128,1024]{1,0:T(8,128)(2,1)S(1)} %collective-permute-done.6.refs_1_), channel_id=1, source_target_pairs={{0,4},{4,0},{8,12},{12,8},{16,20},{20,16},{24,28},{28,24},{1,5},{5... | collective-permute-start | bytes 786440 | tf_op jit(solution)/shard_map/ppermute | solution.py:777
  124.0 4.9 collective-permute-start.25
  124.5 5.5 collective-permute-start.26
  124.6 26.1 %collective-permute-start.24 = (bf16[128,1024]{1,0:T(8,128)(2,1)S(1)}, bf16[128,1024]{1,0:T(8,128)(2,1)S(1)}, u32[]{:S(2)}, u32[]{:S(2)}) collective-permute-start(bf16[128,1024]{1,0:T(8,128)(2,1)S(1)} %collective-permute-done.16.refs_2_), channel_id=1, source_target_pairs={{0,4},{4,0},{8,12},{12,8},{16,20},{20,16},{24,28},{28,24},{1,5},{5... | collective-permute-start | bytes 786440 | tf_op jit(solution)/shard_map/ppermute | solution.py:777
  128.4 22.4 %collective-permute-start.30 = (bf16[256,1024]{1,0:T(8,128)(2,1)S(1)}, bf16[256,1024]{1,0:T(8,128)(2,1)S(1)}, u32[]{:S(2)}, u32[]{:S(2)}) collective-permute-start(bf16[256,1024]{1,0:T(8,128)(2,1)S(1)} %slice.223), channel_id=1, source_target_pairs={{0,1},{1,0},{2,3},{3,2},{4,5},{5,4},{6,7},{7,6},{8,9},{9,8},{10,11... | collective-permute-start | bytes 1572872 | tf_op jit(solution)/shard_map/ppermute | solution.py:777
  129.0 21.8 %collective-permute-start.29 = (bf16[256,1024]{1,0:T(8,128)(2,1)S(1)}, bf16[256,1024]{1,0:T(8,128)(2,1)S(1)}, u32[]{:S(2)}, u32[]{:S(2)}) collective-permute-start(bf16[256,1024]{1,0:T(8,128)(2,1)S(1)} %slice.222), channel_id=1, source_target_pairs={{0,2},{1,3},{2,0},{3,1},{4,6},{5,7},{6,4},{7,5},{8,10},{9,11},{10,... | collective-permute-start | bytes 1572872 | tf_op jit(solution)/shard_map/ppermute | solution.py:777
  130.0 23.5 %collective-permute-start.28 = (bf16[64,4096]{1,0:T(8,128)(2,1)S(1)}, bf16[64,4096]{1,0:T(8,128)(2,1)S(1)}, u32[]{:S(2)}, u32[]{:S(2)}) collective-permute-start(bf16[64,4096]{1,0:T(8,128)(2,1)S(1)} %slice.221), channel_id=1, source_target_pairs={{0,1},{1,0},{2,3},{3,2},{4,5},{5,4},{6,7},{7,6},{8,9},{9,8},{10,11... | collective-permute-start | bytes 1572872 | tf_op jit(solution)/shard_map/ppermute | solution.py:777
  131.5 22.4 %collective-permute-start.27 = (bf16[64,4096]{1,0:T(8,128)(2,1)S(1)}, bf16[64,4096]{1,0:T(8,128)(2,1)}, u32[]{:S(2)}, u32[]{:S(2)}) collective-permute-start(bf16[64,4096]{1,0:T(8,128)(2,1)S(1)} %slice.220), channel_id=1, source_target_pairs={{0,2},{1,3},{2,0},{3,1},{4,6},{5,7},{6,4},{7,5},{8,10},{9,11},{10,... | collective-permute-start | bytes 1572872 | tf_op jit(solution)/shard_map/ppermute | solution.py:777
  154.4 5.1 collective-permute-start.38
  154.4 18.0 %collective-permute-start.36 = (bf16[512,1024]{1,0:T(8,128)(2,1)}, bf16[512,1024]{1,0:T(8,128)(2,1)S(1)}, u32[]{:S(2)}, u32[]{:S(2)}) collective-permute-start(bf16[512,1024]{1,0:T(8,128)(2,1)} %collective-permute-done.22.refs_2_), channel_id=1, source_target_pairs={{0,4},{4,0},{8,12},{12,8},{16,20},{20,16},{24,28},{28,24},{1,5},{5... | collective-permute-start | bytes 3145736 | tf_op jit(solution)/shard_map/ppermute | solution.py:777
  155.0 17.5 %collective-permute-start.35 = (bf16[512,1024]{1,0:T(8,128)(2,1)}, bf16[512,1024]{1,0:T(8,128)(2,1)S(1)}, u32[]{:S(2)}, u32[]{:S(2)}) collective-permute-start(bf16[512,1024]{1,0:T(8,128)(2,1)} %collective-permute-done.21.refs_1_), channel_id=1, source_target_pairs={{0,4},{4,0},{8,12},{12,8},{16,20},{20,16},{24,28},{28,24},{1,5},{5... | collective-permute-start | bytes 3145736 | tf_op jit(solution)/shard_map/ppermute | solution.py:777
  155.8 16.6 %collective-permute-start.32 = (bf16[128,4096]{1,0:T(8,128)(2,1)S(1)}, bf16[128,4096]{1,0:T(8,128)(2,1)}, u32[]{:S(2)}, u32[]{:S(2)}) collective-permute-start(bf16[128,4096]{1,0:T(8,128)(2,1)S(1)} %collective-permute-done.20.refs_2_), channel_id=1, source_target_pairs={{0,4},{4,0},{8,12},{12,8},{16,20},{20,16},{24,28},{28,24},{1,5},{5... | collective-permute-start | bytes 3145736 | tf_op jit(solution)/shard_map/ppermute | solution.py:777
  157.3 15.1 %collective-permute-start.31 = (bf16[128,4096]{1,0:T(8,128)(2,1)}, bf16[128,4096]{1,0:T(8,128)(2,1)}, u32[]{:S(2)}, u32[]{:S(2)}) collective-permute-start(bf16[128,4096]{1,0:T(8,128)(2,1)} %collective-permute-done.19.refs_1_), channel_id=1, source_target_pairs={{0,4},{4,0},{8,12},{12,8},{16,20},{20,16},{24,28},{28,24},{1,5},{5... | collective-permute-start | bytes 3145736 | tf_op jit(solution)/shard_map/ppermute | solution.py:777
  159.6 12.8 %collective-permute-start.33 = (bf16[64,4096]{1,0:T(8,128)(2,1)}, bf16[64,4096]{1,0:T(8,128)(2,1)}, u32[]{:S(2)}, u32[]{:S(2)}) collective-permute-start(bf16[64,4096]{1,0:T(8,128)(2,1)} %collective-permute-done.27.refs_3_), channel_id=1, source_target_pairs={{0,4},{4,0},{8,12},{12,8},{16,20},{20,16},{24,28},{28,24},{1,5},{5... | collective-permute-start | bytes 1572872 | tf_op jit(solution)/shard_map/ppermute | solution.py:777
  239.1 19.2 %collective-permute-start.39 = (bf16[4,512,1024]{2,1,0:T(8,128)(2,1)}, bf16[4,512,1024]{2,1,0:T(8,128)(2,1)}, u32[]{:S(2)}, u32[]{:S(2)}) collective-permute-start(bf16[4,512,1024]{2,1,0:T(8,128)(2,1)} %get-tuple-element.344), channel_id=1, source_target_pairs={{0,4},{4,0},{8,12},{12,8},{16,20},{20,16},{24,28},{28,24},{1,5},{5... | collective-permute-start | bytes 12582920 | tf_op jit(solution)/shard_map/ppermute | solution.py:777
  264.6 140.3 %reduce-scatter.9.cloned.1.call-start = ((), (), s32[]{:S(2)}) async-start(), calls=%async_computation.4 | async-start | bytes 6553600
  307.9 9.1 %collective-permute-start.40 = (bf16[4,128,5120]{2,1,0:T(8,128)(2,1)}, bf16[4,128,5120]{2,1,0:T(8,128)(2,1)}, u32[]{:S(2)}, u32[]{:S(2)}) collective-permute-start(bf16[4,128,5120]{2,1,0:T(8,128)(2,1)} %get-tuple-element.360), channel_id=1, source_target_pairs={{0,4},{4,0},{8,12},{12,8},{16,20},{20,16},{24,28},{28,24},{1,5},{5... | collective-permute-start | bytes 15728648 | tf_op jit(solution)/shard_map/ppermute | solution.py:777
  323.8 193.8 %all-reduce.5.cloned.1.call-start = ((), (), s32[]{:S(2)}) async-start(), calls=%async_computation.2 | async-start | bytes 2621440 | tf_op jit(solution)/shard_map/psum | solution.py:888
  325.6 25.2 %collective-permute-start.42 = (bf16[512,1024]{1,0:T(8,128)(2,1)S(1)}, bf16[512,1024]{1,0:T(8,128)(2,1)S(1)}, u32[]{:S(2)}, u32[]{:S(2)}) collective-permute-start(bf16[512,1024]{1,0:T(8,128)(2,1)S(1)} %get-tuple-element.438), channel_id=1, source_target_pairs={{4,0},{8,4},{12,8},{16,12},{20,16},{24,20},{28,24},{5,1},{9,5},{13... | collective-permute-start | bytes 3145736 | tf_op jit(solution)/shard_map/ppermute | solution.py:1058
  326.9 23.9 %collective-permute-start.41 = (bf16[512,1024]{1,0:T(8,128)(2,1)S(1)}, bf16[512,1024]{1,0:T(8,128)(2,1)S(1)}, u32[]{:S(2)}, u32[]{:S(2)}) collective-permute-start(bf16[512,1024]{1,0:T(8,128)(2,1)S(1)} %get-tuple-element.439), channel_id=1, source_target_pairs={{0,4},{4,8},{8,12},{12,16},{16,20},{20,24},{24,28},{1,5},{5,9},{9,... | collective-permute-start | bytes 3145736 | tf_op jit(solution)/shard_map/ppermute | solution.py:1057
  330.0 6.3 %collective-permute-start.43 = (f32[2,4,8,512]{3,2,1,0:T(8,128)S(1)}, f32[2,4,8,512]{3,2,1,0:T(8,128)S(1)}, u32[]{:S(2)}, u32[]{:S(2)}) collective-permute-start(f32[2,4,8,512]{3,2,1,0:T(8,128)S(1)} %get-tuple-element.458), channel_id=1, source_target_pairs={{0,4},{4,8},{8,12},{12,16},{16,20},{20,24},{24,28},{1,5},{5,9},{9,... | collective-permute-start | bytes 393224 | tf_op jit(solution)/shard_map/ppermute | solution.py:1057
  338.5 51.1 %collective-permute-start.45 = (bf16[512,1024]{1,0:T(8,128)(2,1)S(1)}, bf16[512,1024]{1,0:T(8,128)(2,1)S(1)}, u32[]{:S(2)}, u32[]{:S(2)}) collective-permute-start(bf16[512,1024]{1,0:T(8,128)(2,1)S(1)} %bitcast.144), channel_id=1, source_target_pairs={{0,8},{4,12},{24,16},{28,20},{1,9},{5,13},{25,17},{29,21},{2,10},{... | collective-permute-start | bytes 3145736 | tf_op jit(solution)/shard_map/ppermute | solution.py:854
  390.1 14.4 %collective-permute-start.46 = (bf16[512,1024]{1,0:T(8,128)(2,1)S(1)}, bf16[512,1024]{1,0:T(8,128)(2,1)S(1)}, u32[]{:S(2)}, u32[]{:S(2)}) collective-permute-start(bf16[512,1024]{1,0:T(8,128)(2,1)S(1)} %add_convert_fusion.3), channel_id=1, source_target_pairs={{8,16},{12,20},{16,8},{20,12},{9,17},{13,21},{17,9},{21,13},{10,18... | collective-permute-start | bytes 3145736 | tf_op jit(solution)/shard_map/ppermute | solution.py:854
  399.3 43.1 %collective-permute-start.47 = (bf16[4,128,1536]{2,1,0:T(8,128)(2,1)}, bf16[4,128,1536]{2,1,0:T(8,128)(2,1)}, u32[]{:S(2)}, u32[]{:S(2)}) collective-permute-start(bf16[4,128,1536]{2,1,0:T(8,128)(2,1)} %get-tuple-element.384), channel_id=1, source_target_pairs={{0,4},{4,0},{8,12},{12,8},{16,20},{20,16},{24,28},{28,24},{1,5},{5... | collective-permute-start | bytes 4718600 | tf_op jit(solution)/shard_map/ppermute | solution.py:777
  444.2 16.2 %collective-permute-start.49 = (bf16[2,64,1536]{2,1,0:T(8,128)(2,1)S(1)}, bf16[2,64,1536]{2,1,0:T(8,128)(2,1)S(1)}, u32[]{:S(2)}, u32[]{:S(2)}) collective-permute-start(bf16[2,64,1536]{2,1,0:T(8,128)(2,1)S(1)} %slice_bitcast_fusion.6), channel_id=1, source_target_pairs={{0,2},{1,3},{2,0},{3,1},{4,6},{5,7},{6,4},{7,5},{8,10},{9,11},{10,... | collective-permute-start | bytes 1179656 | tf_op jit(solution)/shard_map/ppermute | solution.py:777
  448.5 12.1 %collective-permute-start.48 = (bf16[2,64,1536]{2,1,0:T(8,128)(2,1)S(1)}, bf16[2,64,1536]{2,1,0:T(8,128)(2,1)S(1)}, u32[]{:S(2)}, u32[]{:S(2)}) collective-permute-start(bf16[2,64,1536]{2,1,0:T(8,128)(2,1)S(1)} %slice_bitcast_fusion.8), channel_id=1, source_target_pairs={{0,1},{1,0},{2,3},{3,2},{4,5},{5,4},{6,7},{7,6},{8,9},{9,8},{10,11... | collective-permute-start | bytes 1179656 | tf_op jit(solution)/shard_map/ppermute | solution.py:777
  448.6 61.2 %collective-permute-start.59 = (bf16[512,1024]{1,0:T(8,128)(2,1)S(1)}, bf16[512,1024]{1,0:T(8,128)(2,1)S(1)}, u32[]{:S(2)}, u32[]{:S(2)}) collective-permute-start(bf16[512,1024]{1,0:T(8,128)(2,1)S(1)} %fusion.1), channel_id=1, source_target_pairs={{8,0},{12,4},{16,24},{20,28},{9,1},{13,5},{17,25},{21,29},{10,2},{... | collective-permute-start | bytes 3145736 | tf_op jit(solution)/shard_map/ppermute | solution.py:854
  458.5 18.0 %collective-permute-start.50 = (bf16[4,128,1664]{2,1,0:T(8,128)(2,1)}, bf16[4,128,1664]{2,1,0:T(8,128)(2,1)S(1)}, u32[]{:S(2)}, u32[]{:S(2)}) collective-permute-start(bf16[4,128,1664]{2,1,0:T(8,128)(2,1)} %get-tuple-element.398), channel_id=1, source_target_pairs={{0,4},{4,0},{8,12},{12,8},{16,20},{20,16},{24,28},{28,24},{1,5},{5... | collective-permute-start | bytes 5111816 | tf_op jit(solution)/shard_map/ppermute | solution.py:777
  460.7 15.6 %collective-permute-start.52 = (bf16[1,64,1536]{2,1,0:T(8,128)(2,1)S(1)}, bf16[1,64,1536]{2,1,0:T(8,128)(2,1)S(1)}, u32[]{:S(2)}, u32[]{:S(2)}) collective-permute-start(bf16[1,64,1536]{2,1,0:T(8,128)(2,1)S(1)} %slice_bitcast_fusion.14), channel_id=1, source_target_pairs={{0,1},{1,0},{2,3},{3,2},{4,5},{5,4},{6,7},{7,6},{8,9},{9,8},{10,11... | collective-permute-start | bytes 589832 | tf_op jit(solution)/shard_map/ppermute | solution.py:777
  462.5 13.8 %collective-permute-start.51 = (bf16[1,64,1536]{2,1,0:T(8,128)(2,1)S(1)}, bf16[1,64,1536]{2,1,0:T(8,128)(2,1)S(1)}, u32[]{:S(2)}, u32[]{:S(2)}) collective-permute-start(bf16[1,64,1536]{2,1,0:T(8,128)(2,1)S(1)} %slice_bitcast_fusion.16), channel_id=1, source_target_pairs={{0,2},{1,3},{2,0},{3,1},{4,6},{5,7},{6,4},{7,5},{8,10},{9,11},{10,... | collective-permute-start | bytes 589832 | tf_op jit(solution)/shard_map/ppermute | solution.py:777
  478.2 26.6 %collective-permute-start.55 = (bf16[128,1536]{1,0:T(8,128)(2,1)S(1)}, bf16[128,1536]{1,0:T(8,128)(2,1)S(1)}, u32[]{:S(2)}, u32[]{:S(2)}) collective-permute-start(bf16[128,1536]{1,0:T(8,128)(2,1)S(1)} %pad_maximum_fusion.6), channel_id=1, source_target_pairs={{0,8},{4,12},{24,16},{28,20},{1,9},{5,13},{25,17},{29,21},{2,10},{... | collective-permute-start | bytes 1179656 | tf_op jit(solution)/shard_map/ppermute | solution.py:854
  497.0 11.0 %collective-permute-start.53 = (bf16[2,64,1664]{2,1,0:T(8,128)(2,1)S(1)}, bf16[2,64,1664]{2,1,0:T(8,128)(2,1)S(1)}, u32[]{:S(2)}, u32[]{:S(2)}) collective-permute-start(bf16[2,64,1664]{2,1,0:T(8,128)(2,1)S(1)} %slice_bitcast_fusion.4), channel_id=1, source_target_pairs={{0,1},{1,0},{2,3},{3,2},{4,5},{5,4},{6,7},{7,6},{8,9},{9,8},{10,11... | collective-permute-start | bytes 1277960 | tf_op jit(solution)/shard_map/ppermute | solution.py:777
  498.8 10.7 %collective-permute-start.54 = (bf16[2,64,1664]{2,1,0:T(8,128)(2,1)S(1)}, bf16[2,64,1664]{2,1,0:T(8,128)(2,1)S(1)}, u32[]{:S(2)}, u32[]{:S(2)}) collective-permute-start(bf16[2,64,1664]{2,1,0:T(8,128)(2,1)S(1)} %slice_bitcast_fusion.2), channel_id=1, source_target_pairs={{0,2},{1,3},{2,0},{3,1},{4,6},{5,7},{6,4},{7,5},{8,10},{9,11},{10,... | collective-permute-start | bytes 1277960 | tf_op jit(solution)/shard_map/ppermute | solution.py:777
  509.8 5.9 %collective-permute-start.56 = (bf16[1,64,1664]{2,1,0:T(8,128)(2,1)S(1)}, bf16[1,64,1664]{2,1,0:T(8,128)(2,1)S(1)}, u32[]{:S(2)}, u32[]{:S(2)}) collective-permute-start(bf16[1,64,1664]{2,1,0:T(8,128)(2,1)S(1)} %slice_bitcast_fusion.12), channel_id=1, source_target_pairs={{0,2},{1,3},{2,0},{3,1},{4,6},{5,7},{6,4},{7,5},{8,10},{9,11},{10,... | collective-permute-start | bytes 638984 | tf_op jit(solution)/shard_map/ppermute | solution.py:777
  511.6 5.8 collective-permute-start.57
  511.9 5.6 collective-permute-start.58
  517.7 19.7 %collective-permute-start.63 = (bf16[128,1536]{1,0:T(8,128)(2,1)S(1)}, bf16[128,1536]{1,0:T(8,128)(2,1)S(1)}, u32[]{:S(2)}, u32[]{:S(2)}) collective-permute-start(bf16[128,1536]{1,0:T(8,128)(2,1)S(1)} %fusion.6), channel_id=1, source_target_pairs={{8,0},{12,4},{16,24},{20,28},{9,1},{13,5},{17,25},{21,29},{10,2},{... | collective-permute-start | bytes 1179656 | tf_op jit(solution)/shard_map/ppermute | solution.py:854
  519.6 23.3 %collective-permute-start.60 = (bf16[128,1664]{1,0:T(8,128)(2,1)S(1)}, bf16[128,1664]{1,0:T(8,128)(2,1)S(1)}, u32[]{:S(2)}, u32[]{:S(2)}) collective-permute-start(bf16[128,1664]{1,0:T(8,128)(2,1)S(1)} %pad_maximum_fusion.5), channel_id=1, source_target_pairs={{0,8},{4,12},{8,0},{12,4},{16,24},{20,28},{24,16},{28,20},{1,9},{5... | collective-permute-start | bytes 1277960 | tf_op jit(solution)/shard_map/ppermute | solution.py:777
  528.1 32.9 %collective-permute-start.66 = (bf16[512,1024]{1,0:T(8,128)(2,1)S(1)}, bf16[512,1024]{1,0:T(8,128)(2,1)S(1)}, u32[]{:S(2)}, u32[]{:S(2)}) collective-permute-start(bf16[512,1024]{1,0:T(8,128)(2,1)S(1)} %broadcast_select_fusion.4), channel_id=1, source_target_pairs={{0,4},{4,0},{8,12},{12,8},{16,20},{20,16},{24,28},{28,24},{1,5},{5... | collective-permute-start | bytes 3145736 | tf_op jit(solution)/shard_map/ppermute | solution.py:777
  528.1 46.1 %collective-permute-start.65 = (bf16[128,5120]{1,0:T(8,128)(2,1)}, bf16[128,5120]{1,0:T(8,128)(2,1)}, u32[]{:S(2)}, u32[]{:S(2)}) collective-permute-start(bf16[128,5120]{1,0:T(8,128)(2,1)} %all-reduce.5.cloned.1.call-done), channel_id=1, source_target_pairs={{0,4},{4,0},{8,12},{12,8},{16,20},{20,16},{24,28},{28,24},{1,5},{5... | collective-permute-start | bytes 3932168 | tf_op jit(solution)/shard_map/ppermute | solution.py:777
  537.4 6.1 %collective-permute-start.64 = (bf16[128,1536]{1,0:T(8,128)(2,1)S(1)}, bf16[128,1536]{1,0:T(8,128)(2,1)S(1)}, u32[]{:S(2)}, u32[]{:S(2)}) collective-permute-start(bf16[128,1536]{1,0:T(8,128)(2,1)S(1)} %broadcast_select_fusion.7), channel_id=1, source_target_pairs={{0,4},{4,0},{8,12},{12,8},{16,20},{20,16},{24,28},{28,24},{1,5},{5... | collective-permute-start | bytes 1179656 | tf_op jit(solution)/shard_map/ppermute | solution.py:777
  543.0 17.8 %collective-permute-start.61 = (bf16[128,1664]{1,0:T(8,128)(2,1)S(1)}, bf16[128,1664]{1,0:T(8,128)(2,1)S(1)}, u32[]{:S(2)}, u32[]{:S(2)}) collective-permute-start(bf16[128,1664]{1,0:T(8,128)(2,1)S(1)} %add_convert_fusion.9), channel_id=1, source_target_pairs={{0,16},{4,20},{8,24},{12,28},{16,0},{20,4},{24,8},{28,12},{1,17},{... | collective-permute-start | bytes 1277960 | tf_op jit(solution)/shard_map/ppermute | solution.py:777
  (37 other events, 456.1 us)
Sparse Core Ops, SparseCore 0:
  264.7 55.1 reduce-scatter.6
  323.9 63.9 reduce-scatter.8
  405.1 81.0 all-reduce.4

commit v4 on v3

--- a/solution.py
+++ b/solution.py
@@ -290,9 +290,9 @@
 
 
 def attn_bwd_kernel(
-    lo_ref, hi_ref, q_ref, before_ref, do_ref, behind_ref, k_ref, kt_ref, v_ref, stats_ref, idq_ref, idk_ref,
-    dq_ref, joined_ref, qs, dos, qst, dost, dk_acc, dv_acc, dq_acc,
+    lo_ref, hi_ref, q_ref, before_ref, do_ref, behind_ref, k_ref, kt_ref, v_ref, stats_ref, idq_ref, idk_ref, *refs
 ):
+    dq_ref, joined_ref, qs, dos, qst, dost, dk_acc, dv_acc, dq_acc = refs[-9:]
     t = pl.program_id(1)
     low, high = lo_ref[t], hi_ref[t]
     end = pl.num_programs(1) - RIM
@@ -352,9 +352,9 @@
         joined_ref[1] = dv_acc[...].astype(bf16)
 
 
-def attn_bwd(lo, hi, q_near, before, do, behind, k_near, kt_near, v_near, stats, idq_rows, idk_col, side, quads):
+def attn_bwd(lo, hi, q_near, before, do, behind, k_near, kt_near, v_near, stats, idq_rows, idk_col, side, begin=0, quads=2, so_far=()):
     rows, span = do.shape[0], k_near.shape[0]
-    tiles, first = rows // TILE, side * quads
+    tiles, first = rows // TILE, 2 * side + begin
     near = pl.BlockSpec((span, 256), lambda g, t, *_: (0, g + first))
     return pl.pallas_call(
         attn_bwd_kernel,
@@ -372,10 +372,11 @@
                 pl.BlockSpec((2, 1, 8, TILE), lambda g, t, *_: (0, g + first, 0, t)),
                 pl.BlockSpec((1, 1, TILE), lambda g, t, *_: (t, 0, 0)),
                 pl.BlockSpec((span, 1), lambda g, t, *_: (0, 0)),
-            ],
+            ]
+            + [pl.BlockSpec(memory_space=pl.ANY)] * len(so_far),
             out_specs=[
-                pl.BlockSpec((TILE, 256), lambda g, t, *_: (jnp.clip(t - RIM, 0, tiles - 1), g)),
-                pl.BlockSpec((2, rows, 256), lambda g, t, *_: (0, 0, g)),
+                pl.BlockSpec((TILE, 256), lambda g, t, *_: (jnp.clip(t - RIM, 0, tiles - 1), g + begin)),
+                pl.BlockSpec((2, rows, 256), lambda g, t, *_: (0, 0, g + begin)),
             ],
             scratch_shapes=[
                 pltpu.VMEM((4 * TILE, 256), bf16),
@@ -387,11 +388,12 @@
                 pltpu.VMEM((256, TILE), f32),
             ],
         ),
-        out_shape=[sds((rows, quads * 256), bf16), sds((2, rows, quads * 256), bf16)],
+        out_shape=[sds((rows, 512), bf16), sds((2, rows, 512), bf16)],
+        input_output_aliases={12 + i: i for i in range(len(so_far))},
         compiler_params=params(),
         cost_estimate=cost(quads * 15 * 10**9, 2**22),
         name="attn_backward",
-    )(lo, hi, q_near, before, do, behind, k_near, kt_near, v_near, stats, idq_rows, idk_col)
+    )(lo, hi, q_near, before, do, behind, k_near, kt_near, v_near, stats, idq_rows, idk_col, *so_far)
 
 
 def norm_stats(hidden):
@@ -1061,24 +1063,25 @@
     do_before, do_behind = rims(d_context, 0)
     stats_before, stats_behind = rims(stats, 3)
     stats = jnp.concatenate([stats_before, stats, stats_behind], axis=3)
-    def attend_back(side, tie):
+    def attend_back(tie, *part):
         return attn_bwd(
-            tie, high_tile, query, do_before, d_context, do_behind, keys, keys_t, values, stats, idq, idk, side, 2
+            tie, high_tile, query, do_before, d_context, do_behind, keys, keys_t, values, stats, idq, idk, *part
         )
 
-    parts_a = attend_back(0, boundary(d_context, low_tile, outer, inner))
+    parts_a = attend_back(boundary(d_context, low_tile, outer, inner), 0, 0, 1)
+    parts_a = attend_back(boundary(parts_a[0], low_tile, outer), 0, 1, 1, parts_a)
     *first_pair, sums_a = qkv_gradient(boundary(parts_a[0], order, outer), tokens, *parts_a, n_fsdp)
     first = Staged(reduction, *first_pair, parity)
-    parts_b = attend_back(1, boundary(first_pair[0], low_tile, outer, inner))
+    parts_b = attend_back(boundary(first_pair[0], low_tile, inner, hold=[outer]), 1)
     riders = [(final_sums, 4), (attn_sums, 3), (bias_a, 1), (bias_b, 1), (sums_a, 1)]
     *last_pair, sums_b = qkv_gradient(
-        boundary(parts_b[0], order, first, hold=[outer]), tokens, *parts_b, n_fsdp, riders
+        boundary(parts_b[0], order, first, outer), tokens, *parts_b, n_fsdp, riders
     )
     last = Staged(reduction, *last_pair, parity, True)
     input_grad = input_back(d_sum_one, (*parts_a, *parts_b), boundary(last_pair[0], w_qkv, first))
-    boundary(input_grad, where, last, first)
+    boundary(input_grad, where, last, first, inner)
     boundary(last.values[0], where, last, first)
-    boundary(last.values[0], where, last, first, outer, inner)
+    boundary(last.values[0], where, last, first)
     outer_grad, inner_grad, first, last = (transfer.result()[0] for transfer in (outer, inner, first, last))
     vectors = last[: part // 2, 3 * D // 2 :].reshape(16, D)
     query_sum, value_sum = vectors[11:13].reshape(2, 2, D // 2).transpose(1, 0, 2).reshape(2, D)

time: 593 us -> 577 us (0.973)
  starting transfers between devices: 116 us -> 88.1 us
  waiting for transfers between devices: 69.8 us -> 97.3 us
  Pallas kernels: 313 us -> 294 us
    ppermute x6, waiting for transfers between devices: 13 us -> 37.1 us  [move(): return arrive(gate, lax.ppermute(value, 'ctx', pairs))]
    ppermute x6, starting transfers between devices: 35 us -> 19.2 us  [move(): return arrive(gate, lax.ppermute(value, 'ctx', pairs))]
    ppermute x55, starting transfers between devices: 65.1 us -> 52.6 us  [swap(): lax.ppermute(value, axis, [(i, i ^ bit) for i in range(lax.axis_size(axis...]
    pallas_call x2 -> x3, Pallas kernels: 74.9 us -> 63.3 us  [attn_bwd(): pl.pallas_call(attn_bwd_kernel, grid_spec=pltpu.PrefetchScalarGridSpec(nu...]
    pallas_call x2, Pallas kernels: 36.4 us -> 30 us  [attn_fwd(): pl.pallas_call(attn_fwd_kernel, grid_spec=pltpu.PrefetchScalarGridSpec(nu...]
    unnamed x71 -> x73, local copies, waits for them, and re-layouts: 12.2 us -> 12.4 us
  transfers between devices with their start and end apart: 70 -> 70, of which waited for: 22 -> 26; matrix products, arithmetic and copies ran while one was open for 8% -> 8% of each run, Pallas kernels for 41% -> 39%
where the time goes in v4:
time: 577 us; the launch traced here: 571 us
  Pallas kernels  294 us (51%)
  waiting for transfers between devices  97.3 us (17%)
  starting transfers between devices  88.1 us (15%)
  local copies, waits for them, and re-layouts  35.3 us (6%)
  other arithmetic  34.2 us (6%)
  between operations  22.1 us (4%)
    pallas_call x3, Pallas kernels, attn_bwd(): pl.pallas_call(attn_bwd_kernel, grid_spec=pltpu.PrefetchScalarGridSpec(nu...  63.3 us
    ppermute x55, waiting for transfers between devices, swap(): lax.ppermute(value, axis, [(i, i ^ bit) for i in range(lax.axis_size(axis...  59.4 us
    ppermute x55, starting transfers between devices, swap(): lax.ppermute(value, axis, [(i, i ^ bit) for i in range(lax.axis_size(axis...  52.6 us
    ppermute x6, waiting for transfers between devices, move(): return arrive(gate, lax.ppermute(value, 'ctx', pairs))  37.1 us
    pallas_call x2, Pallas kernels, gram(): pl.pallas_call(functools.partial(gram_kernel, [len(group) - 1 for group i...  32.5 us
    pallas_call x2, Pallas kernels, attn_fwd(): pl.pallas_call(attn_fwd_kernel, grid_spec=pltpu.PrefetchScalarGridSpec(nu...  30 us
    pallas_call x1, Pallas kernels, inner_forward(): pl.pallas_call(functools.partial(inner_kernel, len(pieces)), grid=(FF //...  30 us
    pallas_call x1, Pallas kernels, feed_back(): pl.pallas_call(feed_back_last_kernel, in_specs=in_specs + [whole, pl.Bloc...  24.6 us
  transfers between devices with their start and end apart: 70, of which 26 were waited for; matrix products, arithmetic and copies ran while one was open for 8% of the time, Pallas kernels for 39%

profile of v4, /device:TPU:0, one launch (start us, length us, event | category | flops | bytes accessed | tf_op | source)
XLA Modules:
  0.0 571.3 jit_solution(262933116196403330)
XLA Ops:
  7.8 2.9 pack_shards.1
  10.8 3.0 collective-permute-start.3
  13.7 1.5 collective-permute-start.2
  27.4 1.7 slice_bitcast_fusion
  30.4 4.0 collective-permute-start
  37.8 2.7 collective-permute-done.5
  42.5 5.8 %collective-permute-start.9 = (f32[8,128]{1,0:T(8,128)S(1)}, f32[8,128]{1,0:T(8,128)S(1)}, u32[]{:S(2)}, u32[]{:S(2)}) collective-permute-start(f32[8,128]{1,0:T(8,128)S(1)} %broadcast_in_dim.25), channel_id=1, source_target_pairs={{0,4},{4,0},{8,12},{12,8},{16,20},{20,16},{24,28},{28,24},{1,5},{5... | collective-permute-start | bytes 12296 | tf_op jit(solution)/shard_map/ppermute | solution.py:779
  50.4 1.6 collective-permute-start.8
  52.5 2.5 collective-permute-start.10
  54.9 1.6 collective-permute-done.10
  56.5 3.0 collective-permute-start.11
  69.1 1.5 collective-permute-start.19
  70.6 21.9 %project_qkv.1 = (bf16[2048,1024]{1,0:T(8,128)(2,1)}, bf16[2048,1024]{1,0:T(8,128)(2,1)}, bf16[2048,1024]{1,0:T(8,128)(2,1)}, bf16[1024,2048]{1,0:T(8,128)(2,1)}...) custom-call(s32[2]{0:T(128)} %pad_add_fusion.where_ref.tie_ref, bf16[256,3072]{1,0:T(8,128)(2,1)} %get-tuple-element.230.refs_0_, ...), custom_call_target="tpu_custom_call" | custom-call | flops 10737418240 | bytes 31457280 | tf_op jit(solution)/shard_map/project_qkv/pallas_call | solution.py:173
  92.5 2.0 collective-permute-done.16.refs_2_
  95.7 1.6 collective-permute-start.18
  97.2 1.5 collective-permute-start.17
  98.7 15.0 %attn_forward.2 = (bf16[1024,1024]{1,0:T(8,128)(2,1)}, f32[4,8,1024]{2,1,0:T(8,128)}) custom-call(s32[8]{0:T(128)} %get-tuple-element.386.lo_ref, s32[8]{0:T(128)} %get-tuple-element.254.hi_ref, bf16[2048,1024]{1,0:T(8,128)(2,1)} %get-tuple-element.248.q_ref, bf16[2048,1024]{1,0:T(8,128)(2,1)} %get-tuple-element.255.k_ref, ...), custom_call_target="tpu_custom_call" | custom-call | flops 20000000000 | bytes 2097152 | tf_op jit(solution)/shard_map/attn_forward/pallas_call | solution.py:260
  113.8 10.1 %collective-permute-done.18.refs_4_ = bf16[64,1024]{1,0:T(8,128)(2,1)S(1)} collective-permute-done((bf16[64,1024]{1,0:T(8,128)(2,1)S(1)}, bf16[64,1024]{1,0:T(8,128)(2,1)S(1)}, u32[]{:S(2)}, u32[]{:S(2)}) %collective-permute-start.18) | collective-permute-done | bytes 131104 | tf_op jit(solution)/shard_map/ppermute | solution.py:779
  130.0 1.5 collective-permute-start.28
  132.5 15.0 %attn_forward.3 = (bf16[1024,1024]{1,0:T(8,128)(2,1)}, f32[4,8,1024]{2,1,0:T(8,128)}) custom-call(s32[8]{0:T(128)} %get-tuple-element.386.lo_ref, s32[8]{0:T(128)} %get-tuple-element.254.hi_ref, bf16[2048,1024]{1,0:T(8,128)(2,1)} %get-tuple-element.248.q_ref, ...), custom_call_target="tpu_custom_call", output_to_operand_aliasing={{0}: (7, {}), {1}: (8, {})} | custom-call | flops 20000000000 | bytes 2097152 | tf_op jit(solution)/shard_map/attn_forward/pallas_call | solution.py:260
  147.5 6.0 %collective-permute-done.28.refs_4_ = bf16[64,4096]{1,0:T(8,128)(2,1)S(1)} collective-permute-done((bf16[64,4096]{1,0:T(8,128)(2,1)S(1)}, bf16[64,4096]{1,0:T(8,128)(2,1)S(1)}, u32[]{:S(2)}, u32[]{:S(2)}) %collective-permute-start.28) | collective-permute-done | bytes 524320 | tf_op jit(solution)/shard_map/ppermute | solution.py:779
  157.5 2.1 collective-permute-done.38.refs_8_
  162.9 9.7 %mix_and_norm.1 = (f32[1024,1024]{1,0:T(8,128)}, bf16[1024,1024]{1,0:T(8,128)(2,1)}, f32[1024,1]{1,0:T(8,128)}, bf16[1024,1024]{1,0:T(8,128)(2,1)}) custom-call(s32[2]{0:T(128)} %pad_add_fusion.where_ref.tie_ref, bf16[256,1024]{1,0:T(8,128)(2,1)} %refs_0_, bf16[128,1024]{1,0:T(8,128)(2,1)} %copy-done.17, bf16[128,1024]{1,0:T(8,128)(2,1)} %copy-done.16, ...), custom_call_target="tpu_custom_call" | custom-call | flops 2147483648 | bytes 14680064 | tf_op jit(solution)/shard_map/mix_and_norm/pallas_call | solution.py:427
  172.6 30.0 %inner_forward.1 = (bf16[1024,4096]{1,0:T(8,128)(2,1)}, bf16[1024,4096]{1,0:T(8,128)(2,1)}, bf16[1024,4096]{1,0:T(8,128)(2,1)}) custom-call(s32[2]{0:T(128)} %pad_add_fusion.where_ref.tie_ref, bf16[256,4096]{1,0:T(8,128)(2,1)} %refs_0_.1, bf16[128,4096]{1,0:T(8,128)(2,1)} %collective-permute-done.19.refs_1_, bf16[128,4096]{1,0:T(8,128)(2,1)} %copy-done.13, ...), custom_call_target="tpu_custom_call" | custom-call | flops 8589934592 | bytes 27262976 | tf_op jit(solution)/shard_map/inner_forward/pallas_call | solution.py:469
  202.6 22.6 %outer_forward.1 = (bf16[1024,1024]{1,0:T(8,128)(2,1)}, f32[1024,1024]{1,0:T(8,128)}, bf16[1024,1024]{1,0:T(8,128)(2,1)}, f32[8,1024]{1,0:T(8,128)}, bf16[4096,1024]{1,0:T(8,128)(2,1)}) custom-call(s32[2]{0:T(128)} %pad_add_fusion.where_ref.tie_ref, bf16[1024,1024]{1,0:T(8,128)(2,1)} %refs_0_.2, bf16[512,1024]{1,0:T(8,128)(2,1)} %collective-permute-done.21.refs_1_, ...), custom_call_target="tpu_custom_call" | custom-call | flops 8589934592 | bytes 33554432 | tf_op jit(solution)/shard_map/outer_forward/pallas_call | solution.py:515
  225.2 13.9 %gram.2 = (bf16[4,512,1024]{2,1,0:T(8,128)(2,1)}, bf16[4,512,1024]{2,1,0:T(8,128)(2,1)}) custom-call(s32[5]{0:T(128)} %pad_add_fusion.1.order_ref, bf16[1024,4096]{1,0:T(8,128)(2,1)} %get-tuple-element.339.refs_10_.refs_0_, bf16[1024,1024]{1,0:T(8,128)(2,1)} %get-tuple-element.345.refs_1_.db_ref), custom_call_target="tpu_custom_call" | custom-call | flops 8589934592 | bytes 18874368 | tf_op jit(solution)/shard_map/gram/pallas_call | solution.py:567
  239.5 19.1 %feed_back_first.1 = (bf16[1024,2048]{1,0:T(8,128)(2,1)}, f32[8,2048]{1,0:T(8,128)}, f32[1024,1024]{1,0:T(8,128)}) custom-call(s32[2]{0:T(128)} %pad_add_fusion.where_ref.tie_ref, bf16[1024,1024]{1,0:T(8,128)(2,1)} %get-tuple-element.345.refs_1_.db_ref, bf16[4096,1024]{1,0:T(8,128)(2,1)} %get-tuple-element.348.wo_ref, ...), custom_call_target="tpu_custom_call" | custom-call | flops 8589934592 | bytes 31457280 | tf_op jit(solution)/shard_map/feed_back_first/pallas_call | solution.py:645
  258.6 6.3 %add_convert_fusion.1 = bf16[4,512,1024]{2,1,0:T(8,128)(2,1)} fusion(bf16[4,512,1024]{2,1,0:T(8,128)(2,1)} %collective-permute-done.39, bf16[4,512,1024]{2,1,0:T(8,128)(2,1)S(1)} %copy-done.1), kind=kLoop, calls=%fused_computation.1 | loop fusion | flops 8388608 | bytes 12582912 | tf_op jit(solution)/shard_map/convert_element_type | solution.py:816
  264.9 24.6 %feed_back_last.1 = (bf16[1024,2048]{1,0:T(8,128)(2,1)}, f32[8,2048]{1,0:T(8,128)}, f32[1024,1024]{1,0:T(8,128)}, bf16[1024,1024]{1,0:T(8,128)(2,1)}, f32[8,1024]{1,0:T(8,128)}) custom-call(s32[2]{0:T(128)} %pad_add_fusion.where_ref.tie_ref, bf16[1024,1024]{1,0:T(8,128)(2,1)} %get-tuple-element.345.refs_1_.db_ref, ...), custom_call_target="tpu_custom_call" | custom-call | flops 8589934592 | bytes 31457280 | tf_op jit(solution)/shard_map/feed_back_last/pallas_call | solution.py:653
  289.5 18.7 %gram.3 = (bf16[4,128,5120]{2,1,0:T(8,128)(2,1)}, bf16[4,128,5120]{2,1,0:T(8,128)(2,1)}) custom-call(s32[5]{0:T(128)} %pad_add_fusion.1.order_ref, bf16[1024,1024]{1,0:T(8,128)(2,1)} %get-tuple-element.337.refs_9_.refs_0_, bf16[1024,2048]{1,0:T(8,128)(2,1)} %get-tuple-element.352.refs_1_, bf16[1024,2048]{1,0:T(8,128)(2,1)} %get-tuple-element.361.refs_2_, ...), custom_call_target="tpu_custom_call" | custom-call | flops 10737418240 | bytes 23068672 | tf_op jit(solution)/shard_map/gram/pallas_call | solution.py:567
  308.3 7.0 %context_back.1 = (bf16[1024,1024]{1,0:T(8,128)(2,1)}, f32[4,8,1024]{2,1,0:T(8,128)}) custom-call(bf16[1024,1024]{1,0:T(8,128)(2,1)} %get-tuple-element.364.refs_4_.d_ref, bf16[1024,1024]{1,0:T(8,128)(2,1)} %get-tuple-element.365.w_ref, bf16[1024,1024]{1,0:T(8,128)(2,1)} %get-tuple-element.274.refs_9_.refs_3_.context_ref), custom_call_target="tpu_custom_call" | custom-call | flops 2147483648 | bytes 8388608 | tf_op jit(solution)/shard_map/context_back/pallas_call | solution.py:681
  315.3 1.9 collective-permute-done.40
  317.2 6.8 %add_convert_fusion = bf16[4,128,5120]{2,1,0:T(8,128)(2,1)} fusion(bf16[4,128,5120]{2,1,0:T(8,128)(2,1)} %collective-permute-done.40, bf16[4,128,5120]{2,1,0:T(8,128)(2,1)S(1)} %copy-done), kind=kLoop, calls=%fused_computation | loop fusion | flops 10485760 | bytes 15728640 | tf_op jit(solution)/shard_map/convert_element_type | solution.py:816
  324.1 1.5 copy-done.2
  325.6 1.5 fusion.19
  328.4 4.0 collective-permute-start.42
  332.4 4.3 collective-permute-start.44
  340.8 12.5 %collective-permute-start.41 = (bf16[512,1024]{1,0:T(8,128)(2,1)S(1)}, bf16[512,1024]{1,0:T(8,128)(2,1)S(1)}, u32[]{:S(2)}, u32[]{:S(2)}) collective-permute-start(bf16[512,1024]{1,0:T(8,128)(2,1)S(1)} %bitcast.144), channel_id=1, source_target_pairs={{0,8},{4,12},{24,16},{28,20},{1,9},{5,13},{25,17},{29,21},{2,10},{... | collective-permute-start | bytes 3145736 | tf_op jit(solution)/shard_map/ppermute | solution.py:856
  354.3 16.5 %attn_backward.3 = (bf16[1024,512]{1,0:T(8,128)(2,1)}, bf16[2,1024,512]{2,1,0:T(8,128)(2,1)}) custom-call(s32[8]{0:T(128)} %get-tuple-element.386.lo_ref, s32[8]{0:T(128)} %get-tuple-element.254.hi_ref, bf16[2048,1024]{1,0:T(8,128)(2,1)} %get-tuple-element.248.q_ref, bf16[512,1024]{1,0:T(8,128)(2,1)} %collective-permute-done.42.before_ref, ...), custom_call_target="tpu_custom_call" | custom-call | flops 15000000512 | bytes 4194304 | tf_op jit(solution)/shard_map/attn_backward/pallas_call | solution.py:359
  370.8 4.4 collective-permute-done.41
  376.3 16.1 %attn_backward.4 = (bf16[1024,512]{1,0:T(8,128)(2,1)}, bf16[2,1024,512]{2,1,0:T(8,128)(2,1)}) custom-call(s32[8]{0:T(128)} %get-tuple-element.386.lo_ref, s32[8]{0:T(128)} %get-tuple-element.254.hi_ref, bf16[2048,1024]{1,0:T(8,128)(2,1)} %get-tuple-element.248.q_ref, ...), custom_call_target="tpu_custom_call", output_to_operand_aliasing={{0}: (12, {}), {1}: (13, {})} | custom-call | flops 15000000512 | bytes 4194304 | tf_op jit(solution)/shard_map/attn_backward/pallas_call | solution.py:359
  392.8 8.5 %qkv_gradient.2 = (bf16[4,128,1536]{2,1,0:T(8,128)(2,1)}, bf16[4,128,1536]{2,1,0:T(8,128)(2,1)}, f32[8,1024]{1,0:T(8,128)}) custom-call(s32[5]{0:T(128)} %pad_add_fusion.2.order_ref, bf16[1024,1024]{1,0:T(8,128)(2,1)} %bitcast.133, bf16[1024,512]{1,0:T(8,128)(2,1)} %get-tuple-element.378.dq_ref.refs_0_, ...), custom_call_target="tpu_custom_call" | custom-call | flops 3221225472 | bytes 16777216 | tf_op jit(solution)/shard_map/qkv_gradient/pallas_call | solution.py:735
  401.3 3.3 collective-permute-start.47
  404.7 1.4 collective-permute-start.48
  406.1 30.8 %attn_backward.5 = (bf16[1024,512]{1,0:T(8,128)(2,1)}, bf16[2,1024,512]{2,1,0:T(8,128)(2,1)}) custom-call(s32[8]{0:T(128)} %get-tuple-element.386.lo_ref, s32[8]{0:T(128)} %get-tuple-element.254.hi_ref, bf16[2048,1024]{1,0:T(8,128)(2,1)} %get-tuple-element.248.q_ref, bf16[512,1024]{1,0:T(8,128)(2,1)} %collective-permute-done.42.before_ref, ...), custom_call_target="tpu_custom_call" | custom-call | flops 30000001024 | bytes 4194304 | tf_op jit(solution)/shard_map/attn_backward/pallas_call | solution.py:359
  436.9 1.8 add_convert_fusion.6
  438.7 20.1 %collective-permute-done.48 = bf16[512,1024]{1,0:T(8,128)(2,1)S(1)} collective-permute-done((bf16[512,1024]{1,0:T(8,128)(2,1)S(1)}, bf16[512,1024]{1,0:T(8,128)(2,1)S(1)}, u32[]{:S(2)}, u32[]{:S(2)}) %collective-permute-start.48) | collective-permute-done | bytes 1048608 | tf_op jit(solution)/shard_map/ppermute | solution.py:856
  461.2 8.6 %qkv_gradient.3 = (bf16[4,128,1664]{2,1,0:T(8,128)(2,1)}, bf16[4,128,1664]{2,1,0:T(8,128)(2,1)}, f32[8,1024]{1,0:T(8,128)}) custom-call(s32[5]{0:T(128)} %pad_add_fusion.2.order_ref, bf16[1024,1024]{1,0:T(8,128)(2,1)} %bitcast.134, bf16[1024,512]{1,0:T(8,128)(2,1)} %get-tuple-element.387.dq_ref.refs_2_, ...), custom_call_target="tpu_custom_call" | custom-call | flops 3489660928 | bytes 16777216 | tf_op jit(solution)/shard_map/qkv_gradient/pallas_call | solution.py:735
  472.9 12.2 %input_back.1 = f32[1024,1024]{1,0:T(8,128)} custom-call(f32[1024,1024]{1,0:T(8,128)} %get-tuple-element.357.base_ref, bf16[1024,512]{1,0:T(8,128)(2,1)} %get-tuple-element.378.dq_ref.refs_0_, bf16[2,1024,512]{2,1,0:T(8,128)(2,1)} %get-tuple-element.379.joined_ref.refs_1_, bf16[1024,512]{1,0:T(8,128)(2,1)} %get-tuple-element.387.dq_ref.refs_2_, ...), custom_call_target="tpu_custom_call" | custom-call | flops 6442450944 | bytes 20971520 | tf_op jit(solution)/shard_map/input_back/pallas_call | solution.py:766
  487.4 2.6 collective-permute-start.56
  490.9 1.8 collective-permute-start.55
  492.7 5.2 collective-permute-done.56
  498.0 3.0 collective-permute-done.54
  501.8 1.8 collective-permute-start.57
  504.7 3.0 collective-permute-done.57
  507.7 1.8 collective-permute-done.58
  511.2 2.4 maximum_convert_fusion
  513.6 4.9 collective-permute-start.60
  518.6 7.4 %collective-permute-done.63 = bf16[128,1536]{1,0:T(8,128)(2,1)S(1)} collective-permute-done((bf16[128,1536]{1,0:T(8,128)(2,1)S(1)}, bf16[128,1536]{1,0:T(8,128)(2,1)S(1)}, u32[]{:S(2)}, u32[]{:S(2)}) %collective-permute-start.63) | collective-permute-done | bytes 393248 | tf_op jit(solution)/shard_map/ppermute | solution.py:856
  526.1 5.3 collective-permute-done.60
  532.9 2.5 fusion
  535.5 13.3 %collective-permute-done.61 = bf16[128,1664]{1,0:T(8,128)(2,1)S(1)} collective-permute-done((bf16[128,1664]{1,0:T(8,128)(2,1)S(1)}, bf16[128,1664]{1,0:T(8,128)(2,1)S(1)}, u32[]{:S(2)}, u32[]{:S(2)}) %collective-permute-start.61) | collective-permute-done | bytes 426016 | tf_op jit(solution)/shard_map/ppermute | solution.py:779
  549.3 1.4 collective-permute-done.62
  559.2 2.2 pad_maximum_fusion.3
  (272 shorter events, 74.1 us)
Async XLA Ops:
  7.2 316.8 %reduce-scatter.7.cloned.1.call-start = ((), (), s32[]{:S(2)}) async-start(), calls=%async_computation.3 | async-start | bytes 5242880
  10.8 29.8 %collective-permute-start.3 = (bf16[128,3072]{1,0:T(8,128)(2,1)}, bf16[128,3072]{1,0:T(8,128)(2,1)}, u32[]{:S(2)}, u32[]{:S(2)}) collective-permute-start(bf16[128,3072]{1,0:T(8,128)(2,1)} %get-tuple-element.227), channel_id=1, source_target_pairs={{0,2},{1,3},{2,0},{3,1},{4,6},{5,7},{6,4},{7,5},{8,10},{9,11},{10,... | collective-permute-start | bytes 2359304 | tf_op jit(solution)/shard_map/ppermute | solution.py:779
  13.7 26.8 %collective-permute-start.2 = (bf16[128,3072]{1,0:T(8,128)(2,1)}, bf16[128,3072]{1,0:T(8,128)(2,1)}, u32[]{:S(2)}, u32[]{:S(2)}) collective-permute-start(bf16[128,3072]{1,0:T(8,128)(2,1)} %get-tuple-element.227), channel_id=1, source_target_pairs={{0,1},{1,0},{2,3},{3,2},{4,5},{5,4},{6,7},{7,6},{8,9},{9,8},{10,11... | collective-permute-start | bytes 2359304 | tf_op jit(solution)/shard_map/ppermute | solution.py:779
  26.8 9.9 %collective-permute-start.4 = (bf16[1,3200]{1,0:T(2,128)(2,1)S(1)}, bf16[1,3200]{1,0:T(2,128)(2,1)S(1)}, u32[]{:S(2)}, u32[]{:S(2)}) collective-permute-start(bf16[1,3200]{1,0:T(2,128)(2,1)S(1)} %reshape.188), channel_id=1, source_target_pairs={{0,1},{1,0},{2,3},{3,2},{4,5},{5,4},{6,7},{7,6},{8,9},{9,8},{10,11... | collective-permute-start | bytes 19208 | tf_op jit(solution)/shard_map/ppermute | solution.py:779
  29.1 11.5 %collective-permute-start.1 = (bf16[512,1024]{1,0:T(8,128)(2,1)S(1)}, bf16[512,1024]{1,0:T(8,128)(2,1)}, u32[]{:S(2)}, u32[]{:S(2)}) collective-permute-start(bf16[512,1024]{1,0:T(8,128)(2,1)S(1)} %get-tuple-element.446), channel_id=1, source_target_pairs={{4,0},{8,4},{12,8},{16,12},{20,16},{24,20},{28,24},{5,1},{9,5},{13... | collective-permute-start | bytes 3145736 | tf_op jit(solution)/shard_map/ppermute | solution.py:975
  30.4 10.2 %collective-permute-start = (bf16[512,1024]{1,0:T(8,128)(2,1)S(1)}, bf16[512,1024]{1,0:T(8,128)(2,1)}, u32[]{:S(2)}, u32[]{:S(2)}) collective-permute-start(bf16[512,1024]{1,0:T(8,128)(2,1)S(1)} %get-tuple-element.447), channel_id=1, source_target_pairs={{0,4},{4,8},{8,12},{12,16},{16,20},{20,24},{24,28},{1,5},{5,9},{9,... | collective-permute-start | bytes 3145736 | tf_op jit(solution)/shard_map/ppermute | solution.py:974
  42.5 10.0 %collective-permute-start.9 = (f32[8,128]{1,0:T(8,128)S(1)}, f32[8,128]{1,0:T(8,128)S(1)}, u32[]{:S(2)}, u32[]{:S(2)}) collective-permute-start(f32[8,128]{1,0:T(8,128)S(1)} %broadcast_in_dim.25), channel_id=1, source_target_pairs={{0,4},{4,0},{8,12},{12,8},{16,20},{20,16},{24,28},{28,24},{1,5},{5... | collective-permute-start | bytes 12296 | tf_op jit(solution)/shard_map/ppermute | solution.py:779
  50.4 11.3 %collective-permute-start.8 = (bf16[64,3072]{1,0:T(8,128)(2,1)S(1)}, bf16[64,3072]{1,0:T(8,128)(2,1)}, u32[]{:S(2)}, u32[]{:S(2)}) collective-permute-start(bf16[64,3072]{1,0:T(8,128)(2,1)S(1)} %slice.213), channel_id=1, source_target_pairs={{0,1},{1,0},{2,3},{3,2},{4,5},{5,4},{6,7},{7,6},{8,9},{9,8},{10,11... | collective-permute-start | bytes 1179656 | tf_op jit(solution)/shard_map/ppermute | solution.py:779
  51.9 10.9 %collective-permute-start.7 = (bf16[64,3072]{1,0:T(8,128)(2,1)S(1)}, bf16[64,3072]{1,0:T(8,128)(2,1)}, u32[]{:S(2)}, u32[]{:S(2)}) collective-permute-start(bf16[64,3072]{1,0:T(8,128)(2,1)S(1)} %slice.212), channel_id=1, source_target_pairs={{0,2},{1,3},{2,0},{3,1},{4,6},{5,7},{6,4},{7,5},{8,10},{9,11},{10,... | collective-permute-start | bytes 1179656 | tf_op jit(solution)/shard_map/ppermute | solution.py:779
  52.5 4.1 collective-permute-start.10
  56.5 4.6 collective-permute-start.11
  62.8 6.2 %collective-permute-start.12 = (bf16[128,3072]{1,0:T(8,128)(2,1)}, bf16[128,3072]{1,0:T(8,128)(2,1)}, u32[]{:S(2)}, u32[]{:S(2)}) collective-permute-start(bf16[128,3072]{1,0:T(8,128)(2,1)} %collective-permute-done.2.refs_1_), channel_id=1, source_target_pairs={{0,4},{4,0},{8,12},{12,8},{16,20},{20,16},{24,28},{28,24},{1,5},{5... | collective-permute-start | bytes 2359304 | tf_op jit(solution)/shard_map/ppermute | solution.py:779
  62.8 7.7 %collective-permute-start.13 = (bf16[128,3072]{1,0:T(8,128)(2,1)}, bf16[128,3072]{1,0:T(8,128)(2,1)}, u32[]{:S(2)}, u32[]{:S(2)}) collective-permute-start(bf16[128,3072]{1,0:T(8,128)(2,1)} %collective-permute-done.3.refs_2_), channel_id=1, source_target_pairs={{0,4},{4,0},{8,12},{12,8},{16,20},{20,16},{24,28},{28,24},{1,5},{5... | collective-permute-start | bytes 2359304 | tf_op jit(solution)/shard_map/ppermute | solution.py:779
  63.3 5.2 collective-permute-start.15
  63.8 33.4 %collective-permute-start.20 = (bf16[128,4096]{1,0:T(8,128)(2,1)S(1)}, bf16[128,4096]{1,0:T(8,128)(2,1)S(1)}, u32[]{:S(2)}, u32[]{:S(2)}) collective-permute-start(bf16[128,4096]{1,0:T(8,128)(2,1)S(1)} %constant_dynamic-slice_fusion.1), channel_id=1, source_target_pairs={{0,2},{1,3},{2,0},{3,1},{4,6},{5,7},{6,4},{7,5},{8,10},{9,11},{10,... | collective-permute-start | bytes 3145736 | tf_op jit(solution)/shard_map/ppermute | solution.py:779
  67.1 27.4 %collective-permute-start.16 = (bf16[128,1024]{1,0:T(8,128)(2,1)S(1)}, bf16[128,1024]{1,0:T(8,128)(2,1)S(1)}, u32[]{:S(2)}, u32[]{:S(2)}) collective-permute-start(bf16[128,1024]{1,0:T(8,128)(2,1)S(1)} %constant_dynamic-slice_fusion.2), channel_id=1, source_target_pairs={{0,2},{1,3},{2,0},{3,1},{4,6},{5,7},{6,4},{7,5},{8,10},{9,11},{10,... | collective-permute-start | bytes 786440 | tf_op jit(solution)/shard_map/ppermute | solution.py:779
  68.5 26.0 %collective-permute-start.6 = (bf16[128,1024]{1,0:T(8,128)(2,1)S(1)}, bf16[128,1024]{1,0:T(8,128)(2,1)S(1)}, u32[]{:S(2)}, u32[]{:S(2)}) collective-permute-start(bf16[128,1024]{1,0:T(8,128)(2,1)S(1)} %constant_dynamic-slice_fusion.2), channel_id=1, source_target_pairs={{0,1},{1,0},{2,3},{3,2},{4,5},{5,4},{6,7},{7,6},{8,9},{9,8},{10,11... | collective-permute-start | bytes 786440 | tf_op jit(solution)/shard_map/ppermute | solution.py:779
  69.1 44.7 %collective-permute-start.19 = (bf16[128,4096]{1,0:T(8,128)(2,1)S(1)}, bf16[128,4096]{1,0:T(8,128)(2,1)}, u32[]{:S(2)}, u32[]{:S(2)}) collective-permute-start(bf16[128,4096]{1,0:T(8,128)(2,1)S(1)} %constant_dynamic-slice_fusion.1), channel_id=1, source_target_pairs={{0,1},{1,0},{2,3},{3,2},{4,5},{5,4},{6,7},{7,6},{8,9},{9,8},{10,11... | collective-permute-start | bytes 3145736 | tf_op jit(solution)/shard_map/ppermute | solution.py:779
  94.5 29.4 %collective-permute-start.22 = (bf16[512,1024]{1,0:T(8,128)(2,1)S(1)}, bf16[512,1024]{1,0:T(8,128)(2,1)}, u32[]{:S(2)}, u32[]{:S(2)}) collective-permute-start(bf16[512,1024]{1,0:T(8,128)(2,1)S(1)} %constant_dynamic-slice_fusion), channel_id=1, source_target_pairs={{0,2},{1,3},{2,0},{3,1},{4,6},{5,7},{6,4},{7,5},{8,10},{9,11},{10,... | collective-permute-start | bytes 3145736 | tf_op jit(solution)/shard_map/ppermute | solution.py:779
  95.1 28.8 %collective-permute-start.21 = (bf16[512,1024]{1,0:T(8,128)(2,1)S(1)}, bf16[512,1024]{1,0:T(8,128)(2,1)}, u32[]{:S(2)}, u32[]{:S(2)}) collective-permute-start(bf16[512,1024]{1,0:T(8,128)(2,1)S(1)} %constant_dynamic-slice_fusion), channel_id=1, source_target_pairs={{0,1},{1,0},{2,3},{3,2},{4,5},{5,4},{6,7},{7,6},{8,9},{9,8},{10,11... | collective-permute-start | bytes 3145736 | tf_op jit(solution)/shard_map/ppermute | solution.py:779
  95.7 28.3 %collective-permute-start.18 = (bf16[64,1024]{1,0:T(8,128)(2,1)S(1)}, bf16[64,1024]{1,0:T(8,128)(2,1)S(1)}, u32[]{:S(2)}, u32[]{:S(2)}) collective-permute-start(bf16[64,1024]{1,0:T(8,128)(2,1)S(1)} %slice.219), channel_id=1, source_target_pairs={{0,1},{1,0},{2,3},{3,2},{4,5},{5,4},{6,7},{7,6},{8,9},{9,8},{10,11... | collective-permute-start | bytes 393224 | tf_op jit(solution)/shard_map/ppermute | solution.py:779
  97.2 26.7 %collective-permute-start.17 = (bf16[64,1024]{1,0:T(8,128)(2,1)S(1)}, bf16[64,1024]{1,0:T(8,128)(2,1)S(1)}, u32[]{:S(2)}, u32[]{:S(2)}) collective-permute-start(bf16[64,1024]{1,0:T(8,128)(2,1)S(1)} %slice.218), channel_id=1, source_target_pairs={{0,2},{1,3},{2,0},{3,1},{4,6},{5,7},{6,4},{7,5},{8,10},{9,11},{10,... | collective-permute-start | bytes 393224 | tf_op jit(solution)/shard_map/ppermute | solution.py:779
  124.0 7.5 %collective-permute-start.23 = (bf16[128,1024]{1,0:T(8,128)(2,1)S(1)}, bf16[128,1024]{1,0:T(8,128)(2,1)S(1)}, u32[]{:S(2)}, u32[]{:S(2)}) collective-permute-start(bf16[128,1024]{1,0:T(8,128)(2,1)S(1)} %collective-permute-done.6.refs_1_), channel_id=1, source_target_pairs={{0,4},{4,0},{8,12},{12,8},{16,20},{20,16},{24,28},{28,24},{1,5},{5... | collective-permute-start | bytes 786440 | tf_op jit(solution)/shard_map/ppermute | solution.py:779
  124.0 4.9 collective-permute-start.25
  124.5 5.5 collective-permute-start.26
  124.6 22.9 %collective-permute-start.24 = (bf16[128,1024]{1,0:T(8,128)(2,1)S(1)}, bf16[128,1024]{1,0:T(8,128)(2,1)S(1)}, u32[]{:S(2)}, u32[]{:S(2)}) collective-permute-start(bf16[128,1024]{1,0:T(8,128)(2,1)S(1)} %collective-permute-done.16.refs_2_), channel_id=1, source_target_pairs={{0,4},{4,0},{8,12},{12,8},{16,20},{20,16},{24,28},{28,24},{1,5},{5... | collective-permute-start | bytes 786440 | tf_op jit(solution)/shard_map/ppermute | solution.py:779
  128.4 19.1 %collective-permute-start.30 = (bf16[256,1024]{1,0:T(8,128)(2,1)S(1)}, bf16[256,1024]{1,0:T(8,128)(2,1)S(1)}, u32[]{:S(2)}, u32[]{:S(2)}) collective-permute-start(bf16[256,1024]{1,0:T(8,128)(2,1)S(1)} %slice.223), channel_id=1, source_target_pairs={{0,1},{1,0},{2,3},{3,2},{4,5},{5,4},{6,7},{7,6},{8,9},{9,8},{10,11... | collective-permute-start | bytes 1572872 | tf_op jit(solution)/shard_map/ppermute | solution.py:779
  129.0 18.6 %collective-permute-start.29 = (bf16[256,1024]{1,0:T(8,128)(2,1)S(1)}, bf16[256,1024]{1,0:T(8,128)(2,1)S(1)}, u32[]{:S(2)}, u32[]{:S(2)}) collective-permute-start(bf16[256,1024]{1,0:T(8,128)(2,1)S(1)} %slice.222), channel_id=1, source_target_pairs={{0,2},{1,3},{2,0},{3,1},{4,6},{5,7},{6,4},{7,5},{8,10},{9,11},{10,... | collective-permute-start | bytes 1572872 | tf_op jit(solution)/shard_map/ppermute | solution.py:779
  130.0 23.6 %collective-permute-start.28 = (bf16[64,4096]{1,0:T(8,128)(2,1)S(1)}, bf16[64,4096]{1,0:T(8,128)(2,1)S(1)}, u32[]{:S(2)}, u32[]{:S(2)}) collective-permute-start(bf16[64,4096]{1,0:T(8,128)(2,1)S(1)} %slice.221), channel_id=1, source_target_pairs={{0,1},{1,0},{2,3},{3,2},{4,5},{5,4},{6,7},{7,6},{8,9},{9,8},{10,11... | collective-permute-start | bytes 1572872 | tf_op jit(solution)/shard_map/ppermute | solution.py:779
  131.5 22.4 %collective-permute-start.27 = (bf16[64,4096]{1,0:T(8,128)(2,1)S(1)}, bf16[64,4096]{1,0:T(8,128)(2,1)}, u32[]{:S(2)}, u32[]{:S(2)}) collective-permute-start(bf16[64,4096]{1,0:T(8,128)(2,1)S(1)} %slice.220), channel_id=1, source_target_pairs={{0,2},{1,3},{2,0},{3,1},{4,6},{5,7},{6,4},{7,5},{8,10},{9,11},{10,... | collective-permute-start | bytes 1572872 | tf_op jit(solution)/shard_map/ppermute | solution.py:779
  154.4 5.1 collective-permute-start.38
  154.4 18.1 %collective-permute-start.36 = (bf16[512,1024]{1,0:T(8,128)(2,1)}, bf16[512,1024]{1,0:T(8,128)(2,1)S(1)}, u32[]{:S(2)}, u32[]{:S(2)}) collective-permute-start(bf16[512,1024]{1,0:T(8,128)(2,1)} %collective-permute-done.22.refs_2_), channel_id=1, source_target_pairs={{0,4},{4,0},{8,12},{12,8},{16,20},{20,16},{24,28},{28,24},{1,5},{5... | collective-permute-start | bytes 3145736 | tf_op jit(solution)/shard_map/ppermute | solution.py:779
  154.9 17.6 %collective-permute-start.35 = (bf16[512,1024]{1,0:T(8,128)(2,1)}, bf16[512,1024]{1,0:T(8,128)(2,1)S(1)}, u32[]{:S(2)}, u32[]{:S(2)}) collective-permute-start(bf16[512,1024]{1,0:T(8,128)(2,1)} %collective-permute-done.21.refs_1_), channel_id=1, source_target_pairs={{0,4},{4,0},{8,12},{12,8},{16,20},{20,16},{24,28},{28,24},{1,5},{5... | collective-permute-start | bytes 3145736 | tf_op jit(solution)/shard_map/ppermute | solution.py:779
  155.8 16.8 %collective-permute-start.32 = (bf16[128,4096]{1,0:T(8,128)(2,1)S(1)}, bf16[128,4096]{1,0:T(8,128)(2,1)}, u32[]{:S(2)}, u32[]{:S(2)}) collective-permute-start(bf16[128,4096]{1,0:T(8,128)(2,1)S(1)} %collective-permute-done.20.refs_2_), channel_id=1, source_target_pairs={{0,4},{4,0},{8,12},{12,8},{16,20},{20,16},{24,28},{28,24},{1,5},{5... | collective-permute-start | bytes 3145736 | tf_op jit(solution)/shard_map/ppermute | solution.py:779
  157.3 15.3 %collective-permute-start.31 = (bf16[128,4096]{1,0:T(8,128)(2,1)}, bf16[128,4096]{1,0:T(8,128)(2,1)}, u32[]{:S(2)}, u32[]{:S(2)}) collective-permute-start(bf16[128,4096]{1,0:T(8,128)(2,1)} %collective-permute-done.19.refs_1_), channel_id=1, source_target_pairs={{0,4},{4,0},{8,12},{12,8},{16,20},{20,16},{24,28},{28,24},{1,5},{5... | collective-permute-start | bytes 3145736 | tf_op jit(solution)/shard_map/ppermute | solution.py:779
  160.4 12.1 %collective-permute-start.33 = (bf16[64,4096]{1,0:T(8,128)(2,1)}, bf16[64,4096]{1,0:T(8,128)(2,1)}, u32[]{:S(2)}, u32[]{:S(2)}) collective-permute-start(bf16[64,4096]{1,0:T(8,128)(2,1)} %collective-permute-done.27.refs_3_), channel_id=1, source_target_pairs={{0,4},{4,0},{8,12},{12,8},{16,20},{20,16},{24,28},{28,24},{1,5},{5... | collective-permute-start | bytes 1572872 | tf_op jit(solution)/shard_map/ppermute | solution.py:779
  239.1 19.5 %collective-permute-start.39 = (bf16[4,512,1024]{2,1,0:T(8,128)(2,1)}, bf16[4,512,1024]{2,1,0:T(8,128)(2,1)}, u32[]{:S(2)}, u32[]{:S(2)}) collective-permute-start(bf16[4,512,1024]{2,1,0:T(8,128)(2,1)} %get-tuple-element.347), channel_id=1, source_target_pairs={{0,4},{4,0},{8,12},{12,8},{16,20},{20,16},{24,28},{28,24},{1,5},{5... | collective-permute-start | bytes 12582920 | tf_op jit(solution)/shard_map/ppermute | solution.py:779
  264.9 139.8 %reduce-scatter.9.cloned.1.call-start = ((), (), s32[]{:S(2)}) async-start(), calls=%async_computation.4 | async-start | bytes 6553600
  308.2 9.0 %collective-permute-start.40 = (bf16[4,128,5120]{2,1,0:T(8,128)(2,1)}, bf16[4,128,5120]{2,1,0:T(8,128)(2,1)}, u32[]{:S(2)}, u32[]{:S(2)}) collective-permute-start(bf16[4,128,5120]{2,1,0:T(8,128)(2,1)} %get-tuple-element.363), channel_id=1, source_target_pairs={{0,4},{4,0},{8,12},{12,8},{16,20},{20,16},{24,28},{28,24},{1,5},{5... | collective-permute-start | bytes 15728648 | tf_op jit(solution)/shard_map/ppermute | solution.py:779
  324.1 163.3 %all-reduce.5.cloned.1.call-start = ((), (), s32[]{:S(2)}) async-start(), calls=%async_computation.2 | async-start | bytes 2621440 | tf_op jit(solution)/shard_map/psum | solution.py:890
  327.1 26.2 %collective-permute-start.43 = (bf16[512,1024]{1,0:T(8,128)(2,1)}, bf16[512,1024]{1,0:T(8,128)(2,1)S(1)}, u32[]{:S(2)}, u32[]{:S(2)}) collective-permute-start(bf16[512,1024]{1,0:T(8,128)(2,1)} %get-tuple-element.444), channel_id=1, source_target_pairs={{4,0},{8,4},{12,8},{16,12},{20,16},{24,20},{28,24},{5,1},{9,5},{13... | collective-permute-start | bytes 3145736 | tf_op jit(solution)/shard_map/ppermute | solution.py:1060
  328.4 24.9 %collective-permute-start.42 = (bf16[512,1024]{1,0:T(8,128)(2,1)}, bf16[512,1024]{1,0:T(8,128)(2,1)}, u32[]{:S(2)}, u32[]{:S(2)}) collective-permute-start(bf16[512,1024]{1,0:T(8,128)(2,1)} %get-tuple-element.445), channel_id=1, source_target_pairs={{0,4},{4,8},{8,12},{12,16},{16,20},{20,24},{24,28},{1,5},{5,9},{9,... | collective-permute-start | bytes 3145736 | tf_op jit(solution)/shard_map/ppermute | solution.py:1059
  332.4 6.9 %collective-permute-start.44 = (f32[2,4,8,512]{3,2,1,0:T(8,128)S(1)}, f32[2,4,8,512]{3,2,1,0:T(8,128)S(1)}, u32[]{:S(2)}, u32[]{:S(2)}) collective-permute-start(f32[2,4,8,512]{3,2,1,0:T(8,128)S(1)} %get-tuple-element.464), channel_id=1, source_target_pairs={{0,4},{4,8},{8,12},{12,16},{16,20},{20,24},{24,28},{1,5},{5,9},{9,... | collective-permute-start | bytes 393224 | tf_op jit(solution)/shard_map/ppermute | solution.py:1059
  340.8 34.3 %collective-permute-start.41 = (bf16[512,1024]{1,0:T(8,128)(2,1)S(1)}, bf16[512,1024]{1,0:T(8,128)(2,1)S(1)}, u32[]{:S(2)}, u32[]{:S(2)}) collective-permute-start(bf16[512,1024]{1,0:T(8,128)(2,1)S(1)} %bitcast.144), channel_id=1, source_target_pairs={{0,8},{4,12},{24,16},{28,20},{1,9},{5,13},{25,17},{29,21},{2,10},{... | collective-permute-start | bytes 3145736 | tf_op jit(solution)/shard_map/ppermute | solution.py:856
  375.6 16.8 %collective-permute-start.46 = (bf16[512,1024]{1,0:T(8,128)(2,1)S(1)}, bf16[512,1024]{1,0:T(8,128)(2,1)S(1)}, u32[]{:S(2)}, u32[]{:S(2)}) collective-permute-start(bf16[512,1024]{1,0:T(8,128)(2,1)S(1)} %add_convert_fusion.3), channel_id=1, source_target_pairs={{8,16},{12,20},{16,8},{20,12},{9,17},{13,21},{17,9},{21,13},{10,18... | collective-permute-start | bytes 3145736 | tf_op jit(solution)/shard_map/ppermute | solution.py:856
  401.3 35.6 %collective-permute-start.47 = (bf16[4,128,1536]{2,1,0:T(8,128)(2,1)}, bf16[4,128,1536]{2,1,0:T(8,128)(2,1)}, u32[]{:S(2)}, u32[]{:S(2)}) collective-permute-start(bf16[4,128,1536]{2,1,0:T(8,128)(2,1)} %get-tuple-element.390), channel_id=1, source_target_pairs={{0,4},{4,0},{8,12},{12,8},{16,20},{20,16},{24,28},{28,24},{1,5},{5... | collective-permute-start | bytes 4718600 | tf_op jit(solution)/shard_map/ppermute | solution.py:779
  404.7 54.1 %collective-permute-start.48 = (bf16[512,1024]{1,0:T(8,128)(2,1)S(1)}, bf16[512,1024]{1,0:T(8,128)(2,1)S(1)}, u32[]{:S(2)}, u32[]{:S(2)}) collective-permute-start(bf16[512,1024]{1,0:T(8,128)(2,1)S(1)} %fusion.1), channel_id=1, source_target_pairs={{8,0},{12,4},{16,24},{20,28},{9,1},{13,5},{17,25},{21,29},{10,2},{... | collective-permute-start | bytes 3145736 | tf_op jit(solution)/shard_map/ppermute | solution.py:856
  459.0 11.4 %collective-permute-start.50 = (bf16[2,64,1536]{2,1,0:T(8,128)(2,1)S(1)}, bf16[2,64,1536]{2,1,0:T(8,128)(2,1)S(1)}, u32[]{:S(2)}, u32[]{:S(2)}) collective-permute-start(bf16[2,64,1536]{2,1,0:T(8,128)(2,1)S(1)} %slice_bitcast_fusion.6), channel_id=1, source_target_pairs={{0,2},{1,3},{2,0},{3,1},{4,6},{5,7},{6,4},{7,5},{8,10},{9,11},{10,... | collective-permute-start | bytes 1179656 | tf_op jit(solution)/shard_map/ppermute | solution.py:779
  460.3 10.7 %collective-permute-start.49 = (bf16[2,64,1536]{2,1,0:T(8,128)(2,1)S(1)}, bf16[2,64,1536]{2,1,0:T(8,128)(2,1)S(1)}, u32[]{:S(2)}, u32[]{:S(2)}) collective-permute-start(bf16[2,64,1536]{2,1,0:T(8,128)(2,1)S(1)} %slice_bitcast_fusion.8), channel_id=1, source_target_pairs={{0,1},{1,0},{2,3},{3,2},{4,5},{5,4},{6,7},{7,6},{8,9},{9,8},{10,11... | collective-permute-start | bytes 1179656 | tf_op jit(solution)/shard_map/ppermute | solution.py:779
  461.2 24.1 %collective-permute-start.66 = (bf16[512,1024]{1,0:T(8,128)(2,1)S(1)}, bf16[512,1024]{1,0:T(8,128)(2,1)S(1)}, u32[]{:S(2)}, u32[]{:S(2)}) collective-permute-start(bf16[512,1024]{1,0:T(8,128)(2,1)S(1)} %broadcast_select_fusion.4), channel_id=1, source_target_pairs={{0,4},{4,0},{8,12},{12,8},{16,20},{20,16},{24,28},{28,24},{1,5},{5... | collective-permute-start | bytes 3145736 | tf_op jit(solution)/shard_map/ppermute | solution.py:779
  469.9 15.4 %collective-permute-start.51 = (bf16[4,128,1664]{2,1,0:T(8,128)(2,1)}, bf16[4,128,1664]{2,1,0:T(8,128)(2,1)S(1)}, u32[]{:S(2)}, u32[]{:S(2)}) collective-permute-start(bf16[4,128,1664]{2,1,0:T(8,128)(2,1)} %get-tuple-element.406), channel_id=1, source_target_pairs={{0,4},{4,0},{8,12},{12,8},{16,20},{20,16},{24,28},{28,24},{1,5},{5... | collective-permute-start | bytes 5111816 | tf_op jit(solution)/shard_map/ppermute | solution.py:779
  471.1 14.0 %collective-permute-start.53 = (bf16[1,64,1536]{2,1,0:T(8,128)(2,1)S(1)}, bf16[1,64,1536]{2,1,0:T(8,128)(2,1)S(1)}, u32[]{:S(2)}, u32[]{:S(2)}) collective-permute-start(bf16[1,64,1536]{2,1,0:T(8,128)(2,1)S(1)} %slice_bitcast_fusion.14), channel_id=1, source_target_pairs={{0,1},{1,0},{2,3},{3,2},{4,5},{5,4},{6,7},{7,6},{8,9},{9,8},{10,11... | collective-permute-start | bytes 589832 | tf_op jit(solution)/shard_map/ppermute | solution.py:779
  472.1 13.1 %collective-permute-start.52 = (bf16[1,64,1536]{2,1,0:T(8,128)(2,1)S(1)}, bf16[1,64,1536]{2,1,0:T(8,128)(2,1)S(1)}, u32[]{:S(2)}, u32[]{:S(2)}) collective-permute-start(bf16[1,64,1536]{2,1,0:T(8,128)(2,1)S(1)} %slice_bitcast_fusion.16), channel_id=1, source_target_pairs={{0,2},{1,3},{2,0},{3,1},{4,6},{5,7},{6,4},{7,5},{8,10},{9,11},{10,... | collective-permute-start | bytes 589832 | tf_op jit(solution)/shard_map/ppermute | solution.py:779
  487.4 10.5 %collective-permute-start.56 = (bf16[128,1536]{1,0:T(8,128)(2,1)S(1)}, bf16[128,1536]{1,0:T(8,128)(2,1)S(1)}, u32[]{:S(2)}, u32[]{:S(2)}) collective-permute-start(bf16[128,1536]{1,0:T(8,128)(2,1)S(1)} %pad_maximum_fusion.6), channel_id=1, source_target_pairs={{0,8},{4,12},{24,16},{28,20},{1,9},{5,13},{25,17},{29,21},{2,10},{... | collective-permute-start | bytes 1179656 | tf_op jit(solution)/shard_map/ppermute | solution.py:856
  490.0 10.9 %collective-permute-start.54 = (bf16[2,64,1664]{2,1,0:T(8,128)(2,1)S(1)}, bf16[2,64,1664]{2,1,0:T(8,128)(2,1)S(1)}, u32[]{:S(2)}, u32[]{:S(2)}) collective-permute-start(bf16[2,64,1664]{2,1,0:T(8,128)(2,1)S(1)} %slice_bitcast_fusion.4), channel_id=1, source_target_pairs={{0,1},{1,0},{2,3},{3,2},{4,5},{5,4},{6,7},{7,6},{8,9},{9,8},{10,11... | collective-permute-start | bytes 1277960 | tf_op jit(solution)/shard_map/ppermute | solution.py:779
  490.9 10.7 %collective-permute-start.55 = (bf16[2,64,1664]{2,1,0:T(8,128)(2,1)S(1)}, bf16[2,64,1664]{2,1,0:T(8,128)(2,1)S(1)}, u32[]{:S(2)}, u32[]{:S(2)}) collective-permute-start(bf16[2,64,1664]{2,1,0:T(8,128)(2,1)S(1)} %slice_bitcast_fusion.2), channel_id=1, source_target_pairs={{0,2},{1,3},{2,0},{3,1},{4,6},{5,7},{6,4},{7,5},{8,10},{9,11},{10,... | collective-permute-start | bytes 1277960 | tf_op jit(solution)/shard_map/ppermute | solution.py:779
  492.7 39.0 %collective-permute-start.65 = (bf16[128,5120]{1,0:T(8,128)(2,1)}, bf16[128,5120]{1,0:T(8,128)(2,1)S(1)}, u32[]{:S(2)}, u32[]{:S(2)}) collective-permute-start(bf16[128,5120]{1,0:T(8,128)(2,1)} %all-reduce.5.cloned.1.call-done), channel_id=1, source_target_pairs={{0,4},{4,0},{8,12},{12,8},{16,20},{20,16},{24,28},{28,24},{1,5},{5... | collective-permute-start | bytes 3932168 | tf_op jit(solution)/shard_map/ppermute | solution.py:779
  501.8 5.9 %collective-permute-start.57 = (bf16[1,64,1664]{2,1,0:T(8,128)(2,1)S(1)}, bf16[1,64,1664]{2,1,0:T(8,128)(2,1)S(1)}, u32[]{:S(2)}, u32[]{:S(2)}) collective-permute-start(bf16[1,64,1664]{2,1,0:T(8,128)(2,1)S(1)} %slice_bitcast_fusion.12), channel_id=1, source_target_pairs={{0,2},{1,3},{2,0},{3,1},{4,6},{5,7},{6,4},{7,5},{8,10},{9,11},{10,... | collective-permute-start | bytes 638984 | tf_op jit(solution)/shard_map/ppermute | solution.py:779
  503.6 5.9 %collective-permute-start.58 = (bf16[1,64,1664]{2,1,0:T(8,128)(2,1)S(1)}, bf16[1,64,1664]{2,1,0:T(8,128)(2,1)S(1)}, u32[]{:S(2)}, u32[]{:S(2)}) collective-permute-start(bf16[1,64,1664]{2,1,0:T(8,128)(2,1)S(1)} %slice_bitcast_fusion.10), channel_id=1, source_target_pairs={{0,1},{1,0},{2,3},{3,2},{4,5},{5,4},{6,7},{7,6},{8,9},{9,8},{10,11... | collective-permute-start | bytes 638984 | tf_op jit(solution)/shard_map/ppermute | solution.py:779
  504.0 5.6 collective-permute-start.59
  509.7 16.2 %collective-permute-start.63 = (bf16[128,1536]{1,0:T(8,128)(2,1)S(1)}, bf16[128,1536]{1,0:T(8,128)(2,1)S(1)}, u32[]{:S(2)}, u32[]{:S(2)}) collective-permute-start(bf16[128,1536]{1,0:T(8,128)(2,1)S(1)} %fusion.6), channel_id=1, source_target_pairs={{8,0},{12,4},{16,24},{20,28},{9,1},{13,5},{17,25},{21,29},{10,2},{... | collective-permute-start | bytes 1179656 | tf_op jit(solution)/shard_map/ppermute | solution.py:856
  513.6 17.8 %collective-permute-start.60 = (bf16[128,1664]{1,0:T(8,128)(2,1)S(1)}, bf16[128,1664]{1,0:T(8,128)(2,1)S(1)}, u32[]{:S(2)}, u32[]{:S(2)}) collective-permute-start(bf16[128,1664]{1,0:T(8,128)(2,1)S(1)} %pad_maximum_fusion.5), channel_id=1, source_target_pairs={{0,8},{4,12},{8,0},{12,4},{16,24},{20,28},{24,16},{28,20},{1,9},{5... | collective-permute-start | bytes 1277960 | tf_op jit(solution)/shard_map/ppermute | solution.py:779
  526.0 9.4 %collective-permute-start.64 = (bf16[128,1536]{1,0:T(8,128)(2,1)S(1)}, bf16[128,1536]{1,0:T(8,128)(2,1)S(1)}, u32[]{:S(2)}, u32[]{:S(2)}) collective-permute-start(bf16[128,1536]{1,0:T(8,128)(2,1)S(1)} %broadcast_select_fusion.7), channel_id=1, source_target_pairs={{0,4},{4,0},{8,12},{12,8},{16,20},{20,16},{24,28},{28,24},{1,5},{5... | collective-permute-start | bytes 1179656 | tf_op jit(solution)/shard_map/ppermute | solution.py:779
  531.5 17.2 %collective-permute-start.61 = (bf16[128,1664]{1,0:T(8,128)(2,1)S(1)}, bf16[128,1664]{1,0:T(8,128)(2,1)S(1)}, u32[]{:S(2)}, u32[]{:S(2)}) collective-permute-start(bf16[128,1664]{1,0:T(8,128)(2,1)S(1)} %add_convert_fusion.9), channel_id=1, source_target_pairs={{0,16},{4,20},{8,24},{12,28},{16,0},{20,4},{24,8},{28,12},{1,17},{... | collective-permute-start | bytes 1277960 | tf_op jit(solution)/shard_map/ppermute | solution.py:779
  (38 other events, 453.7 us)
Sparse Core Ops, SparseCore 0:
  265.0 54.8 reduce-scatter.6
  324.2 63.6 reduce-scatter.8
  404.8 75.9 all-reduce.4

commit v5 on v4

--- a/solution.py
+++ b/solution.py
@@ -1003,13 +1003,12 @@
     idq = near_starts.reshape(tiles, 1, TILE)
     idk = near_starts[:, None]
 
-    before, behind, idq, idk, low_tile, high_tile, flags, own_proj, own_inner = boundary(
-        None, (before, behind, idq, idk, low_tile, high_tile, flags, own_half(proj_weight), own_half(inner_weight)),
-        w_qkv, small,
-    )
+    own_proj, own_inner = boundary(None, (own_half(proj_weight), own_half(inner_weight)), w_qkv, small)
     w_proj = Staged(gathering, proj_weight, own_proj)
     w_inner = Staged(gathering, inner_weight, own_inner)
-    boundary(None, where, w_qkv)
+    before, behind, idq, idk, low_tile, high_tile, flags = boundary(
+        None, (before, behind, idq, idk, low_tile, high_tile, flags), w_qkv
+    )
     small = small.result()[0]
     valid = jnp.sum(small[:, -128:].astype(f32), axis=0)
     counted = valid[0] * 64 + valid[1]

time: 577 us -> 576 us (level)
  Pallas kernels: 294 us -> 325 us
  waiting for transfers between devices: 97.3 us -> 73.8 us
  starting transfers between devices: 88.1 us -> 79.9 us
    pallas_call x3, Pallas kernels: 63.3 us -> 82.8 us  [attn_bwd(): pl.pallas_call(attn_bwd_kernel, grid_spec=pltpu.PrefetchScalarGridSpec(nu...]
    ppermute x6, waiting for transfers between devices: 37.1 us -> 22.4 us  [move(): return arrive(gate, lax.ppermute(value, 'ctx', pairs))]
    pallas_call x2, Pallas kernels: 30 us -> 40.8 us  [attn_fwd(): pl.pallas_call(attn_fwd_kernel, grid_spec=pltpu.PrefetchScalarGridSpec(nu...]
    ppermute x55, starting transfers between devices: 52.6 us -> 43.4 us  [swap(): lax.ppermute(value, axis, [(i, i ^ bit) for i in range(lax.axis_size(axis...]
    ppermute x55, waiting for transfers between devices: 59.4 us -> 50.6 us  [swap(): lax.ppermute(value, axis, [(i, i ^ bit) for i in range(lax.axis_size(axis...]
  transfers between devices with their start and end apart: 70 -> 70, of which waited for: 26 -> 25; matrix products, arithmetic and copies ran while one was open for 8% -> 8% of each run, Pallas kernels for 39% -> 45%
where the time goes in v5:
time: 576 us; the launch traced here: 570 us
  Pallas kernels  325 us (56%)
  starting transfers between devices  79.9 us (14%)
  waiting for transfers between devices  73.8 us (13%)
  local copies, waits for them, and re-layouts  35.3 us (6%)
  other arithmetic  34.3 us (6%)
  between operations  22.1 us (4%)
    pallas_call x3, Pallas kernels, attn_bwd(): pl.pallas_call(attn_bwd_kernel, grid_spec=pltpu.PrefetchScalarGridSpec(nu...  82.8 us
    ppermute x55, waiting for transfers between devices, swap(): lax.ppermute(value, axis, [(i, i ^ bit) for i in range(lax.axis_size(axis...  50.6 us
    ppermute x55, starting transfers between devices, swap(): lax.ppermute(value, axis, [(i, i ^ bit) for i in range(lax.axis_size(axis...  43.4 us
    pallas_call x2, Pallas kernels, attn_fwd(): pl.pallas_call(attn_fwd_kernel, grid_spec=pltpu.PrefetchScalarGridSpec(nu...  40.8 us
    pallas_call x2, Pallas kernels, gram(): pl.pallas_call(functools.partial(gram_kernel, [len(group) - 1 for group i...  32.5 us
    pallas_call x1, Pallas kernels, inner_forward(): pl.pallas_call(functools.partial(inner_kernel, len(pieces)), grid=(FF //...  30 us
    pallas_call x1, Pallas kernels, feed_back(): pl.pallas_call(feed_back_last_kernel, in_specs=in_specs + [whole, pl.Bloc...  24.6 us
    pallas_call x1, Pallas kernels, outer_forward(): pl.pallas_call(functools.partial(outer_kernel, len(pieces)), grid=(rows /...  22.6 us
  transfers between devices with their start and end apart: 70, of which 25 were waited for; matrix products, arithmetic and copies ran while one was open for 8% of the time, Pallas kernels for 45%

profile of v5, /device:TPU:0, one launch (start us, length us, event | category | flops | bytes accessed | tf_op | source)
XLA Modules:
  0.0 570.2 jit_solution(14667903737073020014)
XLA Ops:
  7.8 2.9 pack_shards.1
  10.8 3.0 collective-permute-start.3
  13.7 1.5 collective-permute-start.2
  15.2 1.4 fusion.23
  27.4 1.7 slice_bitcast_fusion
  30.4 4.0 collective-permute-start
  37.0 3.6 collective-permute-done.5
  46.8 1.6 collective-permute-start.7
  48.9 3.4 collective-permute-start.11
  52.9 1.4 unpack_vectors.1
  54.8 3.3 collective-permute-done.7.refs_4_
  63.6 1.4 collective-permute-start.16
  65.5 1.5 collective-permute-start.19
  67.0 21.9 %project_qkv.1 = (bf16[2048,1024]{1,0:T(8,128)(2,1)}, bf16[2048,1024]{1,0:T(8,128)(2,1)}, bf16[2048,1024]{1,0:T(8,128)(2,1)}, bf16[1024,2048]{1,0:T(8,128)(2,1)}...) custom-call(s32[2]{0:T(128)} %pad_add_fusion.where_ref.tie_ref, bf16[256,3072]{1,0:T(8,128)(2,1)} %get-tuple-element.232.refs_0_, ...), custom_call_target="tpu_custom_call" | custom-call | flops 10737418240 | bytes 31457280 | tf_op jit(solution)/shard_map/project_qkv/pallas_call | solution.py:173
  88.9 2.0 collective-permute-done.16.refs_2_
  92.1 1.6 collective-permute-start.18
  93.7 1.5 collective-permute-start.17
  95.2 20.4 %attn_forward.2 = (bf16[1024,1024]{1,0:T(8,128)(2,1)}, f32[4,8,1024]{2,1,0:T(8,128)}) custom-call(s32[8]{0:T(128)} %get-tuple-element.386.lo_ref, s32[8]{0:T(128)} %get-tuple-element.254.hi_ref, bf16[2048,1024]{1,0:T(8,128)(2,1)} %get-tuple-element.248.q_ref, bf16[2048,1024]{1,0:T(8,128)(2,1)} %get-tuple-element.255.k_ref, ...), custom_call_target="tpu_custom_call" | custom-call | flops 20000000000 | bytes 2097152 | tf_op jit(solution)/shard_map/attn_forward/pallas_call | solution.py:260
  115.6 4.8 collective-permute-done.18.refs_4_
  126.5 1.5 collective-permute-start.28
  128.9 20.4 %attn_forward.3 = (bf16[1024,1024]{1,0:T(8,128)(2,1)}, f32[4,8,1024]{2,1,0:T(8,128)}) custom-call(s32[8]{0:T(128)} %get-tuple-element.386.lo_ref, s32[8]{0:T(128)} %get-tuple-element.254.hi_ref, bf16[2048,1024]{1,0:T(8,128)(2,1)} %get-tuple-element.248.q_ref, ...), custom_call_target="tpu_custom_call", output_to_operand_aliasing={{0}: (7, {}), {1}: (8, {})} | custom-call | flops 20000000000 | bytes 2097152 | tf_op jit(solution)/shard_map/attn_forward/pallas_call | solution.py:260
  153.9 2.1 collective-permute-done.38.refs_8_
  159.3 9.7 %mix_and_norm.1 = (f32[1024,1024]{1,0:T(8,128)}, bf16[1024,1024]{1,0:T(8,128)(2,1)}, f32[1024,1]{1,0:T(8,128)}, bf16[1024,1024]{1,0:T(8,128)(2,1)}) custom-call(s32[2]{0:T(128)} %pad_add_fusion.where_ref.tie_ref, bf16[256,1024]{1,0:T(8,128)(2,1)} %refs_0_, bf16[128,1024]{1,0:T(8,128)(2,1)} %copy-done.17, bf16[128,1024]{1,0:T(8,128)(2,1)} %copy-done.16, ...), custom_call_target="tpu_custom_call" | custom-call | flops 2147483648 | bytes 14680064 | tf_op jit(solution)/shard_map/mix_and_norm/pallas_call | solution.py:427
  169.1 30.0 %inner_forward.1 = (bf16[1024,4096]{1,0:T(8,128)(2,1)}, bf16[1024,4096]{1,0:T(8,128)(2,1)}, bf16[1024,4096]{1,0:T(8,128)(2,1)}) custom-call(s32[2]{0:T(128)} %pad_add_fusion.where_ref.tie_ref, bf16[256,4096]{1,0:T(8,128)(2,1)} %refs_0_.1, bf16[128,4096]{1,0:T(8,128)(2,1)} %collective-permute-done.19.refs_1_, bf16[128,4096]{1,0:T(8,128)(2,1)} %copy-done.13, ...), custom_call_target="tpu_custom_call" | custom-call | flops 8589934592 | bytes 27262976 | tf_op jit(solution)/shard_map/inner_forward/pallas_call | solution.py:469
  199.1 22.6 %outer_forward.1 = (bf16[1024,1024]{1,0:T(8,128)(2,1)}, f32[1024,1024]{1,0:T(8,128)}, bf16[1024,1024]{1,0:T(8,128)(2,1)}, f32[8,1024]{1,0:T(8,128)}, bf16[4096,1024]{1,0:T(8,128)(2,1)}) custom-call(s32[2]{0:T(128)} %pad_add_fusion.where_ref.tie_ref, bf16[1024,1024]{1,0:T(8,128)(2,1)} %refs_0_.2, bf16[512,1024]{1,0:T(8,128)(2,1)} %collective-permute-done.21.refs_1_, ...), custom_call_target="tpu_custom_call" | custom-call | flops 8589934592 | bytes 33554432 | tf_op jit(solution)/shard_map/outer_forward/pallas_call | solution.py:515
  221.7 13.9 %gram.2 = (bf16[4,512,1024]{2,1,0:T(8,128)(2,1)}, bf16[4,512,1024]{2,1,0:T(8,128)(2,1)}) custom-call(s32[5]{0:T(128)} %pad_add_fusion.1.order_ref, bf16[1024,4096]{1,0:T(8,128)(2,1)} %get-tuple-element.339.refs_10_.refs_0_, bf16[1024,1024]{1,0:T(8,128)(2,1)} %get-tuple-element.345.refs_1_.db_ref), custom_call_target="tpu_custom_call" | custom-call | flops 8589934592 | bytes 18874368 | tf_op jit(solution)/shard_map/gram/pallas_call | solution.py:567
  235.9 19.1 %feed_back_first.1 = (bf16[1024,2048]{1,0:T(8,128)(2,1)}, f32[8,2048]{1,0:T(8,128)}, f32[1024,1024]{1,0:T(8,128)}) custom-call(s32[2]{0:T(128)} %pad_add_fusion.where_ref.tie_ref, bf16[1024,1024]{1,0:T(8,128)(2,1)} %get-tuple-element.345.refs_1_.db_ref, bf16[4096,1024]{1,0:T(8,128)(2,1)} %get-tuple-element.348.wo_ref, ...), custom_call_target="tpu_custom_call" | custom-call | flops 8589934592 | bytes 31457280 | tf_op jit(solution)/shard_map/feed_back_first/pallas_call | solution.py:645
  255.0 6.3 %add_convert_fusion.1 = bf16[4,512,1024]{2,1,0:T(8,128)(2,1)} fusion(bf16[4,512,1024]{2,1,0:T(8,128)(2,1)} %collective-permute-done.39, bf16[4,512,1024]{2,1,0:T(8,128)(2,1)S(1)} %copy-done.1), kind=kLoop, calls=%fused_computation.1 | loop fusion | flops 8388608 | bytes 12582912 | tf_op jit(solution)/shard_map/convert_element_type | solution.py:816
  261.4 24.6 %feed_back_last.1 = (bf16[1024,2048]{1,0:T(8,128)(2,1)}, f32[8,2048]{1,0:T(8,128)}, f32[1024,1024]{1,0:T(8,128)}, bf16[1024,1024]{1,0:T(8,128)(2,1)}, f32[8,1024]{1,0:T(8,128)}) custom-call(s32[2]{0:T(128)} %pad_add_fusion.where_ref.tie_ref, bf16[1024,1024]{1,0:T(8,128)(2,1)} %get-tuple-element.345.refs_1_.db_ref, ...), custom_call_target="tpu_custom_call" | custom-call | flops 8589934592 | bytes 31457280 | tf_op jit(solution)/shard_map/feed_back_last/pallas_call | solution.py:653
  286.0 18.7 %gram.3 = (bf16[4,128,5120]{2,1,0:T(8,128)(2,1)}, bf16[4,128,5120]{2,1,0:T(8,128)(2,1)}) custom-call(s32[5]{0:T(128)} %pad_add_fusion.1.order_ref, bf16[1024,1024]{1,0:T(8,128)(2,1)} %get-tuple-element.337.refs_9_.refs_0_, bf16[1024,2048]{1,0:T(8,128)(2,1)} %get-tuple-element.352.refs_1_, bf16[1024,2048]{1,0:T(8,128)(2,1)} %get-tuple-element.361.refs_2_, ...), custom_call_target="tpu_custom_call" | custom-call | flops 10737418240 | bytes 23068672 | tf_op jit(solution)/shard_map/gram/pallas_call | solution.py:567
  304.7 7.1 %context_back.1 = (bf16[1024,1024]{1,0:T(8,128)(2,1)}, f32[4,8,1024]{2,1,0:T(8,128)}) custom-call(bf16[1024,1024]{1,0:T(8,128)(2,1)} %get-tuple-element.364.refs_4_.d_ref, bf16[1024,1024]{1,0:T(8,128)(2,1)} %get-tuple-element.365.w_ref, bf16[1024,1024]{1,0:T(8,128)(2,1)} %get-tuple-element.274.refs_9_.refs_3_.context_ref), custom_call_target="tpu_custom_call" | custom-call | flops 2147483648 | bytes 8388608 | tf_op jit(solution)/shard_map/context_back/pallas_call | solution.py:681
  311.8 1.8 collective-permute-done.40
  313.6 6.9 %add_convert_fusion = bf16[4,128,5120]{2,1,0:T(8,128)(2,1)} fusion(bf16[4,128,5120]{2,1,0:T(8,128)(2,1)} %collective-permute-done.40, bf16[4,128,5120]{2,1,0:T(8,128)(2,1)S(1)} %copy-done), kind=kLoop, calls=%fused_computation | loop fusion | flops 10485760 | bytes 15728640 | tf_op jit(solution)/shard_map/convert_element_type | solution.py:816
  320.6 1.5 copy-done.2
  322.1 1.5 fusion.19
  324.9 4.0 collective-permute-start.42
  328.9 3.5 collective-permute-start.44
  336.6 12.5 %collective-permute-start.41 = (bf16[512,1024]{1,0:T(8,128)(2,1)S(1)}, bf16[512,1024]{1,0:T(8,128)(2,1)S(1)}, u32[]{:S(2)}, u32[]{:S(2)}) collective-permute-start(bf16[512,1024]{1,0:T(8,128)(2,1)S(1)} %bitcast.144), channel_id=1, source_target_pairs={{0,8},{4,12},{24,16},{28,20},{1,9},{5,13},{25,17},{29,21},{2,10},{... | collective-permute-start | bytes 3145736 | tf_op jit(solution)/shard_map/ppermute | solution.py:856
  350.0 21.8 %attn_backward.3 = (bf16[1024,512]{1,0:T(8,128)(2,1)}, bf16[2,1024,512]{2,1,0:T(8,128)(2,1)}) custom-call(s32[8]{0:T(128)} %get-tuple-element.386.lo_ref, s32[8]{0:T(128)} %get-tuple-element.254.hi_ref, bf16[2048,1024]{1,0:T(8,128)(2,1)} %get-tuple-element.248.q_ref, bf16[512,1024]{1,0:T(8,128)(2,1)} %collective-permute-done.42.before_ref, ...), custom_call_target="tpu_custom_call" | custom-call | flops 15000000512 | bytes 4194304 | tf_op jit(solution)/shard_map/attn_backward/pallas_call | solution.py:359
  372.9 21.3 %attn_backward.4 = (bf16[1024,512]{1,0:T(8,128)(2,1)}, bf16[2,1024,512]{2,1,0:T(8,128)(2,1)}) custom-call(s32[8]{0:T(128)} %get-tuple-element.386.lo_ref, s32[8]{0:T(128)} %get-tuple-element.254.hi_ref, bf16[2048,1024]{1,0:T(8,128)(2,1)} %get-tuple-element.248.q_ref, ...), custom_call_target="tpu_custom_call", output_to_operand_aliasing={{0}: (12, {}), {1}: (13, {})} | custom-call | flops 15000000512 | bytes 4194304 | tf_op jit(solution)/shard_map/attn_backward/pallas_call | solution.py:359
  394.7 8.5 %qkv_gradient.2 = (bf16[4,128,1536]{2,1,0:T(8,128)(2,1)}, bf16[4,128,1536]{2,1,0:T(8,128)(2,1)}, f32[8,1024]{1,0:T(8,128)}) custom-call(s32[5]{0:T(128)} %pad_add_fusion.2.order_ref, bf16[1024,1024]{1,0:T(8,128)(2,1)} %bitcast.133, bf16[1024,512]{1,0:T(8,128)(2,1)} %get-tuple-element.378.dq_ref.refs_0_, ...), custom_call_target="tpu_custom_call" | custom-call | flops 3221225472 | bytes 16777216 | tf_op jit(solution)/shard_map/qkv_gradient/pallas_call | solution.py:735
  403.7 1.4 collective-permute-start.48
  405.1 39.7 %attn_backward.5 = (bf16[1024,512]{1,0:T(8,128)(2,1)}, bf16[2,1024,512]{2,1,0:T(8,128)(2,1)}) custom-call(s32[8]{0:T(128)} %get-tuple-element.386.lo_ref, s32[8]{0:T(128)} %get-tuple-element.254.hi_ref, bf16[2048,1024]{1,0:T(8,128)(2,1)} %get-tuple-element.248.q_ref, bf16[512,1024]{1,0:T(8,128)(2,1)} %collective-permute-done.42.before_ref, ...), custom_call_target="tpu_custom_call" | custom-call | flops 30000001024 | bytes 4194304 | tf_op jit(solution)/shard_map/attn_backward/pallas_call | solution.py:359
  444.9 1.8 add_convert_fusion.6
  446.7 9.1 %collective-permute-done.48 = bf16[512,1024]{1,0:T(8,128)(2,1)S(1)} collective-permute-done((bf16[512,1024]{1,0:T(8,128)(2,1)S(1)}, bf16[512,1024]{1,0:T(8,128)(2,1)S(1)}, u32[]{:S(2)}, u32[]{:S(2)}) %collective-permute-start.48) | collective-permute-done | bytes 1048608 | tf_op jit(solution)/shard_map/ppermute | solution.py:856
  456.0 2.0 collective-permute-start.50
  458.2 8.6 %qkv_gradient.3 = (bf16[4,128,1664]{2,1,0:T(8,128)(2,1)}, bf16[4,128,1664]{2,1,0:T(8,128)(2,1)}, f32[8,1024]{1,0:T(8,128)}) custom-call(s32[5]{0:T(128)} %pad_add_fusion.2.order_ref, bf16[1024,1024]{1,0:T(8,128)(2,1)} %bitcast.134, bf16[1024,512]{1,0:T(8,128)(2,1)} %get-tuple-element.387.dq_ref.refs_2_, ...), custom_call_target="tpu_custom_call" | custom-call | flops 3489660928 | bytes 16777216 | tf_op jit(solution)/shard_map/qkv_gradient/pallas_call | solution.py:735
  469.6 12.2 %input_back.1 = f32[1024,1024]{1,0:T(8,128)} custom-call(f32[1024,1024]{1,0:T(8,128)} %get-tuple-element.357.base_ref, bf16[1024,512]{1,0:T(8,128)(2,1)} %get-tuple-element.378.dq_ref.refs_0_, bf16[2,1024,512]{2,1,0:T(8,128)(2,1)} %get-tuple-element.379.joined_ref.refs_1_, bf16[1024,512]{1,0:T(8,128)(2,1)} %get-tuple-element.387.dq_ref.refs_2_, ...), custom_call_target="tpu_custom_call" | custom-call | flops 6442450944 | bytes 20971520 | tf_op jit(solution)/shard_map/input_back/pallas_call | solution.py:766
  484.2 4.4 collective-permute-start.56
  488.8 1.9 collective-permute-start.55
  490.8 5.9 %collective-permute-done.56 = bf16[128,1536]{1,0:T(8,128)(2,1)S(1)} collective-permute-done((bf16[128,1536]{1,0:T(8,128)(2,1)S(1)}, bf16[128,1536]{1,0:T(8,128)(2,1)S(1)}, u32[]{:S(2)}, u32[]{:S(2)}) %collective-permute-start.56) | collective-permute-done | bytes 393248 | tf_op jit(solution)/shard_map/ppermute | solution.py:856
  496.8 3.0 collective-permute-done.54
  500.1 1.8 collective-permute-start.57
  501.9 1.7 collective-permute-start.58
  504.3 1.7 collective-permute-done.57
  506.1 1.7 collective-permute-done.58
  509.5 2.4 maximum_convert_fusion
  511.9 6.0 %collective-permute-start.60 = (bf16[128,1664]{1,0:T(8,128)(2,1)S(1)}, bf16[128,1664]{1,0:T(8,128)(2,1)S(1)}, u32[]{:S(2)}, u32[]{:S(2)}) collective-permute-start(bf16[128,1664]{1,0:T(8,128)(2,1)S(1)} %pad_maximum_fusion.5), channel_id=1, source_target_pairs={{0,8},{4,12},{8,0},{12,4},{16,24},{20,28},{24,16},{28,20},{1,9},{5... | collective-permute-start | bytes 1277960 | tf_op jit(solution)/shard_map/ppermute | solution.py:779
  517.9 7.4 %collective-permute-done.63 = bf16[128,1536]{1,0:T(8,128)(2,1)S(1)} collective-permute-done((bf16[128,1536]{1,0:T(8,128)(2,1)S(1)}, bf16[128,1536]{1,0:T(8,128)(2,1)S(1)}, u32[]{:S(2)}, u32[]{:S(2)}) %collective-permute-start.63) | collective-permute-done | bytes 393248 | tf_op jit(solution)/shard_map/ppermute | solution.py:856
  525.4 5.1 collective-permute-done.60
  532.0 2.5 fusion
  534.5 13.1 %collective-permute-done.61 = bf16[128,1664]{1,0:T(8,128)(2,1)S(1)} collective-permute-done((bf16[128,1664]{1,0:T(8,128)(2,1)S(1)}, bf16[128,1664]{1,0:T(8,128)(2,1)S(1)}, u32[]{:S(2)}, u32[]{:S(2)}) %collective-permute-start.61) | collective-permute-done | bytes 426016 | tf_op jit(solution)/shard_map/ppermute | solution.py:779
  548.2 1.4 collective-permute-done.62
  558.0 2.2 pad_maximum_fusion.3
  (272 shorter events, 68.9 us)
Async XLA Ops:
  7.2 313.3 %reduce-scatter.7.cloned.1.call-start = ((), (), s32[]{:S(2)}) async-start(), calls=%async_computation.3 | async-start | bytes 5242880
  10.8 29.8 %collective-permute-start.3 = (bf16[128,3072]{1,0:T(8,128)(2,1)}, bf16[128,3072]{1,0:T(8,128)(2,1)}, u32[]{:S(2)}, u32[]{:S(2)}) collective-permute-start(bf16[128,3072]{1,0:T(8,128)(2,1)} %get-tuple-element.227), channel_id=1, source_target_pairs={{0,2},{1,3},{2,0},{3,1},{4,6},{5,7},{6,4},{7,5},{8,10},{9,11},{10,... | collective-permute-start | bytes 2359304 | tf_op jit(solution)/shard_map/ppermute | solution.py:779
  13.7 26.9 %collective-permute-start.2 = (bf16[128,3072]{1,0:T(8,128)(2,1)}, bf16[128,3072]{1,0:T(8,128)(2,1)}, u32[]{:S(2)}, u32[]{:S(2)}) collective-permute-start(bf16[128,3072]{1,0:T(8,128)(2,1)} %get-tuple-element.227), channel_id=1, source_target_pairs={{0,1},{1,0},{2,3},{3,2},{4,5},{5,4},{6,7},{7,6},{8,9},{9,8},{10,11... | collective-permute-start | bytes 2359304 | tf_op jit(solution)/shard_map/ppermute | solution.py:779
  26.8 9.9 %collective-permute-start.4 = (bf16[1,3200]{1,0:T(2,128)(2,1)S(1)}, bf16[1,3200]{1,0:T(2,128)(2,1)S(1)}, u32[]{:S(2)}, u32[]{:S(2)}) collective-permute-start(bf16[1,3200]{1,0:T(2,128)(2,1)S(1)} %reshape.188), channel_id=1, source_target_pairs={{0,1},{1,0},{2,3},{3,2},{4,5},{5,4},{6,7},{7,6},{8,9},{9,8},{10,11... | collective-permute-start | bytes 19208 | tf_op jit(solution)/shard_map/ppermute | solution.py:779
  29.1 25.7 %collective-permute-start.1 = (bf16[512,1024]{1,0:T(8,128)(2,1)S(1)}, bf16[512,1024]{1,0:T(8,128)(2,1)}, u32[]{:S(2)}, u32[]{:S(2)}) collective-permute-start(bf16[512,1024]{1,0:T(8,128)(2,1)S(1)} %get-tuple-element.446), channel_id=1, source_target_pairs={{4,0},{8,4},{12,8},{16,12},{20,16},{24,20},{28,24},{5,1},{9,5},{13... | collective-permute-start | bytes 3145736 | tf_op jit(solution)/shard_map/ppermute | solution.py:975
  30.4 24.4 %collective-permute-start = (bf16[512,1024]{1,0:T(8,128)(2,1)S(1)}, bf16[512,1024]{1,0:T(8,128)(2,1)}, u32[]{:S(2)}, u32[]{:S(2)}) collective-permute-start(bf16[512,1024]{1,0:T(8,128)(2,1)S(1)} %get-tuple-element.447), channel_id=1, source_target_pairs={{0,4},{4,8},{8,12},{12,16},{16,20},{20,24},{24,28},{1,5},{5,9},{9,... | collective-permute-start | bytes 3145736 | tf_op jit(solution)/shard_map/ppermute | solution.py:974
  43.8 5.1 collective-permute-start.10
  46.8 11.3 %collective-permute-start.7 = (bf16[64,3072]{1,0:T(8,128)(2,1)S(1)}, bf16[64,3072]{1,0:T(8,128)(2,1)}, u32[]{:S(2)}, u32[]{:S(2)}) collective-permute-start(bf16[64,3072]{1,0:T(8,128)(2,1)S(1)} %slice.213), channel_id=1, source_target_pairs={{0,1},{1,0},{2,3},{3,2},{4,5},{5,4},{6,7},{7,6},{8,9},{9,8},{10,11... | collective-permute-start | bytes 1179656 | tf_op jit(solution)/shard_map/ppermute | solution.py:779
  48.4 10.9 %collective-permute-start.6 = (bf16[64,3072]{1,0:T(8,128)(2,1)S(1)}, bf16[64,3072]{1,0:T(8,128)(2,1)}, u32[]{:S(2)}, u32[]{:S(2)}) collective-permute-start(bf16[64,3072]{1,0:T(8,128)(2,1)S(1)} %slice.212), channel_id=1, source_target_pairs={{0,2},{1,3},{2,0},{3,1},{4,6},{5,7},{6,4},{7,5},{8,10},{9,11},{10,... | collective-permute-start | bytes 1179656 | tf_op jit(solution)/shard_map/ppermute | solution.py:779
  48.9 5.4 collective-permute-start.11
  59.3 6.2 %collective-permute-start.12 = (bf16[128,3072]{1,0:T(8,128)(2,1)}, bf16[128,3072]{1,0:T(8,128)(2,1)}, u32[]{:S(2)}, u32[]{:S(2)}) collective-permute-start(bf16[128,3072]{1,0:T(8,128)(2,1)} %collective-permute-done.2.refs_1_), channel_id=1, source_target_pairs={{0,4},{4,0},{8,12},{12,8},{16,20},{20,16},{24,28},{28,24},{1,5},{5... | collective-permute-start | bytes 2359304 | tf_op jit(solution)/shard_map/ppermute | solution.py:779
  59.3 7.7 %collective-permute-start.13 = (bf16[128,3072]{1,0:T(8,128)(2,1)}, bf16[128,3072]{1,0:T(8,128)(2,1)}, u32[]{:S(2)}, u32[]{:S(2)}) collective-permute-start(bf16[128,3072]{1,0:T(8,128)(2,1)} %collective-permute-done.3.refs_2_), channel_id=1, source_target_pairs={{0,4},{4,0},{8,12},{12,8},{16,20},{20,16},{24,28},{28,24},{1,5},{5... | collective-permute-start | bytes 2359304 | tf_op jit(solution)/shard_map/ppermute | solution.py:779
  59.8 3.8 collective-permute-start.14
  59.8 5.2 collective-permute-start.15
  60.3 33.4 %collective-permute-start.20 = (bf16[128,4096]{1,0:T(8,128)(2,1)S(1)}, bf16[128,4096]{1,0:T(8,128)(2,1)S(1)}, u32[]{:S(2)}, u32[]{:S(2)}) collective-permute-start(bf16[128,4096]{1,0:T(8,128)(2,1)S(1)} %constant_dynamic-slice_fusion.1), channel_id=1, source_target_pairs={{0,2},{1,3},{2,0},{3,1},{4,6},{5,7},{6,4},{7,5},{8,10},{9,11},{10,... | collective-permute-start | bytes 3145736 | tf_op jit(solution)/shard_map/ppermute | solution.py:779
  63.6 27.4 %collective-permute-start.16 = (bf16[128,1024]{1,0:T(8,128)(2,1)S(1)}, bf16[128,1024]{1,0:T(8,128)(2,1)S(1)}, u32[]{:S(2)}, u32[]{:S(2)}) collective-permute-start(bf16[128,1024]{1,0:T(8,128)(2,1)S(1)} %constant_dynamic-slice_fusion.2), channel_id=1, source_target_pairs={{0,2},{1,3},{2,0},{3,1},{4,6},{5,7},{6,4},{7,5},{8,10},{9,11},{10,... | collective-permute-start | bytes 786440 | tf_op jit(solution)/shard_map/ppermute | solution.py:779
  65.0 26.0 %collective-permute-start.8 = (bf16[128,1024]{1,0:T(8,128)(2,1)S(1)}, bf16[128,1024]{1,0:T(8,128)(2,1)S(1)}, u32[]{:S(2)}, u32[]{:S(2)}) collective-permute-start(bf16[128,1024]{1,0:T(8,128)(2,1)S(1)} %constant_dynamic-slice_fusion.2), channel_id=1, source_target_pairs={{0,1},{1,0},{2,3},{3,2},{4,5},{5,4},{6,7},{7,6},{8,9},{9,8},{10,11... | collective-permute-start | bytes 786440 | tf_op jit(solution)/shard_map/ppermute | solution.py:779
  65.5 50.1 %collective-permute-start.19 = (bf16[128,4096]{1,0:T(8,128)(2,1)S(1)}, bf16[128,4096]{1,0:T(8,128)(2,1)}, u32[]{:S(2)}, u32[]{:S(2)}) collective-permute-start(bf16[128,4096]{1,0:T(8,128)(2,1)S(1)} %constant_dynamic-slice_fusion.1), channel_id=1, source_target_pairs={{0,1},{1,0},{2,3},{3,2},{4,5},{5,4},{6,7},{7,6},{8,9},{9,8},{10,11... | collective-permute-start | bytes 3145736 | tf_op jit(solution)/shard_map/ppermute | solution.py:779
  91.0 29.4 %collective-permute-start.22 = (bf16[512,1024]{1,0:T(8,128)(2,1)S(1)}, bf16[512,1024]{1,0:T(8,128)(2,1)}, u32[]{:S(2)}, u32[]{:S(2)}) collective-permute-start(bf16[512,1024]{1,0:T(8,128)(2,1)S(1)} %constant_dynamic-slice_fusion), channel_id=1, source_target_pairs={{0,2},{1,3},{2,0},{3,1},{4,6},{5,7},{6,4},{7,5},{8,10},{9,11},{10,... | collective-permute-start | bytes 3145736 | tf_op jit(solution)/shard_map/ppermute | solution.py:779
  91.6 28.8 %collective-permute-start.21 = (bf16[512,1024]{1,0:T(8,128)(2,1)S(1)}, bf16[512,1024]{1,0:T(8,128)(2,1)}, u32[]{:S(2)}, u32[]{:S(2)}) collective-permute-start(bf16[512,1024]{1,0:T(8,128)(2,1)S(1)} %constant_dynamic-slice_fusion), channel_id=1, source_target_pairs={{0,1},{1,0},{2,3},{3,2},{4,5},{5,4},{6,7},{7,6},{8,9},{9,8},{10,11... | collective-permute-start | bytes 3145736 | tf_op jit(solution)/shard_map/ppermute | solution.py:779
  92.1 28.3 %collective-permute-start.18 = (bf16[64,1024]{1,0:T(8,128)(2,1)S(1)}, bf16[64,1024]{1,0:T(8,128)(2,1)S(1)}, u32[]{:S(2)}, u32[]{:S(2)}) collective-permute-start(bf16[64,1024]{1,0:T(8,128)(2,1)S(1)} %slice.219), channel_id=1, source_target_pairs={{0,1},{1,0},{2,3},{3,2},{4,5},{5,4},{6,7},{7,6},{8,9},{9,8},{10,11... | collective-permute-start | bytes 393224 | tf_op jit(solution)/shard_map/ppermute | solution.py:779
  93.7 26.7 %collective-permute-start.17 = (bf16[64,1024]{1,0:T(8,128)(2,1)S(1)}, bf16[64,1024]{1,0:T(8,128)(2,1)S(1)}, u32[]{:S(2)}, u32[]{:S(2)}) collective-permute-start(bf16[64,1024]{1,0:T(8,128)(2,1)S(1)} %slice.218), channel_id=1, source_target_pairs={{0,2},{1,3},{2,0},{3,1},{4,6},{5,7},{6,4},{7,5},{8,10},{9,11},{10,... | collective-permute-start | bytes 393224 | tf_op jit(solution)/shard_map/ppermute | solution.py:779
  120.4 7.5 %collective-permute-start.23 = (bf16[128,1024]{1,0:T(8,128)(2,1)S(1)}, bf16[128,1024]{1,0:T(8,128)(2,1)S(1)}, u32[]{:S(2)}, u32[]{:S(2)}) collective-permute-start(bf16[128,1024]{1,0:T(8,128)(2,1)S(1)} %collective-permute-done.8.refs_1_), channel_id=1, source_target_pairs={{0,4},{4,0},{8,12},{12,8},{16,20},{20,16},{24,28},{28,24},{1,5},{5... | collective-permute-start | bytes 786440 | tf_op jit(solution)/shard_map/ppermute | solution.py:779
  120.5 4.9 collective-permute-start.25
  121.0 5.5 collective-permute-start.26
  121.1 28.2 %collective-permute-start.24 = (bf16[128,1024]{1,0:T(8,128)(2,1)S(1)}, bf16[128,1024]{1,0:T(8,128)(2,1)S(1)}, u32[]{:S(2)}, u32[]{:S(2)}) collective-permute-start(bf16[128,1024]{1,0:T(8,128)(2,1)S(1)} %collective-permute-done.16.refs_2_), channel_id=1, source_target_pairs={{0,4},{4,0},{8,12},{12,8},{16,20},{20,16},{24,28},{28,24},{1,5},{5... | collective-permute-start | bytes 786440 | tf_op jit(solution)/shard_map/ppermute | solution.py:779
  124.8 24.5 %collective-permute-start.30 = (bf16[256,1024]{1,0:T(8,128)(2,1)S(1)}, bf16[256,1024]{1,0:T(8,128)(2,1)S(1)}, u32[]{:S(2)}, u32[]{:S(2)}) collective-permute-start(bf16[256,1024]{1,0:T(8,128)(2,1)S(1)} %slice.223), channel_id=1, source_target_pairs={{0,1},{1,0},{2,3},{3,2},{4,5},{5,4},{6,7},{7,6},{8,9},{9,8},{10,11... | collective-permute-start | bytes 1572872 | tf_op jit(solution)/shard_map/ppermute | solution.py:779
  125.4 23.9 %collective-permute-start.29 = (bf16[256,1024]{1,0:T(8,128)(2,1)S(1)}, bf16[256,1024]{1,0:T(8,128)(2,1)S(1)}, u32[]{:S(2)}, u32[]{:S(2)}) collective-permute-start(bf16[256,1024]{1,0:T(8,128)(2,1)S(1)} %slice.222), channel_id=1, source_target_pairs={{0,2},{1,3},{2,0},{3,1},{4,6},{5,7},{6,4},{7,5},{8,10},{9,11},{10,... | collective-permute-start | bytes 1572872 | tf_op jit(solution)/shard_map/ppermute | solution.py:779
  126.5 23.5 %collective-permute-start.28 = (bf16[64,4096]{1,0:T(8,128)(2,1)S(1)}, bf16[64,4096]{1,0:T(8,128)(2,1)S(1)}, u32[]{:S(2)}, u32[]{:S(2)}) collective-permute-start(bf16[64,4096]{1,0:T(8,128)(2,1)S(1)} %slice.221), channel_id=1, source_target_pairs={{0,1},{1,0},{2,3},{3,2},{4,5},{5,4},{6,7},{7,6},{8,9},{9,8},{10,11... | collective-permute-start | bytes 1572872 | tf_op jit(solution)/shard_map/ppermute | solution.py:779
  128.0 22.4 %collective-permute-start.27 = (bf16[64,4096]{1,0:T(8,128)(2,1)S(1)}, bf16[64,4096]{1,0:T(8,128)(2,1)}, u32[]{:S(2)}, u32[]{:S(2)}) collective-permute-start(bf16[64,4096]{1,0:T(8,128)(2,1)S(1)} %slice.220), channel_id=1, source_target_pairs={{0,2},{1,3},{2,0},{3,1},{4,6},{5,7},{6,4},{7,5},{8,10},{9,11},{10,... | collective-permute-start | bytes 1572872 | tf_op jit(solution)/shard_map/ppermute | solution.py:779
  150.9 5.1 collective-permute-start.38
  150.9 18.1 %collective-permute-start.36 = (bf16[512,1024]{1,0:T(8,128)(2,1)}, bf16[512,1024]{1,0:T(8,128)(2,1)S(1)}, u32[]{:S(2)}, u32[]{:S(2)}) collective-permute-start(bf16[512,1024]{1,0:T(8,128)(2,1)} %collective-permute-done.22.refs_2_), channel_id=1, source_target_pairs={{0,4},{4,0},{8,12},{12,8},{16,20},{20,16},{24,28},{28,24},{1,5},{5... | collective-permute-start | bytes 3145736 | tf_op jit(solution)/shard_map/ppermute | solution.py:779
  151.4 17.6 %collective-permute-start.35 = (bf16[512,1024]{1,0:T(8,128)(2,1)}, bf16[512,1024]{1,0:T(8,128)(2,1)S(1)}, u32[]{:S(2)}, u32[]{:S(2)}) collective-permute-start(bf16[512,1024]{1,0:T(8,128)(2,1)} %collective-permute-done.21.refs_1_), channel_id=1, source_target_pairs={{0,4},{4,0},{8,12},{12,8},{16,20},{20,16},{24,28},{28,24},{1,5},{5... | collective-permute-start | bytes 3145736 | tf_op jit(solution)/shard_map/ppermute | solution.py:779
  152.3 16.8 %collective-permute-start.32 = (bf16[128,4096]{1,0:T(8,128)(2,1)S(1)}, bf16[128,4096]{1,0:T(8,128)(2,1)}, u32[]{:S(2)}, u32[]{:S(2)}) collective-permute-start(bf16[128,4096]{1,0:T(8,128)(2,1)S(1)} %collective-permute-done.20.refs_2_), channel_id=1, source_target_pairs={{0,4},{4,0},{8,12},{12,8},{16,20},{20,16},{24,28},{28,24},{1,5},{5... | collective-permute-start | bytes 3145736 | tf_op jit(solution)/shard_map/ppermute | solution.py:779
  153.8 15.3 %collective-permute-start.31 = (bf16[128,4096]{1,0:T(8,128)(2,1)}, bf16[128,4096]{1,0:T(8,128)(2,1)}, u32[]{:S(2)}, u32[]{:S(2)}) collective-permute-start(bf16[128,4096]{1,0:T(8,128)(2,1)} %collective-permute-done.19.refs_1_), channel_id=1, source_target_pairs={{0,4},{4,0},{8,12},{12,8},{16,20},{20,16},{24,28},{28,24},{1,5},{5... | collective-permute-start | bytes 3145736 | tf_op jit(solution)/shard_map/ppermute | solution.py:779
  156.9 12.1 %collective-permute-start.33 = (bf16[64,4096]{1,0:T(8,128)(2,1)}, bf16[64,4096]{1,0:T(8,128)(2,1)}, u32[]{:S(2)}, u32[]{:S(2)}) collective-permute-start(bf16[64,4096]{1,0:T(8,128)(2,1)} %collective-permute-done.27.refs_3_), channel_id=1, source_target_pairs={{0,4},{4,0},{8,12},{12,8},{16,20},{20,16},{24,28},{28,24},{1,5},{5... | collective-permute-start | bytes 1572872 | tf_op jit(solution)/shard_map/ppermute | solution.py:779
  235.6 19.4 %collective-permute-start.39 = (bf16[4,512,1024]{2,1,0:T(8,128)(2,1)}, bf16[4,512,1024]{2,1,0:T(8,128)(2,1)}, u32[]{:S(2)}, u32[]{:S(2)}) collective-permute-start(bf16[4,512,1024]{2,1,0:T(8,128)(2,1)} %get-tuple-element.347), channel_id=1, source_target_pairs={{0,4},{4,0},{8,12},{12,8},{16,20},{20,16},{24,28},{28,24},{1,5},{5... | collective-permute-start | bytes 12582920 | tf_op jit(solution)/shard_map/ppermute | solution.py:779
  261.3 142.3 %reduce-scatter.9.cloned.1.call-start = ((), (), s32[]{:S(2)}) async-start(), calls=%async_computation.4 | async-start | bytes 6553600
  304.6 9.0 %collective-permute-start.40 = (bf16[4,128,5120]{2,1,0:T(8,128)(2,1)}, bf16[4,128,5120]{2,1,0:T(8,128)(2,1)}, u32[]{:S(2)}, u32[]{:S(2)}) collective-permute-start(bf16[4,128,5120]{2,1,0:T(8,128)(2,1)} %get-tuple-element.363), channel_id=1, source_target_pairs={{0,4},{4,0},{8,12},{12,8},{16,20},{20,16},{24,28},{28,24},{1,5},{5... | collective-permute-start | bytes 15728648 | tf_op jit(solution)/shard_map/ppermute | solution.py:779
  320.6 163.5 %all-reduce.5.cloned.1.call-start = ((), (), s32[]{:S(2)}) async-start(), calls=%async_computation.2 | async-start | bytes 2621440 | tf_op jit(solution)/shard_map/psum | solution.py:890
  323.6 25.4 %collective-permute-start.43 = (bf16[512,1024]{1,0:T(8,128)(2,1)}, bf16[512,1024]{1,0:T(8,128)(2,1)S(1)}, u32[]{:S(2)}, u32[]{:S(2)}) collective-permute-start(bf16[512,1024]{1,0:T(8,128)(2,1)} %get-tuple-element.444), channel_id=1, source_target_pairs={{4,0},{8,4},{12,8},{16,12},{20,16},{24,20},{28,24},{5,1},{9,5},{13... | collective-permute-start | bytes 3145736 | tf_op jit(solution)/shard_map/ppermute | solution.py:1059
  324.9 24.2 %collective-permute-start.42 = (bf16[512,1024]{1,0:T(8,128)(2,1)}, bf16[512,1024]{1,0:T(8,128)(2,1)}, u32[]{:S(2)}, u32[]{:S(2)}) collective-permute-start(bf16[512,1024]{1,0:T(8,128)(2,1)} %get-tuple-element.445), channel_id=1, source_target_pairs={{0,4},{4,8},{8,12},{12,16},{16,20},{20,24},{24,28},{1,5},{5,9},{9,... | collective-permute-start | bytes 3145736 | tf_op jit(solution)/shard_map/ppermute | solution.py:1058
  328.9 6.1 %collective-permute-start.44 = (f32[2,4,8,512]{3,2,1,0:T(8,128)S(1)}, f32[2,4,8,512]{3,2,1,0:T(8,128)S(1)}, u32[]{:S(2)}, u32[]{:S(2)}) collective-permute-start(f32[2,4,8,512]{3,2,1,0:T(8,128)S(1)} %get-tuple-element.464), channel_id=1, source_target_pairs={{0,4},{4,8},{8,12},{12,16},{16,20},{20,24},{24,28},{1,5},{5,9},{9,... | collective-permute-start | bytes 393224 | tf_op jit(solution)/shard_map/ppermute | solution.py:1058
  336.6 35.2 %collective-permute-start.41 = (bf16[512,1024]{1,0:T(8,128)(2,1)S(1)}, bf16[512,1024]{1,0:T(8,128)(2,1)S(1)}, u32[]{:S(2)}, u32[]{:S(2)}) collective-permute-start(bf16[512,1024]{1,0:T(8,128)(2,1)S(1)} %bitcast.144), channel_id=1, source_target_pairs={{0,8},{4,12},{24,16},{28,20},{1,9},{5,13},{25,17},{29,21},{2,10},{... | collective-permute-start | bytes 3145736 | tf_op jit(solution)/shard_map/ppermute | solution.py:856
  372.2 22.1 %collective-permute-start.46 = (bf16[512,1024]{1,0:T(8,128)(2,1)S(1)}, bf16[512,1024]{1,0:T(8,128)(2,1)S(1)}, u32[]{:S(2)}, u32[]{:S(2)}) collective-permute-start(bf16[512,1024]{1,0:T(8,128)(2,1)S(1)} %add_convert_fusion.3), channel_id=1, source_target_pairs={{8,16},{12,20},{16,8},{20,12},{9,17},{13,21},{17,9},{21,13},{10,18... | collective-permute-start | bytes 3145736 | tf_op jit(solution)/shard_map/ppermute | solution.py:856
  403.2 41.6 %collective-permute-start.47 = (bf16[4,128,1536]{2,1,0:T(8,128)(2,1)}, bf16[4,128,1536]{2,1,0:T(8,128)(2,1)}, u32[]{:S(2)}, u32[]{:S(2)}) collective-permute-start(bf16[4,128,1536]{2,1,0:T(8,128)(2,1)} %get-tuple-element.390), channel_id=1, source_target_pairs={{0,4},{4,0},{8,12},{12,8},{16,20},{20,16},{24,28},{28,24},{1,5},{5... | collective-permute-start | bytes 4718600 | tf_op jit(solution)/shard_map/ppermute | solution.py:779
  403.7 52.1 %collective-permute-start.48 = (bf16[512,1024]{1,0:T(8,128)(2,1)S(1)}, bf16[512,1024]{1,0:T(8,128)(2,1)S(1)}, u32[]{:S(2)}, u32[]{:S(2)}) collective-permute-start(bf16[512,1024]{1,0:T(8,128)(2,1)S(1)} %fusion.1), channel_id=1, source_target_pairs={{8,0},{12,4},{16,24},{20,28},{9,1},{13,5},{17,25},{21,29},{10,2},{... | collective-permute-start | bytes 3145736 | tf_op jit(solution)/shard_map/ppermute | solution.py:856
  456.0 11.4 %collective-permute-start.50 = (bf16[2,64,1536]{2,1,0:T(8,128)(2,1)S(1)}, bf16[2,64,1536]{2,1,0:T(8,128)(2,1)S(1)}, u32[]{:S(2)}, u32[]{:S(2)}) collective-permute-start(bf16[2,64,1536]{2,1,0:T(8,128)(2,1)S(1)} %slice_bitcast_fusion.6), channel_id=1, source_target_pairs={{0,2},{1,3},{2,0},{3,1},{4,6},{5,7},{6,4},{7,5},{8,10},{9,11},{10,... | collective-permute-start | bytes 1179656 | tf_op jit(solution)/shard_map/ppermute | solution.py:779
  458.0 10.5 %collective-permute-start.49 = (bf16[2,64,1536]{2,1,0:T(8,128)(2,1)S(1)}, bf16[2,64,1536]{2,1,0:T(8,128)(2,1)S(1)}, u32[]{:S(2)}, u32[]{:S(2)}) collective-permute-start(bf16[2,64,1536]{2,1,0:T(8,128)(2,1)S(1)} %slice_bitcast_fusion.8), channel_id=1, source_target_pairs={{0,1},{1,0},{2,3},{3,2},{4,5},{5,4},{6,7},{7,6},{8,9},{9,8},{10,11... | collective-permute-start | bytes 1179656 | tf_op jit(solution)/shard_map/ppermute | solution.py:779
  458.1 23.9 %collective-permute-start.66 = (bf16[512,1024]{1,0:T(8,128)(2,1)S(1)}, bf16[512,1024]{1,0:T(8,128)(2,1)S(1)}, u32[]{:S(2)}, u32[]{:S(2)}) collective-permute-start(bf16[512,1024]{1,0:T(8,128)(2,1)S(1)} %broadcast_select_fusion.4), channel_id=1, source_target_pairs={{0,4},{4,0},{8,12},{12,8},{16,20},{20,16},{24,28},{28,24},{1,5},{5... | collective-permute-start | bytes 3145736 | tf_op jit(solution)/shard_map/ppermute | solution.py:779
  466.8 15.2 %collective-permute-start.51 = (bf16[4,128,1664]{2,1,0:T(8,128)(2,1)}, bf16[4,128,1664]{2,1,0:T(8,128)(2,1)S(1)}, u32[]{:S(2)}, u32[]{:S(2)}) collective-permute-start(bf16[4,128,1664]{2,1,0:T(8,128)(2,1)} %get-tuple-element.406), channel_id=1, source_target_pairs={{0,4},{4,0},{8,12},{12,8},{16,20},{20,16},{24,28},{28,24},{1,5},{5... | collective-permute-start | bytes 5111816 | tf_op jit(solution)/shard_map/ppermute | solution.py:779
  468.7 13.2 %collective-permute-start.53 = (bf16[1,64,1536]{2,1,0:T(8,128)(2,1)S(1)}, bf16[1,64,1536]{2,1,0:T(8,128)(2,1)S(1)}, u32[]{:S(2)}, u32[]{:S(2)}) collective-permute-start(bf16[1,64,1536]{2,1,0:T(8,128)(2,1)S(1)} %slice_bitcast_fusion.14), channel_id=1, source_target_pairs={{0,1},{1,0},{2,3},{3,2},{4,5},{5,4},{6,7},{7,6},{8,9},{9,8},{10,11... | collective-permute-start | bytes 589832 | tf_op jit(solution)/shard_map/ppermute | solution.py:779
  469.6 12.3 %collective-permute-start.52 = (bf16[1,64,1536]{2,1,0:T(8,128)(2,1)S(1)}, bf16[1,64,1536]{2,1,0:T(8,128)(2,1)S(1)}, u32[]{:S(2)}, u32[]{:S(2)}) collective-permute-start(bf16[1,64,1536]{2,1,0:T(8,128)(2,1)S(1)} %slice_bitcast_fusion.16), channel_id=1, source_target_pairs={{0,2},{1,3},{2,0},{3,1},{4,6},{5,7},{6,4},{7,5},{8,10},{9,11},{10,... | collective-permute-start | bytes 589832 | tf_op jit(solution)/shard_map/ppermute | solution.py:779
  484.2 12.5 %collective-permute-start.56 = (bf16[128,1536]{1,0:T(8,128)(2,1)S(1)}, bf16[128,1536]{1,0:T(8,128)(2,1)S(1)}, u32[]{:S(2)}, u32[]{:S(2)}) collective-permute-start(bf16[128,1536]{1,0:T(8,128)(2,1)S(1)} %pad_maximum_fusion.6), channel_id=1, source_target_pairs={{0,8},{4,12},{24,16},{28,20},{1,9},{5,13},{25,17},{29,21},{2,10},{... | collective-permute-start | bytes 1179656 | tf_op jit(solution)/shard_map/ppermute | solution.py:856
  488.6 11.1 %collective-permute-start.54 = (bf16[2,64,1664]{2,1,0:T(8,128)(2,1)S(1)}, bf16[2,64,1664]{2,1,0:T(8,128)(2,1)S(1)}, u32[]{:S(2)}, u32[]{:S(2)}) collective-permute-start(bf16[2,64,1664]{2,1,0:T(8,128)(2,1)S(1)} %slice_bitcast_fusion.4), channel_id=1, source_target_pairs={{0,1},{1,0},{2,3},{3,2},{4,5},{5,4},{6,7},{7,6},{8,9},{9,8},{10,11... | collective-permute-start | bytes 1277960 | tf_op jit(solution)/shard_map/ppermute | solution.py:779
  488.8 11.1 %collective-permute-start.55 = (bf16[2,64,1664]{2,1,0:T(8,128)(2,1)S(1)}, bf16[2,64,1664]{2,1,0:T(8,128)(2,1)S(1)}, u32[]{:S(2)}, u32[]{:S(2)}) collective-permute-start(bf16[2,64,1664]{2,1,0:T(8,128)(2,1)S(1)} %slice_bitcast_fusion.2), channel_id=1, source_target_pairs={{0,2},{1,3},{2,0},{3,1},{4,6},{5,7},{6,4},{7,5},{8,10},{9,11},{10,... | collective-permute-start | bytes 1277960 | tf_op jit(solution)/shard_map/ppermute | solution.py:779
  490.8 39.9 %collective-permute-start.65 = (bf16[128,5120]{1,0:T(8,128)(2,1)}, bf16[128,5120]{1,0:T(8,128)(2,1)S(1)}, u32[]{:S(2)}, u32[]{:S(2)}) collective-permute-start(bf16[128,5120]{1,0:T(8,128)(2,1)} %all-reduce.5.cloned.1.call-done), channel_id=1, source_target_pairs={{0,4},{4,0},{8,12},{12,8},{16,20},{20,16},{24,28},{28,24},{1,5},{5... | collective-permute-start | bytes 3932168 | tf_op jit(solution)/shard_map/ppermute | solution.py:779
  500.1 5.9 %collective-permute-start.57 = (bf16[1,64,1664]{2,1,0:T(8,128)(2,1)S(1)}, bf16[1,64,1664]{2,1,0:T(8,128)(2,1)S(1)}, u32[]{:S(2)}, u32[]{:S(2)}) collective-permute-start(bf16[1,64,1664]{2,1,0:T(8,128)(2,1)S(1)} %slice_bitcast_fusion.12), channel_id=1, source_target_pairs={{0,2},{1,3},{2,0},{3,1},{4,6},{5,7},{6,4},{7,5},{8,10},{9,11},{10,... | collective-permute-start | bytes 638984 | tf_op jit(solution)/shard_map/ppermute | solution.py:779
  501.9 5.9 %collective-permute-start.58 = (bf16[1,64,1664]{2,1,0:T(8,128)(2,1)S(1)}, bf16[1,64,1664]{2,1,0:T(8,128)(2,1)S(1)}, u32[]{:S(2)}, u32[]{:S(2)}) collective-permute-start(bf16[1,64,1664]{2,1,0:T(8,128)(2,1)S(1)} %slice_bitcast_fusion.10), channel_id=1, source_target_pairs={{0,1},{1,0},{2,3},{3,2},{4,5},{5,4},{6,7},{7,6},{8,9},{9,8},{10,11... | collective-permute-start | bytes 638984 | tf_op jit(solution)/shard_map/ppermute | solution.py:779
  503.6 4.3 collective-permute-start.59
  508.0 17.2 %collective-permute-start.63 = (bf16[128,1536]{1,0:T(8,128)(2,1)S(1)}, bf16[128,1536]{1,0:T(8,128)(2,1)S(1)}, u32[]{:S(2)}, u32[]{:S(2)}) collective-permute-start(bf16[128,1536]{1,0:T(8,128)(2,1)S(1)} %fusion.6), channel_id=1, source_target_pairs={{8,0},{12,4},{16,24},{20,28},{9,1},{13,5},{17,25},{21,29},{10,2},{... | collective-permute-start | bytes 1179656 | tf_op jit(solution)/shard_map/ppermute | solution.py:856
  511.9 18.5 %collective-permute-start.60 = (bf16[128,1664]{1,0:T(8,128)(2,1)S(1)}, bf16[128,1664]{1,0:T(8,128)(2,1)S(1)}, u32[]{:S(2)}, u32[]{:S(2)}) collective-permute-start(bf16[128,1664]{1,0:T(8,128)(2,1)S(1)} %pad_maximum_fusion.5), channel_id=1, source_target_pairs={{0,8},{4,12},{8,0},{12,4},{16,24},{20,28},{24,16},{28,20},{1,9},{5... | collective-permute-start | bytes 1277960 | tf_op jit(solution)/shard_map/ppermute | solution.py:779
  525.3 9.1 %collective-permute-start.64 = (bf16[128,1536]{1,0:T(8,128)(2,1)S(1)}, bf16[128,1536]{1,0:T(8,128)(2,1)S(1)}, u32[]{:S(2)}, u32[]{:S(2)}) collective-permute-start(bf16[128,1536]{1,0:T(8,128)(2,1)S(1)} %broadcast_select_fusion.7), channel_id=1, source_target_pairs={{0,4},{4,0},{8,12},{12,8},{16,20},{20,16},{24,28},{28,24},{1,5},{5... | collective-permute-start | bytes 1179656 | tf_op jit(solution)/shard_map/ppermute | solution.py:779
  530.6 17.1 %collective-permute-start.61 = (bf16[128,1664]{1,0:T(8,128)(2,1)S(1)}, bf16[128,1664]{1,0:T(8,128)(2,1)S(1)}, u32[]{:S(2)}, u32[]{:S(2)}) collective-permute-start(bf16[128,1664]{1,0:T(8,128)(2,1)S(1)} %add_convert_fusion.9), channel_id=1, source_target_pairs={{0,16},{4,20},{8,24},{12,28},{16,0},{20,4},{24,8},{28,12},{1,17},{... | collective-permute-start | bytes 1277960 | tf_op jit(solution)/shard_map/ppermute | solution.py:779
  (38 other events, 438.0 us)
Sparse Core Ops, SparseCore 0:
  261.5 53.2 reduce-scatter.6
  320.7 61.8 reduce-scatter.8
  403.8 73.8 all-reduce.4

commit v6 on v5

--- a/solution.py
+++ b/solution.py
@@ -321,7 +321,7 @@
         )
         dq_acc[...] = jnp.zeros_like(dq_acc)
 
-        def step(own, kt, carry):
+        def step(own, answer, kt, carry):
             rows = pl.ds(pl.multiple_of(kt * TILE, TILE), TILE)
             bias = jnp.where(idk_ref[rows, :] == idq_ref[0], 0.0, NEG)
             s = nn(k_ref[rows, :], qst[...])
@@ -332,18 +332,22 @@
                 inside = pl.ds(pl.multiple_of((kt - RIM) * TILE, TILE), TILE)
                 dv_acc[inside, :] += nn(p.astype(bf16), dos[...])
                 dk_acc[inside, :] += nn(ds, qs[...])
-            kt_tile = kt_ref[:, rows]
-            for h in range(4):
-                heads = slice(h * HEAD, (h + 1) * HEAD)
-                dq_acc[heads, :] += nn(kt_tile[heads, :], ds[:, h * TILE : (h + 1) * TILE])
+            if answer:
+                kt_tile = kt_ref[:, rows]
+                for h in range(4):
+                    heads = slice(h * HEAD, (h + 1) * HEAD)
+                    dq_acc[heads, :] += nn(kt_tile[heads, :], ds[:, h * TILE : (h + 1) * TILE])
             return carry
 
-        lax.fori_loop(low, jnp.minimum(high, RIM), functools.partial(step, False), 0)
-        lax.fori_loop(own_low, own_high, functools.partial(step, True), 0)
-        lax.fori_loop(jnp.maximum(low, end), high, functools.partial(step, False), 0)
+        @pl.when((t < RIM) | (t >= end))
+        def _():
+            lax.fori_loop(own_low, own_high, functools.partial(step, True, False), 0)
 
         @pl.when((t >= RIM) & (t < end))
         def _():
+            lax.fori_loop(low, jnp.minimum(high, RIM), functools.partial(step, False, True), 0)
+            lax.fori_loop(own_low, own_high, functools.partial(step, True, True), 0)
+            lax.fori_loop(jnp.maximum(low, end), high, functools.partial(step, False, True), 0)
             dq_ref[...] = (jnp.transpose(dq_acc[...]) * (HEAD**-0.5)).astype(bf16)
 
     @pl.when(t == pl.num_programs(1) - 1)

time: 576 us -> 574 us (level)
  Pallas kernels: 325 us -> 314 us
  waiting for transfers between devices: 73.8 us -> 83.4 us
    ppermute x55, waiting for transfers between devices: 50.6 us -> 58.9 us  [swap(): lax.ppermute(value, axis, [(i, i ^ bit) for i in range(lax.axis_size(axis...]
    pallas_call x3, Pallas kernels: 82.8 us -> 76.1 us  [attn_bwd(): pl.pallas_call(attn_bwd_kernel, grid_spec=pltpu.PrefetchScalarGridSpec(nu...]
  transfers between devices with their start and end apart: 70 -> 70, of which waited for: 25 -> 25; matrix products, arithmetic and copies ran while one was open for 8% -> 8% of each run, Pallas kernels for 45% -> 43%
where the time goes in v6:
time: 574 us; the launch traced here: 571 us
  Pallas kernels  314 us (55%)
  waiting for transfers between devices  83.4 us (15%)
  starting transfers between devices  81.7 us (14%)
  local copies, waits for them, and re-layouts  35.3 us (6%)
  other arithmetic  34.3 us (6%)
  between operations  22.4 us (4%)
    pallas_call x3, Pallas kernels, attn_bwd(): pl.pallas_call(attn_bwd_kernel, grid_spec=pltpu.PrefetchScalarGridSpec(nu...  76.1 us
    ppermute x55, waiting for transfers between devices, swap(): lax.ppermute(value, axis, [(i, i ^ bit) for i in range(lax.axis_size(axis...  58.9 us
    ppermute x55, starting transfers between devices, swap(): lax.ppermute(value, axis, [(i, i ^ bit) for i in range(lax.axis_size(axis...  48.9 us
    pallas_call x2, Pallas kernels, attn_fwd(): pl.pallas_call(attn_fwd_kernel, grid_spec=pltpu.PrefetchScalarGridSpec(nu...  36.5 us
    pallas_call x2, Pallas kernels, gram(): pl.pallas_call(functools.partial(gram_kernel, [len(group) - 1 for group i...  32.5 us
    pallas_call x1, Pallas kernels, inner_forward(): pl.pallas_call(functools.partial(inner_kernel, len(pieces)), grid=(FF //...  30 us
    pallas_call x1, Pallas kernels, feed_back(): pl.pallas_call(feed_back_last_kernel, in_specs=in_specs + [whole, pl.Bloc...  24.5 us
    ppermute x6, waiting for transfers between devices, move(): return arrive(gate, lax.ppermute(value, 'ctx', pairs))  23.8 us
  transfers between devices with their start and end apart: 70, of which 25 were waited for; matrix products, arithmetic and copies ran while one was open for 8% of the time, Pallas kernels for 43%

profile of v6, /device:TPU:0, one launch (start us, length us, event | category | flops | bytes accessed | tf_op | source)
XLA Modules:
  0.0 570.6 jit_solution(7101737904976612920)
XLA Ops:
  7.8 2.9 pack_shards.1
  10.8 3.0 collective-permute-start.3
  13.7 1.5 collective-permute-start.2
  27.4 1.7 slice_bitcast_fusion
  30.4 4.0 collective-permute-start
  37.0 3.6 collective-permute-done.5
  46.8 1.6 collective-permute-start.7
  48.9 3.4 collective-permute-start.11
  54.8 3.3 collective-permute-done.7.refs_4_
  65.5 1.5 collective-permute-start.19
  67.0 21.6 %project_qkv.1 = (bf16[2048,1024]{1,0:T(8,128)(2,1)}, bf16[2048,1024]{1,0:T(8,128)(2,1)}, bf16[2048,1024]{1,0:T(8,128)(2,1)}, bf16[1024,2048]{1,0:T(8,128)(2,1)}...) custom-call(s32[2]{0:T(128)} %pad_add_fusion.where_ref.tie_ref, bf16[256,3072]{1,0:T(8,128)(2,1)} %get-tuple-element.232.refs_0_, ...), custom_call_target="tpu_custom_call" | custom-call | flops 10737418240 | bytes 31457280 | tf_op jit(solution)/shard_map/project_qkv/pallas_call | solution.py:173
  88.6 2.4 collective-permute-done.16.refs_2_
  92.1 1.6 collective-permute-start.18
  93.7 1.5 collective-permute-start.17
  95.2 18.3 %attn_forward.2 = (bf16[1024,1024]{1,0:T(8,128)(2,1)}, f32[4,8,1024]{2,1,0:T(8,128)}) custom-call(s32[8]{0:T(128)} %get-tuple-element.386.lo_ref, s32[8]{0:T(128)} %get-tuple-element.254.hi_ref, bf16[2048,1024]{1,0:T(8,128)(2,1)} %get-tuple-element.248.q_ref, bf16[2048,1024]{1,0:T(8,128)(2,1)} %get-tuple-element.255.k_ref, ...), custom_call_target="tpu_custom_call" | custom-call | flops 20000000000 | bytes 2097152 | tf_op jit(solution)/shard_map/attn_forward/pallas_call | solution.py:260
  113.5 6.9 %collective-permute-done.18.refs_4_ = bf16[64,1024]{1,0:T(8,128)(2,1)S(1)} collective-permute-done((bf16[64,1024]{1,0:T(8,128)(2,1)S(1)}, bf16[64,1024]{1,0:T(8,128)(2,1)S(1)}, u32[]{:S(2)}, u32[]{:S(2)}) %collective-permute-start.18) | collective-permute-done | bytes 131104 | tf_op jit(solution)/shard_map/ppermute | solution.py:783
  126.5 1.5 collective-permute-start.28
  128.9 18.2 %attn_forward.3 = (bf16[1024,1024]{1,0:T(8,128)(2,1)}, f32[4,8,1024]{2,1,0:T(8,128)}) custom-call(s32[8]{0:T(128)} %get-tuple-element.386.lo_ref, s32[8]{0:T(128)} %get-tuple-element.254.hi_ref, bf16[2048,1024]{1,0:T(8,128)(2,1)} %get-tuple-element.248.q_ref, ...), custom_call_target="tpu_custom_call", output_to_operand_aliasing={{0}: (7, {}), {1}: (8, {})} | custom-call | flops 20000000000 | bytes 2097152 | tf_op jit(solution)/shard_map/attn_forward/pallas_call | solution.py:260
  147.2 2.8 collective-permute-done.28.refs_4_
  153.9 2.1 collective-permute-done.38.refs_8_
  159.3 9.7 %mix_and_norm.1 = (f32[1024,1024]{1,0:T(8,128)}, bf16[1024,1024]{1,0:T(8,128)(2,1)}, f32[1024,1]{1,0:T(8,128)}, bf16[1024,1024]{1,0:T(8,128)(2,1)}) custom-call(s32[2]{0:T(128)} %pad_add_fusion.where_ref.tie_ref, bf16[256,1024]{1,0:T(8,128)(2,1)} %refs_0_, bf16[128,1024]{1,0:T(8,128)(2,1)} %copy-done.17, bf16[128,1024]{1,0:T(8,128)(2,1)} %copy-done.16, ...), custom_call_target="tpu_custom_call" | custom-call | flops 2147483648 | bytes 14680064 | tf_op jit(solution)/shard_map/mix_and_norm/pallas_call | solution.py:431
  169.1 30.0 %inner_forward.1 = (bf16[1024,4096]{1,0:T(8,128)(2,1)}, bf16[1024,4096]{1,0:T(8,128)(2,1)}, bf16[1024,4096]{1,0:T(8,128)(2,1)}) custom-call(s32[2]{0:T(128)} %pad_add_fusion.where_ref.tie_ref, bf16[256,4096]{1,0:T(8,128)(2,1)} %refs_0_.1, bf16[128,4096]{1,0:T(8,128)(2,1)} %collective-permute-done.19.refs_1_, bf16[128,4096]{1,0:T(8,128)(2,1)} %copy-done.13, ...), custom_call_target="tpu_custom_call" | custom-call | flops 8589934592 | bytes 27262976 | tf_op jit(solution)/shard_map/inner_forward/pallas_call | solution.py:473
  199.1 22.8 %outer_forward.1 = (bf16[1024,1024]{1,0:T(8,128)(2,1)}, f32[1024,1024]{1,0:T(8,128)}, bf16[1024,1024]{1,0:T(8,128)(2,1)}, f32[8,1024]{1,0:T(8,128)}, bf16[4096,1024]{1,0:T(8,128)(2,1)}) custom-call(s32[2]{0:T(128)} %pad_add_fusion.where_ref.tie_ref, bf16[1024,1024]{1,0:T(8,128)(2,1)} %refs_0_.2, bf16[512,1024]{1,0:T(8,128)(2,1)} %collective-permute-done.21.refs_1_, ...), custom_call_target="tpu_custom_call" | custom-call | flops 8589934592 | bytes 33554432 | tf_op jit(solution)/shard_map/outer_forward/pallas_call | solution.py:519
  222.0 13.9 %gram.2 = (bf16[4,512,1024]{2,1,0:T(8,128)(2,1)}, bf16[4,512,1024]{2,1,0:T(8,128)(2,1)}) custom-call(s32[5]{0:T(128)} %pad_add_fusion.1.order_ref, bf16[1024,4096]{1,0:T(8,128)(2,1)} %get-tuple-element.339.refs_10_.refs_0_, bf16[1024,1024]{1,0:T(8,128)(2,1)} %get-tuple-element.345.refs_1_.db_ref), custom_call_target="tpu_custom_call" | custom-call | flops 8589934592 | bytes 18874368 | tf_op jit(solution)/shard_map/gram/pallas_call | solution.py:571
  236.2 19.0 %feed_back_first.1 = (bf16[1024,2048]{1,0:T(8,128)(2,1)}, f32[8,2048]{1,0:T(8,128)}, f32[1024,1024]{1,0:T(8,128)}) custom-call(s32[2]{0:T(128)} %pad_add_fusion.where_ref.tie_ref, bf16[1024,1024]{1,0:T(8,128)(2,1)} %get-tuple-element.345.refs_1_.db_ref, bf16[4096,1024]{1,0:T(8,128)(2,1)} %get-tuple-element.348.wo_ref, ...), custom_call_target="tpu_custom_call" | custom-call | flops 8589934592 | bytes 31457280 | tf_op jit(solution)/shard_map/feed_back_first/pallas_call | solution.py:649
  255.2 6.3 %add_convert_fusion.1 = bf16[4,512,1024]{2,1,0:T(8,128)(2,1)} fusion(bf16[4,512,1024]{2,1,0:T(8,128)(2,1)} %collective-permute-done.39, bf16[4,512,1024]{2,1,0:T(8,128)(2,1)S(1)} %copy-done.1), kind=kLoop, calls=%fused_computation.1 | loop fusion | flops 8388608 | bytes 12582912 | tf_op jit(solution)/shard_map/convert_element_type | solution.py:820
  261.6 24.5 %feed_back_last.1 = (bf16[1024,2048]{1,0:T(8,128)(2,1)}, f32[8,2048]{1,0:T(8,128)}, f32[1024,1024]{1,0:T(8,128)}, bf16[1024,1024]{1,0:T(8,128)(2,1)}, f32[8,1024]{1,0:T(8,128)}) custom-call(s32[2]{0:T(128)} %pad_add_fusion.where_ref.tie_ref, bf16[1024,1024]{1,0:T(8,128)(2,1)} %get-tuple-element.345.refs_1_.db_ref, ...), custom_call_target="tpu_custom_call" | custom-call | flops 8589934592 | bytes 31457280 | tf_op jit(solution)/shard_map/feed_back_last/pallas_call | solution.py:657
  286.1 18.7 %gram.3 = (bf16[4,128,5120]{2,1,0:T(8,128)(2,1)}, bf16[4,128,5120]{2,1,0:T(8,128)(2,1)}) custom-call(s32[5]{0:T(128)} %pad_add_fusion.1.order_ref, bf16[1024,1024]{1,0:T(8,128)(2,1)} %get-tuple-element.337.refs_9_.refs_0_, bf16[1024,2048]{1,0:T(8,128)(2,1)} %get-tuple-element.352.refs_1_, bf16[1024,2048]{1,0:T(8,128)(2,1)} %get-tuple-element.361.refs_2_, ...), custom_call_target="tpu_custom_call" | custom-call | flops 10737418240 | bytes 23068672 | tf_op jit(solution)/shard_map/gram/pallas_call | solution.py:571
  304.9 7.1 %context_back.1 = (bf16[1024,1024]{1,0:T(8,128)(2,1)}, f32[4,8,1024]{2,1,0:T(8,128)}) custom-call(bf16[1024,1024]{1,0:T(8,128)(2,1)} %get-tuple-element.364.refs_4_.d_ref, bf16[1024,1024]{1,0:T(8,128)(2,1)} %get-tuple-element.365.w_ref, bf16[1024,1024]{1,0:T(8,128)(2,1)} %get-tuple-element.274.refs_9_.refs_3_.context_ref), custom_call_target="tpu_custom_call" | custom-call | flops 2147483648 | bytes 8388608 | tf_op jit(solution)/shard_map/context_back/pallas_call | solution.py:685
  312.0 1.8 collective-permute-done.40
  313.8 6.9 %add_convert_fusion = bf16[4,128,5120]{2,1,0:T(8,128)(2,1)} fusion(bf16[4,128,5120]{2,1,0:T(8,128)(2,1)} %collective-permute-done.40, bf16[4,128,5120]{2,1,0:T(8,128)(2,1)S(1)} %copy-done), kind=kLoop, calls=%fused_computation | loop fusion | flops 10485760 | bytes 15728640 | tf_op jit(solution)/shard_map/convert_element_type | solution.py:820
  320.8 1.5 copy-done.2
  322.3 1.5 fusion.19
  325.1 4.0 collective-permute-start.42
  329.1 2.4 collective-permute-start.44
  335.7 12.5 %collective-permute-start.41 = (bf16[512,1024]{1,0:T(8,128)(2,1)S(1)}, bf16[512,1024]{1,0:T(8,128)(2,1)S(1)}, u32[]{:S(2)}, u32[]{:S(2)}) collective-permute-start(bf16[512,1024]{1,0:T(8,128)(2,1)S(1)} %bitcast.144), channel_id=1, source_target_pairs={{0,8},{4,12},{24,16},{28,20},{1,9},{5,13},{25,17},{29,21},{2,10},{... | collective-permute-start | bytes 3145736 | tf_op jit(solution)/shard_map/ppermute | solution.py:860
  349.1 19.5 %attn_backward.3 = (bf16[1024,512]{1,0:T(8,128)(2,1)}, bf16[2,1024,512]{2,1,0:T(8,128)(2,1)}) custom-call(s32[8]{0:T(128)} %get-tuple-element.386.lo_ref, s32[8]{0:T(128)} %get-tuple-element.254.hi_ref, bf16[2048,1024]{1,0:T(8,128)(2,1)} %get-tuple-element.248.q_ref, bf16[512,1024]{1,0:T(8,128)(2,1)} %collective-permute-done.42.before_ref, ...), custom_call_target="tpu_custom_call" | custom-call | flops 15000000512 | bytes 4194304 | tf_op jit(solution)/shard_map/attn_backward/pallas_call | solution.py:363
  368.6 1.6 collective-permute-done.41
  371.3 19.3 %attn_backward.4 = (bf16[1024,512]{1,0:T(8,128)(2,1)}, bf16[2,1024,512]{2,1,0:T(8,128)(2,1)}) custom-call(s32[8]{0:T(128)} %get-tuple-element.386.lo_ref, s32[8]{0:T(128)} %get-tuple-element.254.hi_ref, bf16[2048,1024]{1,0:T(8,128)(2,1)} %get-tuple-element.248.q_ref, ...), custom_call_target="tpu_custom_call", output_to_operand_aliasing={{0}: (12, {}), {1}: (13, {})} | custom-call | flops 15000000512 | bytes 4194304 | tf_op jit(solution)/shard_map/attn_backward/pallas_call | solution.py:363
  391.0 8.5 %qkv_gradient.2 = (bf16[4,128,1536]{2,1,0:T(8,128)(2,1)}, bf16[4,128,1536]{2,1,0:T(8,128)(2,1)}, f32[8,1024]{1,0:T(8,128)}) custom-call(s32[5]{0:T(128)} %pad_add_fusion.2.order_ref, bf16[1024,1024]{1,0:T(8,128)(2,1)} %bitcast.133, bf16[1024,512]{1,0:T(8,128)(2,1)} %get-tuple-element.378.dq_ref.refs_0_, ...), custom_call_target="tpu_custom_call" | custom-call | flops 3221225472 | bytes 16777216 | tf_op jit(solution)/shard_map/qkv_gradient/pallas_call | solution.py:739
  399.6 3.3 collective-permute-start.47
  404.3 37.3 %attn_backward.5 = (bf16[1024,512]{1,0:T(8,128)(2,1)}, bf16[2,1024,512]{2,1,0:T(8,128)(2,1)}) custom-call(s32[8]{0:T(128)} %get-tuple-element.386.lo_ref, s32[8]{0:T(128)} %get-tuple-element.254.hi_ref, bf16[2048,1024]{1,0:T(8,128)(2,1)} %get-tuple-element.248.q_ref, bf16[512,1024]{1,0:T(8,128)(2,1)} %collective-permute-done.42.before_ref, ...), custom_call_target="tpu_custom_call" | custom-call | flops 30000001024 | bytes 4194304 | tf_op jit(solution)/shard_map/attn_backward/pallas_call | solution.py:363
  441.6 1.8 add_convert_fusion.6
  443.5 10.7 %collective-permute-done.48 = bf16[512,1024]{1,0:T(8,128)(2,1)S(1)} collective-permute-done((bf16[512,1024]{1,0:T(8,128)(2,1)S(1)}, bf16[512,1024]{1,0:T(8,128)(2,1)S(1)}, u32[]{:S(2)}, u32[]{:S(2)}) %collective-permute-start.48) | collective-permute-done | bytes 1048608 | tf_op jit(solution)/shard_map/ppermute | solution.py:860
  455.5 1.6 collective-permute-start.49
  457.1 8.6 %qkv_gradient.3 = (bf16[4,128,1664]{2,1,0:T(8,128)(2,1)}, bf16[4,128,1664]{2,1,0:T(8,128)(2,1)}, f32[8,1024]{1,0:T(8,128)}) custom-call(s32[5]{0:T(128)} %pad_add_fusion.2.order_ref, bf16[1024,1024]{1,0:T(8,128)(2,1)} %bitcast.134, bf16[1024,512]{1,0:T(8,128)(2,1)} %get-tuple-element.387.dq_ref.refs_2_, ...), custom_call_target="tpu_custom_call" | custom-call | flops 3489660928 | bytes 16777216 | tf_op jit(solution)/shard_map/qkv_gradient/pallas_call | solution.py:739
  466.5 1.5 collective-permute-start.53
  468.8 12.2 %input_back.1 = f32[1024,1024]{1,0:T(8,128)} custom-call(f32[1024,1024]{1,0:T(8,128)} %get-tuple-element.357.base_ref, bf16[1024,512]{1,0:T(8,128)(2,1)} %get-tuple-element.378.dq_ref.refs_0_, bf16[2,1024,512]{2,1,0:T(8,128)(2,1)} %get-tuple-element.379.joined_ref.refs_1_, bf16[1024,512]{1,0:T(8,128)(2,1)} %get-tuple-element.387.dq_ref.refs_2_, ...), custom_call_target="tpu_custom_call" | custom-call | flops 6442450944 | bytes 20971520 | tf_op jit(solution)/shard_map/input_back/pallas_call | solution.py:770
  483.3 1.5 collective-permute-start.56
  484.9 1.5 collective-permute-start.54
  486.4 1.5 collective-permute-start.55
  487.9 4.5 collective-permute-done.56
  492.5 3.0 collective-permute-done.54
  497.1 1.6 collective-permute-start.57
  499.8 3.2 collective-permute-done.57
  503.0 1.6 collective-permute-done.58
  504.8 1.6 collective-permute-start.63
  506.6 2.4 maximum_convert_fusion
  509.0 6.7 %collective-permute-start.60 = (bf16[128,1664]{1,0:T(8,128)(2,1)S(1)}, bf16[128,1664]{1,0:T(8,128)(2,1)S(1)}, u32[]{:S(2)}, u32[]{:S(2)}) collective-permute-start(bf16[128,1664]{1,0:T(8,128)(2,1)S(1)} %pad_maximum_fusion.5), channel_id=1, source_target_pairs={{0,8},{4,12},{8,0},{12,4},{16,24},{20,28},{24,16},{28,20},{1,9},{5... | collective-permute-start | bytes 1277960 | tf_op jit(solution)/shard_map/ppermute | solution.py:783
  515.7 7.1 %collective-permute-done.63 = bf16[128,1536]{1,0:T(8,128)(2,1)S(1)} collective-permute-done((bf16[128,1536]{1,0:T(8,128)(2,1)S(1)}, bf16[128,1536]{1,0:T(8,128)(2,1)S(1)}, u32[]{:S(2)}, u32[]{:S(2)}) %collective-permute-start.63) | collective-permute-done | bytes 393248 | tf_op jit(solution)/shard_map/ppermute | solution.py:860
  522.9 6.2 %collective-permute-done.60 = bf16[128,1664]{1,0:T(8,128)(2,1)S(1)} collective-permute-done((bf16[128,1664]{1,0:T(8,128)(2,1)S(1)}, bf16[128,1664]{1,0:T(8,128)(2,1)S(1)}, u32[]{:S(2)}, u32[]{:S(2)}) %collective-permute-start.60) | collective-permute-done | bytes 426016 | tf_op jit(solution)/shard_map/ppermute | solution.py:783
  531.0 2.5 fusion
  533.6 14.2 %collective-permute-done.61 = bf16[128,1664]{1,0:T(8,128)(2,1)S(1)} collective-permute-done((bf16[128,1664]{1,0:T(8,128)(2,1)S(1)}, bf16[128,1664]{1,0:T(8,128)(2,1)S(1)}, u32[]{:S(2)}, u32[]{:S(2)}) %collective-permute-start.61) | collective-permute-done | bytes 426016 | tf_op jit(solution)/shard_map/ppermute | solution.py:783
  558.2 2.2 pad_maximum_fusion.3
  (272 shorter events, 75.5 us)
Async XLA Ops:
  7.2 313.5 %reduce-scatter.7.cloned.1.call-start = ((), (), s32[]{:S(2)}) async-start(), calls=%async_computation.3 | async-start | bytes 5242880
  10.8 29.8 %collective-permute-start.3 = (bf16[128,3072]{1,0:T(8,128)(2,1)}, bf16[128,3072]{1,0:T(8,128)(2,1)}, u32[]{:S(2)}, u32[]{:S(2)}) collective-permute-start(bf16[128,3072]{1,0:T(8,128)(2,1)} %get-tuple-element.227), channel_id=1, source_target_pairs={{0,2},{1,3},{2,0},{3,1},{4,6},{5,7},{6,4},{7,5},{8,10},{9,11},{10,... | collective-permute-start | bytes 2359304 | tf_op jit(solution)/shard_map/ppermute | solution.py:783
  13.7 26.9 %collective-permute-start.2 = (bf16[128,3072]{1,0:T(8,128)(2,1)}, bf16[128,3072]{1,0:T(8,128)(2,1)}, u32[]{:S(2)}, u32[]{:S(2)}) collective-permute-start(bf16[128,3072]{1,0:T(8,128)(2,1)} %get-tuple-element.227), channel_id=1, source_target_pairs={{0,1},{1,0},{2,3},{3,2},{4,5},{5,4},{6,7},{7,6},{8,9},{9,8},{10,11... | collective-permute-start | bytes 2359304 | tf_op jit(solution)/shard_map/ppermute | solution.py:783
  26.8 9.9 %collective-permute-start.4 = (bf16[1,3200]{1,0:T(2,128)(2,1)S(1)}, bf16[1,3200]{1,0:T(2,128)(2,1)S(1)}, u32[]{:S(2)}, u32[]{:S(2)}) collective-permute-start(bf16[1,3200]{1,0:T(2,128)(2,1)S(1)} %reshape.188), channel_id=1, source_target_pairs={{0,1},{1,0},{2,3},{3,2},{4,5},{5,4},{6,7},{7,6},{8,9},{9,8},{10,11... | collective-permute-start | bytes 19208 | tf_op jit(solution)/shard_map/ppermute | solution.py:783
  29.1 25.7 %collective-permute-start.1 = (bf16[512,1024]{1,0:T(8,128)(2,1)S(1)}, bf16[512,1024]{1,0:T(8,128)(2,1)}, u32[]{:S(2)}, u32[]{:S(2)}) collective-permute-start(bf16[512,1024]{1,0:T(8,128)(2,1)S(1)} %get-tuple-element.446), channel_id=1, source_target_pairs={{4,0},{8,4},{12,8},{16,12},{20,16},{24,20},{28,24},{5,1},{9,5},{13... | collective-permute-start | bytes 3145736 | tf_op jit(solution)/shard_map/ppermute | solution.py:979
  30.4 24.4 %collective-permute-start = (bf16[512,1024]{1,0:T(8,128)(2,1)S(1)}, bf16[512,1024]{1,0:T(8,128)(2,1)}, u32[]{:S(2)}, u32[]{:S(2)}) collective-permute-start(bf16[512,1024]{1,0:T(8,128)(2,1)S(1)} %get-tuple-element.447), channel_id=1, source_target_pairs={{0,4},{4,8},{8,12},{12,16},{16,20},{20,24},{24,28},{1,5},{5,9},{9,... | collective-permute-start | bytes 3145736 | tf_op jit(solution)/shard_map/ppermute | solution.py:978
  43.8 5.1 collective-permute-start.10
  46.8 11.3 %collective-permute-start.7 = (bf16[64,3072]{1,0:T(8,128)(2,1)S(1)}, bf16[64,3072]{1,0:T(8,128)(2,1)}, u32[]{:S(2)}, u32[]{:S(2)}) collective-permute-start(bf16[64,3072]{1,0:T(8,128)(2,1)S(1)} %slice.213), channel_id=1, source_target_pairs={{0,1},{1,0},{2,3},{3,2},{4,5},{5,4},{6,7},{7,6},{8,9},{9,8},{10,11... | collective-permute-start | bytes 1179656 | tf_op jit(solution)/shard_map/ppermute | solution.py:783
  48.4 10.9 %collective-permute-start.6 = (bf16[64,3072]{1,0:T(8,128)(2,1)S(1)}, bf16[64,3072]{1,0:T(8,128)(2,1)}, u32[]{:S(2)}, u32[]{:S(2)}) collective-permute-start(bf16[64,3072]{1,0:T(8,128)(2,1)S(1)} %slice.212), channel_id=1, source_target_pairs={{0,2},{1,3},{2,0},{3,1},{4,6},{5,7},{6,4},{7,5},{8,10},{9,11},{10,... | collective-permute-start | bytes 1179656 | tf_op jit(solution)/shard_map/ppermute | solution.py:783
  48.9 5.4 collective-permute-start.11
  59.3 6.2 %collective-permute-start.12 = (bf16[128,3072]{1,0:T(8,128)(2,1)}, bf16[128,3072]{1,0:T(8,128)(2,1)}, u32[]{:S(2)}, u32[]{:S(2)}) collective-permute-start(bf16[128,3072]{1,0:T(8,128)(2,1)} %collective-permute-done.2.refs_1_), channel_id=1, source_target_pairs={{0,4},{4,0},{8,12},{12,8},{16,20},{20,16},{24,28},{28,24},{1,5},{5... | collective-permute-start | bytes 2359304 | tf_op jit(solution)/shard_map/ppermute | solution.py:783
  59.3 7.7 %collective-permute-start.13 = (bf16[128,3072]{1,0:T(8,128)(2,1)}, bf16[128,3072]{1,0:T(8,128)(2,1)}, u32[]{:S(2)}, u32[]{:S(2)}) collective-permute-start(bf16[128,3072]{1,0:T(8,128)(2,1)} %collective-permute-done.3.refs_2_), channel_id=1, source_target_pairs={{0,4},{4,0},{8,12},{12,8},{16,20},{20,16},{24,28},{28,24},{1,5},{5... | collective-permute-start | bytes 2359304 | tf_op jit(solution)/shard_map/ppermute | solution.py:783
  59.8 3.8 collective-permute-start.14
  59.8 5.2 collective-permute-start.15
  60.3 33.4 %collective-permute-start.20 = (bf16[128,4096]{1,0:T(8,128)(2,1)S(1)}, bf16[128,4096]{1,0:T(8,128)(2,1)S(1)}, u32[]{:S(2)}, u32[]{:S(2)}) collective-permute-start(bf16[128,4096]{1,0:T(8,128)(2,1)S(1)} %constant_dynamic-slice_fusion.1), channel_id=1, source_target_pairs={{0,2},{1,3},{2,0},{3,1},{4,6},{5,7},{6,4},{7,5},{8,10},{9,11},{10,... | collective-permute-start | bytes 3145736 | tf_op jit(solution)/shard_map/ppermute | solution.py:783
  63.6 27.4 %collective-permute-start.16 = (bf16[128,1024]{1,0:T(8,128)(2,1)S(1)}, bf16[128,1024]{1,0:T(8,128)(2,1)S(1)}, u32[]{:S(2)}, u32[]{:S(2)}) collective-permute-start(bf16[128,1024]{1,0:T(8,128)(2,1)S(1)} %constant_dynamic-slice_fusion.2), channel_id=1, source_target_pairs={{0,2},{1,3},{2,0},{3,1},{4,6},{5,7},{6,4},{7,5},{8,10},{9,11},{10,... | collective-permute-start | bytes 786440 | tf_op jit(solution)/shard_map/ppermute | solution.py:783
  65.0 26.0 %collective-permute-start.8 = (bf16[128,1024]{1,0:T(8,128)(2,1)S(1)}, bf16[128,1024]{1,0:T(8,128)(2,1)S(1)}, u32[]{:S(2)}, u32[]{:S(2)}) collective-permute-start(bf16[128,1024]{1,0:T(8,128)(2,1)S(1)} %constant_dynamic-slice_fusion.2), channel_id=1, source_target_pairs={{0,1},{1,0},{2,3},{3,2},{4,5},{5,4},{6,7},{7,6},{8,9},{9,8},{10,11... | collective-permute-start | bytes 786440 | tf_op jit(solution)/shard_map/ppermute | solution.py:783
  65.5 48.0 %collective-permute-start.19 = (bf16[128,4096]{1,0:T(8,128)(2,1)S(1)}, bf16[128,4096]{1,0:T(8,128)(2,1)}, u32[]{:S(2)}, u32[]{:S(2)}) collective-permute-start(bf16[128,4096]{1,0:T(8,128)(2,1)S(1)} %constant_dynamic-slice_fusion.1), channel_id=1, source_target_pairs={{0,1},{1,0},{2,3},{3,2},{4,5},{5,4},{6,7},{7,6},{8,9},{9,8},{10,11... | collective-permute-start | bytes 3145736 | tf_op jit(solution)/shard_map/ppermute | solution.py:783
  91.0 29.4 %collective-permute-start.22 = (bf16[512,1024]{1,0:T(8,128)(2,1)S(1)}, bf16[512,1024]{1,0:T(8,128)(2,1)}, u32[]{:S(2)}, u32[]{:S(2)}) collective-permute-start(bf16[512,1024]{1,0:T(8,128)(2,1)S(1)} %constant_dynamic-slice_fusion), channel_id=1, source_target_pairs={{0,2},{1,3},{2,0},{3,1},{4,6},{5,7},{6,4},{7,5},{8,10},{9,11},{10,... | collective-permute-start | bytes 3145736 | tf_op jit(solution)/shard_map/ppermute | solution.py:783
  91.6 28.8 %collective-permute-start.21 = (bf16[512,1024]{1,0:T(8,128)(2,1)S(1)}, bf16[512,1024]{1,0:T(8,128)(2,1)}, u32[]{:S(2)}, u32[]{:S(2)}) collective-permute-start(bf16[512,1024]{1,0:T(8,128)(2,1)S(1)} %constant_dynamic-slice_fusion), channel_id=1, source_target_pairs={{0,1},{1,0},{2,3},{3,2},{4,5},{5,4},{6,7},{7,6},{8,9},{9,8},{10,11... | collective-permute-start | bytes 3145736 | tf_op jit(solution)/shard_map/ppermute | solution.py:783
  92.1 28.3 %collective-permute-start.18 = (bf16[64,1024]{1,0:T(8,128)(2,1)S(1)}, bf16[64,1024]{1,0:T(8,128)(2,1)S(1)}, u32[]{:S(2)}, u32[]{:S(2)}) collective-permute-start(bf16[64,1024]{1,0:T(8,128)(2,1)S(1)} %slice.219), channel_id=1, source_target_pairs={{0,1},{1,0},{2,3},{3,2},{4,5},{5,4},{6,7},{7,6},{8,9},{9,8},{10,11... | collective-permute-start | bytes 393224 | tf_op jit(solution)/shard_map/ppermute | solution.py:783
  93.7 26.7 %collective-permute-start.17 = (bf16[64,1024]{1,0:T(8,128)(2,1)S(1)}, bf16[64,1024]{1,0:T(8,128)(2,1)S(1)}, u32[]{:S(2)}, u32[]{:S(2)}) collective-permute-start(bf16[64,1024]{1,0:T(8,128)(2,1)S(1)} %slice.218), channel_id=1, source_target_pairs={{0,2},{1,3},{2,0},{3,1},{4,6},{5,7},{6,4},{7,5},{8,10},{9,11},{10,... | collective-permute-start | bytes 393224 | tf_op jit(solution)/shard_map/ppermute | solution.py:783
  120.4 7.5 %collective-permute-start.23 = (bf16[128,1024]{1,0:T(8,128)(2,1)S(1)}, bf16[128,1024]{1,0:T(8,128)(2,1)S(1)}, u32[]{:S(2)}, u32[]{:S(2)}) collective-permute-start(bf16[128,1024]{1,0:T(8,128)(2,1)S(1)} %collective-permute-done.8.refs_1_), channel_id=1, source_target_pairs={{0,4},{4,0},{8,12},{12,8},{16,20},{20,16},{24,28},{28,24},{1,5},{5... | collective-permute-start | bytes 786440 | tf_op jit(solution)/shard_map/ppermute | solution.py:783
  120.5 4.9 collective-permute-start.25
  121.0 5.5 collective-permute-start.26
  121.1 26.1 %collective-permute-start.24 = (bf16[128,1024]{1,0:T(8,128)(2,1)S(1)}, bf16[128,1024]{1,0:T(8,128)(2,1)S(1)}, u32[]{:S(2)}, u32[]{:S(2)}) collective-permute-start(bf16[128,1024]{1,0:T(8,128)(2,1)S(1)} %collective-permute-done.16.refs_2_), channel_id=1, source_target_pairs={{0,4},{4,0},{8,12},{12,8},{16,20},{20,16},{24,28},{28,24},{1,5},{5... | collective-permute-start | bytes 786440 | tf_op jit(solution)/shard_map/ppermute | solution.py:783
  124.8 22.4 %collective-permute-start.30 = (bf16[256,1024]{1,0:T(8,128)(2,1)S(1)}, bf16[256,1024]{1,0:T(8,128)(2,1)S(1)}, u32[]{:S(2)}, u32[]{:S(2)}) collective-permute-start(bf16[256,1024]{1,0:T(8,128)(2,1)S(1)} %slice.223), channel_id=1, source_target_pairs={{0,1},{1,0},{2,3},{3,2},{4,5},{5,4},{6,7},{7,6},{8,9},{9,8},{10,11... | collective-permute-start | bytes 1572872 | tf_op jit(solution)/shard_map/ppermute | solution.py:783
  125.4 21.8 %collective-permute-start.29 = (bf16[256,1024]{1,0:T(8,128)(2,1)S(1)}, bf16[256,1024]{1,0:T(8,128)(2,1)S(1)}, u32[]{:S(2)}, u32[]{:S(2)}) collective-permute-start(bf16[256,1024]{1,0:T(8,128)(2,1)S(1)} %slice.222), channel_id=1, source_target_pairs={{0,2},{1,3},{2,0},{3,1},{4,6},{5,7},{6,4},{7,5},{8,10},{9,11},{10,... | collective-permute-start | bytes 1572872 | tf_op jit(solution)/shard_map/ppermute | solution.py:783
  126.5 23.5 %collective-permute-start.28 = (bf16[64,4096]{1,0:T(8,128)(2,1)S(1)}, bf16[64,4096]{1,0:T(8,128)(2,1)S(1)}, u32[]{:S(2)}, u32[]{:S(2)}) collective-permute-start(bf16[64,4096]{1,0:T(8,128)(2,1)S(1)} %slice.221), channel_id=1, source_target_pairs={{0,1},{1,0},{2,3},{3,2},{4,5},{5,4},{6,7},{7,6},{8,9},{9,8},{10,11... | collective-permute-start | bytes 1572872 | tf_op jit(solution)/shard_map/ppermute | solution.py:783
  128.0 22.4 %collective-permute-start.27 = (bf16[64,4096]{1,0:T(8,128)(2,1)S(1)}, bf16[64,4096]{1,0:T(8,128)(2,1)}, u32[]{:S(2)}, u32[]{:S(2)}) collective-permute-start(bf16[64,4096]{1,0:T(8,128)(2,1)S(1)} %slice.220), channel_id=1, source_target_pairs={{0,2},{1,3},{2,0},{3,1},{4,6},{5,7},{6,4},{7,5},{8,10},{9,11},{10,... | collective-permute-start | bytes 1572872 | tf_op jit(solution)/shard_map/ppermute | solution.py:783
  150.9 5.1 collective-permute-start.38
  150.9 18.1 %collective-permute-start.36 = (bf16[512,1024]{1,0:T(8,128)(2,1)}, bf16[512,1024]{1,0:T(8,128)(2,1)S(1)}, u32[]{:S(2)}, u32[]{:S(2)}) collective-permute-start(bf16[512,1024]{1,0:T(8,128)(2,1)} %collective-permute-done.22.refs_2_), channel_id=1, source_target_pairs={{0,4},{4,0},{8,12},{12,8},{16,20},{20,16},{24,28},{28,24},{1,5},{5... | collective-permute-start | bytes 3145736 | tf_op jit(solution)/shard_map/ppermute | solution.py:783
  151.4 17.6 %collective-permute-start.35 = (bf16[512,1024]{1,0:T(8,128)(2,1)}, bf16[512,1024]{1,0:T(8,128)(2,1)S(1)}, u32[]{:S(2)}, u32[]{:S(2)}) collective-permute-start(bf16[512,1024]{1,0:T(8,128)(2,1)} %collective-permute-done.21.refs_1_), channel_id=1, source_target_pairs={{0,4},{4,0},{8,12},{12,8},{16,20},{20,16},{24,28},{28,24},{1,5},{5... | collective-permute-start | bytes 3145736 | tf_op jit(solution)/shard_map/ppermute | solution.py:783
  152.3 16.8 %collective-permute-start.32 = (bf16[128,4096]{1,0:T(8,128)(2,1)S(1)}, bf16[128,4096]{1,0:T(8,128)(2,1)}, u32[]{:S(2)}, u32[]{:S(2)}) collective-permute-start(bf16[128,4096]{1,0:T(8,128)(2,1)S(1)} %collective-permute-done.20.refs_2_), channel_id=1, source_target_pairs={{0,4},{4,0},{8,12},{12,8},{16,20},{20,16},{24,28},{28,24},{1,5},{5... | collective-permute-start | bytes 3145736 | tf_op jit(solution)/shard_map/ppermute | solution.py:783
  153.8 15.3 %collective-permute-start.31 = (bf16[128,4096]{1,0:T(8,128)(2,1)}, bf16[128,4096]{1,0:T(8,128)(2,1)}, u32[]{:S(2)}, u32[]{:S(2)}) collective-permute-start(bf16[128,4096]{1,0:T(8,128)(2,1)} %collective-permute-done.19.refs_1_), channel_id=1, source_target_pairs={{0,4},{4,0},{8,12},{12,8},{16,20},{20,16},{24,28},{28,24},{1,5},{5... | collective-permute-start | bytes 3145736 | tf_op jit(solution)/shard_map/ppermute | solution.py:783
  156.9 12.1 %collective-permute-start.33 = (bf16[64,4096]{1,0:T(8,128)(2,1)}, bf16[64,4096]{1,0:T(8,128)(2,1)}, u32[]{:S(2)}, u32[]{:S(2)}) collective-permute-start(bf16[64,4096]{1,0:T(8,128)(2,1)} %collective-permute-done.27.refs_3_), channel_id=1, source_target_pairs={{0,4},{4,0},{8,12},{12,8},{16,20},{20,16},{24,28},{28,24},{1,5},{5... | collective-permute-start | bytes 1572872 | tf_op jit(solution)/shard_map/ppermute | solution.py:783
  235.8 19.4 %collective-permute-start.39 = (bf16[4,512,1024]{2,1,0:T(8,128)(2,1)}, bf16[4,512,1024]{2,1,0:T(8,128)(2,1)}, u32[]{:S(2)}, u32[]{:S(2)}) collective-permute-start(bf16[4,512,1024]{2,1,0:T(8,128)(2,1)} %get-tuple-element.347), channel_id=1, source_target_pairs={{0,4},{4,0},{8,12},{12,8},{16,20},{20,16},{24,28},{28,24},{1,5},{5... | collective-permute-start | bytes 12582920 | tf_op jit(solution)/shard_map/ppermute | solution.py:783
  261.6 141.3 %reduce-scatter.9.cloned.1.call-start = ((), (), s32[]{:S(2)}) async-start(), calls=%async_computation.4 | async-start | bytes 6553600
  304.8 9.0 %collective-permute-start.40 = (bf16[4,128,5120]{2,1,0:T(8,128)(2,1)}, bf16[4,128,5120]{2,1,0:T(8,128)(2,1)}, u32[]{:S(2)}, u32[]{:S(2)}) collective-permute-start(bf16[4,128,5120]{2,1,0:T(8,128)(2,1)} %get-tuple-element.363), channel_id=1, source_target_pairs={{0,4},{4,0},{8,12},{12,8},{16,20},{20,16},{24,28},{28,24},{1,5},{5... | collective-permute-start | bytes 15728648 | tf_op jit(solution)/shard_map/ppermute | solution.py:783
  320.8 162.6 %all-reduce.5.cloned.1.call-start = ((), (), s32[]{:S(2)}) async-start(), calls=%async_computation.2 | async-start | bytes 2621440 | tf_op jit(solution)/shard_map/psum | solution.py:894
  323.8 24.4 %collective-permute-start.43 = (bf16[512,1024]{1,0:T(8,128)(2,1)}, bf16[512,1024]{1,0:T(8,128)(2,1)S(1)}, u32[]{:S(2)}, u32[]{:S(2)}) collective-permute-start(bf16[512,1024]{1,0:T(8,128)(2,1)} %get-tuple-element.444), channel_id=1, source_target_pairs={{4,0},{8,4},{12,8},{16,12},{20,16},{24,20},{28,24},{5,1},{9,5},{13... | collective-permute-start | bytes 3145736 | tf_op jit(solution)/shard_map/ppermute | solution.py:1063
  325.1 23.1 %collective-permute-start.42 = (bf16[512,1024]{1,0:T(8,128)(2,1)}, bf16[512,1024]{1,0:T(8,128)(2,1)}, u32[]{:S(2)}, u32[]{:S(2)}) collective-permute-start(bf16[512,1024]{1,0:T(8,128)(2,1)} %get-tuple-element.445), channel_id=1, source_target_pairs={{0,4},{4,8},{8,12},{12,16},{16,20},{20,24},{24,28},{1,5},{5,9},{9,... | collective-permute-start | bytes 3145736 | tf_op jit(solution)/shard_map/ppermute | solution.py:1062
  329.1 5.0 collective-permute-start.44
  335.7 34.5 %collective-permute-start.41 = (bf16[512,1024]{1,0:T(8,128)(2,1)S(1)}, bf16[512,1024]{1,0:T(8,128)(2,1)S(1)}, u32[]{:S(2)}, u32[]{:S(2)}) collective-permute-start(bf16[512,1024]{1,0:T(8,128)(2,1)S(1)} %bitcast.144), channel_id=1, source_target_pairs={{0,8},{4,12},{24,16},{28,20},{1,9},{5,13},{25,17},{29,21},{2,10},{... | collective-permute-start | bytes 3145736 | tf_op jit(solution)/shard_map/ppermute | solution.py:860
  370.6 20.0 %collective-permute-start.46 = (bf16[512,1024]{1,0:T(8,128)(2,1)S(1)}, bf16[512,1024]{1,0:T(8,128)(2,1)S(1)}, u32[]{:S(2)}, u32[]{:S(2)}) collective-permute-start(bf16[512,1024]{1,0:T(8,128)(2,1)S(1)} %add_convert_fusion.3), channel_id=1, source_target_pairs={{8,16},{12,20},{16,8},{20,12},{9,17},{13,21},{17,9},{21,13},{10,18... | collective-permute-start | bytes 3145736 | tf_op jit(solution)/shard_map/ppermute | solution.py:860
  399.6 42.1 %collective-permute-start.47 = (bf16[4,128,1536]{2,1,0:T(8,128)(2,1)}, bf16[4,128,1536]{2,1,0:T(8,128)(2,1)}, u32[]{:S(2)}, u32[]{:S(2)}) collective-permute-start(bf16[4,128,1536]{2,1,0:T(8,128)(2,1)} %get-tuple-element.390), channel_id=1, source_target_pairs={{0,4},{4,0},{8,12},{12,8},{16,20},{20,16},{24,28},{28,24},{1,5},{5... | collective-permute-start | bytes 4718600 | tf_op jit(solution)/shard_map/ppermute | solution.py:783
  402.9 51.2 %collective-permute-start.48 = (bf16[512,1024]{1,0:T(8,128)(2,1)S(1)}, bf16[512,1024]{1,0:T(8,128)(2,1)S(1)}, u32[]{:S(2)}, u32[]{:S(2)}) collective-permute-start(bf16[512,1024]{1,0:T(8,128)(2,1)S(1)} %fusion.1), channel_id=1, source_target_pairs={{8,0},{12,4},{16,24},{20,28},{9,1},{13,5},{17,25},{21,29},{10,2},{... | collective-permute-start | bytes 3145736 | tf_op jit(solution)/shard_map/ppermute | solution.py:860
  454.3 12.0 %collective-permute-start.50 = (bf16[2,64,1536]{2,1,0:T(8,128)(2,1)S(1)}, bf16[2,64,1536]{2,1,0:T(8,128)(2,1)S(1)}, u32[]{:S(2)}, u32[]{:S(2)}) collective-permute-start(bf16[2,64,1536]{2,1,0:T(8,128)(2,1)S(1)} %slice_bitcast_fusion.6), channel_id=1, source_target_pairs={{0,2},{1,3},{2,0},{3,1},{4,6},{5,7},{6,4},{7,5},{8,10},{9,11},{10,... | collective-permute-start | bytes 1179656 | tf_op jit(solution)/shard_map/ppermute | solution.py:783
  455.5 10.9 %collective-permute-start.49 = (bf16[2,64,1536]{2,1,0:T(8,128)(2,1)S(1)}, bf16[2,64,1536]{2,1,0:T(8,128)(2,1)S(1)}, u32[]{:S(2)}, u32[]{:S(2)}) collective-permute-start(bf16[2,64,1536]{2,1,0:T(8,128)(2,1)S(1)} %slice_bitcast_fusion.8), channel_id=1, source_target_pairs={{0,1},{1,0},{2,3},{3,2},{4,5},{5,4},{6,7},{7,6},{8,9},{9,8},{10,11... | collective-permute-start | bytes 1179656 | tf_op jit(solution)/shard_map/ppermute | solution.py:783
  457.1 24.1 %collective-permute-start.66 = (bf16[512,1024]{1,0:T(8,128)(2,1)S(1)}, bf16[512,1024]{1,0:T(8,128)(2,1)S(1)}, u32[]{:S(2)}, u32[]{:S(2)}) collective-permute-start(bf16[512,1024]{1,0:T(8,128)(2,1)S(1)} %broadcast_select_fusion.4), channel_id=1, source_target_pairs={{0,4},{4,0},{8,12},{12,8},{16,20},{20,16},{24,28},{28,24},{1,5},{5... | collective-permute-start | bytes 3145736 | tf_op jit(solution)/shard_map/ppermute | solution.py:783
  465.8 15.5 %collective-permute-start.51 = (bf16[4,128,1664]{2,1,0:T(8,128)(2,1)}, bf16[4,128,1664]{2,1,0:T(8,128)(2,1)S(1)}, u32[]{:S(2)}, u32[]{:S(2)}) collective-permute-start(bf16[4,128,1664]{2,1,0:T(8,128)(2,1)} %get-tuple-element.406), channel_id=1, source_target_pairs={{0,4},{4,0},{8,12},{12,8},{16,20},{20,16},{24,28},{28,24},{1,5},{5... | collective-permute-start | bytes 5111816 | tf_op jit(solution)/shard_map/ppermute | solution.py:783
  466.5 14.5 %collective-permute-start.53 = (bf16[1,64,1536]{2,1,0:T(8,128)(2,1)S(1)}, bf16[1,64,1536]{2,1,0:T(8,128)(2,1)S(1)}, u32[]{:S(2)}, u32[]{:S(2)}) collective-permute-start(bf16[1,64,1536]{2,1,0:T(8,128)(2,1)S(1)} %slice_bitcast_fusion.14), channel_id=1, source_target_pairs={{0,1},{1,0},{2,3},{3,2},{4,5},{5,4},{6,7},{7,6},{8,9},{9,8},{10,11... | collective-permute-start | bytes 589832 | tf_op jit(solution)/shard_map/ppermute | solution.py:783
  468.0 13.1 %collective-permute-start.52 = (bf16[1,64,1536]{2,1,0:T(8,128)(2,1)S(1)}, bf16[1,64,1536]{2,1,0:T(8,128)(2,1)S(1)}, u32[]{:S(2)}, u32[]{:S(2)}) collective-permute-start(bf16[1,64,1536]{2,1,0:T(8,128)(2,1)S(1)} %slice_bitcast_fusion.16), channel_id=1, source_target_pairs={{0,2},{1,3},{2,0},{3,1},{4,6},{5,7},{6,4},{7,5},{8,10},{9,11},{10,... | collective-permute-start | bytes 589832 | tf_op jit(solution)/shard_map/ppermute | solution.py:783
  483.3 9.1 %collective-permute-start.56 = (bf16[128,1536]{1,0:T(8,128)(2,1)S(1)}, bf16[128,1536]{1,0:T(8,128)(2,1)S(1)}, u32[]{:S(2)}, u32[]{:S(2)}) collective-permute-start(bf16[128,1536]{1,0:T(8,128)(2,1)S(1)} %pad_maximum_fusion.6), channel_id=1, source_target_pairs={{0,8},{4,12},{24,16},{28,20},{1,9},{5,13},{25,17},{29,21},{2,10},{... | collective-permute-start | bytes 1179656 | tf_op jit(solution)/shard_map/ppermute | solution.py:860
  484.9 10.6 %collective-permute-start.54 = (bf16[2,64,1664]{2,1,0:T(8,128)(2,1)S(1)}, bf16[2,64,1664]{2,1,0:T(8,128)(2,1)S(1)}, u32[]{:S(2)}, u32[]{:S(2)}) collective-permute-start(bf16[2,64,1664]{2,1,0:T(8,128)(2,1)S(1)} %slice_bitcast_fusion.4), channel_id=1, source_target_pairs={{0,1},{1,0},{2,3},{3,2},{4,5},{5,4},{6,7},{7,6},{8,9},{9,8},{10,11... | collective-permute-start | bytes 1277960 | tf_op jit(solution)/shard_map/ppermute | solution.py:783
  486.4 10.5 %collective-permute-start.55 = (bf16[2,64,1664]{2,1,0:T(8,128)(2,1)S(1)}, bf16[2,64,1664]{2,1,0:T(8,128)(2,1)S(1)}, u32[]{:S(2)}, u32[]{:S(2)}) collective-permute-start(bf16[2,64,1664]{2,1,0:T(8,128)(2,1)S(1)} %slice_bitcast_fusion.2), channel_id=1, source_target_pairs={{0,2},{1,3},{2,0},{3,1},{4,6},{5,7},{6,4},{7,5},{8,10},{9,11},{10,... | collective-permute-start | bytes 1277960 | tf_op jit(solution)/shard_map/ppermute | solution.py:783
  487.9 41.9 %collective-permute-start.65 = (bf16[128,5120]{1,0:T(8,128)(2,1)}, bf16[128,5120]{1,0:T(8,128)(2,1)S(1)}, u32[]{:S(2)}, u32[]{:S(2)}) collective-permute-start(bf16[128,5120]{1,0:T(8,128)(2,1)} %all-reduce.5.cloned.1.call-done), channel_id=1, source_target_pairs={{0,4},{4,0},{8,12},{12,8},{16,20},{20,16},{24,28},{28,24},{1,5},{5... | collective-permute-start | bytes 3932168 | tf_op jit(solution)/shard_map/ppermute | solution.py:783
  497.1 5.9 %collective-permute-start.57 = (bf16[1,64,1664]{2,1,0:T(8,128)(2,1)S(1)}, bf16[1,64,1664]{2,1,0:T(8,128)(2,1)S(1)}, u32[]{:S(2)}, u32[]{:S(2)}) collective-permute-start(bf16[1,64,1664]{2,1,0:T(8,128)(2,1)S(1)} %slice_bitcast_fusion.12), channel_id=1, source_target_pairs={{0,2},{1,3},{2,0},{3,1},{4,6},{5,7},{6,4},{7,5},{8,10},{9,11},{10,... | collective-permute-start | bytes 638984 | tf_op jit(solution)/shard_map/ppermute | solution.py:783
  498.7 5.9 %collective-permute-start.58 = (bf16[1,64,1664]{2,1,0:T(8,128)(2,1)S(1)}, bf16[1,64,1664]{2,1,0:T(8,128)(2,1)S(1)}, u32[]{:S(2)}, u32[]{:S(2)}) collective-permute-start(bf16[1,64,1664]{2,1,0:T(8,128)(2,1)S(1)} %slice_bitcast_fusion.10), channel_id=1, source_target_pairs={{0,1},{1,0},{2,3},{3,2},{4,5},{5,4},{6,7},{7,6},{8,9},{9,8},{10,11... | collective-permute-start | bytes 638984 | tf_op jit(solution)/shard_map/ppermute | solution.py:783
  499.1 5.6 collective-permute-start.59
  504.8 17.9 %collective-permute-start.63 = (bf16[128,1536]{1,0:T(8,128)(2,1)S(1)}, bf16[128,1536]{1,0:T(8,128)(2,1)S(1)}, u32[]{:S(2)}, u32[]{:S(2)}) collective-permute-start(bf16[128,1536]{1,0:T(8,128)(2,1)S(1)} %fusion.6), channel_id=1, source_target_pairs={{8,0},{12,4},{16,24},{20,28},{9,1},{13,5},{17,25},{21,29},{10,2},{... | collective-permute-start | bytes 1179656 | tf_op jit(solution)/shard_map/ppermute | solution.py:860
  509.0 20.1 %collective-permute-start.60 = (bf16[128,1664]{1,0:T(8,128)(2,1)S(1)}, bf16[128,1664]{1,0:T(8,128)(2,1)S(1)}, u32[]{:S(2)}, u32[]{:S(2)}) collective-permute-start(bf16[128,1664]{1,0:T(8,128)(2,1)S(1)} %pad_maximum_fusion.5), channel_id=1, source_target_pairs={{0,8},{4,12},{8,0},{12,4},{16,24},{20,28},{24,16},{28,20},{1,9},{5... | collective-permute-start | bytes 1277960 | tf_op jit(solution)/shard_map/ppermute | solution.py:783
  522.8 10.7 %collective-permute-start.64 = (bf16[128,1536]{1,0:T(8,128)(2,1)S(1)}, bf16[128,1536]{1,0:T(8,128)(2,1)S(1)}, u32[]{:S(2)}, u32[]{:S(2)}) collective-permute-start(bf16[128,1536]{1,0:T(8,128)(2,1)S(1)} %broadcast_select_fusion.7), channel_id=1, source_target_pairs={{0,4},{4,0},{8,12},{12,8},{16,20},{20,16},{24,28},{28,24},{1,5},{5... | collective-permute-start | bytes 1179656 | tf_op jit(solution)/shard_map/ppermute | solution.py:783
  529.2 18.6 %collective-permute-start.61 = (bf16[128,1664]{1,0:T(8,128)(2,1)S(1)}, bf16[128,1664]{1,0:T(8,128)(2,1)S(1)}, u32[]{:S(2)}, u32[]{:S(2)}) collective-permute-start(bf16[128,1664]{1,0:T(8,128)(2,1)S(1)} %add_convert_fusion.9), channel_id=1, source_target_pairs={{0,16},{4,20},{8,24},{12,28},{16,0},{20,4},{24,8},{28,12},{1,17},{... | collective-permute-start | bytes 1277960 | tf_op jit(solution)/shard_map/ppermute | solution.py:783
  (38 other events, 440.9 us)
Sparse Core Ops, SparseCore 0:
  261.7 53.2 reduce-scatter.6
  320.8 61.9 reduce-scatter.8
  403.0 74.1 all-reduce.4
